TPU v7x, 32 devices: a whole 2x2x4 slice. The times are simulated.
32 devices in a mesh: groups: 2 (over y), row: 4 (over z), col: 4 (over x, core).
Axes of the slice: x: 2, y: 2, z: 4, core: 2. Of those that a mesh axis runs over, the one named last changes fastest.
Arguments:
- wavefunction: bfloat16 [2048, 4096], P(('groups', 'row'), 'col'), parts along dimension 0, may hold values from -18 to 18, as said below
- left_ops: bfloat16 [8, 8, 256, 256], P(None, ('groups', 'row')), parts along dimension 1, may hold values from -0.125 to 0.125
- right_ops: bfloat16 [8, 32, 256, 256], P(None, ('groups', 'col')), parts along dimension 1, may hold values from -0.375 to 0.375
- left_dest: int32 [8, 8], P(None, 'groups'), parts along dimension 1, may hold values from 0 to 3
- right_src: int32 [8, 32], P(None, 'groups'), parts along dimension 1, may hold values from 0 to 15
- left_sizes: int32 [8], P('groups'), parts along dimension 0, may hold values from 64 to 256, as said below
- right_sizes: int32 [32], P('groups'), parts along dimension 0, may hold values from 64 to 256, as said below
Outputs:
- first_product: bfloat16 [2048, 4096], P(('groups', 'row'), 'col'), parts along dimension 0
- second_product: bfloat16 [2048, 4096], P(('groups', 'row'), 'col'), parts along dimension 0
There are 2 independent parts, one for each index of `groups`. A program takes and returns all parts, laid end to end along the dimension named above; each array names one. Nothing has to cross between parts.
Inputs may be any that keep to these rules, and one draw needn't show every extreme that they name: `wavefunction`: entries of order one. `left_sizes`: each left sector size is between 64 and 256; both ends are taken. `right_sizes`: each right sector size is between 64 and 256; both ends are taken.
All inputs are finite; a program needn't handle non-finite values.
Results may differ from a plain program's by a relative error of at most 0.02.
Values may be sent and summed in bfloat16 or wider, within the bound.
No kernel may reach another device: no remote copies, remote signals or barrier semaphores. Data moves between devices by JAX's collectives and lax.ppermute only.
A program may use at most 64 MiB of HBM per device.

v0:
```python
import jax
import jax.numpy as jnp
from jax import lax
from jax.sharding import PartitionSpec as P


def on_device(wavefunction, left_ops, right_ops, left_dest, right_src, left_sizes, right_sizes):
    tile_size = left_ops.shape[2]
    term_count = left_ops.shape[0]
    right_local = right_ops.shape[1]
    entry_count = (
        wavefunction.shape[0] * lax.axis_size("row") * wavefunction.shape[1] * lax.axis_size("col")
    )
    row_block = lax.axis_index("row")
    col_block = lax.axis_index("col")
    dest_here = lax.dynamic_index_in_dim(left_dest, row_block, 1, keepdims=False)
    source_here = lax.dynamic_slice_in_dim(right_src, col_block * right_local, right_local, 1)
    left_size = lax.dynamic_index_in_dim(left_sizes, row_block, 0, keepdims=False)
    right_here = lax.dynamic_slice_in_dim(right_sizes, col_block * right_local, right_local, 0)
    offsets = jnp.arange(tile_size)
    row_valid = offsets < left_size
    col_valid = (offsets[None, :] < right_here[:, None]).reshape(-1)
    valid_mask = (row_valid[:, None] & col_valid[None, :]).astype(jnp.bfloat16)
    mask_float = valid_mask.astype(jnp.float32)
    left_here = left_ops[:, 0]

    def apply_once(vector):
        gathered = lax.all_gather(vector, "col", axis=1, tiled=True)
        blocks = gathered.reshape(tile_size, -1, tile_size)
        chosen = jnp.take(blocks, source_here, axis=1)
        inner_terms = jnp.einsum(
            "rtjc,tjdc->trjd", chosen, right_ops, preferred_element_type=jnp.float32
        )
        inner_terms = inner_terms.astype(jnp.bfloat16).reshape(term_count, tile_size, -1)
        contrib = jnp.einsum(
            "tab,tbn->tan", left_here, inner_terms, preferred_element_type=jnp.float32
        )
        block_count = tile_size * lax.axis_size("row") // tile_size
        targets = jnp.arange(block_count)
        onehot = (dest_here[:, None] == targets[None, :]).astype(jnp.float32)
        summed = lax.psum_scatter(
            jnp.einsum("tk,tan->kan", onehot, contrib)
            .reshape(tile_size * lax.axis_size("row"), -1)
            .astype(jnp.bfloat16),
            "row",
            scatter_dimension=0,
            tiled=True,
        ).astype(jnp.float32)
        return summed * mask_float

    masked = wavefunction * valid_mask
    masked_float = masked.astype(jnp.float32)
    image = apply_once(masked)
    norm_total, correlation_total = lax.psum(
        (jnp.sum(masked_float * masked_float), jnp.sum(masked_float * image)), ("row", "col")
    )
    scale = lax.rsqrt(norm_total / entry_count + 1e-06)
    theta = correlation_total / norm_total
    first_product = (image * scale).astype(jnp.bfloat16)
    residual = ((image - theta * masked_float) * scale).astype(jnp.bfloat16)
    second_product = apply_once(residual).astype(jnp.bfloat16)
    return (first_product, second_product)


def solution(mesh):
    placed = (
        P(("groups", "row"), "col"),
        P(None, ("groups", "row"), None, None),
        P(None, ("groups", "col"), None, None),
        P(None, "groups"),
        P(None, "groups"),
        P("groups"),
        P("groups"),
    )
    return jax.shard_map(
        on_device,
        mesh=mesh,
        in_specs=placed,
        out_specs=(P(("groups", "row"), "col"), P(("groups", "row"), "col")),
        check_vma=False,
    )
```

profile of v0, /device:TPU:0, one launch (start us, length us, event | category | flops | bytes accessed | tf_op | source)
XLA Modules:
  0.0 248.3 jit_solution(12779049722175850043)
XLA Ops:
  7.2 0.0 copy-start
  7.2 0.0 all-gather.3.cloned.1.call-start
  7.2 1.3 dynamic_slice.15
  8.5 0.6 iota_compare_fusion.2
  9.2 0.7 dynamic_slice.16
  9.9 0.1 iota_compare_fusion
  10.0 1.2 copy.13
  11.3 0.0 copy-start.1
  11.3 1.0 and_select_fusion
  12.3 0.0 all-gather.3.cloned.1.call-update
  12.3 0.0 reduce-scatter.3.cloned.1.call-start
  12.4 0.8 compare_and_fusion
  13.2 0.1 reshape.68
  13.2 0.7 dynamic-slice_bitcast_fusion
  13.9 23.9 %all-gather.3.cloned.1.call-done = bf16[256,4096]{0,1:T(8,128)(2,1)} async-done(((bf16[256,1024]{0,1:T(8,128)(2,1)}), bf16[256,4096]{0,1:T(8,128)(2,1)}) %all-gather.3.cloned.1.call-update) | async-done | bytes 2097168 | tf_op jit(solution)/shard_map/all_gather | solution.py:28
  37.8 0.0 copy-done.1
  37.8 2.8 %copy.14 = bf16[256,16,256]{2,0,1:T(8,128)(2,1)S(1)} copy(bf16[256,16,256]{0,2,1:T(8,128)(2,1)} %bitcast.50) | data formatting | bytes 4194304 | tf_op jit(solution)/shard_map/reshape | solution.py:29
  40.7 2.8 %gather_fusion = bf16[32,256,256]{2,1,0:T(8,128)(2,1)} fusion(bf16[256,16,256]{2,0,1:T(8,128)(2,1)S(1)} %copy.14, s32[1024]{0:T(1024)S(1)} %pad_clamp_fusion), kind=kCustom, calls=%fused_computation.clone | custom fusion | bytes 8388736 | tf_op jit(solution)/shard_map/jit(_take)/gather | solution.py:30
  43.5 4.8 %fusion.8 = bf16[8,4,256,256]{2,3,1,0:T(8,128)(2,1)S(1)} fusion(bf16[8,4,256,256]{3,2,1,0:T(8,128)(2,1)} %param.11, bf16[8,4,256,256]{3,2,1,0:T(8,128)(2,1)} %bitcast.49, pred[8,4]{1,0:T(8,128)(4,1)S(1)} %get-tuple-element.9), kind=kOutput, calls=%fused_computation.12 | convolution fusion | flops 1077936128 | bytes 12582944 | tf_op jit(solution)/shard_map/rtjc,tjdc->trjd/dot_general | solution.py:31
  48.3 0.0 copy-done
  48.3 3.2 %convolution_bitcast_fusion.1 = bf16[8,256,1024]{1,2,0:T(8,128)(2,1)} fusion(bf16[8,256,1024]{1,2,0:T(8,128)(2,1)S(1)} %bitcast.47, bf16[8,1,256,256]{3,2,1,0:T(8,128)(2,1)S(1)} %copy-done), kind=kOutput, calls=%fused_computation.11 | convolution fusion | flops 1073741824 | bytes 9437184 | tf_op jit(solution)/shard_map/tab,tbn->tan/dot_general | solution.py:35
  51.6 6.8 %copy.15 = bf16[8,256,1024]{2,0,1:T(8,128)(2,1)} copy(bf16[8,256,1024]{1,2,0:T(8,128)(2,1)} %convolution_bitcast_fusion.1) | data formatting | bytes 8388608 | tf_op jit(solution)/shard_map/tab,tbn->tan/dot_general | solution.py:35
  58.4 3.4 %convolution_convert_fusion.1 = bf16[4,256,1024]{2,0,1:T(4,128)(2,1)S(1)} fusion(bf16[8,256,1024]{2,0,1:T(8,128)(2,1)} %copy.15, s32[8]{0:T(128)S(1)} %dynamic-slice_bitcast_fusion), kind=kOutput, calls=%fused_computation.17 | convolution fusion | flops 16777248 | bytes 6291488 | tf_op jit(solution)/shard_map/tk,tan->kan/dot_general | solution.py:42
  61.8 0.6 copy.16
  62.4 2.6 %copy.17 = bf16[1024,1024]{0,1:T(8,128)(2,1)} copy(bf16[1024,1024]{1,0:T(8,128)(2,1)S(1)} %bitcast.44) | data formatting | bytes 4194304 | tf_op jit(solution)/shard_map/convert_element_type | solution.py:44
  65.0 0.0 reduce-scatter.3.cloned.1.call-update
  65.0 0.0 all-gather.5.cloned.1.call-start
  65.1 44.0 %reduce-scatter.3.cloned.1.call-done = bf16[256,1024]{0,1:T(8,128)(2,1)} async-done(((bf16[1024,1024]{0,1:T(8,128)(2,1)}), bf16[256,1024]{0,1:T(8,128)(2,1)}) %reduce-scatter.3.cloned.1.call-update) | async-done | bytes 524304 | tf_op jit(solution)/shard_map/reduce_scatter | solution.py:41
  109.1 2.4 fusion.18
  111.5 32.1 %all-reduce = (f32[]{:T(128)}, f32[]{:T(128)}) all-reduce(f32[]{:T(128)} %get-tuple-element.6, f32[]{:T(128)} %get-tuple-element.5), channel_id=1, replica_groups=mesh['groups'=2,'row'=4,'col'=4] {'row','col'}, use_global_device_ids=true, to_apply=%region_2.4 | all-reduce | flops 2 | bytes 16 | tf_op jit(solution)/shard_map/psum | solution.py:54
  145.6 2.6 %fusion.21 = (bf16[256,1024]{0,1:T(8,128)(2,1)}, bf16[256,1024]{0,1:T(8,128)(2,1)}) fusion(bf16[256,1024]{0,1:T(8,128)(2,1)} %reduce-scatter.3.cloned.1.call-done, f32[]{:T(128)S(6)} %div.7, f32[]{:T(128)S(6)} %rsqrt.3, pred[256]{0:T(512)(128)(4,1)S(1)} %iota_compare_fusion.2, pred[1024]{0:T(1024)(128)(4,1)S(1)} %lt.53, bf16[256,1024]{0,1:T(8,128)(2,1)} %copy-done.1), kind=kLoop, calls=%fused_computation.30 | loop fusion | flops 3407872 | bytes 2098440 | tf_op jit(solution)/shard_map/convert_element_type | solution.py:60
  148.2 0.0 all-gather.5.cloned.1.call-update
  148.3 0.2 reduce-scatter.5.cloned.1.call-start
  148.5 19.7 %all-gather.5.cloned.1.call-done = bf16[256,4096]{0,1:T(8,128)(2,1)} async-done(((bf16[256,1024]{0,1:T(8,128)(2,1)}), bf16[256,4096]{0,1:T(8,128)(2,1)}) %all-gather.5.cloned.1.call-update) | async-done | bytes 2097168 | tf_op jit(solution)/shard_map/all_gather | solution.py:28
  168.2 2.8 %copy.18 = bf16[256,16,256]{2,0,1:T(8,128)(2,1)S(1)} copy(bf16[256,16,256]{0,2,1:T(8,128)(2,1)} %bitcast.51) | data formatting | bytes 4194304 | tf_op jit(solution)/shard_map/reshape | solution.py:29
  171.1 2.8 %gather_fusion.1 = bf16[32,256,256]{2,1,0:T(8,128)(2,1)} fusion(bf16[256,16,256]{2,0,1:T(8,128)(2,1)S(1)} %copy.18, s32[1024]{0:T(1024)S(1)} %pad_clamp_fusion), kind=kCustom, calls=%fused_computation.1.clone | custom fusion | bytes 8388736 | tf_op jit(solution)/shard_map/jit(_take)/gather | solution.py:30
  173.9 4.8 %fusion.11 = bf16[8,4,256,256]{2,3,1,0:T(8,128)(2,1)S(1)} fusion(bf16[8,4,256,256]{3,2,1,0:T(8,128)(2,1)} %param.11, bf16[8,4,256,256]{3,2,1,0:T(8,128)(2,1)} %bitcast.48, pred[8,4]{1,0:T(8,128)(4,1)S(1)} %get-tuple-element.9), kind=kOutput, calls=%fused_computation.13 | convolution fusion | flops 1077936128 | bytes 12582944 | tf_op jit(solution)/shard_map/rtjc,tjdc->trjd/dot_general | solution.py:31
  178.7 3.2 %convolution_bitcast_fusion = bf16[8,256,1024]{1,2,0:T(8,128)(2,1)} fusion(bf16[8,256,1024]{1,2,0:T(8,128)(2,1)S(1)} %bitcast.46, bf16[8,1,256,256]{3,2,1,0:T(8,128)(2,1)S(1)} %copy-done), kind=kOutput, calls=%fused_computation.10 | convolution fusion | flops 1073741824 | bytes 9437184 | tf_op jit(solution)/shard_map/tab,tbn->tan/dot_general | solution.py:35
  181.9 6.8 %copy.19 = bf16[8,256,1024]{2,0,1:T(8,128)(2,1)} copy(bf16[8,256,1024]{1,2,0:T(8,128)(2,1)} %convolution_bitcast_fusion) | data formatting | bytes 8388608 | tf_op jit(solution)/shard_map/tab,tbn->tan/dot_general | solution.py:35
  188.8 3.4 %convolution_convert_fusion = bf16[4,256,1024]{2,0,1:T(4,128)(2,1)S(1)} fusion(bf16[8,256,1024]{2,0,1:T(8,128)(2,1)} %copy.19, s32[8]{0:T(128)S(1)} %dynamic-slice_bitcast_fusion), kind=kOutput, calls=%fused_computation.16 | convolution fusion | flops 16777248 | bytes 6291488 | tf_op jit(solution)/shard_map/tk,tan->kan/dot_general | solution.py:42
  192.2 0.6 copy.20
  192.8 2.6 %copy.21 = bf16[1024,1024]{0,1:T(8,128)(2,1)} copy(bf16[1024,1024]{1,0:T(8,128)(2,1)S(1)} %bitcast.45) | data formatting | bytes 4194304 | tf_op jit(solution)/shard_map/convert_element_type | solution.py:44
  195.4 0.0 reduce-scatter.5.cloned.1.call-update
  195.4 2.0 copy.22
  197.5 42.0 %reduce-scatter.5.cloned.1.call-done = bf16[256,1024]{0,1:T(8,128)(2,1)} async-done(((bf16[1024,1024]{0,1:T(8,128)(2,1)}), bf16[256,1024]{0,1:T(8,128)(2,1)}) %reduce-scatter.5.cloned.1.call-update) | async-done | bytes 524304 | tf_op jit(solution)/shard_map/reduce_scatter | solution.py:41
  239.5 1.3 fusion.16
  240.8 1.0 copy.23
  (2 shorter events, 0.0 us)
Async XLA Ops:
  7.2 41.1 %copy-start = (bf16[8,1,256,256]{3,2,1,0:T(8,128)(2,1)S(1)}, bf16[8,1,256,256]{3,2,1,0:T(8,128)(2,1)}, u32[]{:S(2)}) copy-start(bf16[8,1,256,256]{3,2,1,0:T(8,128)(2,1)} %param.10) | copy-start | bytes 3145732
  7.2 30.7 %all-gather.3.cloned.1.call-start = ((), (), s32[]{:S(2)}) async-start(), calls=%async_computation.2 | async-start | bytes 2621440 | tf_op jit(solution)/shard_map/all_gather | solution.py:28
  11.3 26.6 %copy-start.1 = (bf16[256,1024]{0,1:T(8,128)(2,1)}, bf16[256,1024]{0,1:T(8,128)(2,1)S(1)}, u32[]{:S(2)}) copy-start(bf16[256,1024]{0,1:T(8,128)(2,1)S(1)} %copy.13) | copy-start | bytes 1572868
  12.3 96.7 %reduce-scatter.3.cloned.1.call-start = ((), (), s32[]{:S(2)}) async-start(), calls=%async_computation.3 | async-start | bytes 2621440 | tf_op jit(solution)/shard_map/reduce_scatter | solution.py:41
  65.0 103.2 %all-gather.5.cloned.1.call-start = ((), (), s32[]{:S(2)}) async-start(), calls=%async_computation.4 | async-start | bytes 2621440 | tf_op jit(solution)/shard_map/all_gather | solution.py:28
  148.3 91.2 %reduce-scatter.5.cloned.1.call-start = ((), (), s32[]{:S(2)}) async-start(), calls=%async_computation.5 | async-start | bytes 2621440 | tf_op jit(solution)/shard_map/reduce_scatter | solution.py:41
Sparse Core Ops, SparseCore 0:
  12.5 25.3 all-gather.2
  65.2 43.8 reduce-scatter.2
  148.4 19.8 all-gather.4
  195.5 43.8 reduce-scatter.4
where the time goes:
time: 249 us; the launch traced here: 248 us
  waiting for transfers between devices  130 us (52%)
  local copies, waits for them, and re-layouts  38.4 us (15%)
  blocking collectives  32.1 us (13%)
  matrix products  23 us (9%)
  between operations  15.8 us (6%)
  other arithmetic  8.87 us (4%)
    reduce_scatter x2, waiting for transfers between devices, apply_once(): lax.psum_scatter(jnp.einsum('tk,tan->kan', onehot, contrib).reshape(tile_...  86 us
    all_gather x2, waiting for transfers between devices, apply_once(): gathered = lax.all_gather(vector, 'col', axis=1, tiled=True)  43.6 us
    psum x1, blocking collectives, on_device(): lax.psum((jnp.sum(masked_float * masked_float), jnp.sum(masked_float * im...  32.1 us
    dot_general x2, local copies, waits for them, and re-layouts, apply_once(): jnp.einsum('tab,tbn->tan', left_here, inner_terms, preferred_element_type...  13.7 us
    dot_general x2, matrix products, apply_once(): jnp.einsum('rtjc,tjdc->trjd', chosen, right_ops, preferred_element_type=j...  9.68 us
    dot_general x2, matrix products, apply_once(): jnp.einsum('tk,tan->kan', onehot, contrib)  6.84 us
    dot_general x2, matrix products, apply_once(): jnp.einsum('tab,tbn->tan', left_here, inner_terms, preferred_element_type...  6.49 us
    convert_element_type x4, local copies, waits for them, and re-layouts, apply_once(): summed = lax.psum_scatter(jnp.einsum('tk,tan->kan', onehot, contrib).resh...  6.39 us
  transfers between devices with their start and end apart: 4, of which 4 were waited for; matrix products, arithmetic and copies ran while one was open for 1% of the time, Pallas kernels for 0%

commit v1 on v0

v1 whole, which is shorter than its diff:
```python
import functools

import jax
import jax.numpy as jnp
from jax import lax
from jax.experimental import pallas as pl
from jax.experimental.pallas import tpu as pltpu
from jax.sharding import PartitionSpec as P

CHUNKS = 2


def swap(axis, bit):
    size = lax.axis_size(axis)
    return [(place, place ^ bit) for place in range(size)]


def bits_of(size):
    count = size.bit_length() - 1
    assert 1 << count == size
    return count


def reverse_bits(value, count):
    out = jnp.zeros_like(value)
    for bit in range(count):
        out = out | (((value >> bit) & 1) << (count - 1 - bit))
    return out


def product_kernel(first, piece_count, local, slots, src_ref, dest_ref, *refs):
    pieces = refs[:piece_count]
    left_ref, right_ref, out_ref, blocks, total = refs[piece_count:]
    tile = left_ref.shape[1]
    terms = left_ref.shape[0]
    step = pl.program_id(0)

    @pl.when(step == 0)
    def _():
        for piece in range(piece_count):
            for place in range(local):
                blocks[piece * local + place] = pieces[piece][:, place * tile:(place + 1) * tile]

    total[...] = jnp.zeros_like(total)
    for term in range(terms):
        rows = blocks[src_ref[term, first + step]]
        inner = lax.dot_general(
            rows, right_ref[term, 0], (((1,), (1,)), ((), ())), preferred_element_type=jnp.float32
        ).astype(jnp.bfloat16)
        total[dest_ref[term]] += jnp.dot(left_ref[term], inner, preferred_element_type=jnp.float32)
    out_ref[...] = total[...].astype(jnp.bfloat16)


def products(pieces, left, right, source, target, slots, first, count):
    terms, tile = left.shape[:2]
    local = right.shape[1]
    whole = lambda step, *tables: (0, 0)
    return pl.pallas_call(
        functools.partial(product_kernel, first, len(pieces), local, slots),
        grid_spec=pltpu.PrefetchScalarGridSpec(
            num_scalar_prefetch=2,
            grid=(count,),
            in_specs=[pl.BlockSpec((tile, local * tile), whole) for _ in pieces] + [
                pl.BlockSpec((terms, tile, tile), lambda step, *tables: (0, 0, 0)),
                pl.BlockSpec((terms, 1, tile, tile), lambda step, *tables: (0, first + step, 0, 0)),
            ],
            out_specs=pl.BlockSpec((slots, tile, tile), lambda step, *tables: (0, 0, step)),
            scratch_shapes=[
                pltpu.VMEM((len(pieces) * local, tile, tile), jnp.bfloat16),
                pltpu.VMEM((slots, tile, tile), jnp.float32),
            ],
        ),
        out_shape=jax.ShapeDtypeStruct((slots, tile, count * tile), jnp.bfloat16),
        compiler_params=pltpu.CompilerParams(vmem_limit_bytes=40 * 1024 * 1024),
        cost_estimate=pl.CostEstimate(
            flops=4 * terms * count * tile**3, bytes_accessed=terms * (count + 1) * tile * tile * 2, transcendentals=0
        ),
    )(source, target, *pieces, left, right)


def on_device(wavefunction, left_ops, right_ops, left_dest, right_src, left_sizes, right_sizes):
    tile = left_ops.shape[2]
    local = right_ops.shape[1]
    row_count, col_count = lax.axis_size("row"), lax.axis_size("col")
    row_bits, col_bits = bits_of(row_count), bits_of(col_count)
    entry_count = wavefunction.shape[0] * row_count * wavefunction.shape[1] * col_count
    row, col = lax.axis_index("row"), lax.axis_index("col")
    dest_here = lax.dynamic_index_in_dim(left_dest, row, 1, keepdims=False)
    source_here = lax.dynamic_slice_in_dim(right_src, col * local, local, 1)
    left_size = lax.dynamic_index_in_dim(left_sizes, row, 0, keepdims=False)
    right_here = lax.dynamic_slice_in_dim(right_sizes, col * local, local, 0)
    offsets = jnp.arange(tile)
    row_valid = offsets < left_size
    col_valid = (offsets[None, :] < right_here[:, None]).reshape(-1)
    valid = row_valid[:, None] & col_valid[None, :]
    left_here = left_ops[:, 0]
    source = ((source_here // local) ^ col) * local + source_here % local
    target = reverse_bits(dest_here ^ row, row_bits)

    def gather(part):
        pieces = {0: part}
        for bit in reversed(range(col_bits)):
            for place in list(pieces):
                pieces[place | (1 << bit)] = lax.ppermute(pieces[place], "col", swap("col", 1 << bit))
        return [pieces[place] for place in range(col_count)]

    def scatter_sum(sums):
        for bit in range(row_bits):
            half = sums.shape[0] // 2
            arrived = lax.ppermute(sums[half:], "row", swap("row", 1 << bit))
            total = sums[:half].astype(jnp.float32) + arrived.astype(jnp.float32)
            sums = total.astype(jnp.bfloat16) if bit < row_bits - 1 else total
        return sums[0]

    def apply_h(pieces):
        step = local // CHUNKS
        out = []
        for first in range(0, local, step):
            sums = products(pieces, left_here, right_ops, source, target, row_count, first, step)
            out.append(scatter_sum(sums))
        return out

    masked = jnp.where(valid, wavefunction, 0)
    masked_float = masked.astype(jnp.float32)
    width = wavefunction.shape[1] // CHUNKS
    parts = apply_h(gather(masked))
    parts = [jnp.where(valid[:, i * width:(i + 1) * width], part, 0.0) for i, part in enumerate(parts)]
    image_pieces = [gather(part.astype(jnp.bfloat16)) for part in parts]
    image_pieces = [jnp.concatenate(several, 1) for several in zip(*image_pieces)]
    image = jnp.concatenate(parts, 1)
    own = jnp.stack([jnp.sum(masked_float * masked_float), jnp.sum(masked_float * image)])
    sums = jnp.sum(lax.all_gather(jnp.broadcast_to(own[:, None], (2, 128)), ("row", "col")), 0)
    norm_total, correlation_total = sums[0, 0], sums[1, 0]
    scale = lax.rsqrt(norm_total / entry_count + 1e-06)
    theta = correlation_total / norm_total
    first_product = (image * scale).astype(jnp.bfloat16)
    again = jnp.concatenate(apply_h(image_pieces), 1)
    second_product = jnp.where(valid, (again - theta * image) * scale, 0.0).astype(jnp.bfloat16)
    return (first_product, second_product)


def solution(mesh):
    placed = (
        P(("groups", "row"), "col"),
        P(None, ("groups", "row"), None, None),
        P(None, ("groups", "col"), None, None),
        P(None, "groups"),
        P(None, "groups"),
        P("groups"),
        P("groups"),
    )
    return jax.shard_map(
        on_device,
        mesh=mesh,
        in_specs=placed,
        out_specs=(P(("groups", "row"), "col"), P(("groups", "row"), "col")),
        check_vma=False,
    )
```

time: 249 us -> 167 us (0.67)
  waiting for transfers between devices: 130 us -> 70.6 us
  local copies, waits for them, and re-layouts: 38.4 us -> 13.3 us
  matrix products: 23 us -> 0 us
  starting transfers between devices: 0.34 us -> 17.4 us
  Pallas kernels: 0 us -> 13.2 us
  between operations: 15.8 us -> 3.56 us
  blocking collectives: 32.1 us -> 36.5 us
  other arithmetic: 8.87 us -> 11.6 us
    reduce_scatter x2 -> x0, waiting for transfers between devices: 86 us -> none  [apply_once(): lax.psum_scatter(jnp.einsum('tk,tan->kan', onehot, contrib).reshape(tile_...]
    ppermute x0 -> x17, waiting for transfers between devices: none -> 70.6 us  [the longest x8 46.5 us: scatter_sum(): arrived = lax.ppermute(sums[half:], 'row', swap('row', 1 << bit))]
    all_gather x2 -> x0, waiting for transfers between devices: 43.6 us -> none  [apply_once(): gathered = lax.all_gather(vector, 'col', axis=1, tiled=True)]
    unnamed x0 -> x1, blocking collectives: none -> 36.5 us
    psum x1 -> x0, blocking collectives: 32.1 us -> none  [on_device(): lax.psum((jnp.sum(masked_float * masked_float), jnp.sum(masked_float * im...]
    dot_general x6 -> x0, matrix products: 23 us -> none  [the longest x2 9.68 us: apply_once(): jnp.einsum('rtjc,tjdc->trjd', chosen, right_ops, preferred_element_type=j...]
    ppermute x0 -> x17, starting transfers between devices: none -> 17.4 us  [the longest x8 12.1 us: scatter_sum(): arrived = lax.ppermute(sums[half:], 'row', swap('row', 1 << bit))]
    dot_general x2 -> x0, local copies, waits for them, and re-layouts: 13.7 us -> none  [apply_once(): jnp.einsum('tab,tbn->tan', left_here, inner_terms, preferred_element_type...]
  transfers between devices with their start and end apart: 4 -> 17, of which waited for: 4 -> 10; matrix products, arithmetic and copies ran while one was open for 1% -> 5% of each run, Pallas kernels for 0% -> 4%
where the time goes in v1:
time: 167 us; the launch traced here: 166 us
  waiting for transfers between devices  70.6 us (42%)
  blocking collectives  36.5 us (22%)
  starting transfers between devices  17.4 us (10%)
  local copies, waits for them, and re-layouts  13.3 us (8%)
  Pallas kernels  13.2 us (8%)
  other arithmetic  11.6 us (7%)
  between operations  3.56 us (2%)
    ppermute x8, waiting for transfers between devices, scatter_sum(): arrived = lax.ppermute(sums[half:], 'row', swap('row', 1 << bit))  46.5 us
    unnamed x1, blocking collectives  36.5 us
    ppermute x9, waiting for transfers between devices, gather(): lax.ppermute(pieces[place], 'col', swap('col', 1 << bit))  24.1 us
    pallas_call x4, Pallas kernels, products(): pl.pallas_call(functools.partial(product_kernel, first, len(pieces), loca...  13.2 us
    ppermute x8, starting transfers between devices, scatter_sum(): arrived = lax.ppermute(sums[half:], 'row', swap('row', 1 << bit))  12.1 us
    unnamed x37, local copies, waits for them, and re-layouts  9.41 us
    ppermute x9, starting transfers between devices, gather(): lax.ppermute(pieces[place], 'col', swap('col', 1 << bit))  5.27 us
  transfers between devices with their start and end apart: 17, of which 10 were waited for; matrix products, arithmetic and copies ran while one was open for 5% of the time, Pallas kernels for 4%

profile of v1, /device:TPU:0, one launch (start us, length us, event | category | flops | bytes accessed | tf_op | source)
XLA Modules:
  0.0 166.1 jit_solution(6413490170386381127)
XLA Ops:
  0.6 1.2 dynamic_slice.14
  1.9 0.6 iota_compare_fusion.1
  2.5 0.7 dynamic_slice.15
  3.4 1.3 and_select_fusion.refs_0_
  4.6 3.0 %collective-permute-start.1 = (bf16[256,1024]{1,0:T(8,128)(2,1)S(1)}, bf16[256,1024]{1,0:T(8,128)(2,1)S(1)}, u32[]{:S(2)}, u32[]{:S(2)}) collective-permute-start(bf16[256,1024]{1,0:T(8,128)(2,1)S(1)} %and_select_fusion.refs_0_), channel_id=1, source_target_pairs={{0,2},{1,3},{2,0},{3,1},{4,6},{5,7},{6,4},{7,5},{8,10},{9,11},{10,... | collective-permute-start | bytes 1572872 | tf_op jit(solution)/shard_map/ppermute | solution.py:104
  7.6 11.9 %collective-permute-done.1.refs_2_ = bf16[256,1024]{1,0:T(8,128)(2,1)S(1)} collective-permute-done((bf16[256,1024]{1,0:T(8,128)(2,1)S(1)}, bf16[256,1024]{1,0:T(8,128)(2,1)S(1)}, u32[]{:S(2)}, u32[]{:S(2)}) %collective-permute-start.1) | collective-permute-done | bytes 524320 | tf_op jit(solution)/shard_map/ppermute | solution.py:104
  19.6 0.7 or_bitcast_fusion.dest_ref
  20.3 0.8 fusion.7.src_ref
  21.0 0.4 collective-permute-done.2.refs_3_
  21.5 2.2 %copy-done = bf16[8,4,256,256]{3,2,1,0:T(8,128)(2,1)S(1)} copy-done((bf16[8,4,256,256]{3,2,1,0:T(8,128)(2,1)S(1)}, bf16[8,4,256,256]{3,2,1,0:T(8,128)(2,1)}, u32[]{:S(2)}) %copy-start) | copy-done | bytes 4194328
  23.7 1.2 copy-done.3
  24.9 3.3 %shard_map.87 = bf16[4,256,512]{2,1,0:T(8,128)(2,1)S(1)} custom-call(s32[8,4]{1,0:T(8,128)S(1)} %fusion.7.src_ref, s32[8]{0:T(128)S(1)} %or_bitcast_fusion.dest_ref, bf16[256,1024]{1,0:T(8,128)(2,1)S(1)} %and_select_fusion.refs_0_, bf16[256,1024]{1,0:T(8,128)(2,1)S(1)} %collective-permute-done.refs_1_, bf16[256,1024]{1,0:T(8,128)(2,1)S(1)} %collective-permute-done.1.refs_2_, ...), custom_call_target="tpu_custom_call" | custom-call | flops 1073741824 | bytes 3145728 | tf_op jit(solution)/shard_map/pallas_call | solution.py:58
  28.2 1.9 %collective-permute-start.5 = (bf16[2,256,512]{2,1,0:T(8,128)(2,1)S(1)}, bf16[2,256,512]{2,1,0:T(8,128)(2,1)S(1)}, u32[]{:S(2)}, u32[]{:S(2)}) collective-permute-start(bf16[2,256,512]{2,1,0:T(8,128)(2,1)S(1)} %slice.87), channel_id=1, source_target_pairs={{0,4},{4,0},{8,12},{12,8},{1,5},{5,1},{9,13},{13,9},{2,6},{6,2},{1... | collective-permute-start | bytes 1572872 | tf_op jit(solution)/shard_map/ppermute | solution.py:110
  30.1 3.3 %shard_map.86 = bf16[4,256,512]{2,1,0:T(8,128)(2,1)S(1)} custom-call(s32[8,4]{1,0:T(8,128)S(1)} %fusion.7.src_ref, s32[8]{0:T(128)S(1)} %or_bitcast_fusion.dest_ref, bf16[256,1024]{1,0:T(8,128)(2,1)S(1)} %and_select_fusion.refs_0_, bf16[256,1024]{1,0:T(8,128)(2,1)S(1)} %collective-permute-done.refs_1_, bf16[256,1024]{1,0:T(8,128)(2,1)S(1)} %collective-permute-done.1.refs_2_, ...), custom_call_target="tpu_custom_call" | custom-call | flops 1073741824 | bytes 3145728 | tf_op jit(solution)/shard_map/pallas_call | solution.py:58
  33.5 0.3 collective-permute-start.3
  33.7 9.3 %collective-permute-done.5 = bf16[2,256,512]{2,1,0:T(8,128)(2,1)S(1)} collective-permute-done((bf16[2,256,512]{2,1,0:T(8,128)(2,1)S(1)}, bf16[2,256,512]{2,1,0:T(8,128)(2,1)S(1)}, u32[]{:S(2)}, u32[]{:S(2)}) %collective-permute-start.5) | collective-permute-done | bytes 524320 | tf_op jit(solution)/shard_map/ppermute | solution.py:110
  43.2 2.9 %collective-permute-start.6 = (bf16[1,256,512]{2,1,0:T(8,128)(2,1)S(1)}, bf16[1,256,512]{2,1,0:T(8,128)(2,1)S(1)}, u32[]{:S(2)}, u32[]{:S(2)}) collective-permute-start(bf16[1,256,512]{2,1,0:T(8,128)(2,1)S(1)} %slice.89), channel_id=1, source_target_pairs={{0,8},{4,12},{8,0},{12,4},{1,9},{5,13},{9,1},{13,5},{2,10},{6,14},... | collective-permute-start | bytes 786440 | tf_op jit(solution)/shard_map/ppermute | solution.py:110
  46.1 13.1 %collective-permute-done.3 = bf16[2,256,512]{2,1,0:T(8,128)(2,1)S(1)} collective-permute-done((bf16[2,256,512]{2,1,0:T(8,128)(2,1)S(1)}, bf16[2,256,512]{2,1,0:T(8,128)(2,1)S(1)}, u32[]{:S(2)}, u32[]{:S(2)}) %collective-permute-start.3) | collective-permute-done | bytes 524320 | tf_op jit(solution)/shard_map/ppermute | solution.py:110
  59.4 1.9 %collective-permute-start.4 = (bf16[1,256,512]{2,1,0:T(8,128)(2,1)S(1)}, bf16[1,256,512]{2,1,0:T(8,128)(2,1)S(1)}, u32[]{:S(2)}, u32[]{:S(2)}) collective-permute-start(bf16[1,256,512]{2,1,0:T(8,128)(2,1)S(1)} %slice.84), channel_id=1, source_target_pairs={{0,8},{4,12},{8,0},{12,4},{1,9},{5,13},{9,1},{13,5},{2,10},{6,14},... | collective-permute-start | bytes 786440 | tf_op jit(solution)/shard_map/ppermute | solution.py:110
  61.3 0.2 broadcast_and_fusion
  61.5 12.1 %collective-permute-done.4 = bf16[1,256,512]{2,1,0:T(8,128)(2,1)S(1)} collective-permute-done((bf16[1,256,512]{2,1,0:T(8,128)(2,1)S(1)}, bf16[1,256,512]{2,1,0:T(8,128)(2,1)S(1)}, u32[]{:S(2)}, u32[]{:S(2)}) %collective-permute-start.4) | collective-permute-done | bytes 262176 | tf_op jit(solution)/shard_map/ppermute | solution.py:110
  73.6 1.2 fusion.12
  74.8 1.6 collective-permute-start.9
  76.3 0.5 collective-permute-start.10
  76.8 0.2 collective-permute-start.8
  77.1 6.9 %collective-permute-done.9 = bf16[256,512]{1,0:T(8,128)(2,1)S(1)} collective-permute-done((bf16[256,512]{1,0:T(8,128)(2,1)S(1)}, bf16[256,512]{1,0:T(8,128)(2,1)S(1)}, u32[]{:S(2)}, u32[]{:S(2)}) %collective-permute-start.9) | collective-permute-done | bytes 262176 | tf_op jit(solution)/shard_map/ppermute | solution.py:104
  84.1 3.4 %collective-permute-done.10 = bf16[256,512]{1,0:T(8,128)(2,1)S(1)} collective-permute-done((bf16[256,512]{1,0:T(8,128)(2,1)S(1)}, bf16[256,512]{1,0:T(8,128)(2,1)S(1)}, u32[]{:S(2)}, u32[]{:S(2)}) %collective-permute-start.10) | collective-permute-done | bytes 262176 | tf_op jit(solution)/shard_map/ppermute | solution.py:104
  87.7 1.4 collective-permute-done.12
  89.1 3.3 %shard_map.89 = bf16[4,256,512]{2,1,0:T(8,128)(2,1)S(1)} custom-call(s32[8,4]{1,0:T(8,128)S(1)} %fusion.7.src_ref, s32[8]{0:T(128)S(1)} %or_bitcast_fusion.dest_ref, bf16[256,1024]{1,0:T(8,128)(2,1)S(1)} %pad_maximum_fusion.1.refs_0_, bf16[256,1024]{1,0:T(8,128)(2,1)S(1)} %constant_dynamic-update-slice_fusion.refs_1_, ...), custom_call_target="tpu_custom_call" | custom-call | flops 1073741824 | bytes 3145728 | tf_op jit(solution)/shard_map/pallas_call | solution.py:58
  92.5 0.8 slice.95
  93.3 0.9 collective-permute-start.15
  94.3 0.6 dynamic-slice
  95.5 2.2 %copy-done.2 = bf16[8,4,256,256]{3,2,1,0:T(8,128)(2,1)S(1)} copy-done((bf16[8,4,256,256]{3,2,1,0:T(8,128)(2,1)S(1)}, bf16[8,4,256,256]{3,2,1,0:T(8,128)(2,1)}, u32[]{:S(2)}) %copy-start.2) | copy-done | bytes 4194328
  97.7 1.0 copy-done.7
  98.7 1.0 copy-done.9
  99.8 3.3 %shard_map.88 = bf16[4,256,512]{2,1,0:T(8,128)(2,1)S(1)} custom-call(s32[8,4]{1,0:T(8,128)S(1)} %fusion.7.src_ref, s32[8]{0:T(128)S(1)} %or_bitcast_fusion.dest_ref, bf16[256,1024]{1,0:T(8,128)(2,1)S(1)} %pad_maximum_fusion.1.refs_0_, bf16[256,1024]{1,0:T(8,128)(2,1)S(1)} %constant_dynamic-update-slice_fusion.refs_1_, bf16[256,1024]{1,0:T(8,128)(2,1)S(1)} %copy-done.7, ...), custom_call_target="tpu_custom_call" | custom-call | flops 1073741824 | bytes 3145728 | tf_op jit(solution)/shard_map/pallas_call | solution.py:58
  103.1 1.0 copy-done.5
  104.1 1.2 collective-permute-start.13
  105.3 1.1 fusion
  106.4 1.4 maximum_dynamic-update-slice_fusion
  107.9 36.5 %all-reduce = f32[32]{0:T(128)S(1)} all-reduce(f32[32]{0:T(128)S(1)} %maximum_dynamic-update-slice_fusion), channel_id=3, replica_groups=mesh['groups'=2,'row'=4,'col'=4] {'row','col'}, use_global_device_ids=true, to_apply=%add | all-reduce | flops 32 | bytes 256
  144.6 1.2 add_convert_fusion
  145.9 1.2 add_convert_fusion.1
  147.2 3.0 %collective-permute-start.14 = (bf16[1,256,512]{2,1,0:T(8,128)(2,1)S(1)}, bf16[1,256,512]{2,1,0:T(8,128)(2,1)S(1)}, u32[]{:S(2)}, u32[]{:S(2)}) collective-permute-start(bf16[1,256,512]{2,1,0:T(8,128)(2,1)S(1)} %slice.93), channel_id=1, source_target_pairs={{0,8},{4,12},{8,0},{12,4},{1,9},{5,13},{9,1},{13,5},{2,10},{6,14},... | collective-permute-start | bytes 786440 | tf_op jit(solution)/shard_map/ppermute | solution.py:110
  150.1 0.6 fusion.14
  152.6 6.6 %collective-permute-done.16 = bf16[1,256,512]{2,1,0:T(8,128)(2,1)S(1)} collective-permute-done((bf16[1,256,512]{2,1,0:T(8,128)(2,1)S(1)}, bf16[1,256,512]{2,1,0:T(8,128)(2,1)S(1)}, u32[]{:S(2)}, u32[]{:S(2)}) %collective-permute-start.16) | collective-permute-done | bytes 262176 | tf_op jit(solution)/shard_map/ppermute | solution.py:110
  159.3 5.4 %collective-permute-done.14 = bf16[1,256,512]{2,1,0:T(8,128)(2,1)S(1)} collective-permute-done((bf16[1,256,512]{2,1,0:T(8,128)(2,1)S(1)}, bf16[1,256,512]{2,1,0:T(8,128)(2,1)S(1)}, u32[]{:S(2)}, u32[]{:S(2)}) %collective-permute-start.14) | collective-permute-done | bytes 262176 | tf_op jit(solution)/shard_map/ppermute | solution.py:110
  164.8 1.3 fusion.4
  (63 shorter events, 1.3 us)
Async XLA Ops:
  4.6 14.9 %collective-permute-start.1 = (bf16[256,1024]{1,0:T(8,128)(2,1)S(1)}, bf16[256,1024]{1,0:T(8,128)(2,1)S(1)}, u32[]{:S(2)}, u32[]{:S(2)}) collective-permute-start(bf16[256,1024]{1,0:T(8,128)(2,1)S(1)} %and_select_fusion.refs_0_), channel_id=1, source_target_pairs={{0,2},{1,3},{2,0},{3,1},{4,6},{5,7},{6,4},{7,5},{8,10},{9,11},{10,... | collective-permute-start | bytes 1572872 | tf_op jit(solution)/shard_map/ppermute | solution.py:104
  7.6 13.4 %collective-permute-start = (bf16[256,1024]{1,0:T(8,128)(2,1)S(1)}, bf16[256,1024]{1,0:T(8,128)(2,1)S(1)}, u32[]{:S(2)}, u32[]{:S(2)}) collective-permute-start(bf16[256,1024]{1,0:T(8,128)(2,1)S(1)} %and_select_fusion.refs_0_), channel_id=1, source_target_pairs={{0,1},{1,0},{2,3},{3,2},{4,5},{5,4},{6,7},{7,6},{8,9},{9,8},{10,11... | collective-permute-start | bytes 1572872 | tf_op jit(solution)/shard_map/ppermute | solution.py:104
  19.6 1.9 %collective-permute-start.2 = (bf16[256,1024]{1,0:T(8,128)(2,1)S(1)}, bf16[256,1024]{1,0:T(8,128)(2,1)S(1)}, u32[]{:S(2)}, u32[]{:S(2)}) collective-permute-start(bf16[256,1024]{1,0:T(8,128)(2,1)S(1)} %collective-permute-done.1.refs_2_), channel_id=1, source_target_pairs={{0,1},{1,0},{2,3},{3,2},{4,5},{5,4},{6,7},{7,6},{8,9},{9,8},{10,11... | collective-permute-start | bytes 1572872 | tf_op jit(solution)/shard_map/ppermute | solution.py:104
  21.5 2.2 %copy-start = (bf16[8,4,256,256]{3,2,1,0:T(8,128)(2,1)S(1)}, bf16[8,4,256,256]{3,2,1,0:T(8,128)(2,1)}, u32[]{:S(2)}) copy-start(bf16[8,4,256,256]{3,2,1,0:T(8,128)(2,1)} %refs_5_.7) | copy-start | bytes 12582916
  23.7 1.2 copy-start.3
  28.2 14.8 %collective-permute-start.5 = (bf16[2,256,512]{2,1,0:T(8,128)(2,1)S(1)}, bf16[2,256,512]{2,1,0:T(8,128)(2,1)S(1)}, u32[]{:S(2)}, u32[]{:S(2)}) collective-permute-start(bf16[2,256,512]{2,1,0:T(8,128)(2,1)S(1)} %slice.87), channel_id=1, source_target_pairs={{0,4},{4,0},{8,12},{12,8},{1,5},{5,1},{9,13},{13,9},{2,6},{6,2},{1... | collective-permute-start | bytes 1572872 | tf_op jit(solution)/shard_map/ppermute | solution.py:110
  33.5 25.7 %collective-permute-start.3 = (bf16[2,256,512]{2,1,0:T(8,128)(2,1)S(1)}, bf16[2,256,512]{2,1,0:T(8,128)(2,1)S(1)}, u32[]{:S(2)}, u32[]{:S(2)}) collective-permute-start(bf16[2,256,512]{2,1,0:T(8,128)(2,1)S(1)} %slice.82), channel_id=1, source_target_pairs={{0,4},{4,0},{8,12},{12,8},{1,5},{5,1},{9,13},{13,9},{2,6},{6,2},{1... | collective-permute-start | bytes 1572872 | tf_op jit(solution)/shard_map/ppermute | solution.py:110
  43.2 18.3 %collective-permute-start.6 = (bf16[1,256,512]{2,1,0:T(8,128)(2,1)S(1)}, bf16[1,256,512]{2,1,0:T(8,128)(2,1)S(1)}, u32[]{:S(2)}, u32[]{:S(2)}) collective-permute-start(bf16[1,256,512]{2,1,0:T(8,128)(2,1)S(1)} %slice.89), channel_id=1, source_target_pairs={{0,8},{4,12},{8,0},{12,4},{1,9},{5,13},{9,1},{13,5},{2,10},{6,14},... | collective-permute-start | bytes 786440 | tf_op jit(solution)/shard_map/ppermute | solution.py:110
  59.3 29.8 %copy-start.1 = (bf16[8,4,256,256]{3,2,1,0:T(8,128)(2,1)S(1)}, bf16[8,4,256,256]{3,2,1,0:T(8,128)(2,1)}, u32[]{:S(2)}) copy-start(bf16[8,4,256,256]{3,2,1,0:T(8,128)(2,1)} %refs_5_.7) | copy-start | bytes 12582916
  59.4 29.8 %copy-start.4 = (bf16[8,1,256,256]{3,2,1,0:T(8,128)(2,1)S(1)}, bf16[8,1,256,256]{3,2,1,0:T(8,128)(2,1)}, u32[]{:S(2)}) copy-start(bf16[8,1,256,256]{3,2,1,0:T(8,128)(2,1)} %param.8) | copy-start | bytes 3145732
  59.4 14.2 %collective-permute-start.4 = (bf16[1,256,512]{2,1,0:T(8,128)(2,1)S(1)}, bf16[1,256,512]{2,1,0:T(8,128)(2,1)S(1)}, u32[]{:S(2)}, u32[]{:S(2)}) collective-permute-start(bf16[1,256,512]{2,1,0:T(8,128)(2,1)S(1)} %slice.84), channel_id=1, source_target_pairs={{0,8},{4,12},{8,0},{12,4},{1,9},{5,13},{9,1},{13,5},{2,10},{6,14},... | collective-permute-start | bytes 786440 | tf_op jit(solution)/shard_map/ppermute | solution.py:110
  74.8 9.2 %collective-permute-start.9 = (bf16[256,512]{1,0:T(8,128)(2,1)S(1)}, bf16[256,512]{1,0:T(8,128)(2,1)S(1)}, u32[]{:S(2)}, u32[]{:S(2)}) collective-permute-start(bf16[256,512]{1,0:T(8,128)(2,1)S(1)} %get-tuple-element.4), channel_id=1, source_target_pairs={{0,2},{1,3},{2,0},{3,1},{4,6},{5,7},{6,4},{7,5},{8,10},{9,11},{10,... | collective-permute-start | bytes 786440 | tf_op jit(solution)/shard_map/ppermute | solution.py:104
  76.3 7.7 %collective-permute-start.7 = (bf16[256,512]{1,0:T(8,128)(2,1)S(1)}, bf16[256,512]{1,0:T(8,128)(2,1)S(1)}, u32[]{:S(2)}, u32[]{:S(2)}) collective-permute-start(bf16[256,512]{1,0:T(8,128)(2,1)S(1)} %get-tuple-element.4), channel_id=1, source_target_pairs={{0,1},{1,0},{2,3},{3,2},{4,5},{5,4},{6,7},{7,6},{8,9},{9,8},{10,11... | collective-permute-start | bytes 786440 | tf_op jit(solution)/shard_map/ppermute | solution.py:104
  76.3 11.2 %collective-permute-start.10 = (bf16[256,512]{1,0:T(8,128)(2,1)S(1)}, bf16[256,512]{1,0:T(8,128)(2,1)S(1)}, u32[]{:S(2)}, u32[]{:S(2)}) collective-permute-start(bf16[256,512]{1,0:T(8,128)(2,1)S(1)} %get-tuple-element.10), channel_id=1, source_target_pairs={{0,2},{1,3},{2,0},{3,1},{4,6},{5,7},{6,4},{7,5},{8,10},{9,11},{10,... | collective-permute-start | bytes 786440 | tf_op jit(solution)/shard_map/ppermute | solution.py:104
  76.8 10.8 %collective-permute-start.8 = (bf16[256,512]{1,0:T(8,128)(2,1)S(1)}, bf16[256,512]{1,0:T(8,128)(2,1)S(1)}, u32[]{:S(2)}, u32[]{:S(2)}) collective-permute-start(bf16[256,512]{1,0:T(8,128)(2,1)S(1)} %get-tuple-element.10), channel_id=1, source_target_pairs={{0,1},{1,0},{2,3},{3,2},{4,5},{5,4},{6,7},{7,6},{8,9},{9,8},{10,11... | collective-permute-start | bytes 786440 | tf_op jit(solution)/shard_map/ppermute | solution.py:104
  84.0 3.6 %collective-permute-start.11 = (bf16[256,512]{1,0:T(8,128)(2,1)S(1)}, bf16[256,512]{1,0:T(8,128)(2,1)S(1)}, u32[]{:S(2)}, u32[]{:S(2)}) collective-permute-start(bf16[256,512]{1,0:T(8,128)(2,1)S(1)} %collective-permute-done.9), channel_id=1, source_target_pairs={{0,1},{1,0},{2,3},{3,2},{4,5},{5,4},{6,7},{7,6},{8,9},{9,8},{10,11... | collective-permute-start | bytes 786440 | tf_op jit(solution)/shard_map/ppermute | solution.py:104
  87.5 1.5 collective-permute-start.12
  87.6 4.9 %copy-start.6 = (bf16[256,1024]{1,0:T(8,128)(2,1)}, bf16[256,1024]{1,0:T(8,128)(2,1)S(1)}, u32[]{:S(2)}) copy-start(bf16[256,1024]{1,0:T(8,128)(2,1)S(1)} %constant_dynamic-update-slice_fusion.2.refs_2_) | copy-start | bytes 1572868
  89.1 3.3 %copy-start.8 = (bf16[256,1024]{1,0:T(8,128)(2,1)}, bf16[256,1024]{1,0:T(8,128)(2,1)S(1)}, u32[]{:S(2)}) copy-start(bf16[256,1024]{1,0:T(8,128)(2,1)S(1)} %constant_dynamic-update-slice_fusion.4.refs_3_) | copy-start | bytes 1572868
  89.1 5.1 %copy-start.15 = (u32[32]{0:T(128)S(1)}, u32[32]{0:T(128)}, u32[]{:S(2)}) copy-start(u32[32]{0:T(128)} %constant.64) | copy-start | bytes 388
  93.3 51.3 %collective-permute-start.15 = (bf16[2,256,512]{2,1,0:T(8,128)(2,1)}, bf16[2,256,512]{2,1,0:T(8,128)(2,1)}, u32[]{:S(2)}, u32[]{:S(2)}) collective-permute-start(bf16[2,256,512]{2,1,0:T(8,128)(2,1)} %slice.95), channel_id=1, source_target_pairs={{0,4},{4,0},{8,12},{12,8},{1,5},{5,1},{9,13},{13,9},{2,6},{6,2},{1... | collective-permute-start | bytes 1572872 | tf_op jit(solution)/shard_map/ppermute | solution.py:110
  95.5 2.2 %copy-start.2 = (bf16[8,4,256,256]{3,2,1,0:T(8,128)(2,1)S(1)}, bf16[8,4,256,256]{3,2,1,0:T(8,128)(2,1)}, u32[]{:S(2)}) copy-start(bf16[8,4,256,256]{3,2,1,0:T(8,128)(2,1)} %refs_5_.7) | copy-start | bytes 12582916
  97.7 1.0 copy-start.7
  98.7 1.0 copy-start.9
  99.8 5.5 %copy-start.10 = (f32[256,512]{1,0:T(8,128)S(1)}, f32[256,512]{1,0:T(8,128)}, u32[]{:S(2)}) copy-start(f32[256,512]{1,0:T(8,128)} %get-tuple-element.5) | copy-start | bytes 1572868
  99.8 5.5 %copy-start.12 = (f32[256,512]{1,0:T(8,128)S(1)}, f32[256,512]{1,0:T(8,128)}, u32[]{:S(2)}) copy-start(f32[256,512]{1,0:T(8,128)} %get-tuple-element.11) | copy-start | bytes 1572868
  99.8 5.5 %copy-start.14 = (bf16[256,1024]{1,0:T(8,128)(2,1)S(1)}, bf16[256,1024]{1,0:T(8,128)(2,1)}, u32[]{:S(2)}) copy-start(bf16[256,1024]{1,0:T(8,128)(2,1)} %param.7) | copy-start | bytes 1572868
  103.1 1.0 copy-start.5
  104.1 60.7 %copy-start.11 = (f32[256,512]{1,0:T(8,128)S(1)}, f32[256,512]{1,0:T(8,128)}, u32[]{:S(2)}) copy-start(f32[256,512]{1,0:T(8,128)} %get-tuple-element.5) | copy-start | bytes 1572868
  104.1 60.7 %copy-start.13 = (f32[256,512]{1,0:T(8,128)S(1)}, f32[256,512]{1,0:T(8,128)}, u32[]{:S(2)}) copy-start(f32[256,512]{1,0:T(8,128)} %get-tuple-element.11) | copy-start | bytes 1572868
  104.1 41.8 %collective-permute-start.13 = (bf16[2,256,512]{2,1,0:T(8,128)(2,1)S(1)}, bf16[2,256,512]{2,1,0:T(8,128)(2,1)S(1)}, u32[]{:S(2)}, u32[]{:S(2)}) collective-permute-start(bf16[2,256,512]{2,1,0:T(8,128)(2,1)S(1)} %slice.91), channel_id=1, source_target_pairs={{0,4},{4,0},{8,12},{12,8},{1,5},{5,1},{9,13},{13,9},{2,6},{6,2},{1... | collective-permute-start | bytes 1572872 | tf_op jit(solution)/shard_map/ppermute | solution.py:110
  145.9 13.3 %collective-permute-start.16 = (bf16[1,256,512]{2,1,0:T(8,128)(2,1)S(1)}, bf16[1,256,512]{2,1,0:T(8,128)(2,1)S(1)}, u32[]{:S(2)}, u32[]{:S(2)}) collective-permute-start(bf16[1,256,512]{2,1,0:T(8,128)(2,1)S(1)} %slice.97), channel_id=1, source_target_pairs={{0,8},{4,12},{8,0},{12,4},{1,9},{5,13},{9,1},{13,5},{2,10},{6,14},... | collective-permute-start | bytes 786440 | tf_op jit(solution)/shard_map/ppermute | solution.py:110
  147.2 17.6 %collective-permute-start.14 = (bf16[1,256,512]{2,1,0:T(8,128)(2,1)S(1)}, bf16[1,256,512]{2,1,0:T(8,128)(2,1)S(1)}, u32[]{:S(2)}, u32[]{:S(2)}) collective-permute-start(bf16[1,256,512]{2,1,0:T(8,128)(2,1)S(1)} %slice.93), channel_id=1, source_target_pairs={{0,8},{4,12},{8,0},{12,4},{1,9},{5,13},{9,1},{13,5},{2,10},{6,14},... | collective-permute-start | bytes 786440 | tf_op jit(solution)/shard_map/ppermute | solution.py:110

commit v2 on v1

--- a/solution.py
+++ b/solution.py
@@ -37,9 +37,11 @@
 
     @pl.when(step == 0)
     def _():
-        for piece in range(piece_count):
-            for place in range(local):
-                blocks[piece * local + place] = pieces[piece][:, place * tile:(place + 1) * tile]
+        per_piece = local * tile // pieces[0].shape[1]
+        for place in range(len(pieces) // per_piece * local):
+            held = pieces[place * per_piece // local]
+            at = place % (local // per_piece) * tile
+            blocks[place] = held[:, at:at + tile]
 
     total[...] = jnp.zeros_like(total)
     for term in range(terms):
@@ -60,18 +62,18 @@
         grid_spec=pltpu.PrefetchScalarGridSpec(
             num_scalar_prefetch=2,
             grid=(count,),
-            in_specs=[pl.BlockSpec((tile, local * tile), whole) for _ in pieces] + [
+            in_specs=[pl.BlockSpec(piece.shape, whole) for piece in pieces] + [
                 pl.BlockSpec((terms, tile, tile), lambda step, *tables: (0, 0, 0)),
                 pl.BlockSpec((terms, 1, tile, tile), lambda step, *tables: (0, first + step, 0, 0)),
             ],
             out_specs=pl.BlockSpec((slots, tile, tile), lambda step, *tables: (0, 0, step)),
             scratch_shapes=[
-                pltpu.VMEM((len(pieces) * local, tile, tile), jnp.bfloat16),
+                pltpu.VMEM((sum(piece.shape[1] for piece in pieces) // tile, tile, tile), jnp.bfloat16),
                 pltpu.VMEM((slots, tile, tile), jnp.float32),
             ],
         ),
         out_shape=jax.ShapeDtypeStruct((slots, tile, count * tile), jnp.bfloat16),
-        compiler_params=pltpu.CompilerParams(vmem_limit_bytes=40 * 1024 * 1024),
+        compiler_params=pltpu.CompilerParams(vmem_limit_bytes=56 * 1024 * 1024),
         cost_estimate=pl.CostEstimate(
             flops=4 * terms * count * tile**3, bytes_accessed=terms * (count + 1) * tile * tile * 2, transcendentals=0
         ),
@@ -126,10 +128,13 @@
     parts = apply_h(gather(masked))
     parts = [jnp.where(valid[:, i * width:(i + 1) * width], part, 0.0) for i, part in enumerate(parts)]
     image_pieces = [gather(part.astype(jnp.bfloat16)) for part in parts]
-    image_pieces = [jnp.concatenate(several, 1) for several in zip(*image_pieces)]
+    image_pieces = [part for several in zip(*image_pieces) for part in several]
     image = jnp.concatenate(parts, 1)
     own = jnp.stack([jnp.sum(masked_float * masked_float), jnp.sum(masked_float * image)])
-    sums = jnp.sum(lax.all_gather(jnp.broadcast_to(own[:, None], (2, 128)), ("row", "col")), 0)
+    sums = jnp.broadcast_to(own[:, None], (2, 128))
+    for axis, bits in (("col", col_bits), ("row", row_bits)):
+        for bit in range(bits):
+            sums = sums + lax.ppermute(sums, axis, swap(axis, 1 << bit))
     norm_total, correlation_total = sums[0, 0], sums[1, 0]
     scale = lax.rsqrt(norm_total / entry_count + 1e-06)
     theta = correlation_total / norm_total

time: 167 us -> 159 us (0.952)
  blocking collectives: 36.5 us -> 0 us
  waiting for transfers between devices: 70.6 us -> 85.5 us
  Pallas kernels: 13.2 us -> 24.9 us
  starting transfers between devices: 17.4 us -> 23.5 us
  local copies, waits for them, and re-layouts: 13.3 us -> 9.49 us
    unnamed x1 -> x0, blocking collectives: 36.5 us -> none
    ppermute x0 -> x4, waiting for transfers between devices: none -> 14.9 us  [on_device(): sums = sums + lax.ppermute(sums, axis, swap(axis, 1 << bit))]
    pallas_call x4, Pallas kernels: 13.2 us -> 24.9 us  [products(): pl.pallas_call(functools.partial(product_kernel, first, len(pieces), loca...]
    unnamed x37 -> x30, local copies, waits for them, and re-layouts: 9.41 us -> 2.47 us
    ppermute x0 -> x4, starting transfers between devices: none -> 5.58 us  [on_device(): sums = sums + lax.ppermute(sums, axis, swap(axis, 1 << bit))]
    slice x8, local copies, waits for them, and re-layouts: 1.02 us -> 4.44 us  [scatter_sum(): arrived = lax.ppermute(sums[half:], 'row', swap('row', 1 << bit))]
    ppermute x9, waiting for transfers between devices: 24.1 us -> 22.2 us  [gather(): lax.ppermute(pieces[place], 'col', swap('col', 1 << bit))]
    ppermute x8, waiting for transfers between devices: 46.5 us -> 48.4 us  [scatter_sum(): arrived = lax.ppermute(sums[half:], 'row', swap('row', 1 << bit))]
  transfers between devices with their start and end apart: 17 -> 21, of which waited for: 10 -> 11; matrix products, arithmetic and copies ran while one was open for 5% -> 8% of each run, Pallas kernels for 4% -> 12%
where the time goes in v2:
time: 159 us; the launch traced here: 158 us
  waiting for transfers between devices  85.5 us (54%)
  Pallas kernels  24.9 us (16%)
  starting transfers between devices  23.5 us (15%)
  other arithmetic  11.5 us (7%)
  local copies, waits for them, and re-layouts  9.49 us (6%)
  between operations  2.95 us (2%)
    ppermute x8, waiting for transfers between devices, scatter_sum(): arrived = lax.ppermute(sums[half:], 'row', swap('row', 1 << bit))  48.4 us
    pallas_call x4, Pallas kernels, products(): pl.pallas_call(functools.partial(product_kernel, first, len(pieces), loca...  24.9 us
    ppermute x9, waiting for transfers between devices, gather(): lax.ppermute(pieces[place], 'col', swap('col', 1 << bit))  22.2 us
    ppermute x4, waiting for transfers between devices, on_device(): sums = sums + lax.ppermute(sums, axis, swap(axis, 1 << bit))  14.9 us
    ppermute x8, starting transfers between devices, scatter_sum(): arrived = lax.ppermute(sums[half:], 'row', swap('row', 1 << bit))  12.3 us
    ppermute x9, starting transfers between devices, gather(): lax.ppermute(pieces[place], 'col', swap('col', 1 << bit))  5.62 us
    ppermute x4, starting transfers between devices, on_device(): sums = sums + lax.ppermute(sums, axis, swap(axis, 1 << bit))  5.58 us
    slice x8, local copies, waits for them, and re-layouts, scatter_sum(): arrived = lax.ppermute(sums[half:], 'row', swap('row', 1 << bit))  4.44 us
  transfers between devices with their start and end apart: 21, of which 11 were waited for; matrix products, arithmetic and copies ran while one was open for 8% of the time, Pallas kernels for 12%

profile of v2, /device:TPU:0, one launch (start us, length us, event | category | flops | bytes accessed | tf_op | source)
XLA Modules:
  0.0 157.9 jit_solution(17727532095311634711)
XLA Ops:
  0.6 1.2 dynamic_slice.14
  1.9 0.6 iota_compare_fusion.1
  2.5 0.7 dynamic_slice.15
  3.4 1.3 and_select_fusion.refs_0_
  4.6 3.0 %collective-permute-start.1 = (bf16[256,1024]{1,0:T(8,128)(2,1)S(1)}, bf16[256,1024]{1,0:T(8,128)(2,1)S(1)}, u32[]{:S(2)}, u32[]{:S(2)}) collective-permute-start(bf16[256,1024]{1,0:T(8,128)(2,1)S(1)} %and_select_fusion.refs_0_), channel_id=1, source_target_pairs={{0,2},{1,3},{2,0},{3,1},{4,6},{5,7},{6,4},{7,5},{8,10},{9,11},{10,... | collective-permute-start | bytes 1572872 | tf_op jit(solution)/shard_map/ppermute | solution.py:106
  7.6 11.9 %collective-permute-done.1.refs_2_ = bf16[256,1024]{1,0:T(8,128)(2,1)S(1)} collective-permute-done((bf16[256,1024]{1,0:T(8,128)(2,1)S(1)}, bf16[256,1024]{1,0:T(8,128)(2,1)S(1)}, u32[]{:S(2)}, u32[]{:S(2)}) %collective-permute-start.1) | collective-permute-done | bytes 524320 | tf_op jit(solution)/shard_map/ppermute | solution.py:106
  19.6 1.2 or_bitcast_fusion.dest_ref
  20.8 1.4 fusion.7.src_ref
  22.2 0.8 copy-done.7
  23.1 6.2 %shard_map.87 = bf16[4,256,512]{2,1,0:T(8,128)(2,1)} custom-call(s32[8,4]{1,0:T(8,128)} %fusion.7.src_ref, s32[8]{0:T(128)} %or_bitcast_fusion.dest_ref, bf16[256,1024]{1,0:T(8,128)(2,1)} %copy-done, bf16[256,1024]{1,0:T(8,128)(2,1)} %copy-done.7, bf16[256,1024]{1,0:T(8,128)(2,1)} %copy-done.6, bf16[256,1024]{1,0:T(8,128)(2,1)} %copy-done.8, ...), custom_call_target="tpu_custom_call" | custom-call | flops 1073741824 | bytes 3145728 | tf_op jit(solution)/shard_map/pallas_call | solution.py:60
  29.4 1.1 slice.87
  30.5 1.9 %collective-permute-start.5 = (bf16[2,256,512]{2,1,0:T(8,128)(2,1)S(1)}, bf16[2,256,512]{2,1,0:T(8,128)(2,1)S(1)}, u32[]{:S(2)}, u32[]{:S(2)}) collective-permute-start(bf16[2,256,512]{2,1,0:T(8,128)(2,1)S(1)} %slice.87), channel_id=1, source_target_pairs={{0,4},{4,0},{8,12},{12,8},{1,5},{5,1},{9,13},{13,9},{2,6},{6,2},{1... | collective-permute-start | bytes 1572872 | tf_op jit(solution)/shard_map/ppermute | solution.py:112
  32.4 6.2 %shard_map.86 = bf16[4,256,512]{2,1,0:T(8,128)(2,1)} custom-call(s32[8,4]{1,0:T(8,128)} %fusion.7.src_ref, s32[8]{0:T(128)} %or_bitcast_fusion.dest_ref, bf16[256,1024]{1,0:T(8,128)(2,1)} %copy-done, bf16[256,1024]{1,0:T(8,128)(2,1)} %copy-done.7, bf16[256,1024]{1,0:T(8,128)(2,1)} %copy-done.6, bf16[256,1024]{1,0:T(8,128)(2,1)} %copy-done.8, ...), custom_call_target="tpu_custom_call" | custom-call | flops 1073741824 | bytes 3145728 | tf_op jit(solution)/shard_map/pallas_call | solution.py:60
  38.6 1.1 slice.82
  40.1 5.1 %collective-permute-done.5 = bf16[2,256,512]{2,1,0:T(8,128)(2,1)S(1)} collective-permute-done((bf16[2,256,512]{2,1,0:T(8,128)(2,1)S(1)}, bf16[2,256,512]{2,1,0:T(8,128)(2,1)S(1)}, u32[]{:S(2)}, u32[]{:S(2)}) %collective-permute-start.5) | collective-permute-done | bytes 524320 | tf_op jit(solution)/shard_map/ppermute | solution.py:112
  45.4 2.9 %collective-permute-start.6 = (bf16[1,256,512]{2,1,0:T(8,128)(2,1)S(1)}, bf16[1,256,512]{2,1,0:T(8,128)(2,1)S(1)}, u32[]{:S(2)}, u32[]{:S(2)}) collective-permute-start(bf16[1,256,512]{2,1,0:T(8,128)(2,1)S(1)} %slice.89), channel_id=1, source_target_pairs={{0,8},{4,12},{8,0},{12,4},{1,9},{5,13},{9,1},{13,5},{2,10},{6,14},... | collective-permute-start | bytes 786440 | tf_op jit(solution)/shard_map/ppermute | solution.py:112
  48.3 13.5 %collective-permute-done.3 = bf16[2,256,512]{2,1,0:T(8,128)(2,1)S(1)} collective-permute-done((bf16[2,256,512]{2,1,0:T(8,128)(2,1)S(1)}, bf16[2,256,512]{2,1,0:T(8,128)(2,1)S(1)}, u32[]{:S(2)}, u32[]{:S(2)}) %collective-permute-start.3) | collective-permute-done | bytes 524320 | tf_op jit(solution)/shard_map/ppermute | solution.py:112
  61.8 1.2 add_convert_fusion.3
  63.0 1.9 %collective-permute-start.4 = (bf16[1,256,512]{2,1,0:T(8,128)(2,1)S(1)}, bf16[1,256,512]{2,1,0:T(8,128)(2,1)S(1)}, u32[]{:S(2)}, u32[]{:S(2)}) collective-permute-start(bf16[1,256,512]{2,1,0:T(8,128)(2,1)S(1)} %slice.84), channel_id=1, source_target_pairs={{0,8},{4,12},{8,0},{12,4},{1,9},{5,13},{9,1},{13,5},{2,10},{6,14},... | collective-permute-start | bytes 786440 | tf_op jit(solution)/shard_map/ppermute | solution.py:112
  65.1 12.5 %collective-permute-done.4 = bf16[1,256,512]{2,1,0:T(8,128)(2,1)S(1)} collective-permute-done((bf16[1,256,512]{2,1,0:T(8,128)(2,1)S(1)}, bf16[1,256,512]{2,1,0:T(8,128)(2,1)S(1)}, u32[]{:S(2)}, u32[]{:S(2)}) %collective-permute-start.4) | collective-permute-done | bytes 262176 | tf_op jit(solution)/shard_map/ppermute | solution.py:112
  77.8 1.6 %collective-permute-start.13 = (bf16[256,512]{1,0:T(8,128)(2,1)S(1)}, bf16[256,512]{1,0:T(8,128)(2,1)S(1)}, u32[]{:S(2)}, u32[]{:S(2)}) collective-permute-start(bf16[256,512]{1,0:T(8,128)(2,1)S(1)} %get-tuple-element.6.refs_0_), channel_id=1, source_target_pairs={{0,2},{1,3},{2,0},{3,1},{4,6},{5,7},{6,4},{7,5},{8,10},{9,11},{10,... | collective-permute-start | bytes 786440 | tf_op jit(solution)/shard_map/ppermute | solution.py:106
  79.5 0.5 collective-permute-start.14
  79.9 0.5 collective-permute-start.12
  80.4 6.7 %collective-permute-done.13.refs_4_ = bf16[256,512]{1,0:T(8,128)(2,1)S(1)} collective-permute-done((bf16[256,512]{1,0:T(8,128)(2,1)S(1)}, bf16[256,512]{1,0:T(8,128)(2,1)S(1)}, u32[]{:S(2)}, u32[]{:S(2)}) %collective-permute-start.13) | collective-permute-done | bytes 262176 | tf_op jit(solution)/shard_map/ppermute | solution.py:106
  87.1 3.5 %collective-permute-done.14.refs_5_ = bf16[256,512]{1,0:T(8,128)(2,1)S(1)} collective-permute-done((bf16[256,512]{1,0:T(8,128)(2,1)S(1)}, bf16[256,512]{1,0:T(8,128)(2,1)S(1)}, u32[]{:S(2)}, u32[]{:S(2)}) %collective-permute-start.14) | collective-permute-done | bytes 262176 | tf_op jit(solution)/shard_map/ppermute | solution.py:106
  90.7 1.1 fusion
  91.8 1.2 pad_maximum_fusion.1
  93.1 0.5 collective-permute-start.7
  93.7 0.6 copy-done.11
  94.4 0.7 copy-done.14
  95.2 6.2 %shard_map.89 = bf16[4,256,512]{2,1,0:T(8,128)(2,1)} custom-call(s32[8,4]{1,0:T(8,128)} %fusion.7.src_ref, s32[8]{0:T(128)} %or_bitcast_fusion.dest_ref, bf16[256,512]{1,0:T(8,128)(2,1)} %copy-done.3, bf16[256,512]{1,0:T(8,128)(2,1)} %copy-done.4, bf16[256,512]{1,0:T(8,128)(2,1)} %copy-done.11, bf16[256,512]{1,0:T(8,128)(2,1)} %copy-done.12, ...), custom_call_target="tpu_custom_call" | custom-call | flops 1073741824 | bytes 3145728 | tf_op jit(solution)/shard_map/pallas_call | solution.py:60
  101.4 1.1 slice.95
  102.5 1.0 collective-permute-start.19
  103.4 6.3 %shard_map.88 = bf16[4,256,512]{2,1,0:T(8,128)(2,1)} custom-call(s32[8,4]{1,0:T(8,128)} %fusion.7.src_ref, s32[8]{0:T(128)} %or_bitcast_fusion.dest_ref, bf16[256,512]{1,0:T(8,128)(2,1)} %copy-done.3, bf16[256,512]{1,0:T(8,128)(2,1)} %copy-done.4, bf16[256,512]{1,0:T(8,128)(2,1)} %copy-done.11, bf16[256,512]{1,0:T(8,128)(2,1)} %copy-done.12, ...), custom_call_target="tpu_custom_call" | custom-call | flops 1073741824 | bytes 3145728 | tf_op jit(solution)/shard_map/pallas_call | solution.py:60
  109.7 1.1 slice.91
  110.8 1.2 collective-permute-start.17
  112.0 1.6 %collective-permute-start.8 = (f32[2,128]{1,0:T(2,128)S(1)}, f32[2,128]{1,0:T(2,128)S(1)}, u32[]{:S(2)}, u32[]{:S(2)}) collective-permute-start(f32[2,128]{1,0:T(2,128)S(1)} %broadcast_add_fusion), channel_id=1, source_target_pairs={{0,2},{1,3},{2,0},{3,1},{4,6},{5,7},{6,4},{7,5},{8,10},{9,11},{10,... | collective-permute-start | bytes 3080 | tf_op jit(solution)/shard_map/ppermute | solution.py:137
  113.7 1.9 %collective-permute-done.8 = f32[2,128]{1,0:T(2,128)S(1)} collective-permute-done((f32[2,128]{1,0:T(2,128)S(1)}, f32[2,128]{1,0:T(2,128)S(1)}, u32[]{:S(2)}, u32[]{:S(2)}) %collective-permute-start.8) | collective-permute-done | bytes 1056 | tf_op jit(solution)/shard_map/ppermute | solution.py:137
  115.7 0.9 collective-permute-start.9
  116.6 11.1 %collective-permute-done.9 = f32[2,128]{1,0:T(2,128)S(1)} collective-permute-done((f32[2,128]{1,0:T(2,128)S(1)}, f32[2,128]{1,0:T(2,128)S(1)}, u32[]{:S(2)}, u32[]{:S(2)}) %collective-permute-start.9) | collective-permute-done | bytes 1056 | tf_op jit(solution)/shard_map/ppermute | solution.py:137
  127.7 2.5 %collective-permute-start.10 = (f32[2,128]{1,0:T(2,128)S(1)}, f32[2,128]{1,0:T(2,128)S(1)}, u32[]{:S(2)}, u32[]{:S(2)}) collective-permute-start(f32[2,128]{1,0:T(2,128)S(1)} %add.70), channel_id=1, source_target_pairs={{0,8},{4,12},{8,0},{12,4},{1,9},{5,13},{9,1},{13,5},{2,10},{6,14},... | collective-permute-start | bytes 3080 | tf_op jit(solution)/shard_map/ppermute | solution.py:137
  130.2 1.9 %collective-permute-done.10 = f32[2,128]{1,0:T(2,128)S(1)} collective-permute-done((f32[2,128]{1,0:T(2,128)S(1)}, f32[2,128]{1,0:T(2,128)S(1)}, u32[]{:S(2)}, u32[]{:S(2)}) %collective-permute-start.10) | collective-permute-done | bytes 1056 | tf_op jit(solution)/shard_map/ppermute | solution.py:137
  132.3 2.6 %collective-permute-start.20 = (bf16[1,256,512]{2,1,0:T(8,128)(2,1)S(1)}, bf16[1,256,512]{2,1,0:T(8,128)(2,1)S(1)}, u32[]{:S(2)}, u32[]{:S(2)}) collective-permute-start(bf16[1,256,512]{2,1,0:T(8,128)(2,1)S(1)} %slice.97), channel_id=1, source_target_pairs={{0,8},{4,12},{8,0},{12,4},{1,9},{5,13},{9,1},{13,5},{2,10},{6,14},... | collective-permute-start | bytes 786440 | tf_op jit(solution)/shard_map/ppermute | solution.py:112
  134.9 1.2 add_convert_fusion.1
  136.6 0.5 fusion.14
  139.1 12.8 %collective-permute-done.20 = bf16[1,256,512]{2,1,0:T(8,128)(2,1)S(1)} collective-permute-done((bf16[1,256,512]{2,1,0:T(8,128)(2,1)S(1)}, bf16[1,256,512]{2,1,0:T(8,128)(2,1)S(1)}, u32[]{:S(2)}, u32[]{:S(2)}) %collective-permute-start.20) | collective-permute-done | bytes 262176 | tf_op jit(solution)/shard_map/ppermute | solution.py:112
  152.0 4.5 %collective-permute-done.18 = bf16[1,256,512]{2,1,0:T(8,128)(2,1)S(1)} collective-permute-done((bf16[1,256,512]{2,1,0:T(8,128)(2,1)S(1)}, bf16[1,256,512]{2,1,0:T(8,128)(2,1)S(1)}, u32[]{:S(2)}, u32[]{:S(2)}) %collective-permute-start.18) | collective-permute-done | bytes 262176 | tf_op jit(solution)/shard_map/ppermute | solution.py:112
  156.6 1.3 fusion.4
  (61 shorter events, 2.5 us)
Async XLA Ops:
  4.6 17.5 %copy-start = (bf16[256,1024]{1,0:T(8,128)(2,1)}, bf16[256,1024]{1,0:T(8,128)(2,1)S(1)}, u32[]{:S(2)}) copy-start(bf16[256,1024]{1,0:T(8,128)(2,1)S(1)} %and_select_fusion.refs_0_) | copy-start | bytes 1572868
  4.6 14.9 %collective-permute-start.1 = (bf16[256,1024]{1,0:T(8,128)(2,1)S(1)}, bf16[256,1024]{1,0:T(8,128)(2,1)S(1)}, u32[]{:S(2)}, u32[]{:S(2)}) collective-permute-start(bf16[256,1024]{1,0:T(8,128)(2,1)S(1)} %and_select_fusion.refs_0_), channel_id=1, source_target_pairs={{0,2},{1,3},{2,0},{3,1},{4,6},{5,7},{6,4},{7,5},{8,10},{9,11},{10,... | collective-permute-start | bytes 1572872 | tf_op jit(solution)/shard_map/ppermute | solution.py:106
  7.6 14.5 %collective-permute-start = (bf16[256,1024]{1,0:T(8,128)(2,1)S(1)}, bf16[256,1024]{1,0:T(8,128)(2,1)S(1)}, u32[]{:S(2)}, u32[]{:S(2)}) collective-permute-start(bf16[256,1024]{1,0:T(8,128)(2,1)S(1)} %and_select_fusion.refs_0_), channel_id=1, source_target_pairs={{0,1},{1,0},{2,3},{3,2},{4,5},{5,4},{6,7},{7,6},{8,9},{9,8},{10,11... | collective-permute-start | bytes 1572872 | tf_op jit(solution)/shard_map/ppermute | solution.py:106
  19.6 2.6 %copy-start.6 = (bf16[256,1024]{1,0:T(8,128)(2,1)}, bf16[256,1024]{1,0:T(8,128)(2,1)S(1)}, u32[]{:S(2)}) copy-start(bf16[256,1024]{1,0:T(8,128)(2,1)S(1)} %collective-permute-done.1.refs_2_) | copy-start | bytes 1572868
  19.6 2.6 %collective-permute-start.2 = (bf16[256,1024]{1,0:T(8,128)(2,1)S(1)}, bf16[256,1024]{1,0:T(8,128)(2,1)S(1)}, u32[]{:S(2)}, u32[]{:S(2)}) collective-permute-start(bf16[256,1024]{1,0:T(8,128)(2,1)S(1)} %collective-permute-done.1.refs_2_), channel_id=1, source_target_pairs={{0,1},{1,0},{2,3},{3,2},{4,5},{5,4},{6,7},{7,6},{8,9},{9,8},{10,11... | collective-permute-start | bytes 1572872 | tf_op jit(solution)/shard_map/ppermute | solution.py:106
  22.2 0.8 copy-start.7
  22.2 1.0 copy-start.8
  30.4 14.8 %copy-start.2 = (bf16[4,256,512]{2,1,0:T(8,128)(2,1)S(1)}, bf16[4,256,512]{2,1,0:T(8,128)(2,1)}, u32[]{:S(2)}) copy-start(bf16[4,256,512]{2,1,0:T(8,128)(2,1)} %shard_map.87) | copy-start | bytes 3145732
  30.5 14.8 %collective-permute-start.5 = (bf16[2,256,512]{2,1,0:T(8,128)(2,1)S(1)}, bf16[2,256,512]{2,1,0:T(8,128)(2,1)S(1)}, u32[]{:S(2)}, u32[]{:S(2)}) collective-permute-start(bf16[2,256,512]{2,1,0:T(8,128)(2,1)S(1)} %slice.87), channel_id=1, source_target_pairs={{0,4},{4,0},{8,12},{12,8},{1,5},{5,1},{9,13},{13,9},{2,6},{6,2},{1... | collective-permute-start | bytes 1572872 | tf_op jit(solution)/shard_map/ppermute | solution.py:112
  38.6 52.1 %copy-start.5 = (bf16[256,1024]{1,0:T(8,128)(2,1)S(1)}, bf16[256,1024]{1,0:T(8,128)(2,1)}, u32[]{:S(2)}) copy-start(bf16[256,1024]{1,0:T(8,128)(2,1)} %param.7) | copy-start | bytes 1572868
  39.7 22.1 %collective-permute-start.3 = (bf16[2,256,512]{2,1,0:T(8,128)(2,1)S(1)}, bf16[2,256,512]{2,1,0:T(8,128)(2,1)S(1)}, u32[]{:S(2)}, u32[]{:S(2)}) collective-permute-start(bf16[2,256,512]{2,1,0:T(8,128)(2,1)S(1)} %slice.82), channel_id=1, source_target_pairs={{0,4},{4,0},{8,12},{12,8},{1,5},{5,1},{9,13},{13,9},{2,6},{6,2},{1... | collective-permute-start | bytes 1572872 | tf_op jit(solution)/shard_map/ppermute | solution.py:112
  45.4 19.7 %collective-permute-start.6 = (bf16[1,256,512]{2,1,0:T(8,128)(2,1)S(1)}, bf16[1,256,512]{2,1,0:T(8,128)(2,1)S(1)}, u32[]{:S(2)}, u32[]{:S(2)}) collective-permute-start(bf16[1,256,512]{2,1,0:T(8,128)(2,1)S(1)} %slice.89), channel_id=1, source_target_pairs={{0,8},{4,12},{8,0},{12,4},{1,9},{5,13},{9,1},{13,5},{2,10},{6,14},... | collective-permute-start | bytes 786440 | tf_op jit(solution)/shard_map/ppermute | solution.py:112
  63.0 14.6 %collective-permute-start.4 = (bf16[1,256,512]{2,1,0:T(8,128)(2,1)S(1)}, bf16[1,256,512]{2,1,0:T(8,128)(2,1)S(1)}, u32[]{:S(2)}, u32[]{:S(2)}) collective-permute-start(bf16[1,256,512]{2,1,0:T(8,128)(2,1)S(1)} %slice.84), channel_id=1, source_target_pairs={{0,8},{4,12},{8,0},{12,4},{1,9},{5,13},{9,1},{13,5},{2,10},{6,14},... | collective-permute-start | bytes 786440 | tf_op jit(solution)/shard_map/ppermute | solution.py:112
  77.8 15.8 %copy-start.3 = (bf16[256,512]{1,0:T(8,128)(2,1)}, bf16[256,512]{1,0:T(8,128)(2,1)S(1)}, u32[]{:S(2)}) copy-start(bf16[256,512]{1,0:T(8,128)(2,1)S(1)} %get-tuple-element.6.refs_0_) | copy-start | bytes 786436
  77.8 15.8 %copy-start.4 = (bf16[256,512]{1,0:T(8,128)(2,1)}, bf16[256,512]{1,0:T(8,128)(2,1)S(1)}, u32[]{:S(2)}) copy-start(bf16[256,512]{1,0:T(8,128)(2,1)S(1)} %get-tuple-element.10.refs_1_) | copy-start | bytes 786436
  77.8 9.3 %collective-permute-start.13 = (bf16[256,512]{1,0:T(8,128)(2,1)S(1)}, bf16[256,512]{1,0:T(8,128)(2,1)S(1)}, u32[]{:S(2)}, u32[]{:S(2)}) collective-permute-start(bf16[256,512]{1,0:T(8,128)(2,1)S(1)} %get-tuple-element.6.refs_0_), channel_id=1, source_target_pairs={{0,2},{1,3},{2,0},{3,1},{4,6},{5,7},{6,4},{7,5},{8,10},{9,11},{10,... | collective-permute-start | bytes 786440 | tf_op jit(solution)/shard_map/ppermute | solution.py:106
  79.5 11.2 %collective-permute-start.14 = (bf16[256,512]{1,0:T(8,128)(2,1)S(1)}, bf16[256,512]{1,0:T(8,128)(2,1)S(1)}, u32[]{:S(2)}, u32[]{:S(2)}) collective-permute-start(bf16[256,512]{1,0:T(8,128)(2,1)S(1)} %get-tuple-element.10.refs_1_), channel_id=1, source_target_pairs={{0,2},{1,3},{2,0},{3,1},{4,6},{5,7},{6,4},{7,5},{8,10},{9,11},{10,... | collective-permute-start | bytes 786440 | tf_op jit(solution)/shard_map/ppermute | solution.py:106
  79.9 13.6 %collective-permute-start.11 = (bf16[256,512]{1,0:T(8,128)(2,1)S(1)}, bf16[256,512]{1,0:T(8,128)(2,1)S(1)}, u32[]{:S(2)}, u32[]{:S(2)}) collective-permute-start(bf16[256,512]{1,0:T(8,128)(2,1)S(1)} %get-tuple-element.6.refs_0_), channel_id=1, source_target_pairs={{0,1},{1,0},{2,3},{3,2},{4,5},{5,4},{6,7},{7,6},{8,9},{9,8},{10,11... | collective-permute-start | bytes 786440 | tf_op jit(solution)/shard_map/ppermute | solution.py:106
  79.9 13.7 %collective-permute-start.12 = (bf16[256,512]{1,0:T(8,128)(2,1)S(1)}, bf16[256,512]{1,0:T(8,128)(2,1)S(1)}, u32[]{:S(2)}, u32[]{:S(2)}) collective-permute-start(bf16[256,512]{1,0:T(8,128)(2,1)S(1)} %get-tuple-element.10.refs_1_), channel_id=1, source_target_pairs={{0,1},{1,0},{2,3},{3,2},{4,5},{5,4},{6,7},{7,6},{8,9},{9,8},{10,11... | collective-permute-start | bytes 786440 | tf_op jit(solution)/shard_map/ppermute | solution.py:106
  87.1 6.5 %copy-start.9 = (bf16[256,512]{1,0:T(8,128)(2,1)}, bf16[256,512]{1,0:T(8,128)(2,1)S(1)}, u32[]{:S(2)}) copy-start(bf16[256,512]{1,0:T(8,128)(2,1)S(1)} %collective-permute-done.13.refs_4_) | copy-start | bytes 786436
  87.1 6.5 %collective-permute-start.15 = (bf16[256,512]{1,0:T(8,128)(2,1)S(1)}, bf16[256,512]{1,0:T(8,128)(2,1)S(1)}, u32[]{:S(2)}, u32[]{:S(2)}) collective-permute-start(bf16[256,512]{1,0:T(8,128)(2,1)S(1)} %collective-permute-done.13.refs_4_), channel_id=1, source_target_pairs={{0,1},{1,0},{2,3},{3,2},{4,5},{5,4},{6,7},{7,6},{8,9},{9,8},{10,11... | collective-permute-start | bytes 786440 | tf_op jit(solution)/shard_map/ppermute | solution.py:106
  90.7 3.0 %copy-start.10 = (bf16[256,512]{1,0:T(8,128)(2,1)}, bf16[256,512]{1,0:T(8,128)(2,1)S(1)}, u32[]{:S(2)}) copy-start(bf16[256,512]{1,0:T(8,128)(2,1)S(1)} %collective-permute-done.14.refs_5_) | copy-start | bytes 786436
  90.7 2.9 %collective-permute-start.16 = (bf16[256,512]{1,0:T(8,128)(2,1)S(1)}, bf16[256,512]{1,0:T(8,128)(2,1)S(1)}, u32[]{:S(2)}, u32[]{:S(2)}) collective-permute-start(bf16[256,512]{1,0:T(8,128)(2,1)S(1)} %collective-permute-done.14.refs_5_), channel_id=1, source_target_pairs={{0,1},{1,0},{2,3},{3,2},{4,5},{5,4},{6,7},{7,6},{8,9},{9,8},{10,11... | collective-permute-start | bytes 786440 | tf_op jit(solution)/shard_map/ppermute | solution.py:106
  93.1 18.9 %collective-permute-start.7 = (f32[2,128]{1,0:T(2,128)S(1)}, f32[2,128]{1,0:T(2,128)S(1)}, u32[]{:S(2)}, u32[]{:S(2)}) collective-permute-start(f32[2,128]{1,0:T(2,128)S(1)} %broadcast_in_dim.24), channel_id=1, source_target_pairs={{0,1},{1,0},{2,3},{3,2},{4,5},{5,4},{6,7},{7,6},{8,9},{9,8},{10,11... | collective-permute-start | bytes 3080 | tf_op jit(solution)/shard_map/ppermute | solution.py:137
  93.6 0.7 copy-start.11
  93.6 0.8 copy-start.12
  93.6 0.8 copy-start.13
  94.4 0.7 copy-start.14
  102.5 29.7 %copy-start.1 = (bf16[4,256,512]{2,1,0:T(8,128)(2,1)S(1)}, bf16[4,256,512]{2,1,0:T(8,128)(2,1)}, u32[]{:S(2)}) copy-start(bf16[4,256,512]{2,1,0:T(8,128)(2,1)} %shard_map.89) | copy-start | bytes 3145732
  102.5 29.7 %collective-permute-start.19 = (bf16[2,256,512]{2,1,0:T(8,128)(2,1)S(1)}, bf16[2,256,512]{2,1,0:T(8,128)(2,1)S(1)}, u32[]{:S(2)}, u32[]{:S(2)}) collective-permute-start(bf16[2,256,512]{2,1,0:T(8,128)(2,1)S(1)} %slice.95), channel_id=1, source_target_pairs={{0,4},{4,0},{8,12},{12,8},{1,5},{5,1},{9,13},{13,9},{2,6},{6,2},{1... | collective-permute-start | bytes 1572872 | tf_op jit(solution)/shard_map/ppermute | solution.py:112
  110.8 24.2 %collective-permute-start.17 = (bf16[2,256,512]{2,1,0:T(8,128)(2,1)S(1)}, bf16[2,256,512]{2,1,0:T(8,128)(2,1)S(1)}, u32[]{:S(2)}, u32[]{:S(2)}) collective-permute-start(bf16[2,256,512]{2,1,0:T(8,128)(2,1)S(1)} %slice.91), channel_id=1, source_target_pairs={{0,4},{4,0},{8,12},{12,8},{1,5},{5,1},{9,13},{13,9},{2,6},{6,2},{1... | collective-permute-start | bytes 1572872 | tf_op jit(solution)/shard_map/ppermute | solution.py:112
  112.0 3.6 %collective-permute-start.8 = (f32[2,128]{1,0:T(2,128)S(1)}, f32[2,128]{1,0:T(2,128)S(1)}, u32[]{:S(2)}, u32[]{:S(2)}) collective-permute-start(f32[2,128]{1,0:T(2,128)S(1)} %broadcast_add_fusion), channel_id=1, source_target_pairs={{0,2},{1,3},{2,0},{3,1},{4,6},{5,7},{6,4},{7,5},{8,10},{9,11},{10,... | collective-permute-start | bytes 3080 | tf_op jit(solution)/shard_map/ppermute | solution.py:137
  115.7 12.0 %collective-permute-start.9 = (f32[2,128]{1,0:T(2,128)S(1)}, f32[2,128]{1,0:T(2,128)S(1)}, u32[]{:S(2)}, u32[]{:S(2)}) collective-permute-start(f32[2,128]{1,0:T(2,128)S(1)} %fusion.15), channel_id=1, source_target_pairs={{0,4},{4,0},{8,12},{12,8},{1,5},{5,1},{9,13},{13,9},{2,6},{6,2},{1... | collective-permute-start | bytes 3080 | tf_op jit(solution)/shard_map/ppermute | solution.py:137
  127.7 4.5 %collective-permute-start.10 = (f32[2,128]{1,0:T(2,128)S(1)}, f32[2,128]{1,0:T(2,128)S(1)}, u32[]{:S(2)}, u32[]{:S(2)}) collective-permute-start(f32[2,128]{1,0:T(2,128)S(1)} %add.70), channel_id=1, source_target_pairs={{0,8},{4,12},{8,0},{12,4},{1,9},{5,13},{9,1},{13,5},{2,10},{6,14},... | collective-permute-start | bytes 3080 | tf_op jit(solution)/shard_map/ppermute | solution.py:137
  132.3 19.6 %collective-permute-start.20 = (bf16[1,256,512]{2,1,0:T(8,128)(2,1)S(1)}, bf16[1,256,512]{2,1,0:T(8,128)(2,1)S(1)}, u32[]{:S(2)}, u32[]{:S(2)}) collective-permute-start(bf16[1,256,512]{2,1,0:T(8,128)(2,1)S(1)} %slice.97), channel_id=1, source_target_pairs={{0,8},{4,12},{8,0},{12,4},{1,9},{5,13},{9,1},{13,5},{2,10},{6,14},... | collective-permute-start | bytes 786440 | tf_op jit(solution)/shard_map/ppermute | solution.py:112
  136.1 20.4 %collective-permute-start.18 = (bf16[1,256,512]{2,1,0:T(8,128)(2,1)S(1)}, bf16[1,256,512]{2,1,0:T(8,128)(2,1)S(1)}, u32[]{:S(2)}, u32[]{:S(2)}) collective-permute-start(bf16[1,256,512]{2,1,0:T(8,128)(2,1)S(1)} %slice.93), channel_id=1, source_target_pairs={{0,8},{4,12},{8,0},{12,4},{1,9},{5,13},{9,1},{13,5},{2,10},{6,14},... | collective-permute-start | bytes 786440 | tf_op jit(solution)/shard_map/ppermute | solution.py:112

commit v3 on v0

v3 whole, which is shorter than its diff:
```python
import functools

import jax
import jax.numpy as jnp
from jax import lax
from jax.experimental import pallas as pl
from jax.experimental.pallas import tpu as pltpu
from jax.sharding import PartitionSpec as P

CHUNKS = 2
MIB = 1024 * 1024
VMEM = pl.BlockSpec(memory_space=pltpu.VMEM)
SMEM = pl.BlockSpec(memory_space=pltpu.SMEM)


def bits_of(size):
    count = size.bit_length() - 1
    assert 1 << count == size
    return count


def swap(axis, bit):
    return [(place, place ^ bit) for place in range(lax.axis_size(axis))]


def leads(row):
    return (row ^ (row >> 1)) & 1


def leader_swap(bit):
    rows, cols = lax.axis_size("row"), lax.axis_size("col")
    pairs = []
    for row in range(rows):
        for col in range(cols):
            if leads(row):
                pair = (row >> 1) ^ bit
                there = (2 * pair if leads(2 * pair) else 2 * pair + 1, col)
            else:
                there = (row, col ^ 1)
            pairs.append((row * cols + col, there[0] * cols + there[1]))
    return pairs


def reverse_bits(value, count):
    out = 0
    for bit in range(count):
        out = out | (((value >> bit) & 1) << (count - 1 - bit))
    return out


def valid_block(shape, left_sizes, right_sizes, row, block):
    return (lax.broadcasted_iota(jnp.int32, shape, 0) < left_sizes[row]) & (
        lax.broadcasted_iota(jnp.int32, shape, 1) < right_sizes[block]
    )


def fold(values):
    rows = jnp.sum(values.reshape(-1, 8, values.shape[1]), 0)
    return sum(rows[:, at:at + 128] for at in range(0, rows.shape[1], 128))


def prepare_kernel(left_sizes, right_sizes, wavefunction, masked):
    local, tile = masked.shape[:2]
    row, col = lax.axis_index("row"), lax.axis_index("col")
    for place in range(local):
        valid = valid_block((tile, tile), left_sizes, right_sizes, row, col * local + place)
        block = wavefunction[:, place * tile:(place + 1) * tile].astype(jnp.float32)
        masked[place] = jnp.where(valid, block, 0.0).astype(masked.dtype)


def product_kernel(first, count, piece_count, row_count, source, target, *refs):
    pieces, refs = refs[:2 * piece_count], refs[2 * piece_count:]
    left, right, refs = refs[:2], refs[2], refs[3:]
    outs, (blocks, inner, total) = refs[:row_count], refs[row_count:]
    terms, local, tile = right.shape[:3]
    row, col = lax.axis_index("row"), lax.axis_index("col")
    for slot in range(2):
        at = 0
        for piece in pieces[slot * piece_count:(slot + 1) * piece_count]:
            for place in range(piece.shape[0]):
                blocks[at, slot * tile:(slot + 1) * tile] = piece[place]
                at += 1

    def one_block(step, carry):
        place = first + step
        for term in range(terms):
            wanted = source[term, col * local + place]
            held = lax.bitwise_xor(lax.div(wanted, local), col) * local + lax.rem(wanted, local)
            inner[term] = lax.dot_general(
                blocks[held], right[term, place], (((1,), (1,)), ((), ())), preferred_element_type=jnp.float32
            ).astype(jnp.bfloat16)
        total[...] = jnp.zeros_like(total)
        for term in range(terms):
            for slot in range(2):
                to = target[term, row ^ slot]
                to_slot = 2 * reverse_bits((to >> 1) ^ (row >> 1), bits_of(row_count) - 1) + 1 - leads(to)
                total[to_slot] += jnp.dot(
                    left[slot][term], inner[term, slot * tile:(slot + 1) * tile], preferred_element_type=jnp.float32
                )
        for slot in range(row_count):
            outs[slot][step] = total[slot].astype(outs[slot].dtype)
        return carry

    lax.fori_loop(0, count, one_block, 0)


def products(pieces, left, right, source, target, row_count, first, count):
    terms, local, tile = right.shape[:3]
    pieces = [piece for row_pieces in pieces for piece in row_pieces]
    blocks = sum(piece.shape[0] for piece in pieces) // 2
    return pl.pallas_call(
        functools.partial(product_kernel, first, count, len(pieces) // 2, row_count),
        in_specs=[SMEM, SMEM] + [VMEM] * (len(pieces) + 3),
        out_specs=[VMEM] * row_count,
        out_shape=[
            jax.ShapeDtypeStruct((count, tile, tile), jnp.float32 if slot < 2 else jnp.bfloat16)
            for slot in range(row_count)
        ],
        scratch_shapes=[
            pltpu.VMEM((blocks, 2 * tile, tile), jnp.bfloat16),
            pltpu.VMEM((terms, 2 * tile, tile), jnp.bfloat16),
            pltpu.VMEM((row_count, tile, tile), jnp.float32),
        ],
        compiler_params=pltpu.CompilerParams(vmem_limit_bytes=30 * MIB),
        cost_estimate=pl.CostEstimate(flops=8 * terms * count * tile**3, bytes_accessed=8 * MIB, transcendentals=0),
    )(source, target, *pieces, *left, right)


def combine_kernel(slot, first, left_sizes, right_sizes, kept, arrived, masked, image, rounded, stats):
    count, tile = kept.shape[:2]
    row, col = lax.axis_index("row") ^ slot, lax.axis_index("col")
    norm = correlation = jnp.zeros((8, 128), jnp.float32)
    for step in range(count):
        valid = valid_block((tile, tile), left_sizes, right_sizes, row, col * masked.shape[0] + first + step)
        value = jnp.where(valid, kept[step] + arrived[step].astype(jnp.float32), 0.0)
        image[step] = value
        rounded[step] = value.astype(jnp.bfloat16)
        vector = masked[first + step].astype(jnp.float32)
        norm += fold(vector * vector)
        correlation += fold(vector * value)
    stats[0] = norm
    stats[1] = correlation


def combine(slot, first, left_sizes, right_sizes, kept, arrived, masked):
    return pl.pallas_call(
        functools.partial(combine_kernel, slot, first),
        in_specs=[SMEM, SMEM, VMEM, VMEM, VMEM],
        out_specs=[VMEM] * 3,
        out_shape=[
            jax.ShapeDtypeStruct(kept.shape, jnp.float32),
            jax.ShapeDtypeStruct(kept.shape, jnp.bfloat16),
            jax.ShapeDtypeStruct((2, 8, 128), jnp.float32),
        ],
        cost_estimate=pl.CostEstimate(flops=8 * kept.size, bytes_accessed=10 * kept.size, transcendentals=0),
    )(left_sizes, right_sizes, kept, arrived, masked)


def scale_theta(entry_count, stats):
    norm, correlation = jnp.sum(stats[0]), jnp.sum(stats[1])
    norm = jnp.full((1, 128), norm, jnp.float32)
    return lax.rsqrt(norm / entry_count + 1e-06), correlation / norm


def whole(value, like):
    return jnp.broadcast_to(value[:, :1], like.shape)


def first_kernel(entry_count, stats, *refs):
    images, outs = refs[:-2], refs[-2:]
    scale, _ = scale_theta(entry_count, stats)
    half = len(images) // 2
    for slot in range(2):
        at = 0
        for image in images[slot * half:(slot + 1) * half]:
            for step in range(image.shape[0]):
                value = image[step]
                outs[slot][:, at:at + value.shape[1]] = (value * whole(scale, value)).astype(jnp.bfloat16)
                at += value.shape[1]


def first_products(entry_count, stats, images):
    images = [image for row_images in images for image in row_images]
    tile = images[0].shape[1]
    width = sum(image.shape[0] for image in images) // 2 * tile
    return pl.pallas_call(
        functools.partial(first_kernel, entry_count),
        in_specs=[VMEM] * (1 + len(images)),
        out_specs=[VMEM] * 2,
        out_shape=[jax.ShapeDtypeStruct((tile, width), jnp.bfloat16)] * 2,
        cost_estimate=pl.CostEstimate(flops=4 * tile * width, bytes_accessed=12 * tile * width, transcendentals=0),
    )(stats, *images)


def second_value(entry_count, slot, local, first, step, left_sizes, right_sizes, stats, kept, arrived, image):
    tile = kept.shape[1]
    row, col = lax.axis_index("row") ^ slot, lax.axis_index("col")
    scale, theta = scale_theta(entry_count, stats)
    valid = valid_block((tile, tile), left_sizes, right_sizes, row, col * local + first + step)
    value = kept[step] + arrived[step].astype(jnp.float32)
    value = (value - whole(theta, value) * image[step]) * whole(scale, value)
    return jnp.where(valid, value, 0.0).astype(jnp.bfloat16)


def partner_kernel(entry_count, local, first, left_sizes, right_sizes, stats, kept, arrived, image, out):
    for step in range(kept.shape[0]):
        out[step] = second_value(
            entry_count, 1, local, first, step, left_sizes, right_sizes, stats, kept, arrived, image
        )


def partner_second(entry_count, local, first, left_sizes, right_sizes, stats, kept, arrived, image):
    return pl.pallas_call(
        functools.partial(partner_kernel, entry_count, local, first),
        in_specs=[SMEM, SMEM] + [VMEM] * 4,
        out_specs=VMEM,
        out_shape=jax.ShapeDtypeStruct(kept.shape, jnp.bfloat16),
        cost_estimate=pl.CostEstimate(flops=8 * kept.size, bytes_accessed=12 * kept.size, transcendentals=0),
    )(left_sizes, right_sizes, stats, kept, arrived, image)


def second_kernel(entry_count, left_sizes, right_sizes, stats, *refs):
    refs, out = refs[:-1], refs[-1]
    parts = len(refs) // 4
    kept, arrived, images, sent = (refs[i * parts:(i + 1) * parts] for i in range(4))
    local = sum(part.shape[0] for part in kept)
    tile = kept[0].shape[1]
    leading = leads(lax.axis_index("row")) == 1

    @pl.when(leading)
    def _():
        at = 0
        for part in range(parts):
            for step in range(kept[part].shape[0]):
                out[:, (at + step) * tile:(at + step + 1) * tile] = second_value(
                    entry_count, 0, local, at, step, left_sizes, right_sizes, stats, kept[part], arrived[part], images[part]
                )
            at += kept[part].shape[0]

    @pl.when(jnp.logical_not(leading))
    def _():
        at = 0
        for part in range(parts):
            for step in range(kept[part].shape[0]):
                out[:, (at + step) * tile:(at + step + 1) * tile] = sent[part][step]
            at += kept[part].shape[0]


def second_products(entry_count, left_sizes, right_sizes, stats, kept, arrived, images, sent):
    tile = kept[0].shape[1]
    width = sum(part.shape[0] for part in kept) * tile
    return pl.pallas_call(
        functools.partial(second_kernel, entry_count),
        in_specs=[SMEM, SMEM] + [VMEM] * (1 + 4 * len(kept)),
        out_specs=VMEM,
        out_shape=jax.ShapeDtypeStruct((tile, width), jnp.bfloat16),
        cost_estimate=pl.CostEstimate(flops=8 * tile * width, bytes_accessed=14 * tile * width, transcendentals=0),
    )(left_sizes, right_sizes, stats, *kept, *arrived, *images, *sent)


def on_device(wavefunction, left_ops, right_ops, left_dest, right_src, left_sizes, right_sizes):
    tile = left_ops.shape[2]
    local = right_ops.shape[1]
    row_count, col_count = lax.axis_size("row"), lax.axis_size("col")
    pair_bits, col_bits = bits_of(row_count) - 1, bits_of(col_count)
    entry_count = wavefunction.shape[0] * row_count * wavefunction.shape[1] * col_count
    both = ("row", "col")
    leading = leads(lax.axis_index("row")) == 1
    count = local // CHUNKS

    def gather(part):
        pieces = {0: part}
        for bit in reversed(range(col_bits)):
            for place in list(pieces):
                pieces[place | (1 << bit)] = lax.ppermute(pieces[place], "col", swap("col", 1 << bit))
        return [pieces[place] for place in range(col_count)]

    masked = pl.pallas_call(
        prepare_kernel,
        in_specs=[SMEM, SMEM, VMEM],
        out_specs=VMEM,
        out_shape=jax.ShapeDtypeStruct((local, tile, tile), wavefunction.dtype),
    )(left_sizes, right_sizes, wavefunction)
    left_own = left_ops[:, 0]
    masked_rows = [masked, lax.ppermute(masked, "row", swap("row", 1))]
    left = [left_own, lax.ppermute(left_own, "row", swap("row", 1))]

    def apply_h(pieces):
        out = []
        for first in range(0, local, count):
            sums = products(pieces, left, right_ops, right_src, left_dest, row_count, first, count)
            for bit in range(pair_bits):
                half = len(sums) // 2
                arrived = [lax.ppermute(part, both, leader_swap(1 << bit)) for part in sums[:half - 1:-1]][::-1]
                if bit < pair_bits - 1:
                    sums = [
                        (kept.astype(jnp.float32) + more.astype(jnp.float32)).astype(kept.dtype)
                        for kept, more in zip(sums[:half], arrived)
                    ]
            out.append((sums[:2], arrived))
        return out

    stats, images, image_pieces = 0.0, [[], []], [[[] for _ in range(col_count)] for _ in range(2)]
    for chunk, (kept, arrived) in enumerate(apply_h([gather(part) for part in masked_rows])):
        for slot in (1, 0):
            image, rounded, more = combine(
                slot, chunk * count, left_sizes, right_sizes, kept[slot], arrived[slot], masked_rows[slot]
            )
            stats = stats + more
            images[slot].append(image)
            for place, piece in enumerate(gather(rounded)):
                image_pieces[slot][place].append(piece)
    again = apply_h([[piece for place in places for piece in place] for places in image_pieces])
    for bit in range(col_bits):
        stats = stats + lax.ppermute(stats, "col", swap("col", 1 << bit))
    for bit in range(pair_bits):
        stats = stats + lax.ppermute(stats, both, leader_swap(1 << bit))
    firsts = first_products(entry_count, stats, images)
    first_product = jnp.where(leading, firsts[0], lax.ppermute(firsts[1], "row", swap("row", 1)))
    sent = [
        lax.ppermute(
            partner_second(
                entry_count, local, chunk * count, left_sizes, right_sizes, stats, kept[1], arrived[1], images[1][chunk]
            ),
            "row",
            swap("row", 1),
        )
        for chunk, (kept, arrived) in enumerate(again)
    ]
    second_product = second_products(
        entry_count, left_sizes, right_sizes, stats,
        [kept[0] for kept, _ in again], [arrived[0] for _, arrived in again], images[0], sent,
    )
    return (first_product, second_product)


def solution(mesh):
    placed = (
        P(("groups", "row"), "col"),
        P(None, ("groups", "row"), None, None),
        P(None, ("groups", "col"), None, None),
        P(None, "groups"),
        P(None, "groups"),
        P("groups"),
        P("groups"),
    )
    return jax.shard_map(
        on_device,
        mesh=mesh,
        in_specs=placed,
        out_specs=(P(("groups", "row"), "col"), P(("groups", "row"), "col")),
        check_vma=False,
    )
```

time: 249 us -> 161 us (0.65)
  waiting for transfers between devices: 130 us -> 50.5 us
  Pallas kernels: 0 us -> 50.2 us
  blocking collectives: 32.1 us -> 0 us
  starting transfers between devices: 0.34 us -> 27.6 us
  matrix products: 23 us -> 0 us
  between operations: 15.8 us -> 0.8 us
  local copies, waits for them, and re-layouts: 38.4 us -> 27.8 us
  other arithmetic: 8.87 us -> 3.25 us
    reduce_scatter x2 -> x0, waiting for transfers between devices: 86 us -> none  [apply_once(): lax.psum_scatter(jnp.einsum('tk,tan->kan', onehot, contrib).reshape(tile_...]
    ppermute x0 -> x34, waiting for transfers between devices: none -> 50.5 us  [the longest x18 24.3 us: gather(): lax.ppermute(pieces[place], 'col', swap('col', 1 << bit))]
    pallas_call x0 -> x13, Pallas kernels: none -> 50.2 us  [the longest x4 28.7 us: products(): pl.pallas_call(functools.partial(product_kernel, first, count, len(pieces...]
    all_gather x2 -> x0, waiting for transfers between devices: 43.6 us -> none  [apply_once(): gathered = lax.all_gather(vector, 'col', axis=1, tiled=True)]
    psum x1 -> x0, blocking collectives: 32.1 us -> none  [on_device(): lax.psum((jnp.sum(masked_float * masked_float), jnp.sum(masked_float * im...]
    ppermute x0 -> x34, starting transfers between devices: none -> 27.6 us  [the longest x18 9.35 us: gather(): lax.ppermute(pieces[place], 'col', swap('col', 1 << bit))]
    unnamed x7 -> x77, local copies, waits for them, and re-layouts: 4.3 us -> 27.8 us
    dot_general x6 -> x0, matrix products: 23 us -> none  [the longest x2 9.68 us: apply_once(): jnp.einsum('rtjc,tjdc->trjd', chosen, right_ops, preferred_element_type=j...]
  transfers between devices with their start and end apart: 4 -> 34, of which waited for: 4 -> 10; matrix products, arithmetic and copies ran while one was open for 1% -> 2% of each run, Pallas kernels for 0% -> 24%
where the time goes in v3:
time: 161 us; the launch traced here: 160 us
  waiting for transfers between devices  50.5 us (31%)
  Pallas kernels  50.2 us (31%)
  local copies, waits for them, and re-layouts  27.8 us (17%)
  starting transfers between devices  27.6 us (17%)
  other arithmetic  3.25 us (2%)
    pallas_call x4, Pallas kernels, products(): pl.pallas_call(functools.partial(product_kernel, first, count, len(pieces...  28.7 us
    unnamed x77, local copies, waits for them, and re-layouts  27.8 us
    ppermute x18, waiting for transfers between devices, gather(): lax.ppermute(pieces[place], 'col', swap('col', 1 << bit))  24.3 us
    ppermute x1, waiting for transfers between devices, on_device(): masked_rows = [masked, lax.ppermute(masked, 'row', swap('row', 1))]  11 us
    pallas_call x4, Pallas kernels, combine(): pl.pallas_call(functools.partial(combine_kernel, slot, first), in_specs=[...  9.45 us
    ppermute x18, starting transfers between devices, gather(): lax.ppermute(pieces[place], 'col', swap('col', 1 << bit))  9.35 us
    ppermute x1, waiting for transfers between devices, on_device(): left = [left_own, lax.ppermute(left_own, 'row', swap('row', 1))]  6.97 us
    ppermute x2, starting transfers between devices, on_device(): lax.ppermute(partner_second(entry_count, local, chunk * count, left_sizes...  6.48 us
  transfers between devices with their start and end apart: 34, of which 10 were waited for; matrix products, arithmetic and copies ran while one was open for 2% of the time, Pallas kernels for 24%

profile of v3, /device:TPU:0, one launch (start us, length us, event | category | flops | bytes accessed | tf_op | source)
XLA Modules:
  0.0 160.1 jit_solution(10807007170906376141)
XLA Ops:
  0.6 2.0 %shard_map.86.refs_0_.masked = bf16[4,256,256]{2,1,0:T(8,128)(2,1)} custom-call(s32[4]{0:T(128)} %left_sizes.15, s32[16]{0:T(128)} %right_sizes.15, bf16[256,1024]{1,0:T(8,128)(2,1)} %wavefunction.1), custom_call_target="tpu_custom_call" | custom-call | tf_op jit(solution)/shard_map/pallas_call | solution.py:278
  2.6 3.0 %collective-permute-start.3 = (bf16[4,256,256]{2,1,0:T(8,128)(2,1)}, bf16[4,256,256]{2,1,0:T(8,128)(2,1)S(1)}, u32[]{:S(2)}, u32[]{:S(2)}) collective-permute-start(bf16[4,256,256]{2,1,0:T(8,128)(2,1)} %shard_map.86.refs_0_.masked), channel_id=1, source_target_pairs={{0,4},{4,0},{8,12},{12,8},{1,5},{5,1},{9,13},{13,9},{2,6},{6,2},{1... | collective-permute-start | bytes 1572872 | tf_op jit(solution)/shard_map/ppermute | solution.py:285
  5.7 1.5 collective-permute-start.1
  7.6 11.0 %collective-permute-done.3.refs_4_.masked = bf16[4,256,256]{2,1,0:T(8,128)(2,1)S(1)} collective-permute-done((bf16[4,256,256]{2,1,0:T(8,128)(2,1)}, bf16[4,256,256]{2,1,0:T(8,128)(2,1)S(1)}, u32[]{:S(2)}, u32[]{:S(2)}) %collective-permute-start.3) | collective-permute-done | bytes 524320 | tf_op jit(solution)/shard_map/ppermute | solution.py:285
  18.6 2.0 %collective-permute-start.5 = (bf16[4,256,256]{2,1,0:T(8,128)(2,1)S(1)}, bf16[4,256,256]{2,1,0:T(8,128)(2,1)S(1)}, u32[]{:S(2)}, u32[]{:S(2)}) collective-permute-start(bf16[4,256,256]{2,1,0:T(8,128)(2,1)S(1)} %collective-permute-done.3.refs_4_.masked), channel_id=1, source_target_pairs={{0,2},{1,3},{2,0},{3,1},{4,6},{5,7},{6,4},{7,5},{8,10},{9,11},{10,... | collective-permute-start | bytes 1572872 | tf_op jit(solution)/shard_map/ppermute | solution.py:275
  21.1 9.8 %collective-permute-done.5.refs_6_ = bf16[4,256,256]{2,1,0:T(8,128)(2,1)S(1)} collective-permute-done((bf16[4,256,256]{2,1,0:T(8,128)(2,1)S(1)}, bf16[4,256,256]{2,1,0:T(8,128)(2,1)S(1)}, u32[]{:S(2)}, u32[]{:S(2)}) %collective-permute-start.5) | collective-permute-done | bytes 524320 | tf_op jit(solution)/shard_map/ppermute | solution.py:275
  30.9 0.8 copy-done.6
  33.3 7.0 %collective-permute-done.7.refs_9_.refs_17_ = bf16[8,256,256]{2,1,0:T(8,128)(2,1)S(1)} collective-permute-done((bf16[8,256,256]{2,1,0:T(8,128)(2,1)}, bf16[8,256,256]{2,1,0:T(8,128)(2,1)S(1)}, u32[]{:S(2)}, u32[]{:S(2)}) %collective-permute-start.7) | collective-permute-done | bytes 1048608 | tf_op jit(solution)/shard_map/ppermute | solution.py:286
  40.3 2.2 %copy-done = bf16[8,4,256,256]{3,2,1,0:T(8,128)(2,1)S(1)} copy-done((bf16[8,4,256,256]{3,2,1,0:T(8,128)(2,1)S(1)}, bf16[8,4,256,256]{3,2,1,0:T(8,128)(2,1)}, u32[]{:S(2)}) %copy-start) | copy-done | bytes 4194328
  42.5 1.2 copy-done.2
  43.7 1.0 copy-done.4
  44.7 1.0 copy-done.7
  45.8 1.0 copy-done.9
  47.5 7.1 %shard_map.87 = (f32[2,256,256]{2,1,0:T(8,128)S(1)}, f32[2,256,256]{2,1,0:T(8,128)S(1)}, bf16[2,256,256]{2,1,0:T(8,128)(2,1)S(1)}, bf16[2,256,256]{2,1,0:T(8,128)(2,1)}) custom-call(s32[8,16]{1,0:T(8,128)S(1)} %copy-done.26, s32[8,4]{1,0:T(8,128)S(1)} %copy.9.target, bf16[4,256,256]{2,1,0:T(8,128)(2,1)S(1)} %copy-done.4, bf16[4,256,256]{2,1,0:T(8,128)(2,1)S(1)} %copy-done.9, ...), custom_call_target="tpu_custom_call" | custom-call | flops 2147483648 | bytes 8388608 | tf_op jit(solution)/shard_map/pallas_call | solution.py:111
  54.6 0.8 copy-done.20
  55.4 0.8 copy-done.21
  56.7 7.2 %shard_map.90 = (f32[2,256,256]{2,1,0:T(8,128)S(1)}, f32[2,256,256]{2,1,0:T(8,128)S(1)}, bf16[2,256,256]{2,1,0:T(8,128)(2,1)}, bf16[2,256,256]{2,1,0:T(8,128)(2,1)}) custom-call(s32[8,16]{1,0:T(8,128)S(1)} %copy-done.26, s32[8,4]{1,0:T(8,128)S(1)} %copy.9.target, bf16[4,256,256]{2,1,0:T(8,128)(2,1)S(1)} %copy-done.4, bf16[4,256,256]{2,1,0:T(8,128)(2,1)S(1)} %copy-done.9, ...), custom_call_target="tpu_custom_call" | custom-call | flops 2147483648 | bytes 8388608 | tf_op jit(solution)/shard_map/pallas_call | solution.py:111
  64.7 0.8 copy-done.19
  66.7 2.4 %shard_map.89 = (f32[2,256,256]{2,1,0:T(8,128)}, bf16[2,256,256]{2,1,0:T(8,128)(2,1)}, f32[2,8,128]{2,1,0:T(8,128)}) custom-call(s32[4]{0:T(128)} %left_sizes.15, s32[16]{0:T(128)} %right_sizes.15, f32[2,256,256]{2,1,0:T(8,128)} %copy-done.21, bf16[2,256,256]{2,1,0:T(8,128)(2,1)} %copy-done.33, bf16[4,256,256]{2,1,0:T(8,128)(2,1)} %shard_map.86.refs_0_.masked), custom_call_target="tpu_custom_call" | custom-call | flops 1048576 | bytes 1310720 | tf_op jit(solution)/shard_map/pallas_call | solution.py:146
  69.1 1.7 %collective-permute-start.18 = (bf16[2,256,256]{2,1,0:T(8,128)(2,1)}, bf16[2,256,256]{2,1,0:T(8,128)(2,1)S(1)}, u32[]{:S(2)}, u32[]{:S(2)}) collective-permute-start(bf16[2,256,256]{2,1,0:T(8,128)(2,1)} %get-tuple-element.50.refs_0_), channel_id=1, source_target_pairs={{0,2},{1,3},{2,0},{3,1},{4,6},{5,7},{6,4},{7,5},{8,10},{9,11},{10,... | collective-permute-start | bytes 786440 | tf_op jit(solution)/shard_map/ppermute | solution.py:275
  71.5 2.3 %shard_map.88 = (f32[2,256,256]{2,1,0:T(8,128)}, bf16[2,256,256]{2,1,0:T(8,128)(2,1)}, f32[2,8,128]{2,1,0:T(8,128)}) custom-call(s32[4]{0:T(128)} %left_sizes.15, s32[16]{0:T(128)} %right_sizes.15, f32[2,256,256]{2,1,0:T(8,128)} %copy-done.20, bf16[2,256,256]{2,1,0:T(8,128)(2,1)} %copy-done.31, bf16[4,256,256]{2,1,0:T(8,128)(2,1)} %copy-done.5), custom_call_target="tpu_custom_call" | custom-call | flops 1048576 | bytes 1310720 | tf_op jit(solution)/shard_map/pallas_call | solution.py:146
  73.8 2.4 %shard_map.91 = (f32[2,256,256]{2,1,0:T(8,128)}, bf16[2,256,256]{2,1,0:T(8,128)(2,1)}, f32[2,8,128]{2,1,0:T(8,128)}) custom-call(s32[4]{0:T(128)} %left_sizes.15, s32[16]{0:T(128)} %right_sizes.15, f32[2,256,256]{2,1,0:T(8,128)} %copy-done.19, bf16[2,256,256]{2,1,0:T(8,128)(2,1)} %collective-permute-done.10.arrived, bf16[4,256,256]{2,1,0:T(8,128)(2,1)} %copy-done.5), custom_call_target="tpu_custom_call" | custom-call | flops 1048576 | bytes 1310720 | tf_op jit(solution)/shard_map/pallas_call | solution.py:146
  76.9 2.4 %shard_map.92 = (f32[2,256,256]{2,1,0:T(8,128)}, bf16[2,256,256]{2,1,0:T(8,128)(2,1)}, f32[2,8,128]{2,1,0:T(8,128)}) custom-call(s32[4]{0:T(128)} %left_sizes.15, s32[16]{0:T(128)} %right_sizes.15, f32[2,256,256]{2,1,0:T(8,128)} %copy-done.18, bf16[2,256,256]{2,1,0:T(8,128)(2,1)} %copy-done.30, bf16[4,256,256]{2,1,0:T(8,128)(2,1)} %shard_map.86.refs_0_.masked), custom_call_target="tpu_custom_call" | custom-call | flops 1048576 | bytes 1310720 | tf_op jit(solution)/shard_map/pallas_call | solution.py:146
  80.5 0.8 collective-permute-done.12
  81.7 3.3 %collective-permute-done.13 = f32[2,8,128]{2,1,0:T(8,128)S(1)} collective-permute-done((f32[2,8,128]{2,1,0:T(8,128)S(1)}, f32[2,8,128]{2,1,0:T(8,128)S(1)}, u32[]{:S(2)}, u32[]{:S(2)}) %collective-permute-start.13) | collective-permute-done | bytes 8224 | tf_op jit(solution)/shard_map/ppermute | solution.py:315
  86.2 1.1 collective-permute-start.25
  87.3 1.0 collective-permute-start.19
  88.3 6.0 %collective-permute-done.24.refs_12_ = bf16[2,256,256]{2,1,0:T(8,128)(2,1)S(1)} collective-permute-done((bf16[2,256,256]{2,1,0:T(8,128)(2,1)}, bf16[2,256,256]{2,1,0:T(8,128)(2,1)S(1)}, u32[]{:S(2)}, u32[]{:S(2)}) %collective-permute-start.24) | collective-permute-done | bytes 262176 | tf_op jit(solution)/shard_map/ppermute | solution.py:275
  95.6 4.5 %collective-permute-done.25.refs_13_ = bf16[2,256,256]{2,1,0:T(8,128)(2,1)} collective-permute-done((bf16[2,256,256]{2,1,0:T(8,128)(2,1)}, bf16[2,256,256]{2,1,0:T(8,128)(2,1)}, u32[]{:S(2)}, u32[]{:S(2)}) %collective-permute-start.25) | collective-permute-done | bytes 262176 | tf_op jit(solution)/shard_map/ppermute | solution.py:275
  101.3 4.0 %collective-permute-done.19.refs_5_ = bf16[2,256,256]{2,1,0:T(8,128)(2,1)} collective-permute-done((bf16[2,256,256]{2,1,0:T(8,128)(2,1)}, bf16[2,256,256]{2,1,0:T(8,128)(2,1)}, u32[]{:S(2)}, u32[]{:S(2)}) %collective-permute-start.19) | collective-permute-done | bytes 262176 | tf_op jit(solution)/shard_map/ppermute | solution.py:275
  105.9 2.7 %shard_map.93 = (bf16[256,1024]{1,0:T(8,128)(2,1)}, bf16[256,1024]{1,0:T(8,128)(2,1)}) custom-call(f32[2,8,128]{2,1,0:T(8,128)} %add.23.stats, f32[2,256,256]{2,1,0:T(8,128)} %get-tuple-element.44.refs_0_.refs_4_, f32[2,256,256]{2,1,0:T(8,128)} %get-tuple-element.45.refs_1_.refs_5_, f32[2,256,256]{2,1,0:T(8,128)} %get-tuple-element.46.refs_2_.image, ...), custom_call_target="tpu_custom_call" | custom-call | flops 1048576 | bytes 3145728 | tf_op jit(solution)/shard_map/pallas_call | solution.py:186
  108.6 5.4 %collective-permute-start.15 = (bf16[256,1024]{1,0:T(8,128)(2,1)}, bf16[256,1024]{1,0:T(8,128)(2,1)}, u32[]{:S(2)}, u32[]{:S(2)}) collective-permute-start(bf16[256,1024]{1,0:T(8,128)(2,1)} %get-tuple-element.49), channel_id=1, source_target_pairs={{0,4},{4,0},{8,12},{12,8},{1,5},{5,1},{9,13},{13,9},{2,6},{6,2},{1... | collective-permute-start | bytes 1572872 | tf_op jit(solution)/shard_map/ppermute | solution.py:319
  114.1 2.2 %copy-done.1 = bf16[8,4,256,256]{3,2,1,0:T(8,128)(2,1)S(1)} copy-done((bf16[8,4,256,256]{3,2,1,0:T(8,128)(2,1)S(1)}, bf16[8,4,256,256]{3,2,1,0:T(8,128)(2,1)}, u32[]{:S(2)}) %copy-start.1) | copy-done | bytes 4194328
  116.3 0.9 copy-done.12
  117.2 0.9 copy-done.13
  118.2 0.9 copy-done.15
  119.1 0.9 copy-done.17
  120.1 7.1 %shard_map.95 = (f32[2,256,256]{2,1,0:T(8,128)S(1)}, f32[2,256,256]{2,1,0:T(8,128)S(1)}, bf16[2,256,256]{2,1,0:T(8,128)(2,1)S(1)}, bf16[2,256,256]{2,1,0:T(8,128)(2,1)}) custom-call(s32[8,16]{1,0:T(8,128)S(1)} %copy-done.27, s32[8,4]{1,0:T(8,128)S(1)} %copy.9.target, bf16[2,256,256]{2,1,0:T(8,128)(2,1)S(1)} %copy-done.10, ...), custom_call_target="tpu_custom_call" | custom-call | flops 2147483648 | bytes 8388608 | tf_op jit(solution)/shard_map/pallas_call | solution.py:111
  128.0 0.8 copy-done.25
  129.0 7.3 %shard_map.94 = (f32[2,256,256]{2,1,0:T(8,128)S(1)}, f32[2,256,256]{2,1,0:T(8,128)S(1)}, bf16[2,256,256]{2,1,0:T(8,128)(2,1)S(1)}, bf16[2,256,256]{2,1,0:T(8,128)(2,1)}) custom-call(s32[8,16]{1,0:T(8,128)S(1)} %copy-done.27, s32[8,4]{1,0:T(8,128)S(1)} %copy.9.target, bf16[2,256,256]{2,1,0:T(8,128)(2,1)S(1)} %copy-done.10, ...), custom_call_target="tpu_custom_call" | custom-call | flops 2147483648 | bytes 8388608 | tf_op jit(solution)/shard_map/pallas_call | solution.py:111
  137.1 0.8 copy-done.24
  139.5 2.3 %shard_map.97 = bf16[2,256,256]{2,1,0:T(8,128)(2,1)} custom-call(s32[4]{0:T(128)} %left_sizes.15, s32[16]{0:T(128)} %right_sizes.15, f32[2,8,128]{2,1,0:T(8,128)} %add.23.stats, f32[2,256,256]{2,1,0:T(8,128)} %copy-done.25, bf16[2,256,256]{2,1,0:T(8,128)(2,1)} %collective-permute-done.32.arrived, f32[2,256,256]{2,1,0:T(8,128)} %get-tuple-element.47.refs_3_.image), custom_call_target="tpu_custom_call" | custom-call | flops 1048576 | bytes 1572864 | tf_op jit(solution)/shard_map/pallas_call | solution.py:213
  141.8 3.1 %collective-permute-start.33 = (bf16[2,256,256]{2,1,0:T(8,128)(2,1)}, bf16[2,256,256]{2,1,0:T(8,128)(2,1)S(1)}, u32[]{:S(2)}, u32[]{:S(2)}) collective-permute-start(bf16[2,256,256]{2,1,0:T(8,128)(2,1)} %shard_map.97), channel_id=1, source_target_pairs={{0,4},{4,0},{8,12},{12,8},{1,5},{5,1},{9,13},{13,9},{2,6},{6,2},{1... | collective-permute-start | bytes 786440 | tf_op jit(solution)/shard_map/ppermute | solution.py:321
  145.6 2.3 %shard_map.96 = bf16[2,256,256]{2,1,0:T(8,128)(2,1)} custom-call(s32[4]{0:T(128)} %left_sizes.15, s32[16]{0:T(128)} %right_sizes.15, f32[2,8,128]{2,1,0:T(8,128)} %add.23.stats, f32[2,256,256]{2,1,0:T(8,128)} %copy-done.24, bf16[2,256,256]{2,1,0:T(8,128)(2,1)} %copy-done.32, f32[2,256,256]{2,1,0:T(8,128)} %get-tuple-element.46.refs_2_.image), custom_call_target="tpu_custom_call" | custom-call | flops 1048576 | bytes 1572864 | tf_op jit(solution)/shard_map/pallas_call | solution.py:213
  147.9 3.4 %collective-permute-start.31 = (bf16[2,256,256]{2,1,0:T(8,128)(2,1)}, bf16[2,256,256]{2,1,0:T(8,128)(2,1)S(1)}, u32[]{:S(2)}, u32[]{:S(2)}) collective-permute-start(bf16[2,256,256]{2,1,0:T(8,128)(2,1)} %shard_map.96), channel_id=1, source_target_pairs={{0,4},{4,0},{8,12},{12,8},{1,5},{5,1},{9,13},{13,9},{2,6},{6,2},{1... | collective-permute-start | bytes 786440 | tf_op jit(solution)/shard_map/ppermute | solution.py:321
  151.3 1.9 %broadcast_select_fusion = bf16[256,1024]{1,0:T(8,128)(2,1)} fusion(bf16[256,1024]{1,0:T(8,128)(2,1)} %get-tuple-element.48, bf16[256,1024]{1,0:T(8,128)(2,1)} %collective-permute-done.15, pred[]{:T(512)S(6)} %eq.3), kind=kLoop, calls=%fused_computation | loop fusion | flops 262144 | bytes 1572865 | tf_op jit(solution)/shard_map/jit(_where)/select_n | solution.py:319
  153.2 3.5 %collective-permute-done.31.refs_6_ = bf16[2,256,256]{2,1,0:T(8,128)(2,1)S(1)} collective-permute-done((bf16[2,256,256]{2,1,0:T(8,128)(2,1)}, bf16[2,256,256]{2,1,0:T(8,128)(2,1)S(1)}, u32[]{:S(2)}, u32[]{:S(2)}) %collective-permute-start.31) | collective-permute-done | bytes 262176 | tf_op jit(solution)/shard_map/ppermute | solution.py:321
  157.4 2.7 %shard_map.98 = bf16[256,1024]{1,0:T(8,128)(2,1)} custom-call(s32[4]{0:T(128)} %left_sizes.15, s32[16]{0:T(128)} %right_sizes.15, f32[2,8,128]{2,1,0:T(8,128)} %add.23.stats, f32[2,256,256]{2,1,0:T(8,128)} %copy-done.23, f32[2,256,256]{2,1,0:T(8,128)} %copy-done.22, bf16[2,256,256]{2,1,0:T(8,128)(2,1)} %copy-done.35, bf16[2,256,256]{2,1,0:T(8,128)(2,1)} %copy-done.34, ...), custom_call_target="tpu_custom_call" | custom-call | flops 2097152 | bytes 3670016 | tf_op jit(solution)/shard_map/pallas_call | solution.py:252
  (115 shorter events, 17.9 us)
Async XLA Ops:
  2.6 16.0 %collective-permute-start.3 = (bf16[4,256,256]{2,1,0:T(8,128)(2,1)}, bf16[4,256,256]{2,1,0:T(8,128)(2,1)S(1)}, u32[]{:S(2)}, u32[]{:S(2)}) collective-permute-start(bf16[4,256,256]{2,1,0:T(8,128)(2,1)} %shard_map.86.refs_0_.masked), channel_id=1, source_target_pairs={{0,4},{4,0},{8,12},{12,8},{1,5},{5,1},{9,13},{13,9},{2,6},{6,2},{1... | collective-permute-start | bytes 1572872 | tf_op jit(solution)/shard_map/ppermute | solution.py:285
  5.7 15.5 %collective-permute-start.1 = (bf16[4,256,256]{2,1,0:T(8,128)(2,1)}, bf16[4,256,256]{2,1,0:T(8,128)(2,1)S(1)}, u32[]{:S(2)}, u32[]{:S(2)}) collective-permute-start(bf16[4,256,256]{2,1,0:T(8,128)(2,1)} %shard_map.86.refs_0_.masked), channel_id=1, source_target_pairs={{0,2},{1,3},{2,0},{3,1},{4,6},{5,7},{6,4},{7,5},{8,10},{9,11},{10,... | collective-permute-start | bytes 1572872 | tf_op jit(solution)/shard_map/ppermute | solution.py:275
  7.2 33.1 %collective-permute-start.7 = (bf16[8,256,256]{2,1,0:T(8,128)(2,1)}, bf16[8,256,256]{2,1,0:T(8,128)(2,1)S(1)}, u32[]{:S(2)}, u32[]{:S(2)}) collective-permute-start(bf16[8,256,256]{2,1,0:T(8,128)(2,1)} %bitcast.1), channel_id=1, source_target_pairs={{0,4},{4,0},{8,12},{12,8},{1,5},{5,1},{9,13},{13,9},{2,6},{6,2},{1... | collective-permute-start | bytes 3145736 | tf_op jit(solution)/shard_map/ppermute | solution.py:286
  18.6 38.1 %copy-start.5 = (bf16[4,256,256]{2,1,0:T(8,128)(2,1)}, bf16[4,256,256]{2,1,0:T(8,128)(2,1)S(1)}, u32[]{:S(2)}) copy-start(bf16[4,256,256]{2,1,0:T(8,128)(2,1)S(1)} %collective-permute-done.3.refs_4_.masked) | copy-start | bytes 1572868
  18.6 12.3 %collective-permute-start.5 = (bf16[4,256,256]{2,1,0:T(8,128)(2,1)S(1)}, bf16[4,256,256]{2,1,0:T(8,128)(2,1)S(1)}, u32[]{:S(2)}, u32[]{:S(2)}) collective-permute-start(bf16[4,256,256]{2,1,0:T(8,128)(2,1)S(1)} %collective-permute-done.3.refs_4_.masked), channel_id=1, source_target_pairs={{0,2},{1,3},{2,0},{3,1},{4,6},{5,7},{6,4},{7,5},{8,10},{9,11},{10,... | collective-permute-start | bytes 1572872 | tf_op jit(solution)/shard_map/ppermute | solution.py:275
  20.6 11.9 %collective-permute-start = (bf16[4,256,256]{2,1,0:T(8,128)(2,1)}, bf16[4,256,256]{2,1,0:T(8,128)(2,1)S(1)}, u32[]{:S(2)}, u32[]{:S(2)}) collective-permute-start(bf16[4,256,256]{2,1,0:T(8,128)(2,1)} %shard_map.86.refs_0_.masked), channel_id=1, source_target_pairs={{0,1},{1,0},{2,3},{3,2},{4,5},{5,4},{6,7},{7,6},{8,9},{9,8},{10,11... | collective-permute-start | bytes 1572872 | tf_op jit(solution)/shard_map/ppermute | solution.py:275
  20.6 12.7 %collective-permute-start.4 = (bf16[4,256,256]{2,1,0:T(8,128)(2,1)S(1)}, bf16[4,256,256]{2,1,0:T(8,128)(2,1)}, u32[]{:S(2)}, u32[]{:S(2)}) collective-permute-start(bf16[4,256,256]{2,1,0:T(8,128)(2,1)S(1)} %collective-permute-done.3.refs_4_.masked), channel_id=1, source_target_pairs={{0,1},{1,0},{2,3},{3,2},{4,5},{5,4},{6,7},{7,6},{8,9},{9,8},{10,11... | collective-permute-start | bytes 1572872 | tf_op jit(solution)/shard_map/ppermute | solution.py:275
  21.1 12.2 %collective-permute-start.2 = (bf16[4,256,256]{2,1,0:T(8,128)(2,1)S(1)}, bf16[4,256,256]{2,1,0:T(8,128)(2,1)}, u32[]{:S(2)}, u32[]{:S(2)}) collective-permute-start(bf16[4,256,256]{2,1,0:T(8,128)(2,1)S(1)} %collective-permute-done.1.refs_2_), channel_id=1, source_target_pairs={{0,1},{1,0},{2,3},{3,2},{4,5},{5,4},{6,7},{7,6},{8,9},{9,8},{10,11... | collective-permute-start | bytes 1572872 | tf_op jit(solution)/shard_map/ppermute | solution.py:275
  30.9 9.4 %collective-permute-start.6 = (bf16[4,256,256]{2,1,0:T(8,128)(2,1)S(1)}, bf16[4,256,256]{2,1,0:T(8,128)(2,1)}, u32[]{:S(2)}, u32[]{:S(2)}) collective-permute-start(bf16[4,256,256]{2,1,0:T(8,128)(2,1)S(1)} %collective-permute-done.5.refs_6_), channel_id=1, source_target_pairs={{0,1},{1,0},{2,3},{3,2},{4,5},{5,4},{6,7},{7,6},{8,9},{9,8},{10,11... | collective-permute-start | bytes 1572872 | tf_op jit(solution)/shard_map/ppermute | solution.py:275
  40.3 2.2 %copy-start = (bf16[8,4,256,256]{3,2,1,0:T(8,128)(2,1)S(1)}, bf16[8,4,256,256]{3,2,1,0:T(8,128)(2,1)}, u32[]{:S(2)}) copy-start(bf16[8,4,256,256]{3,2,1,0:T(8,128)(2,1)} %refs_18_.3) | copy-start | bytes 12582916
  42.5 1.2 copy-start.2
  43.7 1.0 copy-start.4
  44.7 1.0 copy-start.7
  56.2 9.8 %collective-permute-start.9 = (bf16[2,256,256]{2,1,0:T(8,128)(2,1)S(1)}, bf16[2,256,256]{2,1,0:T(8,128)(2,1)S(1)}, u32[]{:S(2)}, u32[]{:S(2)}) collective-permute-start(bf16[2,256,256]{2,1,0:T(8,128)(2,1)S(1)} %get-tuple-element.36), channel_id=1, source_target_pairs={{0,1},{1,0},{2,3},{3,2},{4,8},{5,9},{6,10},{7,11},{8,4},{9,5},{10,... | collective-permute-start | bytes 786440 | tf_op jit(solution)/shard_map/ppermute | solution.py:294
  56.2 14.6 %collective-permute-start.8 = (bf16[2,256,256]{2,1,0:T(8,128)(2,1)}, bf16[2,256,256]{2,1,0:T(8,128)(2,1)S(1)}, u32[]{:S(2)}, u32[]{:S(2)}) collective-permute-start(bf16[2,256,256]{2,1,0:T(8,128)(2,1)} %get-tuple-element.33), channel_id=1, source_target_pairs={{0,1},{1,0},{2,3},{3,2},{4,8},{5,9},{6,10},{7,11},{8,4},{9,5},{10,... | collective-permute-start | bytes 786440 | tf_op jit(solution)/shard_map/ppermute | solution.py:294
  65.5 48.5 %copy-start.3 = (bf16[8,1,256,256]{3,2,1,0:T(8,128)(2,1)S(1)}, bf16[8,1,256,256]{3,2,1,0:T(8,128)(2,1)}, u32[]{:S(2)}) copy-start(bf16[8,1,256,256]{3,2,1,0:T(8,128)(2,1)} %param.8) | copy-start | bytes 3145732
  65.5 48.5 %copy-start.27 = (s32[8,16]{1,0:T(8,128)S(1)}, s32[8,16]{1,0:T(8,128)}, u32[]{:S(2)}) copy-start(s32[8,16]{1,0:T(8,128)} %source.7) | copy-start | bytes 1540
  65.5 8.3 %collective-permute-start.10 = (bf16[2,256,256]{2,1,0:T(8,128)(2,1)}, bf16[2,256,256]{2,1,0:T(8,128)(2,1)}, u32[]{:S(2)}, u32[]{:S(2)}) collective-permute-start(bf16[2,256,256]{2,1,0:T(8,128)(2,1)} %get-tuple-element.39), channel_id=1, source_target_pairs={{0,1},{1,0},{2,3},{3,2},{4,8},{5,9},{6,10},{7,11},{8,4},{9,5},{10,... | collective-permute-start | bytes 786440 | tf_op jit(solution)/shard_map/ppermute | solution.py:294
  65.5 10.7 %collective-permute-start.11 = (bf16[2,256,256]{2,1,0:T(8,128)(2,1)}, bf16[2,256,256]{2,1,0:T(8,128)(2,1)S(1)}, u32[]{:S(2)}, u32[]{:S(2)}) collective-permute-start(bf16[2,256,256]{2,1,0:T(8,128)(2,1)} %get-tuple-element.42), channel_id=1, source_target_pairs={{0,1},{1,0},{2,3},{3,2},{4,8},{5,9},{6,10},{7,11},{8,4},{9,5},{10,... | collective-permute-start | bytes 786440 | tf_op jit(solution)/shard_map/ppermute | solution.py:294
  69.1 45.0 %copy-start.10 = (bf16[2,256,256]{2,1,0:T(8,128)(2,1)S(1)}, bf16[2,256,256]{2,1,0:T(8,128)(2,1)}, u32[]{:S(2)}) copy-start(bf16[2,256,256]{2,1,0:T(8,128)(2,1)} %get-tuple-element.50.refs_0_) | copy-start | bytes 786436
  69.1 18.2 %collective-permute-start.18 = (bf16[2,256,256]{2,1,0:T(8,128)(2,1)}, bf16[2,256,256]{2,1,0:T(8,128)(2,1)S(1)}, u32[]{:S(2)}, u32[]{:S(2)}) collective-permute-start(bf16[2,256,256]{2,1,0:T(8,128)(2,1)} %get-tuple-element.50.refs_0_), channel_id=1, source_target_pairs={{0,2},{1,3},{2,0},{3,1},{4,6},{5,7},{6,4},{7,5},{8,10},{9,11},{10,... | collective-permute-start | bytes 786440 | tf_op jit(solution)/shard_map/ppermute | solution.py:275
  70.8 16.5 %collective-permute-start.16 = (bf16[2,256,256]{2,1,0:T(8,128)(2,1)}, bf16[2,256,256]{2,1,0:T(8,128)(2,1)S(1)}, u32[]{:S(2)}, u32[]{:S(2)}) collective-permute-start(bf16[2,256,256]{2,1,0:T(8,128)(2,1)} %get-tuple-element.50.refs_0_), channel_id=1, source_target_pairs={{0,1},{1,0},{2,3},{3,2},{4,5},{5,4},{6,7},{7,6},{8,9},{9,8},{10,11... | collective-permute-start | bytes 786440 | tf_op jit(solution)/shard_map/ppermute | solution.py:275
  73.8 40.2 %copy-start.11 = (bf16[2,256,256]{2,1,0:T(8,128)(2,1)S(1)}, bf16[2,256,256]{2,1,0:T(8,128)(2,1)}, u32[]{:S(2)}) copy-start(bf16[2,256,256]{2,1,0:T(8,128)(2,1)} %get-tuple-element.52.refs_8_) | copy-start | bytes 786436
  80.0 1.3 collective-permute-start.12
  81.4 3.7 %collective-permute-start.13 = (f32[2,8,128]{2,1,0:T(8,128)S(1)}, f32[2,8,128]{2,1,0:T(8,128)S(1)}, u32[]{:S(2)}, u32[]{:S(2)}) collective-permute-start(f32[2,8,128]{2,1,0:T(8,128)S(1)} %add.21), channel_id=1, source_target_pairs={{0,2},{1,3},{2,0},{3,1},{4,6},{5,7},{6,4},{7,5},{8,10},{9,11},{10,... | collective-permute-start | bytes 24584 | tf_op jit(solution)/shard_map/ppermute | solution.py:315
  85.0 1.2 collective-permute-start.14
  85.0 9.3 %collective-permute-start.24 = (bf16[2,256,256]{2,1,0:T(8,128)(2,1)}, bf16[2,256,256]{2,1,0:T(8,128)(2,1)S(1)}, u32[]{:S(2)}, u32[]{:S(2)}) collective-permute-start(bf16[2,256,256]{2,1,0:T(8,128)(2,1)} %get-tuple-element.52.refs_8_), channel_id=1, source_target_pairs={{0,2},{1,3},{2,0},{3,1},{4,6},{5,7},{6,4},{7,5},{8,10},{9,11},{10,... | collective-permute-start | bytes 786440 | tf_op jit(solution)/shard_map/ppermute | solution.py:275
  85.4 9.0 %collective-permute-start.22 = (bf16[2,256,256]{2,1,0:T(8,128)(2,1)}, bf16[2,256,256]{2,1,0:T(8,128)(2,1)S(1)}, u32[]{:S(2)}, u32[]{:S(2)}) collective-permute-start(bf16[2,256,256]{2,1,0:T(8,128)(2,1)} %get-tuple-element.52.refs_8_), channel_id=1, source_target_pairs={{0,1},{1,0},{2,3},{3,2},{4,5},{5,4},{6,7},{7,6},{8,9},{9,8},{10,11... | collective-permute-start | bytes 786440 | tf_op jit(solution)/shard_map/ppermute | solution.py:275
  86.2 13.9 %collective-permute-start.25 = (bf16[2,256,256]{2,1,0:T(8,128)(2,1)}, bf16[2,256,256]{2,1,0:T(8,128)(2,1)}, u32[]{:S(2)}, u32[]{:S(2)}) collective-permute-start(bf16[2,256,256]{2,1,0:T(8,128)(2,1)} %get-tuple-element.53.refs_9_), channel_id=1, source_target_pairs={{0,2},{1,3},{2,0},{3,1},{4,6},{5,7},{6,4},{7,5},{8,10},{9,11},{10,... | collective-permute-start | bytes 786440 | tf_op jit(solution)/shard_map/ppermute | solution.py:275
  87.3 12.8 %collective-permute-start.23 = (bf16[2,256,256]{2,1,0:T(8,128)(2,1)}, bf16[2,256,256]{2,1,0:T(8,128)(2,1)S(1)}, u32[]{:S(2)}, u32[]{:S(2)}) collective-permute-start(bf16[2,256,256]{2,1,0:T(8,128)(2,1)} %get-tuple-element.53.refs_9_), channel_id=1, source_target_pairs={{0,1},{1,0},{2,3},{3,2},{4,5},{5,4},{6,7},{7,6},{8,9},{9,8},{10,11... | collective-permute-start | bytes 786440 | tf_op jit(solution)/shard_map/ppermute | solution.py:275
  87.3 18.0 %collective-permute-start.19 = (bf16[2,256,256]{2,1,0:T(8,128)(2,1)}, bf16[2,256,256]{2,1,0:T(8,128)(2,1)}, u32[]{:S(2)}, u32[]{:S(2)}) collective-permute-start(bf16[2,256,256]{2,1,0:T(8,128)(2,1)} %get-tuple-element.51.refs_1_), channel_id=1, source_target_pairs={{0,2},{1,3},{2,0},{3,1},{4,6},{5,7},{6,4},{7,5},{8,10},{9,11},{10,... | collective-permute-start | bytes 786440 | tf_op jit(solution)/shard_map/ppermute | solution.py:275
  94.3 14.3 %collective-permute-start.17 = (bf16[2,256,256]{2,1,0:T(8,128)(2,1)}, bf16[2,256,256]{2,1,0:T(8,128)(2,1)}, u32[]{:S(2)}, u32[]{:S(2)}) collective-permute-start(bf16[2,256,256]{2,1,0:T(8,128)(2,1)} %get-tuple-element.51.refs_1_), channel_id=1, source_target_pairs={{0,1},{1,0},{2,3},{3,2},{4,5},{5,4},{6,7},{7,6},{8,9},{9,8},{10,11... | collective-permute-start | bytes 786440 | tf_op jit(solution)/shard_map/ppermute | solution.py:275
  95.1 19.0 %collective-permute-start.20 = (bf16[2,256,256]{2,1,0:T(8,128)(2,1)S(1)}, bf16[2,256,256]{2,1,0:T(8,128)(2,1)}, u32[]{:S(2)}, u32[]{:S(2)}) collective-permute-start(bf16[2,256,256]{2,1,0:T(8,128)(2,1)S(1)} %collective-permute-done.18.refs_4_), channel_id=1, source_target_pairs={{0,1},{1,0},{2,3},{3,2},{4,5},{5,4},{6,7},{7,6},{8,9},{9,8},{10,11... | collective-permute-start | bytes 786440 | tf_op jit(solution)/shard_map/ppermute | solution.py:275
  100.1 14.0 %collective-permute-start.26 = (bf16[2,256,256]{2,1,0:T(8,128)(2,1)S(1)}, bf16[2,256,256]{2,1,0:T(8,128)(2,1)}, u32[]{:S(2)}, u32[]{:S(2)}) collective-permute-start(bf16[2,256,256]{2,1,0:T(8,128)(2,1)S(1)} %collective-permute-done.24.refs_12_), channel_id=1, source_target_pairs={{0,1},{1,0},{2,3},{3,2},{4,5},{5,4},{6,7},{7,6},{8,9},{9,8},{10,11... | collective-permute-start | bytes 786440 | tf_op jit(solution)/shard_map/ppermute | solution.py:275
  100.8 13.2 %collective-permute-start.27 = (bf16[2,256,256]{2,1,0:T(8,128)(2,1)}, bf16[2,256,256]{2,1,0:T(8,128)(2,1)}, u32[]{:S(2)}, u32[]{:S(2)}) collective-permute-start(bf16[2,256,256]{2,1,0:T(8,128)(2,1)} %collective-permute-done.25.refs_13_), channel_id=1, source_target_pairs={{0,1},{1,0},{2,3},{3,2},{4,5},{5,4},{6,7},{7,6},{8,9},{9,8},{10,11... | collective-permute-start | bytes 786440 | tf_op jit(solution)/shard_map/ppermute | solution.py:275
  105.3 8.7 %collective-permute-start.21 = (bf16[2,256,256]{2,1,0:T(8,128)(2,1)}, bf16[2,256,256]{2,1,0:T(8,128)(2,1)}, u32[]{:S(2)}, u32[]{:S(2)}) collective-permute-start(bf16[2,256,256]{2,1,0:T(8,128)(2,1)} %collective-permute-done.19.refs_5_), channel_id=1, source_target_pairs={{0,1},{1,0},{2,3},{3,2},{4,5},{5,4},{6,7},{7,6},{8,9},{9,8},{10,11... | collective-permute-start | bytes 786440 | tf_op jit(solution)/shard_map/ppermute | solution.py:275
  108.6 42.7 %collective-permute-start.15 = (bf16[256,1024]{1,0:T(8,128)(2,1)}, bf16[256,1024]{1,0:T(8,128)(2,1)}, u32[]{:S(2)}, u32[]{:S(2)}) collective-permute-start(bf16[256,1024]{1,0:T(8,128)(2,1)} %get-tuple-element.49), channel_id=1, source_target_pairs={{0,4},{4,0},{8,12},{12,8},{1,5},{5,1},{9,13},{13,9},{2,6},{6,2},{1... | collective-permute-start | bytes 1572872 | tf_op jit(solution)/shard_map/ppermute | solution.py:319
  114.1 2.2 %copy-start.1 = (bf16[8,4,256,256]{3,2,1,0:T(8,128)(2,1)S(1)}, bf16[8,4,256,256]{3,2,1,0:T(8,128)(2,1)}, u32[]{:S(2)}) copy-start(bf16[8,4,256,256]{3,2,1,0:T(8,128)(2,1)} %refs_18_.3) | copy-start | bytes 12582916
  128.8 7.5 %copy-start.28 = (bf16[2,256,256]{2,1,0:T(8,128)(2,1)}, bf16[2,256,256]{2,1,0:T(8,128)(2,1)S(1)}, u32[]{:S(2)}) copy-start(bf16[2,256,256]{2,1,0:T(8,128)(2,1)S(1)} %get-tuple-element.57) | copy-start | bytes 786436
  128.8 10.7 %collective-permute-start.32 = (bf16[2,256,256]{2,1,0:T(8,128)(2,1)}, bf16[2,256,256]{2,1,0:T(8,128)(2,1)}, u32[]{:S(2)}, u32[]{:S(2)}) collective-permute-start(bf16[2,256,256]{2,1,0:T(8,128)(2,1)} %get-tuple-element.61), channel_id=1, source_target_pairs={{0,1},{1,0},{2,3},{3,2},{4,8},{5,9},{6,10},{7,11},{8,4},{9,5},{10,... | collective-permute-start | bytes 786440 | tf_op jit(solution)/shard_map/ppermute | solution.py:294
  138.6 6.2 %collective-permute-start.30 = (bf16[2,256,256]{2,1,0:T(8,128)(2,1)}, bf16[2,256,256]{2,1,0:T(8,128)(2,1)S(1)}, u32[]{:S(2)}, u32[]{:S(2)}) collective-permute-start(bf16[2,256,256]{2,1,0:T(8,128)(2,1)} %get-tuple-element.59), channel_id=1, source_target_pairs={{0,1},{1,0},{2,3},{3,2},{4,8},{5,9},{6,10},{7,11},{8,4},{9,5},{10,... | collective-permute-start | bytes 786440 | tf_op jit(solution)/shard_map/ppermute | solution.py:294
  138.9 14.2 %collective-permute-start.29 = (bf16[2,256,256]{2,1,0:T(8,128)(2,1)}, bf16[2,256,256]{2,1,0:T(8,128)(2,1)S(1)}, u32[]{:S(2)}, u32[]{:S(2)}) collective-permute-start(bf16[2,256,256]{2,1,0:T(8,128)(2,1)} %copy-done.28), channel_id=1, source_target_pairs={{0,1},{1,0},{2,3},{3,2},{4,8},{5,9},{6,10},{7,11},{8,4},{9,5},{10,... | collective-permute-start | bytes 786440 | tf_op jit(solution)/shard_map/ppermute | solution.py:294
  139.2 14.0 %collective-permute-start.28 = (bf16[2,256,256]{2,1,0:T(8,128)(2,1)}, bf16[2,256,256]{2,1,0:T(8,128)(2,1)S(1)}, u32[]{:S(2)}, u32[]{:S(2)}) collective-permute-start(bf16[2,256,256]{2,1,0:T(8,128)(2,1)} %copy-done.29), channel_id=1, source_target_pairs={{0,1},{1,0},{2,3},{3,2},{4,8},{5,9},{6,10},{7,11},{8,4},{9,5},{10,... | collective-permute-start | bytes 786440 | tf_op jit(solution)/shard_map/ppermute | solution.py:294
  141.8 11.5 %collective-permute-start.33 = (bf16[2,256,256]{2,1,0:T(8,128)(2,1)}, bf16[2,256,256]{2,1,0:T(8,128)(2,1)S(1)}, u32[]{:S(2)}, u32[]{:S(2)}) collective-permute-start(bf16[2,256,256]{2,1,0:T(8,128)(2,1)} %shard_map.97), channel_id=1, source_target_pairs={{0,4},{4,0},{8,12},{12,8},{1,5},{5,1},{9,13},{13,9},{2,6},{6,2},{1... | collective-permute-start | bytes 786440 | tf_op jit(solution)/shard_map/ppermute | solution.py:321
  147.9 8.8 %collective-permute-start.31 = (bf16[2,256,256]{2,1,0:T(8,128)(2,1)}, bf16[2,256,256]{2,1,0:T(8,128)(2,1)S(1)}, u32[]{:S(2)}, u32[]{:S(2)}) collective-permute-start(bf16[2,256,256]{2,1,0:T(8,128)(2,1)} %shard_map.96), channel_id=1, source_target_pairs={{0,4},{4,0},{8,12},{12,8},{1,5},{5,1},{9,13},{13,9},{2,6},{6,2},{1... | collective-permute-start | bytes 786440 | tf_op jit(solution)/shard_map/ppermute | solution.py:321
  153.2 3.5 %copy-start.34 = (bf16[2,256,256]{2,1,0:T(8,128)(2,1)}, bf16[2,256,256]{2,1,0:T(8,128)(2,1)S(1)}, u32[]{:S(2)}) copy-start(bf16[2,256,256]{2,1,0:T(8,128)(2,1)S(1)} %collective-permute-done.29.refs_3_) | copy-start | bytes 786436
  153.2 3.5 %copy-start.35 = (bf16[2,256,256]{2,1,0:T(8,128)(2,1)}, bf16[2,256,256]{2,1,0:T(8,128)(2,1)S(1)}, u32[]{:S(2)}) copy-start(bf16[2,256,256]{2,1,0:T(8,128)(2,1)S(1)} %collective-permute-done.28.refs_2_) | copy-start | bytes 786436
  153.2 3.5 %copy-start.36 = (bf16[2,256,256]{2,1,0:T(8,128)(2,1)}, bf16[2,256,256]{2,1,0:T(8,128)(2,1)S(1)}, u32[]{:S(2)}) copy-start(bf16[2,256,256]{2,1,0:T(8,128)(2,1)S(1)} %collective-permute-done.33.refs_7_) | copy-start | bytes 786436
  (24 other events, 19.3 us)

commit v4 on v0

v4 whole, which is shorter than its diff:
```python
import functools

import jax
import jax.numpy as jnp
from jax import lax
from jax.experimental import pallas as pl
from jax.experimental.pallas import tpu as pltpu
from jax.sharding import PartitionSpec as P

CHUNKS = 2
VMEM_LIMIT = 56 * 1024 * 1024
ANY = pl.BlockSpec(memory_space=pl.ANY)
SMEM = pl.BlockSpec(memory_space=pltpu.SMEM)


def bits_of(size):
    count = size.bit_length() - 1
    assert 1 << count == size
    return count


def swap(axis, bit):
    return [(place, place ^ bit) for place in range(lax.axis_size(axis))]


def leads(row):
    return (row ^ (row >> 1)) & 1


def leader_swap(bit):
    rows, cols = lax.axis_size("row"), lax.axis_size("col")
    pairs = []
    for row in range(rows):
        for col in range(cols):
            if leads(row):
                pair = (row >> 1) ^ bit
                there = (2 * pair if leads(2 * pair) else 2 * pair + 1, col)
            else:
                there = (row, col ^ 1)
            pairs.append((row * cols + col, there[0] * cols + there[1]))
    return pairs


def reverse_bits(value, count):
    out = 0
    for bit in range(count):
        out = out | (((value >> bit) & 1) << (count - 1 - bit))
    return out


def keep_corner(block, rows, cols):
    inside = (lax.broadcasted_iota(jnp.int32, block.shape, 0) < rows) & (
        lax.broadcasted_iota(jnp.int32, block.shape, 1) < cols
    )
    return jnp.where(inside, block.astype(jnp.float32), 0.0).astype(block.dtype)


def mask_left_kernel(left_dest, left_sizes, left, out):
    row = lax.axis_index("row")
    out[0] = keep_corner(left[0, 0], left_sizes[left_dest[pl.program_id(0), row]], left_sizes[row])


def mask_left(left_dest, left_sizes, left):
    terms, _, tile, _ = left.shape
    return pl.pallas_call(
        mask_left_kernel,
        grid=(terms,),
        in_specs=[SMEM, SMEM, pl.BlockSpec((1, 1, tile, tile), lambda term: (term, 0, 0, 0))],
        out_specs=pl.BlockSpec((1, tile, tile), lambda term: (term, 0, 0)),
        out_shape=jax.ShapeDtypeStruct((terms, tile, tile), left.dtype),
        compiler_params=pltpu.CompilerParams(vmem_limit_bytes=VMEM_LIMIT),
        cost_estimate=pl.CostEstimate(flops=left.size, bytes_accessed=4 * left.size, transcendentals=0),
    )(left_dest, left_sizes, left)


def mask_right_kernel(right_src, right_sizes, right, out):
    term, local = pl.program_id(0), right.shape[1]
    col = lax.axis_index("col")
    for place in range(local):
        block = col * local + place
        out[0, place] = keep_corner(right[0, place], right_sizes[block], right_sizes[right_src[term, block]])


def mask_right(right_src, right_sizes, right):
    terms, local, tile, _ = right.shape
    spec = pl.BlockSpec((1, local, tile, tile), lambda term: (term, 0, 0, 0))
    return pl.pallas_call(
        mask_right_kernel,
        grid=(terms,),
        in_specs=[SMEM, SMEM, spec],
        out_specs=spec,
        out_shape=jax.ShapeDtypeStruct(right.shape, right.dtype),
        compiler_params=pltpu.CompilerParams(vmem_limit_bytes=VMEM_LIMIT),
        cost_estimate=pl.CostEstimate(flops=right.size, bytes_accessed=4 * right.size, transcendentals=0),
    )(right_src, right_sizes, right)


def product_kernel(first, count, piece_count, row_count, source, target, *refs):
    pieces, refs = refs[:2 * piece_count], refs[2 * piece_count:]
    (left_own, left_near, left_far, right), refs = refs[:4], refs[4:]
    outs, (blocks, left, right_held, inner, total, kept, sent, in_sems, out_sems) = refs[:row_count], refs[row_count:]
    terms, local, tile = right.shape[:3]
    row, col = lax.axis_index("row"), lax.axis_index("col")
    started = []

    def start(here, there):
        copy = pltpu.make_async_copy(here, there, in_sems.at[len(started)])
        copy.start()
        started.append(copy)
        return copy

    right_copies = [start(right.at[:, first], right_held.at[0])]
    piece_copies = []
    for slot in range(2):
        at = 0
        for piece in pieces[slot * piece_count:(slot + 1) * piece_count]:
            for place in range(piece.shape[1] // tile):
                piece_copies.append(
                    start(piece.at[:, place * tile:(place + 1) * tile], blocks.at[at, slot * tile:(slot + 1) * tile])
                )
                at += 1
    half = terms // 2
    near = lax.rem(col, 2) * half
    left_copies = [
        start(left_own, left.at[0]),
        start(left_near, left.at[1, pl.ds(near, half)]),
        start(left_far, left.at[1, pl.ds(half - near, half)]),
    ]
    for step in range(1, count):
        right_copies.append(start(right.at[:, first + step], right_held.at[step]))

    out_copies = []
    for step in range(count):
        right_copies[step].wait()
        if step == 0:
            for copy in piece_copies:
                copy.wait()
        for term in range(terms):
            wanted = source[term, col * local + first + step]
            held = lax.bitwise_xor(lax.div(wanted, local), col) * local + lax.rem(wanted, local)
            inner[term] = lax.dot_general(
                blocks[held], right_held[step, term], (((1,), (1,)), ((), ())), preferred_element_type=jnp.float32
            ).astype(jnp.bfloat16)
        if step == 0:
            for copy in left_copies:
                copy.wait()
        total[...] = jnp.zeros_like(total)
        for term in range(terms):
            for slot in range(2):
                to = target[term, lax.bitwise_xor(row, slot)]
                to_slot = 2 * reverse_bits((to >> 1) ^ (row >> 1), bits_of(row_count) - 1) + 1 - leads(to)
                total[to_slot] += jnp.dot(
                    left[slot, term], inner[term, slot * tile:(slot + 1) * tile], preferred_element_type=jnp.float32
                )
        for slot in range(row_count):
            if slot < 2:
                held = kept.at[slot, step]
                held[...] = total[slot]
            else:
                held = sent.at[slot - 2, step]
                held[...] = total[slot].astype(sent.dtype)
            copy = pltpu.make_async_copy(
                held, outs[slot].at[:, step * tile:(step + 1) * tile], out_sems.at[len(out_copies)]
            )
            copy.start()
            out_copies.append(copy)
    for copy in out_copies:
        copy.wait()


def products(pieces, left, right, source, target, row_count, first, count):
    terms, local, tile = right.shape[:3]
    blocks = sum(piece.shape[1] for piece in pieces[0]) // tile
    pieces = [piece for row_pieces in pieces for piece in row_pieces]
    return pl.pallas_call(
        functools.partial(product_kernel, first, count, len(pieces) // 2, row_count),
        in_specs=[SMEM, SMEM] + [ANY] * (len(pieces) + 4),
        out_specs=[ANY] * row_count,
        out_shape=[
            jax.ShapeDtypeStruct((tile, count * tile), jnp.float32 if slot < 2 else jnp.bfloat16)
            for slot in range(row_count)
        ],
        scratch_shapes=[
            pltpu.VMEM((blocks, 2 * tile, tile), jnp.bfloat16),
            pltpu.VMEM((2, terms, tile, tile), jnp.bfloat16),
            pltpu.VMEM((count, terms, tile, tile), jnp.bfloat16),
            pltpu.VMEM((terms, 2 * tile, tile), jnp.bfloat16),
            pltpu.VMEM((row_count, tile, tile), jnp.float32),
            pltpu.VMEM((2, count, tile, tile), jnp.float32),
            pltpu.VMEM((row_count - 2, count, tile, tile), jnp.bfloat16),
            pltpu.SemaphoreType.DMA((count + 2 * blocks + 3,)),
            pltpu.SemaphoreType.DMA((count * row_count,)),
        ],
        compiler_params=pltpu.CompilerParams(vmem_limit_bytes=VMEM_LIMIT),
        cost_estimate=pl.CostEstimate(
            flops=8 * terms * count * tile**3,
            bytes_accessed=2 * tile * tile * (2 * blocks + terms * (2 + count) + count * (row_count + 2)),
            transcendentals=0,
        ),
    )(source, target, *pieces, *left, right)


def on_device(wavefunction, left_ops, right_ops, left_dest, right_src, left_sizes, right_sizes):
    tile = left_ops.shape[2]
    local = right_ops.shape[1]
    row_count, col_count = lax.axis_size("row"), lax.axis_size("col")
    pair_bits, col_bits = bits_of(row_count) - 1, bits_of(col_count)
    entry_count = wavefunction.shape[0] * row_count * wavefunction.shape[1] * col_count
    both = ("row", "col")
    row, col = lax.axis_index("row"), lax.axis_index("col")
    leading = leads(row) == 1
    count = local // CHUNKS
    width = count * tile

    def gather(part):
        pieces = {0: part}
        for bit in reversed(range(col_bits)):
            for place in list(pieces):
                pieces[place | (1 << bit)] = lax.ppermute(pieces[place], "col", swap("col", 1 << bit))
        return [pieces[place] for place in range(col_count)]

    vectors = [wavefunction, lax.ppermute(wavefunction, "row", swap("row", 1))]
    left_own = mask_left(left_dest, left_sizes, left_ops)
    half = left_ops.shape[0] // 2
    left_near = lax.dynamic_slice_in_dim(left_own, (col & 1) * half, half, 0)
    left_near = lax.ppermute(left_near, "row", swap("row", 1))
    left = [left_own, left_near, lax.ppermute(left_near, "col", swap("col", 1))]
    right = mask_right(right_src, right_sizes, right_ops)

    def apply_h(pieces):
        out = []
        for first in range(0, local, count):
            sums = products(pieces, left, right, right_src, left_dest, row_count, first, count)
            for bit in range(pair_bits):
                half = len(sums) // 2
                arrived = [lax.ppermute(part, both, leader_swap(1 << bit)) for part in sums[:half - 1:-1]][::-1]
                if bit < pair_bits - 1:
                    sums = [
                        (kept.astype(jnp.float32) + more.astype(jnp.float32)).astype(kept.dtype)
                        for kept, more in zip(sums[:half], arrived)
                    ]
            out.append((sums[:2], arrived))
        return out

    once = apply_h([gather(vector) for vector in vectors])
    pieces = [[[] for _ in range(col_count)] for _ in range(2)]
    for kept, arrived in once:
        for slot in (1, 0):
            rounded = (kept[slot] + arrived[slot].astype(jnp.float32)).astype(jnp.bfloat16)
            for place, piece in enumerate(gather(rounded)):
                pieces[slot][place].append(piece)
    again = apply_h([[piece for place in places for piece in place] for places in pieces])
    once, vectors, _ = lax.optimization_barrier((once, vectors, again[-1][0]))
    images = [
        [kept[slot] + arrived[slot].astype(jnp.float32) for kept, arrived in once] for slot in range(2)
    ]
    offsets = jnp.arange(tile)
    right_here = lax.dynamic_slice_in_dim(right_sizes, col * local, local, 0)
    col_valid = (offsets[None, :] < right_here[:, None]).reshape(-1)
    norm = correlation = 0.0
    for slot in range(2):
        row_valid = offsets < lax.dynamic_index_in_dim(left_sizes, row ^ slot, 0, keepdims=False)
        vector = jnp.where(row_valid[:, None] & col_valid[None, :], vectors[slot].astype(jnp.float32), 0.0)
        norm += jnp.sum(vector * vector)
        for chunk, image in enumerate(images[slot]):
            correlation += jnp.sum(vector[:, chunk * width:(chunk + 1) * width] * image)
    stats = jnp.broadcast_to(jnp.stack([norm, correlation])[:, None], (2, 128))
    for bit in range(col_bits):
        stats = stats + lax.ppermute(stats, "col", swap("col", 1 << bit))
    for bit in range(pair_bits):
        stats = stats + lax.ppermute(stats, both, leader_swap(1 << bit))
    norm, correlation = stats[0, 0], stats[1, 0]
    scale = lax.rsqrt(norm / entry_count + 1e-06)
    theta = correlation / norm

    def to_rows(of_slots):
        sent = [lax.ppermute(part, "row", swap("row", 1)) for part in of_slots[1]]
        return jnp.concatenate([jnp.where(leading, mine, theirs) for mine, theirs in zip(of_slots[0], sent)], 1)

    first_product = to_rows([[(image * scale).astype(jnp.bfloat16) for image in parts] for parts in images])
    second_product = to_rows([
        [
            ((kept[slot] - theta * image + arrived[slot].astype(jnp.float32)) * scale).astype(jnp.bfloat16)
            for (kept, arrived), image in zip(again, images[slot])
        ]
        for slot in range(2)
    ])
    return (first_product, second_product)


def solution(mesh):
    placed = (
        P(("groups", "row"), "col"),
        P(None, ("groups", "row"), None, None),
        P(None, ("groups", "col"), None, None),
        P(None, "groups"),
        P(None, "groups"),
        P("groups"),
        P("groups"),
    )
    return jax.shard_map(
        on_device,
        mesh=mesh,
        in_specs=placed,
        out_specs=(P(("groups", "row"), "col"), P(("groups", "row"), "col")),
        check_vma=False,
    )
```

time: 249 us -> 163 us (0.65)
  waiting for transfers between devices: 130 us -> 49.8 us
  Pallas kernels: 0 us -> 50.3 us
  starting transfers between devices: 0.34 us -> 37.2 us
  local copies, waits for them, and re-layouts: 38.4 us -> 5.89 us
  blocking collectives: 32.1 us -> 0 us
  matrix products: 23 us -> 0 us
  between operations: 15.8 us -> 6.73 us
  other arithmetic: 8.87 us -> 12.4 us
    reduce_scatter x2 -> x0, waiting for transfers between devices: 86 us -> none  [apply_once(): lax.psum_scatter(jnp.einsum('tk,tan->kan', onehot, contrib).reshape(tile_...]
    pallas_call x0 -> x6, Pallas kernels: none -> 50.3 us  [the longest x4 37.6 us: products(): pl.pallas_call(functools.partial(product_kernel, first, count, len(pieces...]
    ppermute x0 -> x36, waiting for transfers between devices: none -> 49.8 us  [the longest x18 27.1 us: gather(): lax.ppermute(pieces[place], 'col', swap('col', 1 << bit))]
    all_gather x2 -> x0, waiting for transfers between devices: 43.6 us -> none  [apply_once(): gathered = lax.all_gather(vector, 'col', axis=1, tiled=True)]
    ppermute x0 -> x36, starting transfers between devices: none -> 37.2 us  [the longest x4 19.5 us: to_rows(): sent = [lax.ppermute(part, 'row', swap('row', 1)) for part in of_slots[1]]]
    psum x1 -> x0, blocking collectives: 32.1 us -> none  [on_device(): lax.psum((jnp.sum(masked_float * masked_float), jnp.sum(masked_float * im...]
    dot_general x6 -> x0, matrix products: 23 us -> none  [the longest x2 9.68 us: apply_once(): jnp.einsum('rtjc,tjdc->trjd', chosen, right_ops, preferred_element_type=j...]
    dot_general x2 -> x0, local copies, waits for them, and re-layouts: 13.7 us -> none  [apply_once(): jnp.einsum('tab,tbn->tan', left_here, inner_terms, preferred_element_type...]
  transfers between devices with their start and end apart: 4 -> 36, of which waited for: 4 -> 12; matrix products, arithmetic and copies ran while one was open for 1% -> 6% of each run, Pallas kernels for 0% -> 19%
where the time goes in v4:
time: 163 us; the launch traced here: 162 us
  Pallas kernels  50.3 us (31%)
  waiting for transfers between devices  49.8 us (31%)
  starting transfers between devices  37.2 us (23%)
  other arithmetic  12.4 us (8%)
  between operations  6.73 us (4%)
  local copies, waits for them, and re-layouts  5.89 us (4%)
    pallas_call x4, Pallas kernels, products(): pl.pallas_call(functools.partial(product_kernel, first, count, len(pieces...  37.6 us
    ppermute x18, waiting for transfers between devices, gather(): lax.ppermute(pieces[place], 'col', swap('col', 1 << bit))  27.1 us
    ppermute x4, starting transfers between devices, to_rows(): sent = [lax.ppermute(part, 'row', swap('row', 1)) for part in of_slots[1]]  19.5 us
    ppermute x18, starting transfers between devices, gather(): lax.ppermute(pieces[place], 'col', swap('col', 1 << bit))  10.6 us
    ppermute x4, waiting for transfers between devices, to_rows(): sent = [lax.ppermute(part, 'row', swap('row', 1)) for part in of_slots[1]]  8.56 us
    ppermute x1, waiting for transfers between devices, on_device(): left_near = lax.ppermute(left_near, 'row', swap('row', 1))  7.92 us
    pallas_call x1, Pallas kernels, mask_right(): pl.pallas_call(mask_right_kernel, grid=(terms,), in_specs=[SMEM, SMEM, sp...  7.33 us
    pallas_call x1, Pallas kernels, mask_left(): pl.pallas_call(mask_left_kernel, grid=(terms,), in_specs=[SMEM, SMEM, pl....  5.37 us
  transfers between devices with their start and end apart: 36, of which 12 were waited for; matrix products, arithmetic and copies ran while one was open for 6% of the time, Pallas kernels for 19%

profile of v4, /device:TPU:0, one launch (start us, length us, event | category | flops | bytes accessed | tf_op | source)
XLA Modules:
  0.0 162.3 jit_solution(6766002522237476228)
XLA Ops:
  0.6 3.1 %collective-permute-start.3 = (bf16[256,1024]{1,0:T(8,128)(2,1)}, bf16[256,1024]{1,0:T(8,128)(2,1)S(1)}, u32[]{:S(2)}, u32[]{:S(2)}) collective-permute-start(bf16[256,1024]{1,0:T(8,128)(2,1)} %refs_0_.3), channel_id=1, source_target_pairs={{0,4},{4,0},{8,12},{12,8},{1,5},{5,1},{9,13},{13,9},{2,6},{6,2},{1... | collective-permute-start | bytes 1572872 | tf_op jit(solution)/shard_map/ppermute | solution.py:222
  3.7 1.3 copy.10.left_dest.target
  5.1 5.4 %shard_map.86.refs_8_.refs_16_ = bf16[8,256,256]{2,1,0:T(8,128)(2,1)} custom-call(s32[8,4]{1,0:T(8,128)} %copy.10.left_dest.target, s32[4]{0:T(128)} %left_sizes.1, bf16[8,1,256,256]{3,2,1,0:T(8,128)(2,1)} %left.1), custom_call_target="tpu_custom_call" | custom-call | flops 524288 | bytes 2097152 | tf_op jit(solution)/shard_map/pallas_call | solution.py:65
  10.4 1.1 constant_dynamic-slice_fusion
  11.6 1.9 %collective-permute-start.1 = (bf16[256,1024]{1,0:T(8,128)(2,1)}, bf16[256,1024]{1,0:T(8,128)(2,1)S(1)}, u32[]{:S(2)}, u32[]{:S(2)}) collective-permute-start(bf16[256,1024]{1,0:T(8,128)(2,1)} %refs_0_.3), channel_id=1, source_target_pairs={{0,2},{1,3},{2,0},{3,1},{4,6},{5,7},{6,4},{7,5},{8,10},{9,11},{10,... | collective-permute-start | bytes 1572872 | tf_op jit(solution)/shard_map/ppermute | solution.py:219
  13.5 3.2 %collective-permute-done.3.refs_4_ = bf16[256,1024]{1,0:T(8,128)(2,1)S(1)} collective-permute-done((bf16[256,1024]{1,0:T(8,128)(2,1)}, bf16[256,1024]{1,0:T(8,128)(2,1)S(1)}, u32[]{:S(2)}, u32[]{:S(2)}) %collective-permute-start.3) | collective-permute-done | bytes 524320 | tf_op jit(solution)/shard_map/ppermute | solution.py:222
  16.7 2.0 %collective-permute-start.5 = (bf16[256,1024]{1,0:T(8,128)(2,1)S(1)}, bf16[256,1024]{1,0:T(8,128)(2,1)S(1)}, u32[]{:S(2)}, u32[]{:S(2)}) collective-permute-start(bf16[256,1024]{1,0:T(8,128)(2,1)S(1)} %collective-permute-done.3.refs_4_), channel_id=1, source_target_pairs={{0,2},{1,3},{2,0},{3,1},{4,6},{5,7},{6,4},{7,5},{8,10},{9,11},{10,... | collective-permute-start | bytes 1572872 | tf_op jit(solution)/shard_map/ppermute | solution.py:219
  18.7 0.5 collective-permute-start.4
  19.2 7.9 %collective-permute-done.7.refs_9_.refs_17_ = bf16[4,256,256]{2,1,0:T(8,128)(2,1)S(1)} collective-permute-done((bf16[4,256,256]{2,1,0:T(8,128)(2,1)S(1)}, bf16[4,256,256]{2,1,0:T(8,128)(2,1)S(1)}, u32[]{:S(2)}, u32[]{:S(2)}) %collective-permute-start.7) | collective-permute-done | bytes 524320 | tf_op jit(solution)/shard_map/ppermute | solution.py:226
  27.1 0.5 collective-permute-start.2
  27.6 8.9 %collective-permute-done.5.refs_6_ = bf16[256,1024]{1,0:T(8,128)(2,1)S(1)} collective-permute-done((bf16[256,1024]{1,0:T(8,128)(2,1)S(1)}, bf16[256,1024]{1,0:T(8,128)(2,1)S(1)}, u32[]{:S(2)}, u32[]{:S(2)}) %collective-permute-start.5) | collective-permute-done | bytes 524320 | tf_op jit(solution)/shard_map/ppermute | solution.py:219
  36.5 7.3 %shard_map.87.refs_11_.refs_19_ = bf16[8,4,256,256]{3,2,1,0:T(8,128)(2,1)} custom-call(s32[8,16]{1,0:T(8,128)} %source.7, s32[16]{0:T(128)} %right_sizes.1, bf16[8,4,256,256]{3,2,1,0:T(8,128)(2,1)} %right.1), custom_call_target="tpu_custom_call" | custom-call | flops 2097152 | bytes 8388608 | tf_op jit(solution)/shard_map/pallas_call | solution.py:87
  43.9 0.7 copy-done.21
  45.2 0.8 copy-done.24
  46.0 9.3 %shard_map.89 = (f32[256,512]{1,0:T(8,128)}, f32[256,512]{1,0:T(8,128)}, bf16[256,512]{1,0:T(8,128)(2,1)}, bf16[256,512]{1,0:T(8,128)(2,1)}) custom-call(s32[8,16]{1,0:T(8,128)} %source.7, s32[8,4]{1,0:T(8,128)} %copy.10.left_dest.target, bf16[256,1024]{1,0:T(8,128)(2,1)} %refs_0_.3, bf16[256,1024]{1,0:T(8,128)(2,1)} %copy-done.21, ...), custom_call_target="tpu_custom_call" | custom-call | flops 2147483648 | bytes 9961472 | tf_op jit(solution)/shard_map/pallas_call | solution.py:175
  55.7 9.3 %shard_map.88 = (f32[256,512]{1,0:T(8,128)}, f32[256,512]{1,0:T(8,128)}, bf16[256,512]{1,0:T(8,128)(2,1)}, bf16[256,512]{1,0:T(8,128)(2,1)}) custom-call(s32[8,16]{1,0:T(8,128)} %source.7, s32[8,4]{1,0:T(8,128)} %copy.10.left_dest.target, bf16[256,1024]{1,0:T(8,128)(2,1)} %refs_0_.3, bf16[256,1024]{1,0:T(8,128)(2,1)} %copy-done.21, ...), custom_call_target="tpu_custom_call" | custom-call | flops 2147483648 | bytes 9961472 | tf_op jit(solution)/shard_map/pallas_call | solution.py:175
  66.1 1.6 %collective-permute-start.22 = (bf16[256,512]{1,0:T(8,128)(2,1)S(1)}, bf16[256,512]{1,0:T(8,128)(2,1)}, u32[]{:S(2)}, u32[]{:S(2)}) collective-permute-start(bf16[256,512]{1,0:T(8,128)(2,1)S(1)} %add_convert_fusion.refs_9_), channel_id=1, source_target_pairs={{0,2},{1,3},{2,0},{3,1},{4,6},{5,7},{6,4},{7,5},{8,10},{9,11},{10,... | collective-permute-start | bytes 786440 | tf_op jit(solution)/shard_map/ppermute | solution.py:219
  67.7 1.2 add_convert_fusion.1.refs_8_
  68.9 0.8 collective-permute-start.21
  69.9 1.4 collective-permute-start.16
  71.2 1.1 add_convert_fusion.3.refs_0_
  72.3 0.8 collective-permute-start.15
  73.1 2.2 %collective-permute-done.22.refs_13_ = bf16[256,512]{1,0:T(8,128)(2,1)} collective-permute-done((bf16[256,512]{1,0:T(8,128)(2,1)S(1)}, bf16[256,512]{1,0:T(8,128)(2,1)}, u32[]{:S(2)}, u32[]{:S(2)}) %collective-permute-start.22) | collective-permute-done | bytes 262176 | tf_op jit(solution)/shard_map/ppermute | solution.py:219
  75.4 5.6 %collective-permute-done.21.refs_12_ = bf16[256,512]{1,0:T(8,128)(2,1)} collective-permute-done((bf16[256,512]{1,0:T(8,128)(2,1)S(1)}, bf16[256,512]{1,0:T(8,128)(2,1)}, u32[]{:S(2)}, u32[]{:S(2)}) %collective-permute-start.21) | collective-permute-done | bytes 262176 | tf_op jit(solution)/shard_map/ppermute | solution.py:219
  81.2 5.4 %collective-permute-done.16.refs_5_ = bf16[256,512]{1,0:T(8,128)(2,1)} collective-permute-done((bf16[256,512]{1,0:T(8,128)(2,1)S(1)}, bf16[256,512]{1,0:T(8,128)(2,1)}, u32[]{:S(2)}, u32[]{:S(2)}) %collective-permute-start.16) | collective-permute-done | bytes 262176 | tf_op jit(solution)/shard_map/ppermute | solution.py:219
  86.6 4.9 %collective-permute-done.15.refs_4_ = bf16[256,512]{1,0:T(8,128)(2,1)} collective-permute-done((bf16[256,512]{1,0:T(8,128)(2,1)S(1)}, bf16[256,512]{1,0:T(8,128)(2,1)}, u32[]{:S(2)}, u32[]{:S(2)}) %collective-permute-start.15) | collective-permute-done | bytes 262176 | tf_op jit(solution)/shard_map/ppermute | solution.py:219
  91.5 0.5 collective-permute-start.23
  92.1 0.4 collective-permute-start.17
  92.6 0.6 fusion.9
  93.2 0.6 iota_compare_fusion.1
  93.9 0.7 iota_compare_fusion.2
  94.7 9.5 %shard_map.90 = (f32[256,512]{1,0:T(8,128)}, f32[256,512]{1,0:T(8,128)}, bf16[256,512]{1,0:T(8,128)(2,1)}, bf16[256,512]{1,0:T(8,128)(2,1)}) custom-call(s32[8,16]{1,0:T(8,128)} %source.7, s32[8,4]{1,0:T(8,128)} %copy.10.left_dest.target, bf16[256,512]{1,0:T(8,128)(2,1)} %copy-done.12, bf16[256,512]{1,0:T(8,128)(2,1)} %copy-done.11, ...), custom_call_target="tpu_custom_call" | custom-call | flops 2147483648 | bytes 9961472 | tf_op jit(solution)/shard_map/pallas_call | solution.py:175
  104.2 2.0 %multiply_reduce_fusion = (f32[]{:T(128)}, f32[]{:T(128)}, f32[256,1024]{1,0:T(8,128)S(1)}, f32[256,1024]{1,0:T(8,128)}) fusion(bf16[256,1024]{1,0:T(8,128)(2,1)S(1)} %copy-done.4, pred[1024]{0:T(1024)(128)(4,1)S(1)} %lt.61, pred[256]{0:T(512)(128)(4,1)S(1)} %iota_compare_fusion.1, bf16[256,1024]{1,0:T(8,128)(2,1)S(1)} %copy-done.2, ...), kind=kLoop, calls=%fused_computation | loop fusion | flops 2621438 | bytes 3147272 | tf_op jit(solution)/shard_map/reduce_sum | solution.py:264
  107.6 2.7 %fusion = (f32[]{:T(128)}, f32[]{:T(128)}, f32[]{:T(128)}, f32[]{:T(128)}) fusion(f32[256,1024]{1,0:T(8,128)} %get-tuple-element.69, f32[256,512]{1,0:T(8,128)S(1)} %copy-done.8, bf16[256,512]{1,0:T(8,128)(2,1)} %copy-done.17, f32[256,512]{1,0:T(8,128)S(1)} %copy-done.7, bf16[256,512]{1,0:T(8,128)(2,1)} %copy-done.15, f32[256,512]{1,0:T(8,128)S(1)} %copy-done.5, ...), kind=kLoop, calls=%fused_computation.5 | loop fusion | flops 2097148 | bytes 5242896 | tf_op jit(solution)/shard_map/reduce_sum | solution.py:266
  113.0 1.0 collective-permute-done.25
  114.1 1.6 collective-permute-start.26
  115.7 2.0 %collective-permute-done.26 = f32[2,128]{1,0:T(2,128)S(1)} collective-permute-done((f32[2,128]{1,0:T(2,128)S(1)}, f32[2,128]{1,0:T(2,128)S(1)}, u32[]{:S(2)}, u32[]{:S(2)}) %collective-permute-start.26) | collective-permute-done | bytes 1056 | tf_op jit(solution)/shard_map/ppermute | solution.py:269
  117.8 9.4 %shard_map.91 = (f32[256,512]{1,0:T(8,128)}, f32[256,512]{1,0:T(8,128)}, bf16[256,512]{1,0:T(8,128)(2,1)}, bf16[256,512]{1,0:T(8,128)(2,1)}) custom-call(s32[8,16]{1,0:T(8,128)} %source.7, s32[8,4]{1,0:T(8,128)} %copy.10.left_dest.target, bf16[256,512]{1,0:T(8,128)(2,1)} %copy-done.12, bf16[256,512]{1,0:T(8,128)(2,1)} %copy-done.11, ...), custom_call_target="tpu_custom_call" | custom-call | flops 2147483648 | bytes 9961472 | tf_op jit(solution)/shard_map/pallas_call | solution.py:175
  128.2 0.5 fusion.8
  130.8 8.3 %collective-permute-start.29 = (bf16[256,512]{1,0:T(8,128)(2,1)S(1)}, bf16[256,512]{1,0:T(8,128)(2,1)S(1)}, u32[]{:S(2)}, u32[]{:S(2)}) collective-permute-start(bf16[256,512]{1,0:T(8,128)(2,1)S(1)} %get-tuple-element.67), channel_id=1, source_target_pairs={{0,4},{4,0},{8,12},{12,8},{1,5},{5,1},{9,13},{13,9},{2,6},{6,2},{1... | collective-permute-start | bytes 786440 | tf_op jit(solution)/shard_map/ppermute | solution.py:277
  139.1 1.2 multiply_convert_fusion.2
  140.4 3.4 %collective-permute-start.28 = (bf16[256,512]{1,0:T(8,128)(2,1)S(1)}, bf16[256,512]{1,0:T(8,128)(2,1)S(1)}, u32[]{:S(2)}, u32[]{:S(2)}) collective-permute-start(bf16[256,512]{1,0:T(8,128)(2,1)S(1)} %get-tuple-element.63), channel_id=1, source_target_pairs={{0,4},{4,0},{8,12},{12,8},{1,5},{5,1},{9,13},{13,9},{2,6},{6,2},{1... | collective-permute-start | bytes 786440 | tf_op jit(solution)/shard_map/ppermute | solution.py:277
  143.8 7.7 %collective-permute-start.32 = (bf16[256,512]{1,0:T(8,128)(2,1)S(1)}, bf16[256,512]{1,0:T(8,128)(2,1)S(1)}, u32[]{:S(2)}, u32[]{:S(2)}) collective-permute-start(bf16[256,512]{1,0:T(8,128)(2,1)S(1)} %get-tuple-element.62), channel_id=1, source_target_pairs={{0,4},{4,0},{8,12},{12,8},{1,5},{5,1},{9,13},{13,9},{2,6},{6,2},{1... | collective-permute-start | bytes 786440 | tf_op jit(solution)/shard_map/ppermute | solution.py:277
  151.5 0.4 collective-permute-done.35
  152.2 5.3 %collective-permute-done.28 = bf16[256,512]{1,0:T(8,128)(2,1)S(1)} collective-permute-done((bf16[256,512]{1,0:T(8,128)(2,1)S(1)}, bf16[256,512]{1,0:T(8,128)(2,1)S(1)}, u32[]{:S(2)}, u32[]{:S(2)}) %collective-permute-start.28) | collective-permute-done | bytes 262176 | tf_op jit(solution)/shard_map/ppermute | solution.py:277
  157.5 2.8 %collective-permute-done.32 = bf16[256,512]{1,0:T(8,128)(2,1)S(1)} collective-permute-done((bf16[256,512]{1,0:T(8,128)(2,1)S(1)}, bf16[256,512]{1,0:T(8,128)(2,1)S(1)}, u32[]{:S(2)}, u32[]{:S(2)}) %collective-permute-start.32) | collective-permute-done | bytes 262176 | tf_op jit(solution)/shard_map/ppermute | solution.py:277
  160.5 0.9 pad_maximum_fusion.1
  161.4 0.9 pad_maximum_fusion
  (126 shorter events, 4.7 us)
Async XLA Ops:
  0.6 16.1 %collective-permute-start.3 = (bf16[256,1024]{1,0:T(8,128)(2,1)}, bf16[256,1024]{1,0:T(8,128)(2,1)S(1)}, u32[]{:S(2)}, u32[]{:S(2)}) collective-permute-start(bf16[256,1024]{1,0:T(8,128)(2,1)} %refs_0_.3), channel_id=1, source_target_pairs={{0,4},{4,0},{8,12},{12,8},{1,5},{5,1},{9,13},{13,9},{2,6},{6,2},{1... | collective-permute-start | bytes 1572872 | tf_op jit(solution)/shard_map/ppermute | solution.py:222
  11.5 15.6 %collective-permute-start.7 = (bf16[4,256,256]{2,1,0:T(8,128)(2,1)S(1)}, bf16[4,256,256]{2,1,0:T(8,128)(2,1)S(1)}, u32[]{:S(2)}, u32[]{:S(2)}) collective-permute-start(bf16[4,256,256]{2,1,0:T(8,128)(2,1)S(1)} %constant_dynamic-slice_fusion), channel_id=1, source_target_pairs={{0,4},{4,0},{8,12},{12,8},{1,5},{5,1},{9,13},{13,9},{2,6},{6,2},{1... | collective-permute-start | bytes 1572872 | tf_op jit(solution)/shard_map/ppermute | solution.py:226
  11.6 15.5 %collective-permute-start.1 = (bf16[256,1024]{1,0:T(8,128)(2,1)}, bf16[256,1024]{1,0:T(8,128)(2,1)S(1)}, u32[]{:S(2)}, u32[]{:S(2)}) collective-permute-start(bf16[256,1024]{1,0:T(8,128)(2,1)} %refs_0_.3), channel_id=1, source_target_pairs={{0,2},{1,3},{2,0},{3,1},{4,6},{5,7},{6,4},{7,5},{8,10},{9,11},{10,... | collective-permute-start | bytes 1572872 | tf_op jit(solution)/shard_map/ppermute | solution.py:219
  16.7 27.1 %copy-start.3 = (bf16[256,1024]{1,0:T(8,128)(2,1)}, bf16[256,1024]{1,0:T(8,128)(2,1)S(1)}, u32[]{:S(2)}) copy-start(bf16[256,1024]{1,0:T(8,128)(2,1)S(1)} %collective-permute-done.3.refs_4_) | copy-start | bytes 1572868
  16.7 19.8 %collective-permute-start.5 = (bf16[256,1024]{1,0:T(8,128)(2,1)S(1)}, bf16[256,1024]{1,0:T(8,128)(2,1)S(1)}, u32[]{:S(2)}, u32[]{:S(2)}) collective-permute-start(bf16[256,1024]{1,0:T(8,128)(2,1)S(1)} %collective-permute-done.3.refs_4_), channel_id=1, source_target_pairs={{0,2},{1,3},{2,0},{3,1},{4,6},{5,7},{6,4},{7,5},{8,10},{9,11},{10,... | collective-permute-start | bytes 1572872 | tf_op jit(solution)/shard_map/ppermute | solution.py:219
  18.7 25.2 %collective-permute-start = (bf16[256,1024]{1,0:T(8,128)(2,1)}, bf16[256,1024]{1,0:T(8,128)(2,1)S(1)}, u32[]{:S(2)}, u32[]{:S(2)}) collective-permute-start(bf16[256,1024]{1,0:T(8,128)(2,1)} %refs_0_.3), channel_id=1, source_target_pairs={{0,1},{1,0},{2,3},{3,2},{4,5},{5,4},{6,7},{7,6},{8,9},{9,8},{10,11... | collective-permute-start | bytes 1572872 | tf_op jit(solution)/shard_map/ppermute | solution.py:219
  18.7 25.2 %collective-permute-start.4 = (bf16[256,1024]{1,0:T(8,128)(2,1)S(1)}, bf16[256,1024]{1,0:T(8,128)(2,1)S(1)}, u32[]{:S(2)}, u32[]{:S(2)}) collective-permute-start(bf16[256,1024]{1,0:T(8,128)(2,1)S(1)} %collective-permute-done.3.refs_4_), channel_id=1, source_target_pairs={{0,1},{1,0},{2,3},{3,2},{4,5},{5,4},{6,7},{7,6},{8,9},{9,8},{10,11... | collective-permute-start | bytes 1572872 | tf_op jit(solution)/shard_map/ppermute | solution.py:219
  27.1 16.7 %copy-start = (bf16[4,256,256]{2,1,0:T(8,128)(2,1)}, bf16[4,256,256]{2,1,0:T(8,128)(2,1)S(1)}, u32[]{:S(2)}) copy-start(bf16[4,256,256]{2,1,0:T(8,128)(2,1)S(1)} %collective-permute-done.7.refs_9_.refs_17_) | copy-start | bytes 1572868
  27.1 16.8 %collective-permute-start.8 = (bf16[4,256,256]{2,1,0:T(8,128)(2,1)S(1)}, bf16[4,256,256]{2,1,0:T(8,128)(2,1)S(1)}, u32[]{:S(2)}, u32[]{:S(2)}) collective-permute-start(bf16[4,256,256]{2,1,0:T(8,128)(2,1)S(1)} %collective-permute-done.7.refs_9_.refs_17_), channel_id=1, source_target_pairs={{0,1},{1,0},{2,3},{3,2},{4,5},{5,4},{6,7},{7,6},{8,9},{9,8},{10,11... | collective-permute-start | bytes 1572872 | tf_op jit(solution)/shard_map/ppermute | solution.py:227
  27.1 16.7 %copy-start.19 = (bf16[256,1024]{1,0:T(8,128)(2,1)}, bf16[256,1024]{1,0:T(8,128)(2,1)S(1)}, u32[]{:S(2)}) copy-start(bf16[256,1024]{1,0:T(8,128)(2,1)S(1)} %collective-permute-done.1.refs_2_) | copy-start | bytes 1572868
  27.1 16.8 %collective-permute-start.2 = (bf16[256,1024]{1,0:T(8,128)(2,1)S(1)}, bf16[256,1024]{1,0:T(8,128)(2,1)S(1)}, u32[]{:S(2)}, u32[]{:S(2)}) collective-permute-start(bf16[256,1024]{1,0:T(8,128)(2,1)S(1)} %collective-permute-done.1.refs_2_), channel_id=1, source_target_pairs={{0,1},{1,0},{2,3},{3,2},{4,5},{5,4},{6,7},{7,6},{8,9},{9,8},{10,11... | collective-permute-start | bytes 1572872 | tf_op jit(solution)/shard_map/ppermute | solution.py:219
  36.5 7.4 %collective-permute-start.6 = (bf16[256,1024]{1,0:T(8,128)(2,1)S(1)}, bf16[256,1024]{1,0:T(8,128)(2,1)S(1)}, u32[]{:S(2)}, u32[]{:S(2)}) collective-permute-start(bf16[256,1024]{1,0:T(8,128)(2,1)S(1)} %collective-permute-done.5.refs_6_), channel_id=1, source_target_pairs={{0,1},{1,0},{2,3},{3,2},{4,5},{5,4},{6,7},{7,6},{8,9},{9,8},{10,11... | collective-permute-start | bytes 1572872 | tf_op jit(solution)/shard_map/ppermute | solution.py:219
  55.3 10.6 %collective-permute-start.12 = (bf16[256,512]{1,0:T(8,128)(2,1)}, bf16[256,512]{1,0:T(8,128)(2,1)S(1)}, u32[]{:S(2)}, u32[]{:S(2)}) collective-permute-start(bf16[256,512]{1,0:T(8,128)(2,1)} %get-tuple-element.35), channel_id=1, source_target_pairs={{0,1},{1,0},{2,3},{3,2},{4,8},{5,9},{6,10},{7,11},{8,4},{9,5},{10,... | collective-permute-start | bytes 786440 | tf_op jit(solution)/shard_map/ppermute | solution.py:236
  65.1 27.6 %copy-start.31 = (s32[4]{0:T(128)S(1)}, s32[4]{0:T(128)}, u32[]{:S(2)}) copy-start(s32[4]{0:T(128)} %left_sizes.1) | copy-start | bytes 52
  65.1 2.7 %collective-permute-start.10 = (bf16[256,512]{1,0:T(8,128)(2,1)}, bf16[256,512]{1,0:T(8,128)(2,1)S(1)}, u32[]{:S(2)}, u32[]{:S(2)}) collective-permute-start(bf16[256,512]{1,0:T(8,128)(2,1)} %get-tuple-element.31), channel_id=1, source_target_pairs={{0,1},{1,0},{2,3},{3,2},{4,8},{5,9},{6,10},{7,11},{8,4},{9,5},{10,... | collective-permute-start | bytes 786440 | tf_op jit(solution)/shard_map/ppermute | solution.py:236
  65.5 4.3 %collective-permute-start.11 = (bf16[256,512]{1,0:T(8,128)(2,1)S(1)}, bf16[256,512]{1,0:T(8,128)(2,1)S(1)}, u32[]{:S(2)}, u32[]{:S(2)}) collective-permute-start(bf16[256,512]{1,0:T(8,128)(2,1)S(1)} %copy-done.34), channel_id=1, source_target_pairs={{0,1},{1,0},{2,3},{3,2},{4,8},{5,9},{6,10},{7,11},{8,4},{9,5},{10,... | collective-permute-start | bytes 786440 | tf_op jit(solution)/shard_map/ppermute | solution.py:236
  65.6 5.6 %collective-permute-start.9 = (bf16[256,512]{1,0:T(8,128)(2,1)}, bf16[256,512]{1,0:T(8,128)(2,1)S(1)}, u32[]{:S(2)}, u32[]{:S(2)}) collective-permute-start(bf16[256,512]{1,0:T(8,128)(2,1)} %get-tuple-element.30), channel_id=1, source_target_pairs={{0,1},{1,0},{2,3},{3,2},{4,8},{5,9},{6,10},{7,11},{8,4},{9,5},{10,... | collective-permute-start | bytes 786440 | tf_op jit(solution)/shard_map/ppermute | solution.py:236
  66.1 28.6 %copy-start.9 = (bf16[256,512]{1,0:T(8,128)(2,1)}, bf16[256,512]{1,0:T(8,128)(2,1)S(1)}, u32[]{:S(2)}) copy-start(bf16[256,512]{1,0:T(8,128)(2,1)S(1)} %add_convert_fusion.refs_9_) | copy-start | bytes 786436
  66.1 9.3 %collective-permute-start.22 = (bf16[256,512]{1,0:T(8,128)(2,1)S(1)}, bf16[256,512]{1,0:T(8,128)(2,1)}, u32[]{:S(2)}, u32[]{:S(2)}) collective-permute-start(bf16[256,512]{1,0:T(8,128)(2,1)S(1)} %add_convert_fusion.refs_9_), channel_id=1, source_target_pairs={{0,2},{1,3},{2,0},{3,1},{4,6},{5,7},{6,4},{7,5},{8,10},{9,11},{10,... | collective-permute-start | bytes 786440 | tf_op jit(solution)/shard_map/ppermute | solution.py:219
  68.9 25.7 %copy-start.10 = (bf16[256,512]{1,0:T(8,128)(2,1)}, bf16[256,512]{1,0:T(8,128)(2,1)S(1)}, u32[]{:S(2)}) copy-start(bf16[256,512]{1,0:T(8,128)(2,1)S(1)} %add_convert_fusion.1.refs_8_) | copy-start | bytes 786436
  68.9 12.1 %collective-permute-start.21 = (bf16[256,512]{1,0:T(8,128)(2,1)S(1)}, bf16[256,512]{1,0:T(8,128)(2,1)}, u32[]{:S(2)}, u32[]{:S(2)}) collective-permute-start(bf16[256,512]{1,0:T(8,128)(2,1)S(1)} %add_convert_fusion.1.refs_8_), channel_id=1, source_target_pairs={{0,2},{1,3},{2,0},{3,1},{4,6},{5,7},{6,4},{7,5},{8,10},{9,11},{10,... | collective-permute-start | bytes 786440 | tf_op jit(solution)/shard_map/ppermute | solution.py:219
  69.8 24.8 %copy-start.11 = (bf16[256,512]{1,0:T(8,128)(2,1)}, bf16[256,512]{1,0:T(8,128)(2,1)S(1)}, u32[]{:S(2)}) copy-start(bf16[256,512]{1,0:T(8,128)(2,1)S(1)} %add_convert_fusion.2.refs_1_) | copy-start | bytes 786436
  69.9 16.8 %collective-permute-start.16 = (bf16[256,512]{1,0:T(8,128)(2,1)S(1)}, bf16[256,512]{1,0:T(8,128)(2,1)}, u32[]{:S(2)}, u32[]{:S(2)}) collective-permute-start(bf16[256,512]{1,0:T(8,128)(2,1)S(1)} %add_convert_fusion.2.refs_1_), channel_id=1, source_target_pairs={{0,2},{1,3},{2,0},{3,1},{4,6},{5,7},{6,4},{7,5},{8,10},{9,11},{10,... | collective-permute-start | bytes 786440 | tf_op jit(solution)/shard_map/ppermute | solution.py:219
  72.3 22.3 %copy-start.12 = (bf16[256,512]{1,0:T(8,128)(2,1)}, bf16[256,512]{1,0:T(8,128)(2,1)S(1)}, u32[]{:S(2)}) copy-start(bf16[256,512]{1,0:T(8,128)(2,1)S(1)} %add_convert_fusion.3.refs_0_) | copy-start | bytes 786436
  72.3 19.1 %collective-permute-start.15 = (bf16[256,512]{1,0:T(8,128)(2,1)S(1)}, bf16[256,512]{1,0:T(8,128)(2,1)}, u32[]{:S(2)}, u32[]{:S(2)}) collective-permute-start(bf16[256,512]{1,0:T(8,128)(2,1)S(1)} %add_convert_fusion.3.refs_0_), channel_id=1, source_target_pairs={{0,2},{1,3},{2,0},{3,1},{4,6},{5,7},{6,4},{7,5},{8,10},{9,11},{10,... | collective-permute-start | bytes 786440 | tf_op jit(solution)/shard_map/ppermute | solution.py:219
  73.1 18.3 %collective-permute-start.20 = (bf16[256,512]{1,0:T(8,128)(2,1)S(1)}, bf16[256,512]{1,0:T(8,128)(2,1)S(1)}, u32[]{:S(2)}, u32[]{:S(2)}) collective-permute-start(bf16[256,512]{1,0:T(8,128)(2,1)S(1)} %add_convert_fusion.refs_9_), channel_id=1, source_target_pairs={{0,1},{1,0},{2,3},{3,2},{4,5},{5,4},{6,7},{7,6},{8,9},{9,8},{10,11... | collective-permute-start | bytes 786440 | tf_op jit(solution)/shard_map/ppermute | solution.py:219
  75.4 16.6 %collective-permute-start.19 = (bf16[256,512]{1,0:T(8,128)(2,1)S(1)}, bf16[256,512]{1,0:T(8,128)(2,1)S(1)}, u32[]{:S(2)}, u32[]{:S(2)}) collective-permute-start(bf16[256,512]{1,0:T(8,128)(2,1)S(1)} %add_convert_fusion.1.refs_8_), channel_id=1, source_target_pairs={{0,1},{1,0},{2,3},{3,2},{4,5},{5,4},{6,7},{7,6},{8,9},{9,8},{10,11... | collective-permute-start | bytes 786440 | tf_op jit(solution)/shard_map/ppermute | solution.py:219
  81.0 11.1 %collective-permute-start.14 = (bf16[256,512]{1,0:T(8,128)(2,1)S(1)}, bf16[256,512]{1,0:T(8,128)(2,1)S(1)}, u32[]{:S(2)}, u32[]{:S(2)}) collective-permute-start(bf16[256,512]{1,0:T(8,128)(2,1)S(1)} %add_convert_fusion.2.refs_1_), channel_id=1, source_target_pairs={{0,1},{1,0},{2,3},{3,2},{4,5},{5,4},{6,7},{7,6},{8,9},{9,8},{10,11... | collective-permute-start | bytes 786440 | tf_op jit(solution)/shard_map/ppermute | solution.py:219
  86.6 8.0 %collective-permute-start.13 = (bf16[256,512]{1,0:T(8,128)(2,1)S(1)}, bf16[256,512]{1,0:T(8,128)(2,1)}, u32[]{:S(2)}, u32[]{:S(2)}) collective-permute-start(bf16[256,512]{1,0:T(8,128)(2,1)S(1)} %add_convert_fusion.3.refs_0_), channel_id=1, source_target_pairs={{0,1},{1,0},{2,3},{3,2},{4,5},{5,4},{6,7},{7,6},{8,9},{9,8},{10,11... | collective-permute-start | bytes 786440 | tf_op jit(solution)/shard_map/ppermute | solution.py:219
  91.5 3.1 %collective-permute-start.24 = (bf16[256,512]{1,0:T(8,128)(2,1)}, bf16[256,512]{1,0:T(8,128)(2,1)}, u32[]{:S(2)}, u32[]{:S(2)}) collective-permute-start(bf16[256,512]{1,0:T(8,128)(2,1)} %collective-permute-done.22.refs_13_), channel_id=1, source_target_pairs={{0,1},{1,0},{2,3},{3,2},{4,5},{5,4},{6,7},{7,6},{8,9},{9,8},{10,11... | collective-permute-start | bytes 786440 | tf_op jit(solution)/shard_map/ppermute | solution.py:219
  91.5 3.1 %collective-permute-start.23 = (bf16[256,512]{1,0:T(8,128)(2,1)}, bf16[256,512]{1,0:T(8,128)(2,1)}, u32[]{:S(2)}, u32[]{:S(2)}) collective-permute-start(bf16[256,512]{1,0:T(8,128)(2,1)} %collective-permute-done.21.refs_12_), channel_id=1, source_target_pairs={{0,1},{1,0},{2,3},{3,2},{4,5},{5,4},{6,7},{7,6},{8,9},{9,8},{10,11... | collective-permute-start | bytes 786440 | tf_op jit(solution)/shard_map/ppermute | solution.py:219
  92.0 2.6 %collective-permute-start.18 = (bf16[256,512]{1,0:T(8,128)(2,1)}, bf16[256,512]{1,0:T(8,128)(2,1)}, u32[]{:S(2)}, u32[]{:S(2)}) collective-permute-start(bf16[256,512]{1,0:T(8,128)(2,1)} %collective-permute-done.16.refs_5_), channel_id=1, source_target_pairs={{0,1},{1,0},{2,3},{3,2},{4,5},{5,4},{6,7},{7,6},{8,9},{9,8},{10,11... | collective-permute-start | bytes 786440 | tf_op jit(solution)/shard_map/ppermute | solution.py:219
  92.1 2.5 %collective-permute-start.17 = (bf16[256,512]{1,0:T(8,128)(2,1)}, bf16[256,512]{1,0:T(8,128)(2,1)}, u32[]{:S(2)}, u32[]{:S(2)}) collective-permute-start(bf16[256,512]{1,0:T(8,128)(2,1)} %collective-permute-done.15.refs_4_), channel_id=1, source_target_pairs={{0,1},{1,0},{2,3},{3,2},{4,5},{5,4},{6,7},{7,6},{8,9},{9,8},{10,11... | collective-permute-start | bytes 786440 | tf_op jit(solution)/shard_map/ppermute | solution.py:219
  112.9 1.1 collective-permute-start.25
  114.1 3.6 %collective-permute-start.26 = (f32[2,128]{1,0:T(2,128)S(1)}, f32[2,128]{1,0:T(2,128)S(1)}, u32[]{:S(2)}, u32[]{:S(2)}) collective-permute-start(f32[2,128]{1,0:T(2,128)S(1)} %broadcast_add_fusion), channel_id=1, source_target_pairs={{0,2},{1,3},{2,0},{3,1},{4,6},{5,7},{6,4},{7,5},{8,10},{9,11},{10,... | collective-permute-start | bytes 3080 | tf_op jit(solution)/shard_map/ppermute | solution.py:269
  115.7 14.9 %collective-permute-start.34 = (bf16[256,512]{1,0:T(8,128)(2,1)}, bf16[256,512]{1,0:T(8,128)(2,1)S(1)}, u32[]{:S(2)}, u32[]{:S(2)}) collective-permute-start(bf16[256,512]{1,0:T(8,128)(2,1)} %get-tuple-element.53), channel_id=1, source_target_pairs={{0,1},{1,0},{2,3},{3,2},{4,8},{5,9},{6,10},{7,11},{8,4},{9,5},{10,... | collective-permute-start | bytes 786440 | tf_op jit(solution)/shard_map/ppermute | solution.py:236
  117.7 21.4 %copy-start.16 = (bf16[256,512]{1,0:T(8,128)(2,1)S(1)}, bf16[256,512]{1,0:T(8,128)(2,1)}, u32[]{:S(2)}) copy-start(bf16[256,512]{1,0:T(8,128)(2,1)} %copy-done.15) | copy-start | bytes 786436
  117.7 10.4 %collective-permute-start.27 = (f32[2,128]{1,0:T(2,128)S(1)}, f32[2,128]{1,0:T(2,128)S(1)}, u32[]{:S(2)}, u32[]{:S(2)}) collective-permute-start(f32[2,128]{1,0:T(2,128)S(1)} %fusion.10), channel_id=1, source_target_pairs={{0,1},{1,0},{2,3},{3,2},{4,8},{5,9},{6,10},{7,11},{8,4},{9,5},{10,... | collective-permute-start | bytes 3080 | tf_op jit(solution)/shard_map/ppermute | solution.py:271
  127.2 24.7 %copy-start.14 = (bf16[256,512]{1,0:T(8,128)(2,1)S(1)}, bf16[256,512]{1,0:T(8,128)(2,1)}, u32[]{:S(2)}) copy-start(bf16[256,512]{1,0:T(8,128)(2,1)} %copy-done.13) | copy-start | bytes 786436
  127.2 24.7 %copy-start.28 = (f32[256,512]{1,0:T(8,128)S(1)}, f32[256,512]{1,0:T(8,128)}, u32[]{:S(2)}) copy-start(f32[256,512]{1,0:T(8,128)} %get-tuple-element.36) | copy-start | bytes 1572868
  127.2 33.0 %copy-start.30 = (f32[256,512]{1,0:T(8,128)S(1)}, f32[256,512]{1,0:T(8,128)}, u32[]{:S(2)}) copy-start(f32[256,512]{1,0:T(8,128)} %get-tuple-element.48) | copy-start | bytes 1572868
  127.3 11.9 %collective-permute-start.31 = (bf16[256,512]{1,0:T(8,128)(2,1)}, bf16[256,512]{1,0:T(8,128)(2,1)S(1)}, u32[]{:S(2)}, u32[]{:S(2)}) collective-permute-start(bf16[256,512]{1,0:T(8,128)(2,1)} %get-tuple-element.51), channel_id=1, source_target_pairs={{0,1},{1,0},{2,3},{3,2},{4,8},{5,9},{6,10},{7,11},{8,4},{9,5},{10,... | collective-permute-start | bytes 786440 | tf_op jit(solution)/shard_map/ppermute | solution.py:236
  127.7 24.5 %collective-permute-start.30 = (bf16[256,512]{1,0:T(8,128)(2,1)}, bf16[256,512]{1,0:T(8,128)(2,1)S(1)}, u32[]{:S(2)}, u32[]{:S(2)}) collective-permute-start(bf16[256,512]{1,0:T(8,128)(2,1)} %get-tuple-element.49), channel_id=1, source_target_pairs={{0,1},{1,0},{2,3},{3,2},{4,8},{5,9},{6,10},{7,11},{8,4},{9,5},{10,... | collective-permute-start | bytes 786440 | tf_op jit(solution)/shard_map/ppermute | solution.py:236
  127.8 15.9 %collective-permute-start.33 = (bf16[256,512]{1,0:T(8,128)(2,1)S(1)}, bf16[256,512]{1,0:T(8,128)(2,1)S(1)}, u32[]{:S(2)}, u32[]{:S(2)}) collective-permute-start(bf16[256,512]{1,0:T(8,128)(2,1)S(1)} %copy-done.33), channel_id=1, source_target_pairs={{0,1},{1,0},{2,3},{3,2},{4,8},{5,9},{6,10},{7,11},{8,4},{9,5},{10,... | collective-permute-start | bytes 786440 | tf_op jit(solution)/shard_map/ppermute | solution.py:236
  130.8 20.7 %collective-permute-start.29 = (bf16[256,512]{1,0:T(8,128)(2,1)S(1)}, bf16[256,512]{1,0:T(8,128)(2,1)S(1)}, u32[]{:S(2)}, u32[]{:S(2)}) collective-permute-start(bf16[256,512]{1,0:T(8,128)(2,1)S(1)} %get-tuple-element.67), channel_id=1, source_target_pairs={{0,4},{4,0},{8,12},{12,8},{1,5},{5,1},{9,13},{13,9},{2,6},{6,2},{1... | collective-permute-start | bytes 786440 | tf_op jit(solution)/shard_map/ppermute | solution.py:277
  139.0 12.8 %collective-permute-start.35 = (bf16[256,512]{1,0:T(8,128)(2,1)S(1)}, bf16[256,512]{1,0:T(8,128)(2,1)S(1)}, u32[]{:S(2)}, u32[]{:S(2)}) collective-permute-start(bf16[256,512]{1,0:T(8,128)(2,1)S(1)} %get-tuple-element.66), channel_id=1, source_target_pairs={{0,4},{4,0},{8,12},{12,8},{1,5},{5,1},{9,13},{13,9},{2,6},{6,2},{1... | collective-permute-start | bytes 786440 | tf_op jit(solution)/shard_map/ppermute | solution.py:277
  140.4 17.1 %collective-permute-start.28 = (bf16[256,512]{1,0:T(8,128)(2,1)S(1)}, bf16[256,512]{1,0:T(8,128)(2,1)S(1)}, u32[]{:S(2)}, u32[]{:S(2)}) collective-permute-start(bf16[256,512]{1,0:T(8,128)(2,1)S(1)} %get-tuple-element.63), channel_id=1, source_target_pairs={{0,4},{4,0},{8,12},{12,8},{1,5},{5,1},{9,13},{13,9},{2,6},{6,2},{1... | collective-permute-start | bytes 786440 | tf_op jit(solution)/shard_map/ppermute | solution.py:277
  143.8 16.5 %collective-permute-start.32 = (bf16[256,512]{1,0:T(8,128)(2,1)S(1)}, bf16[256,512]{1,0:T(8,128)(2,1)S(1)}, u32[]{:S(2)}, u32[]{:S(2)}) collective-permute-start(bf16[256,512]{1,0:T(8,128)(2,1)S(1)} %get-tuple-element.62), channel_id=1, source_target_pairs={{0,4},{4,0},{8,12},{12,8},{1,5},{5,1},{9,13},{13,9},{2,6},{6,2},{1... | collective-permute-start | bytes 786440 | tf_op jit(solution)/shard_map/ppermute | solution.py:277
  (23 other events, 190.4 us)

commit v5 on v0

v5 whole, which is shorter than its diff:
```python
import functools

import jax
import jax.numpy as jnp
from jax import lax
from jax.experimental import pallas as pl
from jax.experimental.pallas import tpu as pltpu
from jax.sharding import PartitionSpec as P

MIB = 1024 * 1024
CODE_ROWS = 16
VMEM_LIMIT = 10 * MIB
MASK_LIMIT = 60 * MIB
ANY = pl.BlockSpec(memory_space=pl.ANY)
BRIEF = pl.CostEstimate(flops=10**9, bytes_accessed=0, transcendentals=0)
TOKEN = jax.ShapeDtypeStruct((2, 8, 128), jnp.float32)
VMEM = pl.BlockSpec(memory_space=pltpu.VMEM)
SMEM = pl.BlockSpec(memory_space=pltpu.SMEM)


def bits_of(size):
    count = size.bit_length() - 1
    assert 1 << count == size
    return count


def swap(axis, bit):
    return [(place, place ^ bit) for place in range(lax.axis_size(axis))]


def leads(row):
    return (row ^ (row >> 1)) & 1


def leader_swap(bit):
    rows, cols = lax.axis_size("row"), lax.axis_size("col")
    pairs = []
    for row in range(rows):
        for col in range(cols):
            if leads(row):
                pair = (row >> 1) ^ bit
                there = (2 * pair if leads(2 * pair) else 2 * pair + 1, col)
            else:
                there = (row, col ^ 1)
            pairs.append((row * cols + col, there[0] * cols + there[1]))
    return pairs


def reverse_bits(value, count):
    out = 0
    for bit in range(count):
        out = out | (((value >> bit) & 1) << (count - 1 - bit))
    return out


def keep_corner(block, rows, cols):
    inside = (lax.broadcasted_iota(jnp.int32, block.shape, 0) < rows) & (
        lax.broadcasted_iota(jnp.int32, block.shape, 1) < cols
    )
    return jnp.where(inside, block.astype(jnp.float32), 0.0).astype(block.dtype)


def mask_left_kernel(left_dest, left_sizes, left, out, near):
    row, col = lax.axis_index("row"), lax.axis_index("col")
    terms, half = out.shape[0], near.shape[0]
    for term in range(terms):
        out[term] = keep_corner(left[term, 0], left_sizes[left_dest[term, row]], left_sizes[row])
    for place in range(half):
        near[place] = out[lax.rem(col, 2) * half + place]


def mask_left(left_dest, left_sizes, left):
    terms, _, tile, _ = left.shape
    return pl.pallas_call(
        mask_left_kernel,
        in_specs=[SMEM, SMEM, VMEM],
        out_specs=[VMEM, VMEM],
        out_shape=[jax.ShapeDtypeStruct((count, tile, tile), left.dtype) for count in (terms, terms // 2)],
        compiler_params=pltpu.CompilerParams(vmem_limit_bytes=MASK_LIMIT),
        cost_estimate=BRIEF,
    )(left_dest, left_sizes, left)


def mask_right_kernel(right_src, right_sizes, right, *outs):
    col = lax.axis_index("col")
    for step in range(right.shape[0]):
        term = pl.program_id(0) * right.shape[0] + step
        for place, out in enumerate(outs):
            block = col * len(outs) + place
            out[step] = keep_corner(right[step, place], right_sizes[block], right_sizes[right_src[term, block]])


def mask_right(right_src, right_sizes, right):
    terms, local, tile, _ = right.shape
    return pl.pallas_call(
        mask_right_kernel,
        grid=(terms // 2,),
        in_specs=[SMEM, SMEM, pl.BlockSpec((2, local, tile, tile), lambda step: (step, 0, 0, 0))],
        out_specs=[pl.BlockSpec((2, tile, tile), lambda step: (step, 0, 0))] * local,
        out_shape=[jax.ShapeDtypeStruct((terms, tile, tile), right.dtype)] * local,
        compiler_params=pltpu.CompilerParams(vmem_limit_bytes=MASK_LIMIT),
        cost_estimate=BRIEF,
    )(right_src, right_sizes, right)


def place_kernel(places, *refs):
    pieces, (blocks, sems) = refs[:len(places)], refs[-2:]
    tile = blocks.shape[2]
    copies = []

    def add(here, there):
        copies.append(pltpu.make_async_copy(here, there, sems.at[len(copies)]))

    for (block, slot), piece in zip(places, pieces):
        if len(piece.shape) == 3:
            add(piece.at[:, :blocks.shape[1]], blocks.at[block:block + piece.shape[0]])
        else:
            for at in range(piece.shape[1] // tile):
                rows = piece.shape[0]
                add(piece.at[:, at * tile:(at + 1) * tile], blocks.at[block + at, slot * tile:slot * tile + rows])
    for copy in copies:
        copy.start()
    for copy in copies:
        copy.wait()


def place(blocks, shape, pieces, tokens=()):
    places, pieces = [at for at, _ in pieces], [piece for _, piece in pieces]
    copies = sum(1 if piece.ndim == 3 else piece.shape[1] // shape[2] for piece in pieces)
    rest = list(tokens) if blocks is None else [blocks, *tokens]
    return pl.pallas_call(
        functools.partial(place_kernel, places),
        in_specs=[ANY] * (len(pieces) + len(rest)),
        out_specs=ANY,
        out_shape=jax.ShapeDtypeStruct(shape, jnp.bfloat16),
        scratch_shapes=[pltpu.SemaphoreType.DMA((copies,))],
        input_output_aliases={} if blocks is None else {len(pieces): 0},
        compiler_params=pltpu.CompilerParams(vmem_limit_bytes=VMEM_LIMIT),
        cost_estimate=BRIEF,
    )(*pieces, *rest)


def join_kernel(*refs):
    held, pieces = refs[-1], refs[:refs[-1].shape[0]]
    rows = held.shape[1] - CODE_ROWS
    sums = [jnp.zeros((1, 1), jnp.float32)] * 2
    for at, piece in enumerate(pieces):
        held[at, :rows] = piece[:rows]
        sums = [total + more for total, more in zip(sums, decode(piece[rows:]))]
        if at:
            held[at, rows:] = jnp.zeros((CODE_ROWS, held.shape[2]), held.dtype)
    held[0, rows:] = encode(sums)


def join(pieces, tokens):
    return pl.pallas_call(
        join_kernel,
        in_specs=[VMEM] * len(pieces) + [ANY] * len(tokens),
        out_specs=VMEM,
        out_shape=jax.ShapeDtypeStruct((len(pieces), *pieces[0].shape), pieces[0].dtype),
        compiler_params=pltpu.CompilerParams(vmem_limit_bytes=VMEM_LIMIT),
        cost_estimate=BRIEF,
    )(*pieces, *tokens)


def read_codes(arrays, codes, sems):
    copies = [
        pltpu.make_async_copy(ref.at[0, ref.shape[1] - CODE_ROWS:], codes.at[at], sems.at[at])
        for at, ref in enumerate(arrays)
    ]
    for copy in copies:
        copy.start()
    for copy in copies:
        copy.wait()
    return jnp.stack([jnp.broadcast_to(sum(pair), (8, 128)) for pair in zip(decode(codes[0]), decode(codes[1]))])


def settle_kernel(held, arrived, *refs):
    out, codes, sems = refs[-3:]
    out[...] = read_codes((held, arrived), codes, sems)


def settle(held, arrived, tokens):
    return pl.pallas_call(
        settle_kernel,
        in_specs=[ANY] * (2 + len(tokens)),
        out_specs=VMEM,
        out_shape=jax.ShapeDtypeStruct((2, 8, 128), jnp.float32),
        scratch_shapes=[pltpu.VMEM((2, CODE_ROWS, held.shape[2]), held.dtype), pltpu.SemaphoreType.DMA((2,))],
        compiler_params=pltpu.CompilerParams(vmem_limit_bytes=VMEM_LIMIT),
        cost_estimate=BRIEF,
    )(held, arrived, *tokens)


def product_kernel(first, local, out_slots, coded, source, target, blocks, left_own, left_near, left_far, right, *refs):
    outs, (token, inner, total, held_right, sem, codes, code_sems) = refs[-7 - len(out_slots):-7], refs[-7:]
    pair_count = total.shape[0] // 2
    if coded:
        token[...] = read_codes(refs[:2], codes, code_sems)
    else:
        token[...] = jnp.zeros_like(token)
    copy = pltpu.make_async_copy(right, held_right, sem)
    copy.start()
    total[...] = jnp.zeros_like(total)
    copy.wait()
    terms, tile = right.shape[:2]
    row, col = lax.axis_index("row"), lax.axis_index("col")
    for term in range(terms):
        wanted = source[term, col * local + first]
        place_of = lax.bitwise_xor(lax.div(wanted, local), col)
        place_of = (place_of >> 1) + (place_of & 1) * (blocks.shape[0] // local // 2)
        held = place_of * local + lax.rem(wanted, local)
        inner[term] = lax.dot_general(
            blocks[held], held_right[term], (((1,), (1,)), ((), ())), preferred_element_type=jnp.float32
        ).astype(jnp.bfloat16)

    def add(left, term, slot):
        to = target[term, lax.bitwise_xor(row, slot)]
        to_slot = 2 * reverse_bits((to >> 1) ^ (row >> 1), bits_of(pair_count)) + 1 - leads(to)
        total[to_slot] += jnp.dot(left, inner[term, slot * tile:(slot + 1) * tile], preferred_element_type=jnp.float32)

    half = terms // 2
    near = lax.rem(col, 2) * half
    for term in range(terms):
        add(left_own[term], term, 0)
    for step in range(half):
        add(left_near[step], near + step, 1)
        add(left_far[step], half - near + step, 1)
    for slots, out in zip(out_slots, outs):
        for at, slot in enumerate(slots):
            out[at * tile:(at + 1) * tile] = total[slot].astype(out.dtype)
        if coded and slots[0] >= 2:
            out[len(slots) * tile:] = encode([token[0, :1, :1], token[1, :1, :1]])


def products(blocks, left, right, source, target, out_slots, first, tokens, coded=()):
    local, (terms, tile) = len(right), right[0].shape[:2]
    out_shape = [
        jax.ShapeDtypeStruct((len(slots) * tile + CODE_ROWS, tile), jnp.bfloat16)
        if coded and slots[0] >= 2
        else jax.ShapeDtypeStruct((len(slots) * tile, tile), jnp.bfloat16 if slots[0] >= 2 else jnp.float32)
        for slots in out_slots
    ] + [TOKEN]
    held = 2 * blocks.size + 8 * terms * tile * tile + sum(8 * out.size for out in out_shape)
    return pl.pallas_call(
        functools.partial(product_kernel, first, local, out_slots, bool(coded)),
        in_specs=[SMEM, SMEM] + [VMEM] * 4 + [ANY] * (1 + len(coded) + len(tokens)),
        out_specs=[VMEM] * (len(out_slots) + 1),
        out_shape=out_shape,
        scratch_shapes=[
            pltpu.VMEM((terms, 2 * tile, tile), jnp.bfloat16),
            pltpu.VMEM((sum(len(slots) for slots in out_slots), tile, tile), jnp.float32),
            pltpu.VMEM((terms, tile, tile), jnp.bfloat16),
            pltpu.SemaphoreType.DMA,
            pltpu.VMEM((2, CODE_ROWS, tile), jnp.bfloat16),
            pltpu.SemaphoreType.DMA((2,)),
        ],
        compiler_params=pltpu.CompilerParams(vmem_limit_bytes=held + 4 * MIB),
        cost_estimate=BRIEF,
    )(source, target, blocks, *left, right[first], *coded, *tokens)


def encode(values):
    rows = lax.broadcasted_iota(jnp.int32, (CODE_ROWS, 256), 0)
    out = jnp.zeros((CODE_ROWS, 256), jnp.float32)
    for at, value in enumerate(values):
        rest = jnp.broadcast_to(value, out.shape)
        for part in range(3):
            head = rest.astype(jnp.bfloat16).astype(jnp.float32)
            out = jnp.where(rows == 3 * at + part, head, out)
            rest = rest - head
    return out.astype(jnp.bfloat16)


def decode(code):
    code = code[:6, :1].astype(jnp.float32)
    return [code[at:at + 1] + code[at + 1:at + 2] + code[at + 2:at + 3] for at in (0, 3)]


def combine_kernel(first, local, left_sizes, right_sizes, kept, arrived, blocks, *refs):
    before = refs[0]
    both, near, stats, held, sem = refs[-5:]
    tile = near.shape[0]
    copy = pltpu.make_async_copy(blocks.at[first], held, sem)
    copy.start()
    row, col = lax.axis_index("row"), lax.axis_index("col")
    image = kept[...] + arrived[...].astype(jnp.float32)
    both[:2 * tile] = image.astype(both.dtype)
    near[...] = image[tile:].astype(near.dtype)
    copy.wait()
    norm = correlation = jnp.zeros((8, tile), jnp.float32)
    for slot in range(2):
        rows = pl.ds(slot * tile, tile)
        masked = keep_corner(held[rows], left_sizes[lax.bitwise_xor(row, slot)], right_sizes[col * local + first])
        masked = masked.astype(jnp.float32)
        norm += jnp.sum((masked * masked).reshape(-1, 8, tile), 0)
        correlation += jnp.sum((masked * image[slot * tile:(slot + 1) * tile]).reshape(-1, 8, tile), 0)
    if first:
        norm, correlation = norm + before[0], correlation + before[1]
    stats[0] = norm
    stats[1] = correlation
    if first == local - 1:
        both[2 * tile:] = encode([jnp.sum(norm), jnp.sum(correlation)])


def combine(first, local, left_sizes, right_sizes, kept, arrived, blocks, stats, tokens):
    tile = kept.shape[1]
    rows = 2 * tile + CODE_ROWS * (first == local - 1)
    more = ([stats] if first else []) + tokens
    return pl.pallas_call(
        functools.partial(combine_kernel, first, local),
        in_specs=[SMEM, SMEM, VMEM, VMEM, ANY] + ([VMEM] if first else []) + [ANY] * len(tokens),
        out_specs=[VMEM] * 3,
        out_shape=[jax.ShapeDtypeStruct((height, tile), arrived.dtype) for height in (rows, tile)]
        + [jax.ShapeDtypeStruct((2, 8, tile), jnp.float32)],
        scratch_shapes=[pltpu.VMEM((2 * tile, tile), blocks.dtype), pltpu.SemaphoreType.DMA],
        compiler_params=pltpu.CompilerParams(vmem_limit_bytes=VMEM_LIMIT),
        cost_estimate=BRIEF,
    )(left_sizes, right_sizes, kept, arrived, blocks, *more)


def emit_kernel(start, coded, kept, arrived, *refs):
    outs = refs[-1 - coded:]
    tile = kept.shape[1]
    outs[0][:tile] = (kept[tile:] + arrived[start:start + tile].astype(jnp.float32)).astype(outs[0].dtype)
    if coded:
        more = decode(arrived[arrived.shape[0] - CODE_ROWS:])
        stats = [refs[0][at, :1, :1] + more[at] for at in range(2)]
        outs[0][tile:] = encode(stats)
        for at, value in enumerate(stats):
            outs[1][at] = jnp.broadcast_to(value, outs[1].shape[1:])


def emit(kept, arrived, tokens, stats=None):
    tile, coded = kept.shape[1], stats is not None
    start = tile if arrived.shape[0] >= 2 * tile else 0
    return pl.pallas_call(
        functools.partial(emit_kernel, start, coded),
        in_specs=[VMEM] * (2 + coded) + [ANY] * len(tokens),
        out_specs=[VMEM] * (1 + coded),
        out_shape=[jax.ShapeDtypeStruct((tile + CODE_ROWS * coded, tile), arrived.dtype)] + [TOKEN] * coded,
        compiler_params=pltpu.CompilerParams(vmem_limit_bytes=VMEM_LIMIT),
        cost_estimate=BRIEF,
    )(kept, arrived, *([stats] if coded else []), *tokens)


def scales_kernel(entry_count, own, sent, out, code, sem):
    copy = pltpu.make_async_copy(sent.at[sent.shape[0] - CODE_ROWS:], code, sem)
    copy.start()
    copy.wait()
    leading = leads(lax.axis_index("row")) == 1
    norm, correlation = (
        jnp.where(leading, mine, jnp.broadcast_to(theirs, mine.shape))
        for mine, theirs in zip((own[0], own[1]), decode(code[...]))
    )
    out[0] = lax.rsqrt(norm / entry_count + 1e-06)
    out[1] = correlation / norm


def scales(entry_count, own, sent):
    return pl.pallas_call(
        functools.partial(scales_kernel, entry_count),
        in_specs=[VMEM, ANY],
        out_specs=VMEM,
        out_shape=TOKEN,
        scratch_shapes=[pltpu.VMEM((CODE_ROWS, sent.shape[1]), sent.dtype), pltpu.SemaphoreType.DMA],
        compiler_params=pltpu.CompilerParams(vmem_limit_bytes=VMEM_LIMIT),
        cost_estimate=BRIEF,
    )(own, sent)


def after(value, *others):
    return pl.pallas_call(
        lambda *refs: None,
        in_specs=[ANY] * (1 + len(others)),
        out_specs=ANY,
        out_shape=jax.ShapeDtypeStruct(value.shape, value.dtype),
        input_output_aliases={0: 0},
        cost_estimate=BRIEF,
    )(value, *others)


def on_device(wavefunction, left_ops, right_ops, left_dest, right_src, left_sizes, right_sizes):
    tile = left_ops.shape[2]
    local = right_ops.shape[1]
    row_count, col_count = lax.axis_size("row"), lax.axis_size("col")
    pair_bits, col_bits = bits_of(row_count) - 1, bits_of(col_count)
    entry_count = wavefunction.shape[0] * row_count * wavefunction.shape[1] * col_count
    both = ("row", "col")
    row, col = lax.axis_index("row"), lax.axis_index("col")
    leading = leads(row) == 1
    blocks_shape = (col_count * local, 2 * tile, tile)

    def far(part):
        pieces = [part]
        for bit in range(1, col_bits):
            pieces += [lax.ppermute(piece, "col", swap("col", 1 << bit)) for piece in pieces]
        return pieces

    def other_core(part):
        return lax.ppermute(part, "col", swap("col", 1))

    def block_of(piece, odd):
        return (odd * (col_count // 2) + piece) * local

    def to_partner(part):
        return lax.ppermute(part, "row", swap("row", 1))

    near = to_partner(wavefunction)
    left_own, left_near = mask_left(left_dest, left_sizes, left_ops)
    left_near = to_partner(left_near)
    left = [left_own, left_near, other_core(left_near)]
    right = mask_right(right_src, right_sizes, right_ops)
    near = after(near, left_own, right[0])

    def exchange(sums):
        kept, sums = sums[0], sums[1:]
        per_pair = len(sums) // ((1 << pair_bits) - 1)
        for bit in range(pair_bits):
            half = (len(sums) + per_pair) // 2 - per_pair
            arrived = [lax.ppermute(part, both, leader_swap(1 << bit)) for part in sums[half:][::-1]][::-1]
            if bit < pair_bits - 1:
                mine = arrived[0] if per_pair == 1 else jnp.concatenate(arrived[:per_pair], 0)
                kept = kept + mine.astype(jnp.float32)
                sums = [
                    (part.astype(jnp.float32) + more.astype(jnp.float32)).astype(part.dtype)
                    for part, more in zip(sums[:half], arrived[per_pair:])
                ]
        return kept, arrived

    joined = [(2 * pair, 2 * pair + 1) for pair in range(1 << pair_bits)]
    apart = joined[:1] + [(slot,) for pair in joined[1:] for slot in pair]

    def multiply(blocks, slots, first, tokens, coded=()):
        return products(blocks, left, right, right_src, left_dest, slots, first, tokens, coded)

    pieces = [((block_of(at, 0), 0), piece) for at, piece in enumerate(far(wavefunction))]
    near_pieces = [((block_of(at, 0), 1), piece) for at, piece in enumerate(far(near))]
    blocks = None
    for several in (pieces + near_pieces[:1], near_pieces[1:]):
        blocks = place(blocks, blocks_shape, several + [
            ((block + block_of(0, 1), slot), other_core(piece)) for (block, slot), piece in several
        ])

    once, parts, near_images, stats, token = [], [], [], None, None
    for first in range(local + 1):
        if first < local:
            *sums, token = multiply(blocks, joined, first, ([token] if first else []) + ([stats] if parts else []))
            once.append(exchange(sums))
        for done in range(len(parts), first if first < local else local):
            kept, (arrived,) = once[done]
            image, near_image, stats = combine(
                done, local, left_sizes, right_sizes, kept, arrived, blocks, stats,
                [token] + (parts[0][1:] if done > 1 else []),
            )
            parts.append(far(image))
            near_images.append(to_partner(near_image))
    blocks = None
    for group in (range(local - 1), range(local - 1, local)):
        if blocks is None:
            held = place(
                None,
                (len(group) * col_count // 2, 2 * tile, tile),
                [((at * len(group) + i, 0), parts[first][at]) for at in range(col_count // 2) for i, first in enumerate(group)],
                [parts[-1][0], *near_images[:-2]],
            )
        else:
            held = join(parts[-1], [blocks, *near_images[-2:]])
        arrived_held = other_core(held)
        blocks = place(blocks, blocks_shape, [
            ((block_of(at, odd) + group[0], 0), half[at * len(group):(at + 1) * len(group)])
            for odd, half in enumerate((held, arrived_held))
            for at in range(col_count // 2)
        ])

    carrier = local - 2 if pair_bits == 1 else local
    again, near_again, token, stats = [], [], None, None
    for first in range(local + 1):
        if first < local:
            slots = apart if first == local - 1 else joined
            tokens = ([token] if first else []) + ([near_again[-1]] if near_again else [])
            coded = [held, arrived_held] if first == carrier else []
            *sums, token = multiply(blocks, slots, first, tokens, coded)
            stats = token if coded else stats
            again.append(exchange(sums))
        for done in range(len(near_again), first if first < local else local):
            kept, arrived = again[done]
            tokens = [token]
            if done == carrier:
                near, stats = emit(kept, arrived[-1], tokens, stats)
            else:
                (near,) = emit(kept, arrived[-1], tokens)
            near_again.append(near)
    near_again = [to_partner(part) for part in near_again]
    if carrier < local:
        both_scales = scales(entry_count, stats, near_again[carrier])
        scale, theta = both_scales[0, 0, 0], both_scales[1, 0, 0]
    else:
        stats = settle(held, arrived_held, [token])
        for bit in range(pair_bits):
            stats = stats + lax.ppermute(stats, both, leader_swap(1 << bit))
        stats = jnp.where(leading, stats, to_partner(stats))
        norm, correlation = stats[0, 0, 0], stats[1, 0, 0]
        scale = lax.rsqrt(norm / entry_count + 1e-06)
        theta = correlation / norm

    images = [
        jnp.where(leading, part[0][:tile], near_image).astype(jnp.float32) for part, near_image in zip(parts, near_images)
    ]
    again = [
        jnp.where(leading, kept[:tile] + arrived[0][:tile].astype(jnp.float32), near[:tile].astype(jnp.float32))
        for (kept, arrived), near in zip(again, near_again)
    ]
    first_product = jnp.concatenate([(image * scale).astype(jnp.bfloat16) for image in images], 1)
    second_product = jnp.concatenate(
        [((more - theta * image) * scale).astype(jnp.bfloat16) for more, image in zip(again, images)], 1
    )
    return (first_product, second_product)


def solution(mesh):
    placed = (
        P(("groups", "row"), "col"),
        P(None, ("groups", "row"), None, None),
        P(None, ("groups", "col"), None, None),
        P(None, "groups"),
        P(None, "groups"),
        P("groups"),
        P("groups"),
    )
    return jax.shard_map(
        on_device,
        mesh=mesh,
        in_specs=placed,
        out_specs=(P(("groups", "row"), "col"), P(("groups", "row"), "col")),
        check_vma=False,
    )
```

time: 249 us -> 124 us (0.50)
  waiting for transfers between devices: 130 us -> 26.7 us
  Pallas kernels: 0 us -> 40.1 us
  starting transfers between devices: 0.34 us -> 37.2 us
  blocking collectives: 32.1 us -> 0 us
  local copies, waits for them, and re-layouts: 38.4 us -> 10.2 us
  matrix products: 23 us -> 0 us
  between operations: 15.8 us -> 1.25 us
    reduce_scatter x2 -> x0, waiting for transfers between devices: 86 us -> none  [apply_once(): lax.psum_scatter(jnp.einsum('tk,tan->kan', onehot, contrib).reshape(tile_...]
    all_gather x2 -> x0, waiting for transfers between devices: 43.6 us -> none  [apply_once(): gathered = lax.all_gather(vector, 'col', axis=1, tiled=True)]
    pallas_call x0 -> x26, Pallas kernels: none -> 40.1 us  [the longest x8 25 us: products(): pl.pallas_call(functools.partial(product_kernel, first, local, out_slots,...]
    ppermute x0 -> x32, starting transfers between devices: none -> 37.2 us  [the longest x10 27.2 us: to_partner(): return lax.ppermute(part, 'row', swap('row', 1))]
    psum x1 -> x0, blocking collectives: 32.1 us -> none  [on_device(): lax.psum((jnp.sum(masked_float * masked_float), jnp.sum(masked_float * im...]
    ppermute x0 -> x32, waiting for transfers between devices: none -> 26.7 us  [the longest x6 12.7 us: far(): lax.ppermute(piece, 'col', swap('col', 1 << bit))]
    dot_general x6 -> x0, matrix products: 23 us -> none  [the longest x2 9.68 us: apply_once(): jnp.einsum('rtjc,tjdc->trjd', chosen, right_ops, preferred_element_type=j...]
    dot_general x2 -> x0, local copies, waits for them, and re-layouts: 13.7 us -> none  [apply_once(): jnp.einsum('tab,tbn->tan', left_here, inner_terms, preferred_element_type...]
  transfers between devices with their start and end apart: 4 -> 32, of which waited for: 4 -> 9; matrix products, arithmetic and copies ran while one was open for 1% -> 6% of each run, Pallas kernels for 0% -> 27%
where the time goes in v5:
time: 124 us; the launch traced here: 123 us
  Pallas kernels  40.1 us (32%)
  starting transfers between devices  37.2 us (30%)
  waiting for transfers between devices  26.7 us (22%)
  local copies, waits for them, and re-layouts  10.2 us (8%)
  other arithmetic  7.58 us (6%)
  between operations  1.25 us (1%)
    ppermute x10, starting transfers between devices, to_partner(): return lax.ppermute(part, 'row', swap('row', 1))  27.2 us
    pallas_call x8, Pallas kernels, products(): pl.pallas_call(functools.partial(product_kernel, first, local, out_slots,...  25 us
    ppermute x6, waiting for transfers between devices, far(): lax.ppermute(piece, 'col', swap('col', 1 << bit))  12.7 us
    ppermute x10, waiting for transfers between devices, to_partner(): return lax.ppermute(part, 'row', swap('row', 1))  12.1 us
    unnamed x75, local copies, waits for them, and re-layouts  9.34 us
    ppermute x6, starting transfers between devices, far(): lax.ppermute(piece, 'col', swap('col', 1 << bit))  7.14 us
    convert_element_type x4, other arithmetic, on_device(): ((more - theta * image) * scale).astype(jnp.bfloat16)  6.47 us
    pallas_call x1, Pallas kernels, mask_right(): pl.pallas_call(mask_right_kernel, grid=(terms // 2,), in_specs=[SMEM, SME...  5.04 us
  transfers between devices with their start and end apart: 32, of which 9 were waited for; matrix products, arithmetic and copies ran while one was open for 6% of the time, Pallas kernels for 27%

profile of v5, /device:TPU:0, one launch (start us, length us, event | category | flops | bytes accessed | tf_op | source)
XLA Modules:
  0.0 123.0 jit_solution(10872774862619301927)
XLA Ops:
  0.6 3.1 %collective-permute-start = (bf16[256,1024]{1,0:T(8,128)(2,1)}, bf16[256,1024]{1,0:T(8,128)(2,1)S(1)}, u32[]{:S(2)}, u32[]{:S(2)}) collective-permute-start(bf16[256,1024]{1,0:T(8,128)(2,1)} %refs_0_.1), channel_id=1, source_target_pairs={{0,4},{4,0},{8,12},{12,8},{1,5},{5,1},{9,13},{13,9},{2,6},{6,2},{1... | collective-permute-start | bytes 1572872 | tf_op jit(solution)/shard_map/ppermute | solution.py:407
  3.7 1.5 %collective-permute-start.3 = (bf16[256,1024]{1,0:T(8,128)(2,1)}, bf16[256,1024]{1,0:T(8,128)(2,1)S(1)}, u32[]{:S(2)}, u32[]{:S(2)}) collective-permute-start(bf16[256,1024]{1,0:T(8,128)(2,1)} %refs_0_.1), channel_id=1, source_target_pairs={{0,2},{1,3},{2,0},{3,1},{4,6},{5,7},{6,4},{7,5},{8,10},{9,11},{10,... | collective-permute-start | bytes 1572872 | tf_op jit(solution)/shard_map/ppermute | solution.py:397
  5.2 1.3 %copy.13.left_dest.target = s32[8,4]{1,0:T(8,128)} copy(s32[8,4]{0,1:T(4,128)} %param.10) | data formatting | bytes 256 | tf_op args[3]
  6.6 2.8 %shard_map.86 = (bf16[8,256,256]{2,1,0:T(8,128)(2,1)}, bf16[4,256,256]{2,1,0:T(8,128)(2,1)}) custom-call(s32[8,4]{1,0:T(8,128)} %copy.13.left_dest.target, s32[4]{0:T(128)} %left_sizes.9, bf16[8,1,256,256]{3,2,1,0:T(8,128)(2,1)} %left.1), custom_call_target="tpu_custom_call" | custom-call | flops 1000000000 | tf_op jit(solution)/shard_map/pallas_call | solution.py:74
  9.3 5.0 %shard_map.87 = (bf16[8,256,256]{2,1,0:T(8,128)(2,1)}, bf16[8,256,256]{2,1,0:T(8,128)(2,1)}, bf16[8,256,256]{2,1,0:T(8,128)(2,1)}, bf16[8,256,256]{2,1,0:T(8,128)(2,1)}) custom-call(s32[8,16]{1,0:T(8,128)} %source.15, s32[16]{0:T(128)} %right_sizes.9, bf16[8,4,256,256]{3,2,1,0:T(8,128)(2,1)} %right.1), custom_call_target="tpu_custom_call" | custom-call | flops 1000000000 | tf_op jit(solution)/shard_map/pallas_call | solution.py:95
  14.4 1.5 %collective-permute-done.refs_0_ = bf16[256,1024]{1,0:T(8,128)(2,1)S(1)} collective-permute-done((bf16[256,1024]{1,0:T(8,128)(2,1)}, bf16[256,1024]{1,0:T(8,128)(2,1)S(1)}, u32[]{:S(2)}, u32[]{:S(2)}) %collective-permute-start) | collective-permute-done | bytes 524320 | tf_op jit(solution)/shard_map/ppermute | solution.py:407
  15.9 0.8 copy-done.6
  16.6 1.7 %collective-permute-start.1 = (bf16[256,1024]{1,0:T(8,128)(2,1)}, bf16[256,1024]{1,0:T(8,128)(2,1)S(1)}, u32[]{:S(2)}, u32[]{:S(2)}) collective-permute-start(bf16[256,1024]{1,0:T(8,128)(2,1)} %shard_map.88.refs_2_), channel_id=1, source_target_pairs={{0,2},{1,3},{2,0},{3,1},{4,6},{5,7},{6,4},{7,5},{8,10},{9,11},{10,... | collective-permute-start | bytes 1572872 | tf_op jit(solution)/shard_map/ppermute | solution.py:397
  18.3 1.6 %collective-permute-start.7 = (bf16[4,256,256]{2,1,0:T(8,128)(2,1)S(1)}, bf16[4,256,256]{2,1,0:T(8,128)(2,1)S(1)}, u32[]{:S(2)}, u32[]{:S(2)}) collective-permute-start(bf16[4,256,256]{2,1,0:T(8,128)(2,1)S(1)} %copy-done.36), channel_id=1, source_target_pairs={{0,4},{4,0},{8,12},{12,8},{1,5},{5,1},{9,13},{13,9},{2,6},{6,2},{1... | collective-permute-start | bytes 1572872 | tf_op jit(solution)/shard_map/ppermute | solution.py:407
  20.4 9.6 %collective-permute-done.1.refs_0_ = bf16[256,1024]{1,0:T(8,128)(2,1)S(1)} collective-permute-done((bf16[256,1024]{1,0:T(8,128)(2,1)}, bf16[256,1024]{1,0:T(8,128)(2,1)S(1)}, u32[]{:S(2)}, u32[]{:S(2)}) %collective-permute-start.1) | collective-permute-done | bytes 524320 | tf_op jit(solution)/shard_map/ppermute | solution.py:397
  30.0 0.8 collective-permute-done.7.left_near
  30.9 1.0 copy-done.7
  32.9 0.9 copy-done
  34.1 3.0 %shard_map.91 = (f32[512,256]{1,0:T(8,128)S(1)}, bf16[512,256]{1,0:T(8,128)(2,1)S(1)}, f32[2,8,128]{2,1,0:T(8,128)S(1)}) custom-call(s32[8,16]{1,0:T(8,128)S(1)} %copy-done.8, s32[8,4]{1,0:T(8,128)S(1)} %copy-done.9, bf16[16,512,256]{2,1,0:T(8,128)(2,1)S(1)} %shard_map.90.blocks, bf16[8,256,256]{2,1,0:T(8,128)(2,1)S(1)} %copy-done, ...), custom_call_target="tpu_custom_call" | custom-call | flops 1000000000 | tf_op jit(solution)/shard_map/pallas_call | solution.py:245
  37.7 3.0 %shard_map.92 = (f32[512,256]{1,0:T(8,128)S(1)}, bf16[512,256]{1,0:T(8,128)(2,1)S(1)}, f32[2,8,128]{2,1,0:T(8,128)S(1)}) custom-call(s32[8,16]{1,0:T(8,128)S(1)} %copy-done.8, s32[8,4]{1,0:T(8,128)S(1)} %copy-done.9, bf16[16,512,256]{2,1,0:T(8,128)(2,1)S(1)} %shard_map.90.blocks, bf16[8,256,256]{2,1,0:T(8,128)(2,1)S(1)} %copy-done, ...), custom_call_target="tpu_custom_call" | custom-call | flops 1000000000 | tf_op jit(solution)/shard_map/pallas_call | solution.py:245
  40.9 0.8 shard_map.93
  42.0 3.0 %shard_map.94 = (f32[512,256]{1,0:T(8,128)S(1)}, bf16[512,256]{1,0:T(8,128)(2,1)S(1)}, f32[2,8,128]{2,1,0:T(8,128)S(1)}) custom-call(s32[8,16]{1,0:T(8,128)S(1)} %copy-done.8, s32[8,4]{1,0:T(8,128)S(1)} %copy-done.9, bf16[16,512,256]{2,1,0:T(8,128)(2,1)S(1)} %shard_map.90.blocks, bf16[8,256,256]{2,1,0:T(8,128)(2,1)S(1)} %copy-done, ...), custom_call_target="tpu_custom_call" | custom-call | flops 1000000000 | tf_op jit(solution)/shard_map/pallas_call | solution.py:245
  45.3 0.8 collective-permute-start.14
  46.1 0.8 shard_map.95
  46.9 3.0 %shard_map.96 = (f32[512,256]{1,0:T(8,128)S(1)}, bf16[512,256]{1,0:T(8,128)(2,1)S(1)}, f32[2,8,128]{2,1,0:T(8,128)S(1)}) custom-call(s32[8,16]{1,0:T(8,128)S(1)} %copy-done.8, s32[8,4]{1,0:T(8,128)S(1)} %copy-done.9, bf16[16,512,256]{2,1,0:T(8,128)(2,1)S(1)} %shard_map.90.blocks, bf16[8,256,256]{2,1,0:T(8,128)(2,1)S(1)} %copy-done, ...), custom_call_target="tpu_custom_call" | custom-call | flops 1000000000 | tf_op jit(solution)/shard_map/pallas_call | solution.py:245
  50.0 1.3 %collective-permute-start.16 = (bf16[512,256]{1,0:T(8,128)(2,1)S(1)}, bf16[512,256]{1,0:T(8,128)(2,1)S(1)}, u32[]{:S(2)}, u32[]{:S(2)}) collective-permute-start(bf16[512,256]{1,0:T(8,128)(2,1)S(1)} %get-tuple-element.70.refs_1_), channel_id=1, source_target_pairs={{0,2},{1,3},{2,0},{3,1},{4,6},{5,7},{6,4},{7,5},{8,10},{9,11},{10,... | collective-permute-start | bytes 786440 | tf_op jit(solution)/shard_map/ppermute | solution.py:397
  51.3 3.1 %collective-permute-done.14.refs_2_.refs_3_ = bf16[512,256]{1,0:T(8,128)(2,1)S(1)} collective-permute-done((bf16[512,256]{1,0:T(8,128)(2,1)S(1)}, bf16[512,256]{1,0:T(8,128)(2,1)S(1)}, u32[]{:S(2)}, u32[]{:S(2)}) %collective-permute-start.14) | collective-permute-done | bytes 262176 | tf_op jit(solution)/shard_map/ppermute | solution.py:397
  54.4 1.0 shard_map.97
  55.6 6.4 %collective-permute-start.18 = (bf16[256,256]{1,0:T(8,128)(2,1)S(1)}, bf16[256,256]{1,0:T(8,128)(2,1)S(1)}, u32[]{:S(2)}, u32[]{:S(2)}) collective-permute-start(bf16[256,256]{1,0:T(8,128)(2,1)S(1)} %get-tuple-element.72), channel_id=1, source_target_pairs={{0,4},{4,0},{8,12},{12,8},{1,5},{5,1},{9,13},{13,9},{2,6},{6,2},{1... | collective-permute-start | bytes 393224 | tf_op jit(solution)/shard_map/ppermute | solution.py:407
  62.1 1.4 %shard_map.98 = (bf16[528,256]{1,0:T(8,128)(2,1)S(1)}, bf16[256,256]{1,0:T(8,128)(2,1)S(1)}, f32[2,8,256]{2,1,0:T(8,128)}) custom-call(s32[4]{0:T(128)S(1)} %copy-done.30, s32[16]{0:T(128)S(1)} %copy-done.29, f32[512,256]{1,0:T(8,128)S(1)} %get-tuple-element.63.kept, bf16[512,256]{1,0:T(8,128)(2,1)S(1)} %collective-permute-done.12.arrived, ...), custom_call_target="tpu_custom_call" | custom-call | flops 1000000000 | tf_op jit(solution)/shard_map/pallas_call | solution.py:310
  63.5 2.3 %collective-permute-done.18.refs_8_ = bf16[256,256]{1,0:T(8,128)(2,1)S(1)} collective-permute-done((bf16[256,256]{1,0:T(8,128)(2,1)S(1)}, bf16[256,256]{1,0:T(8,128)(2,1)S(1)}, u32[]{:S(2)}, u32[]{:S(2)}) %collective-permute-start.18) | collective-permute-done | bytes 131104 | tf_op jit(solution)/shard_map/ppermute | solution.py:407
  65.7 1.4 %collective-permute-done.10.refs_7_ = bf16[256,256]{1,0:T(8,128)(2,1)S(1)} collective-permute-done((bf16[256,256]{1,0:T(8,128)(2,1)S(1)}, bf16[256,256]{1,0:T(8,128)(2,1)S(1)}, u32[]{:S(2)}, u32[]{:S(2)}) %collective-permute-start.10) | collective-permute-done | bytes 131104 | tf_op jit(solution)/shard_map/ppermute | solution.py:407
  67.5 1.7 %collective-permute-start.15 = (bf16[528,256]{1,0:T(8,128)(2,1)S(1)}, bf16[528,256]{1,0:T(8,128)(2,1)S(1)}, u32[]{:S(2)}, u32[]{:S(2)}) collective-permute-start(bf16[528,256]{1,0:T(8,128)(2,1)S(1)} %get-tuple-element.69.refs_6_.refs_0_), channel_id=1, source_target_pairs={{0,2},{1,3},{2,0},{3,1},{4,6},{5,7},{6,4},{7,5},{8,10},{9,11},{10,... | collective-permute-start | bytes 811016 | tf_op jit(solution)/shard_map/ppermute | solution.py:397
  69.1 3.4 %collective-permute-start.21 = (bf16[256,256]{1,0:T(8,128)(2,1)S(1)}, bf16[256,256]{1,0:T(8,128)(2,1)S(1)}, u32[]{:S(2)}, u32[]{:S(2)}) collective-permute-start(bf16[256,256]{1,0:T(8,128)(2,1)S(1)} %get-tuple-element.74), channel_id=1, source_target_pairs={{0,4},{4,0},{8,12},{12,8},{1,5},{5,1},{9,13},{13,9},{2,6},{6,2},{1... | collective-permute-start | bytes 393224 | tf_op jit(solution)/shard_map/ppermute | solution.py:407
  73.1 3.7 %collective-permute-done.21.refs_4_ = bf16[256,256]{1,0:T(8,128)(2,1)S(1)} collective-permute-done((bf16[256,256]{1,0:T(8,128)(2,1)S(1)}, bf16[256,256]{1,0:T(8,128)(2,1)S(1)}, u32[]{:S(2)}, u32[]{:S(2)}) %collective-permute-start.21) | collective-permute-done | bytes 131104 | tf_op jit(solution)/shard_map/ppermute | solution.py:407
  76.8 2.4 %collective-permute-done.20.refs_3_ = bf16[256,256]{1,0:T(8,128)(2,1)S(1)} collective-permute-done((bf16[256,256]{1,0:T(8,128)(2,1)S(1)}, bf16[256,256]{1,0:T(8,128)(2,1)S(1)}, u32[]{:S(2)}, u32[]{:S(2)}) %collective-permute-start.20) | collective-permute-done | bytes 131104 | tf_op jit(solution)/shard_map/ppermute | solution.py:407
  79.4 1.9 %collective-permute-done.22.refs_1_ = bf16[2,528,256]{2,1,0:T(8,128)(2,1)S(1)} collective-permute-done((bf16[2,528,256]{2,1,0:T(8,128)(2,1)S(1)}, bf16[2,528,256]{2,1,0:T(8,128)(2,1)S(1)}, u32[]{:S(2)}, u32[]{:S(2)}) %collective-permute-start.22) | collective-permute-done | bytes 540704 | tf_op jit(solution)/shard_map/ppermute | solution.py:401
  81.4 3.0 %shard_map.103 = (f32[512,256]{1,0:T(8,128)S(1)}, bf16[512,256]{1,0:T(8,128)(2,1)S(1)}, f32[2,8,128]{2,1,0:T(8,128)S(1)}) custom-call(s32[8,16]{1,0:T(8,128)S(1)} %copy-done.8, s32[8,4]{1,0:T(8,128)S(1)} %copy-done.9, bf16[16,512,256]{2,1,0:T(8,128)(2,1)S(1)} %shard_map.102.blocks, bf16[8,256,256]{2,1,0:T(8,128)(2,1)S(1)} %copy-done, ...), custom_call_target="tpu_custom_call" | custom-call | flops 1000000000 | tf_op jit(solution)/shard_map/pallas_call | solution.py:245
  84.7 3.0 %shard_map.104 = (f32[512,256]{1,0:T(8,128)S(1)}, bf16[512,256]{1,0:T(8,128)(2,1)S(1)}, f32[2,8,128]{2,1,0:T(8,128)S(1)}) custom-call(s32[8,16]{1,0:T(8,128)S(1)} %copy-done.8, s32[8,4]{1,0:T(8,128)S(1)} %copy-done.9, bf16[16,512,256]{2,1,0:T(8,128)(2,1)S(1)} %shard_map.102.blocks, bf16[8,256,256]{2,1,0:T(8,128)(2,1)S(1)} %copy-done, ...), custom_call_target="tpu_custom_call" | custom-call | flops 1000000000 | tf_op jit(solution)/shard_map/pallas_call | solution.py:245
  88.9 3.2 %shard_map.106 = (f32[512,256]{1,0:T(8,128)S(1)}, bf16[528,256]{1,0:T(8,128)(2,1)S(1)}, f32[2,8,128]{2,1,0:T(8,128)S(1)}) custom-call(s32[8,16]{1,0:T(8,128)S(1)} %copy-done.8, s32[8,4]{1,0:T(8,128)S(1)} %copy-done.9, bf16[16,512,256]{2,1,0:T(8,128)(2,1)S(1)} %shard_map.102.blocks, bf16[8,256,256]{2,1,0:T(8,128)(2,1)S(1)} %copy-done, ...), custom_call_target="tpu_custom_call" | custom-call | flops 1000000000 | tf_op jit(solution)/shard_map/pallas_call | solution.py:245
  92.3 3.9 %shard_map.108 = (f32[512,256]{1,0:T(8,128)S(1)}, bf16[256,256]{1,0:T(8,128)(2,1)S(1)}, bf16[256,256]{1,0:T(8,128)(2,1)}, f32[2,8,128]{2,1,0:T(8,128)S(1)}) custom-call(s32[8,16]{1,0:T(8,128)S(1)} %copy-done.8, s32[8,4]{1,0:T(8,128)S(1)} %copy-done.9, bf16[16,512,256]{2,1,0:T(8,128)(2,1)S(1)} %shard_map.102.blocks, bf16[8,256,256]{2,1,0:T(8,128)(2,1)S(1)} %copy-done, ...), custom_call_target="tpu_custom_call" | custom-call | flops 1000000000 | tf_op jit(solution)/shard_map/pallas_call | solution.py:245
  96.2 0.8 copy-done.12
  97.4 0.8 shard_map.109
  98.8 9.1 %collective-permute-start.26 = (bf16[272,256]{1,0:T(8,128)(2,1)}, bf16[272,256]{1,0:T(8,128)(2,1)}, u32[]{:S(2)}, u32[]{:S(2)}) collective-permute-start(bf16[272,256]{1,0:T(8,128)(2,1)} %get-tuple-element.86), channel_id=1, source_target_pairs={{0,4},{4,0},{8,12},{12,8},{1,5},{5,1},{9,13},{13,9},{2,6},{6,2},{1... | collective-permute-start | bytes 417800 | tf_op jit(solution)/shard_map/ppermute | solution.py:407
  108.0 1.9 %collective-permute-start.28 = (bf16[256,256]{1,0:T(8,128)(2,1)S(1)}, bf16[256,256]{1,0:T(8,128)(2,1)S(1)}, u32[]{:S(2)}, u32[]{:S(2)}) collective-permute-start(bf16[256,256]{1,0:T(8,128)(2,1)S(1)} %shard_map.107.refs_1_), channel_id=1, source_target_pairs={{0,4},{4,0},{8,12},{12,8},{1,5},{5,1},{9,13},{13,9},{2,6},{6,2},{1... | collective-permute-start | bytes 393224 | tf_op jit(solution)/shard_map/ppermute | solution.py:407
  109.9 1.0 copy-done.13
  111.8 1.5 %collective-permute-start.31 = (bf16[256,256]{1,0:T(8,128)(2,1)S(1)}, bf16[256,256]{1,0:T(8,128)(2,1)S(1)}, u32[]{:S(2)}, u32[]{:S(2)}) collective-permute-start(bf16[256,256]{1,0:T(8,128)(2,1)S(1)} %shard_map.111), channel_id=1, source_target_pairs={{0,4},{4,0},{8,12},{12,8},{1,5},{5,1},{9,13},{13,9},{2,6},{6,2},{1... | collective-permute-start | bytes 393224 | tf_op jit(solution)/shard_map/ppermute | solution.py:407
  114.0 0.8 shard_map.110
  115.3 2.4 %fusion.11 = (bf16[256,256]{1,0:T(8,128)(2,1)S(1)}, bf16[256,256]{1,0:T(8,128)(2,1)S(1)}) fusion(f32[512,256]{1,0:T(8,128)S(1)} %copy-done.16, bf16[272,256]{1,0:T(8,128)(2,1)} %collective-permute-done.26.sent, bf16[528,256]{1,0:T(8,128)(2,1)} %copy-done.28, f32[]{:T(128)} %bitcast.1, f32[]{:T(128)} %bitcast, pred[]{:T(512)S(6)} %eq.3, ...), kind=kLoop, calls=%fused_computation.21 | loop fusion | flops 786432 | bytes 1048585 | tf_op jit(solution)/shard_map/convert_element_type | solution.py:516
  117.7 1.4 %fusion.3 = (bf16[256,256]{1,0:T(8,128)(2,1)S(1)}, bf16[256,256]{1,0:T(8,128)(2,1)S(1)}) fusion(bf16[256,256]{1,0:T(8,128)(2,1)S(1)} %collective-permute-done.27, f32[512,256]{1,0:T(8,128)S(1)} %copy-done.11, bf16[512,256]{1,0:T(8,128)(2,1)S(1)} %copy-done.27, f32[]{:T(128)} %bitcast.1, f32[]{:T(128)} %bitcast, pred[]{:T(512)S(6)} %eq.3, ...), kind=kLoop, calls=%fused_computation.13 | loop fusion | flops 786432 | bytes 1048585 | tf_op jit(solution)/shard_map/convert_element_type | solution.py:516
  119.1 1.4 %fusion.7 = (bf16[256,256]{1,0:T(8,128)(2,1)S(1)}, bf16[256,256]{1,0:T(8,128)(2,1)S(1)}) fusion(bf16[256,256]{1,0:T(8,128)(2,1)S(1)} %collective-permute-done.28, f32[512,256]{1,0:T(8,128)S(1)} %get-tuple-element.82.kept, bf16[512,256]{1,0:T(8,128)(2,1)S(1)} %copy-done.25, f32[]{:T(128)} %bitcast.1, f32[]{:T(128)} %bitcast, pred[]{:T(512)S(6)} %eq.3, ...), kind=kLoop, calls=%fused_computation.17 | loop fusion | flops 786432 | bytes 1048585 | tf_op jit(solution)/shard_map/convert_element_type | solution.py:516
  120.5 1.4 %fusion.15 = (bf16[256,256]{1,0:T(8,128)(2,1)S(1)}, bf16[256,256]{1,0:T(8,128)(2,1)S(1)}) fusion(bf16[256,256]{1,0:T(8,128)(2,1)S(1)} %collective-permute-done.31, bf16[256,256]{1,0:T(8,128)(2,1)S(1)} %collective-permute-done.29, f32[512,256]{1,0:T(8,128)S(1)} %copy-done.14, f32[]{:T(128)} %bitcast.1, f32[]{:T(128)} %bitcast, pred[]{:T(512)S(6)} %eq.3, ...), kind=kLoop, calls=%fused_computation.25 | loop fusion | flops 786432 | bytes 1048585 | tf_op jit(solution)/shard_map/convert_element_type | solution.py:516
  121.9 1.1 pad_maximum_fusion
  (127 shorter events, 9.3 us)
Async XLA Ops:
  0.6 15.2 %collective-permute-start = (bf16[256,1024]{1,0:T(8,128)(2,1)}, bf16[256,1024]{1,0:T(8,128)(2,1)S(1)}, u32[]{:S(2)}, u32[]{:S(2)}) collective-permute-start(bf16[256,1024]{1,0:T(8,128)(2,1)} %refs_0_.1), channel_id=1, source_target_pairs={{0,4},{4,0},{8,12},{12,8},{1,5},{5,1},{9,13},{13,9},{2,6},{6,2},{1... | collective-permute-start | bytes 1572872 | tf_op jit(solution)/shard_map/ppermute | solution.py:407
  3.7 16.7 %collective-permute-start.3 = (bf16[256,1024]{1,0:T(8,128)(2,1)}, bf16[256,1024]{1,0:T(8,128)(2,1)S(1)}, u32[]{:S(2)}, u32[]{:S(2)}) collective-permute-start(bf16[256,1024]{1,0:T(8,128)(2,1)} %refs_0_.1), channel_id=1, source_target_pairs={{0,2},{1,3},{2,0},{3,1},{4,6},{5,7},{6,4},{7,5},{8,10},{9,11},{10,... | collective-permute-start | bytes 1572872 | tf_op jit(solution)/shard_map/ppermute | solution.py:397
  9.3 9.0 %copy-start.36 = (bf16[4,256,256]{2,1,0:T(8,128)(2,1)S(1)}, bf16[4,256,256]{2,1,0:T(8,128)(2,1)}, u32[]{:S(2)}) copy-start(bf16[4,256,256]{2,1,0:T(8,128)(2,1)} %get-tuple-element.48) | copy-start | bytes 1572868
  9.3 10.5 %copy-start.5 = (bf16[256,1024]{1,0:T(8,128)(2,1)S(1)}, bf16[256,1024]{1,0:T(8,128)(2,1)}, u32[]{:S(2)}) copy-start(bf16[256,1024]{1,0:T(8,128)(2,1)} %refs_0_.1) | copy-start | bytes 1572868
  16.6 13.3 %collective-permute-start.1 = (bf16[256,1024]{1,0:T(8,128)(2,1)}, bf16[256,1024]{1,0:T(8,128)(2,1)S(1)}, u32[]{:S(2)}, u32[]{:S(2)}) collective-permute-start(bf16[256,1024]{1,0:T(8,128)(2,1)} %shard_map.88.refs_2_), channel_id=1, source_target_pairs={{0,2},{1,3},{2,0},{3,1},{4,6},{5,7},{6,4},{7,5},{8,10},{9,11},{10,... | collective-permute-start | bytes 1572872 | tf_op jit(solution)/shard_map/ppermute | solution.py:397
  18.3 12.5 %collective-permute-start.7 = (bf16[4,256,256]{2,1,0:T(8,128)(2,1)S(1)}, bf16[4,256,256]{2,1,0:T(8,128)(2,1)S(1)}, u32[]{:S(2)}, u32[]{:S(2)}) collective-permute-start(bf16[4,256,256]{2,1,0:T(8,128)(2,1)S(1)} %copy-done.36), channel_id=1, source_target_pairs={{0,4},{4,0},{8,12},{12,8},{1,5},{5,1},{9,13},{13,9},{2,6},{6,2},{1... | collective-permute-start | bytes 1572872 | tf_op jit(solution)/shard_map/ppermute | solution.py:407
  19.9 10.9 %collective-permute-start.4 = (bf16[256,1024]{1,0:T(8,128)(2,1)S(1)}, bf16[256,1024]{1,0:T(8,128)(2,1)S(1)}, u32[]{:S(2)}, u32[]{:S(2)}) collective-permute-start(bf16[256,1024]{1,0:T(8,128)(2,1)S(1)} %copy-done.5), channel_id=1, source_target_pairs={{0,1},{1,0},{2,3},{3,2},{4,5},{5,4},{6,7},{7,6},{8,9},{9,8},{10,11... | collective-permute-start | bytes 1572872 | tf_op jit(solution)/shard_map/ppermute | solution.py:401
  19.9 10.9 %collective-permute-start.6 = (bf16[256,1024]{1,0:T(8,128)(2,1)}, bf16[256,1024]{1,0:T(8,128)(2,1)S(1)}, u32[]{:S(2)}, u32[]{:S(2)}) collective-permute-start(bf16[256,1024]{1,0:T(8,128)(2,1)} %shard_map.88.refs_2_), channel_id=1, source_target_pairs={{0,1},{1,0},{2,3},{3,2},{4,5},{5,4},{6,7},{7,6},{8,9},{9,8},{10,11... | collective-permute-start | bytes 1572872 | tf_op jit(solution)/shard_map/ppermute | solution.py:401
  20.4 10.4 %collective-permute-start.5 = (bf16[256,1024]{1,0:T(8,128)(2,1)S(1)}, bf16[256,1024]{1,0:T(8,128)(2,1)S(1)}, u32[]{:S(2)}, u32[]{:S(2)}) collective-permute-start(bf16[256,1024]{1,0:T(8,128)(2,1)S(1)} %collective-permute-done.3.refs_1_), channel_id=1, source_target_pairs={{0,1},{1,0},{2,3},{3,2},{4,5},{5,4},{6,7},{7,6},{8,9},{9,8},{10,11... | collective-permute-start | bytes 1572872 | tf_op jit(solution)/shard_map/ppermute | solution.py:401
  30.0 2.7 %collective-permute-start.2 = (bf16[256,1024]{1,0:T(8,128)(2,1)S(1)}, bf16[256,1024]{1,0:T(8,128)(2,1)S(1)}, u32[]{:S(2)}, u32[]{:S(2)}) collective-permute-start(bf16[256,1024]{1,0:T(8,128)(2,1)S(1)} %collective-permute-done.1.refs_0_), channel_id=1, source_target_pairs={{0,1},{1,0},{2,3},{3,2},{4,5},{5,4},{6,7},{7,6},{8,9},{9,8},{10,11... | collective-permute-start | bytes 1572872 | tf_op jit(solution)/shard_map/ppermute | solution.py:401
  30.8 2.1 %collective-permute-start.8 = (bf16[4,256,256]{2,1,0:T(8,128)(2,1)S(1)}, bf16[4,256,256]{2,1,0:T(8,128)(2,1)S(1)}, u32[]{:S(2)}, u32[]{:S(2)}) collective-permute-start(bf16[4,256,256]{2,1,0:T(8,128)(2,1)S(1)} %collective-permute-done.7.left_near), channel_id=1, source_target_pairs={{0,1},{1,0},{2,3},{3,2},{4,5},{5,4},{6,7},{7,6},{8,9},{9,8},{10,11... | collective-permute-start | bytes 1572872 | tf_op jit(solution)/shard_map/ppermute | solution.py:401
  32.9 4.9 %copy-start.2 = (bf16[8,256,256]{2,1,0:T(8,128)(2,1)S(1)}, bf16[8,256,256]{2,1,0:T(8,128)(2,1)}, u32[]{:S(2)}) copy-start(bf16[8,256,256]{2,1,0:T(8,128)(2,1)} %get-tuple-element.51.right) | copy-start | bytes 3145732
  37.2 3.7 %collective-permute-start.9 = (bf16[512,256]{1,0:T(8,128)(2,1)S(1)}, bf16[512,256]{1,0:T(8,128)(2,1)S(1)}, u32[]{:S(2)}, u32[]{:S(2)}) collective-permute-start(bf16[512,256]{1,0:T(8,128)(2,1)S(1)} %get-tuple-element.50), channel_id=1, source_target_pairs={{0,1},{1,0},{2,3},{3,2},{4,8},{5,9},{6,10},{7,11},{8,4},{9,5},{10,... | collective-permute-start | bytes 786440 | tf_op jit(solution)/shard_map/ppermute | solution.py:421
  40.8 5.3 %collective-permute-start.11 = (bf16[512,256]{1,0:T(8,128)(2,1)S(1)}, bf16[512,256]{1,0:T(8,128)(2,1)S(1)}, u32[]{:S(2)}, u32[]{:S(2)}) collective-permute-start(bf16[512,256]{1,0:T(8,128)(2,1)S(1)} %get-tuple-element.61), channel_id=1, source_target_pairs={{0,1},{1,0},{2,3},{3,2},{4,8},{5,9},{6,10},{7,11},{8,4},{9,5},{10,... | collective-permute-start | bytes 786440 | tf_op jit(solution)/shard_map/ppermute | solution.py:421
  41.7 25.5 %copy-start.19 = (bf16[512,256]{1,0:T(8,128)(2,1)}, bf16[512,256]{1,0:T(8,128)(2,1)S(1)}, u32[]{:S(2)}) copy-start(bf16[512,256]{1,0:T(8,128)(2,1)S(1)} %get-tuple-element.54.refs_0_) | copy-start | bytes 786436
  45.0 6.3 %collective-permute-start.13 = (bf16[512,256]{1,0:T(8,128)(2,1)S(1)}, bf16[512,256]{1,0:T(8,128)(2,1)S(1)}, u32[]{:S(2)}, u32[]{:S(2)}) collective-permute-start(bf16[512,256]{1,0:T(8,128)(2,1)S(1)} %get-tuple-element.66), channel_id=1, source_target_pairs={{0,1},{1,0},{2,3},{3,2},{4,8},{5,9},{6,10},{7,11},{8,4},{9,5},{10,... | collective-permute-start | bytes 786440 | tf_op jit(solution)/shard_map/ppermute | solution.py:421
  45.3 9.1 %collective-permute-start.14 = (bf16[512,256]{1,0:T(8,128)(2,1)S(1)}, bf16[512,256]{1,0:T(8,128)(2,1)S(1)}, u32[]{:S(2)}, u32[]{:S(2)}) collective-permute-start(bf16[512,256]{1,0:T(8,128)(2,1)S(1)} %get-tuple-element.54.refs_0_), channel_id=1, source_target_pairs={{0,2},{1,3},{2,0},{3,1},{4,6},{5,7},{6,4},{7,5},{8,10},{9,11},{10,... | collective-permute-start | bytes 786440 | tf_op jit(solution)/shard_map/ppermute | solution.py:397
  46.9 20.3 %copy-start.21 = (bf16[512,256]{1,0:T(8,128)(2,1)}, bf16[512,256]{1,0:T(8,128)(2,1)S(1)}, u32[]{:S(2)}) copy-start(bf16[512,256]{1,0:T(8,128)(2,1)S(1)} %get-tuple-element.70.refs_1_) | copy-start | bytes 786436
  49.9 12.2 %collective-permute-start.12 = (bf16[512,256]{1,0:T(8,128)(2,1)S(1)}, bf16[512,256]{1,0:T(8,128)(2,1)S(1)}, u32[]{:S(2)}, u32[]{:S(2)}) collective-permute-start(bf16[512,256]{1,0:T(8,128)(2,1)S(1)} %get-tuple-element.64), channel_id=1, source_target_pairs={{0,1},{1,0},{2,3},{3,2},{4,8},{5,9},{6,10},{7,11},{8,4},{9,5},{10,... | collective-permute-start | bytes 786440 | tf_op jit(solution)/shard_map/ppermute | solution.py:421
  50.0 17.2 %collective-permute-start.16 = (bf16[512,256]{1,0:T(8,128)(2,1)S(1)}, bf16[512,256]{1,0:T(8,128)(2,1)S(1)}, u32[]{:S(2)}, u32[]{:S(2)}) collective-permute-start(bf16[512,256]{1,0:T(8,128)(2,1)S(1)} %get-tuple-element.70.refs_1_), channel_id=1, source_target_pairs={{0,2},{1,3},{2,0},{3,1},{4,6},{5,7},{6,4},{7,5},{8,10},{9,11},{10,... | collective-permute-start | bytes 786440 | tf_op jit(solution)/shard_map/ppermute | solution.py:397
  55.4 12.0 %copy-start.23 = (bf16[512,256]{1,0:T(8,128)(2,1)}, bf16[512,256]{1,0:T(8,128)(2,1)S(1)}, u32[]{:S(2)}) copy-start(bf16[512,256]{1,0:T(8,128)(2,1)S(1)} %get-tuple-element.71.refs_2_) | copy-start | bytes 786436
  55.4 11.7 %collective-permute-start.17 = (bf16[512,256]{1,0:T(8,128)(2,1)S(1)}, bf16[512,256]{1,0:T(8,128)(2,1)S(1)}, u32[]{:S(2)}, u32[]{:S(2)}) collective-permute-start(bf16[512,256]{1,0:T(8,128)(2,1)S(1)} %get-tuple-element.71.refs_2_), channel_id=1, source_target_pairs={{0,2},{1,3},{2,0},{3,1},{4,6},{5,7},{6,4},{7,5},{8,10},{9,11},{10,... | collective-permute-start | bytes 786440 | tf_op jit(solution)/shard_map/ppermute | solution.py:397
  55.6 10.1 %collective-permute-start.18 = (bf16[256,256]{1,0:T(8,128)(2,1)S(1)}, bf16[256,256]{1,0:T(8,128)(2,1)S(1)}, u32[]{:S(2)}, u32[]{:S(2)}) collective-permute-start(bf16[256,256]{1,0:T(8,128)(2,1)S(1)} %get-tuple-element.72), channel_id=1, source_target_pairs={{0,4},{4,0},{8,12},{12,8},{1,5},{5,1},{9,13},{13,9},{2,6},{6,2},{1... | collective-permute-start | bytes 393224 | tf_op jit(solution)/shard_map/ppermute | solution.py:407
  62.0 5.1 %collective-permute-start.10 = (bf16[256,256]{1,0:T(8,128)(2,1)S(1)}, bf16[256,256]{1,0:T(8,128)(2,1)S(1)}, u32[]{:S(2)}, u32[]{:S(2)}) collective-permute-start(bf16[256,256]{1,0:T(8,128)(2,1)S(1)} %get-tuple-element.55), channel_id=1, source_target_pairs={{0,4},{4,0},{8,12},{12,8},{1,5},{5,1},{9,13},{13,9},{2,6},{6,2},{1... | collective-permute-start | bytes 393224 | tf_op jit(solution)/shard_map/ppermute | solution.py:407
  67.2 5.4 %copy-start.17 = (bf16[256,256]{1,0:T(8,128)(2,1)}, bf16[256,256]{1,0:T(8,128)(2,1)S(1)}, u32[]{:S(2)}) copy-start(bf16[256,256]{1,0:T(8,128)(2,1)S(1)} %collective-permute-done.10.refs_7_) | copy-start | bytes 393220
  67.4 5.3 %collective-permute-start.19 = (bf16[6,512,256]{2,1,0:T(8,128)(2,1)S(1)}, bf16[6,512,256]{2,1,0:T(8,128)(2,1)S(1)}, u32[]{:S(2)}, u32[]{:S(2)}) collective-permute-start(bf16[6,512,256]{2,1,0:T(8,128)(2,1)S(1)} %shard_map.99), channel_id=1, source_target_pairs={{0,1},{1,0},{2,3},{3,2},{4,5},{5,4},{6,7},{7,6},{8,9},{9,8},{10,11... | collective-permute-start | bytes 4718600 | tf_op jit(solution)/shard_map/ppermute | solution.py:401
  67.5 11.7 %collective-permute-start.15 = (bf16[528,256]{1,0:T(8,128)(2,1)S(1)}, bf16[528,256]{1,0:T(8,128)(2,1)S(1)}, u32[]{:S(2)}, u32[]{:S(2)}) collective-permute-start(bf16[528,256]{1,0:T(8,128)(2,1)S(1)} %get-tuple-element.69.refs_6_.refs_0_), channel_id=1, source_target_pairs={{0,2},{1,3},{2,0},{3,1},{4,6},{5,7},{6,4},{7,5},{8,10},{9,11},{10,... | collective-permute-start | bytes 811016 | tf_op jit(solution)/shard_map/ppermute | solution.py:397
  69.1 7.7 %collective-permute-start.21 = (bf16[256,256]{1,0:T(8,128)(2,1)S(1)}, bf16[256,256]{1,0:T(8,128)(2,1)S(1)}, u32[]{:S(2)}, u32[]{:S(2)}) collective-permute-start(bf16[256,256]{1,0:T(8,128)(2,1)S(1)} %get-tuple-element.74), channel_id=1, source_target_pairs={{0,4},{4,0},{8,12},{12,8},{1,5},{5,1},{9,13},{13,9},{2,6},{6,2},{1... | collective-permute-start | bytes 393224 | tf_op jit(solution)/shard_map/ppermute | solution.py:407
  72.5 6.6 %collective-permute-start.20 = (bf16[256,256]{1,0:T(8,128)(2,1)S(1)}, bf16[256,256]{1,0:T(8,128)(2,1)S(1)}, u32[]{:S(2)}, u32[]{:S(2)}) collective-permute-start(bf16[256,256]{1,0:T(8,128)(2,1)S(1)} %get-tuple-element.73), channel_id=1, source_target_pairs={{0,4},{4,0},{8,12},{12,8},{1,5},{5,1},{9,13},{13,9},{2,6},{6,2},{1... | collective-permute-start | bytes 393224 | tf_op jit(solution)/shard_map/ppermute | solution.py:407
  79.3 2.0 %collective-permute-start.22 = (bf16[2,528,256]{2,1,0:T(8,128)(2,1)S(1)}, bf16[2,528,256]{2,1,0:T(8,128)(2,1)S(1)}, u32[]{:S(2)}, u32[]{:S(2)}) collective-permute-start(bf16[2,528,256]{2,1,0:T(8,128)(2,1)S(1)} %shard_map.101.refs_0_), channel_id=1, source_target_pairs={{0,1},{1,0},{2,3},{3,2},{4,5},{5,4},{6,7},{7,6},{8,9},{9,8},{10,11... | collective-permute-start | bytes 1622024 | tf_op jit(solution)/shard_map/ppermute | solution.py:401
  84.5 3.7 %collective-permute-start.23 = (bf16[512,256]{1,0:T(8,128)(2,1)S(1)}, bf16[512,256]{1,0:T(8,128)(2,1)S(1)}, u32[]{:S(2)}, u32[]{:S(2)}) collective-permute-start(bf16[512,256]{1,0:T(8,128)(2,1)S(1)} %get-tuple-element.78), channel_id=1, source_target_pairs={{0,1},{1,0},{2,3},{3,2},{4,8},{5,9},{6,10},{7,11},{8,4},{9,5},{10,... | collective-permute-start | bytes 786440 | tf_op jit(solution)/shard_map/ppermute | solution.py:421
  87.7 4.6 %collective-permute-start.25 = (bf16[512,256]{1,0:T(8,128)(2,1)S(1)}, bf16[512,256]{1,0:T(8,128)(2,1)S(1)}, u32[]{:S(2)}, u32[]{:S(2)}) collective-permute-start(bf16[512,256]{1,0:T(8,128)(2,1)S(1)} %get-tuple-element.83), channel_id=1, source_target_pairs={{0,1},{1,0},{2,3},{3,2},{4,8},{5,9},{6,10},{7,11},{8,4},{9,5},{10,... | collective-permute-start | bytes 786440 | tf_op jit(solution)/shard_map/ppermute | solution.py:421
  92.1 5.3 %copy-start.15 = (f32[512,256]{1,0:T(8,128)}, f32[512,256]{1,0:T(8,128)S(1)}, u32[]{:S(2)}) copy-start(f32[512,256]{1,0:T(8,128)S(1)} %get-tuple-element.79.kept) | copy-start | bytes 1572868
  92.1 5.3 %collective-permute-start.24 = (bf16[528,256]{1,0:T(8,128)(2,1)S(1)}, bf16[528,256]{1,0:T(8,128)(2,1)S(1)}, u32[]{:S(2)}, u32[]{:S(2)}) collective-permute-start(bf16[528,256]{1,0:T(8,128)(2,1)S(1)} %get-tuple-element.80), channel_id=1, source_target_pairs={{0,1},{1,0},{2,3},{3,2},{4,8},{5,9},{6,10},{7,11},{8,4},{9,5},{10,... | collective-permute-start | bytes 811016 | tf_op jit(solution)/shard_map/ppermute | solution.py:421
  97.0 10.9 %copy-start.32 = (f32[2,8,128]{2,1,0:T(8,128)}, f32[2,8,128]{2,1,0:T(8,128)S(1)}, u32[]{:S(2)}) copy-start(f32[2,8,128]{2,1,0:T(8,128)S(1)} %get-tuple-element.84.refs_1_.refs_0_) | copy-start | bytes 24580
  97.0 12.9 %collective-permute-start.30 = (bf16[256,256]{1,0:T(8,128)(2,1)}, bf16[256,256]{1,0:T(8,128)(2,1)S(1)}, u32[]{:S(2)}, u32[]{:S(2)}) collective-permute-start(bf16[256,256]{1,0:T(8,128)(2,1)} %get-tuple-element.89), channel_id=1, source_target_pairs={{0,1},{1,0},{2,3},{3,2},{4,8},{5,9},{6,10},{7,11},{8,4},{9,5},{10,... | collective-permute-start | bytes 393224 | tf_op jit(solution)/shard_map/ppermute | solution.py:421
  98.8 14.5 %collective-permute-start.26 = (bf16[272,256]{1,0:T(8,128)(2,1)}, bf16[272,256]{1,0:T(8,128)(2,1)}, u32[]{:S(2)}, u32[]{:S(2)}) collective-permute-start(bf16[272,256]{1,0:T(8,128)(2,1)} %get-tuple-element.86), channel_id=1, source_target_pairs={{0,4},{4,0},{8,12},{12,8},{1,5},{5,1},{9,13},{13,9},{2,6},{6,2},{1... | collective-permute-start | bytes 417800 | tf_op jit(solution)/shard_map/ppermute | solution.py:407
  107.9 9.8 %collective-permute-start.27 = (bf16[256,256]{1,0:T(8,128)(2,1)S(1)}, bf16[256,256]{1,0:T(8,128)(2,1)S(1)}, u32[]{:S(2)}, u32[]{:S(2)}) collective-permute-start(bf16[256,256]{1,0:T(8,128)(2,1)S(1)} %shard_map.105.refs_3_), channel_id=1, source_target_pairs={{0,4},{4,0},{8,12},{12,8},{1,5},{5,1},{9,13},{13,9},{2,6},{6,2},{1... | collective-permute-start | bytes 393224 | tf_op jit(solution)/shard_map/ppermute | solution.py:407
  108.0 11.1 %collective-permute-start.28 = (bf16[256,256]{1,0:T(8,128)(2,1)S(1)}, bf16[256,256]{1,0:T(8,128)(2,1)S(1)}, u32[]{:S(2)}, u32[]{:S(2)}) collective-permute-start(bf16[256,256]{1,0:T(8,128)(2,1)S(1)} %shard_map.107.refs_1_), channel_id=1, source_target_pairs={{0,4},{4,0},{8,12},{12,8},{1,5},{5,1},{9,13},{13,9},{2,6},{6,2},{1... | collective-permute-start | bytes 393224 | tf_op jit(solution)/shard_map/ppermute | solution.py:407
  109.9 10.6 %collective-permute-start.29 = (bf16[256,256]{1,0:T(8,128)(2,1)}, bf16[256,256]{1,0:T(8,128)(2,1)S(1)}, u32[]{:S(2)}, u32[]{:S(2)}) collective-permute-start(bf16[256,256]{1,0:T(8,128)(2,1)} %copy-done.31), channel_id=1, source_target_pairs={{0,1},{1,0},{2,3},{3,2},{4,8},{5,9},{6,10},{7,11},{8,4},{9,5},{10,... | collective-permute-start | bytes 393224 | tf_op jit(solution)/shard_map/ppermute | solution.py:421
  111.7 6.0 %copy-start.11 = (f32[512,256]{1,0:T(8,128)S(1)}, f32[512,256]{1,0:T(8,128)}, u32[]{:S(2)}) copy-start(f32[512,256]{1,0:T(8,128)} %copy-done.10) | copy-start | bytes 1572868
  111.7 6.0 %copy-start.18 = (bf16[256,256]{1,0:T(8,128)(2,1)S(1)}, bf16[256,256]{1,0:T(8,128)(2,1)}, u32[]{:S(2)}) copy-start(bf16[256,256]{1,0:T(8,128)(2,1)} %copy-done.17) | copy-start | bytes 393220
  111.7 6.0 %copy-start.20 = (bf16[512,256]{1,0:T(8,128)(2,1)S(1)}, bf16[512,256]{1,0:T(8,128)(2,1)}, u32[]{:S(2)}) copy-start(bf16[512,256]{1,0:T(8,128)(2,1)} %copy-done.19) | copy-start | bytes 786436
  111.7 6.0 %copy-start.27 = (bf16[512,256]{1,0:T(8,128)(2,1)S(1)}, bf16[512,256]{1,0:T(8,128)(2,1)}, u32[]{:S(2)}) copy-start(bf16[512,256]{1,0:T(8,128)(2,1)} %copy-done.26) | copy-start | bytes 786436
  111.7 7.4 %copy-start.22 = (bf16[512,256]{1,0:T(8,128)(2,1)S(1)}, bf16[512,256]{1,0:T(8,128)(2,1)}, u32[]{:S(2)}) copy-start(bf16[512,256]{1,0:T(8,128)(2,1)} %copy-done.21) | copy-start | bytes 786436
  111.7 7.4 %copy-start.25 = (bf16[512,256]{1,0:T(8,128)(2,1)S(1)}, bf16[512,256]{1,0:T(8,128)(2,1)}, u32[]{:S(2)}) copy-start(bf16[512,256]{1,0:T(8,128)(2,1)} %copy-done.24) | copy-start | bytes 786436
  111.8 8.8 %copy-start.14 = (f32[512,256]{1,0:T(8,128)S(1)}, f32[512,256]{1,0:T(8,128)}, u32[]{:S(2)}) copy-start(f32[512,256]{1,0:T(8,128)} %copy-done.12) | copy-start | bytes 1572868
  111.8 8.7 %collective-permute-start.31 = (bf16[256,256]{1,0:T(8,128)(2,1)S(1)}, bf16[256,256]{1,0:T(8,128)(2,1)S(1)}, u32[]{:S(2)}, u32[]{:S(2)}) collective-permute-start(bf16[256,256]{1,0:T(8,128)(2,1)S(1)} %shard_map.111), channel_id=1, source_target_pairs={{0,4},{4,0},{8,12},{12,8},{1,5},{5,1},{9,13},{13,9},{2,6},{6,2},{1... | collective-permute-start | bytes 393224 | tf_op jit(solution)/shard_map/ppermute | solution.py:407
  (21 other events, 36.5 us)

commit v6 on v5

--- a/solution.py
+++ b/solution.py
@@ -344,29 +344,90 @@
     )(kept, arrived, *([stats] if coded else []), *tokens)
 
 
-def scales_kernel(entry_count, own, sent, out, code, sem):
-    copy = pltpu.make_async_copy(sent.at[sent.shape[0] - CODE_ROWS:], code, sem)
-    copy.start()
-    copy.wait()
+def finish_kernel(entry_count, local, carrier, stats, *refs):
+    parts, near_images, kept, arrived, near_again = (refs[at * local:(at + 1) * local] for at in range(5))
+    outs, (image_held, kept_held, more_held, out_held, code, sems, out_sems) = refs[5 * local:5 * local + 2], refs[-7:]
+    tile = image_held.shape[1]
     leading = leads(lax.axis_index("row")) == 1
-    norm, correlation = (
-        jnp.where(leading, mine, jnp.broadcast_to(theirs, mine.shape))
-        for mine, theirs in zip((own[0], own[1]), decode(code[...]))
-    )
-    out[0] = lax.rsqrt(norm / entry_count + 1e-06)
-    out[1] = correlation / norm
-
-
-def scales(entry_count, own, sent):
-    return pl.pallas_call(
-        functools.partial(scales_kernel, entry_count),
-        in_specs=[VMEM, ANY],
-        out_specs=VMEM,
-        out_shape=TOKEN,
-        scratch_shapes=[pltpu.VMEM((CODE_ROWS, sent.shape[1]), sent.dtype), pltpu.SemaphoreType.DMA],
+
+    def own(first):
+        pairs = [(parts, image_held), (arrived, more_held), (kept, kept_held)]
+        return [
+            pltpu.make_async_copy(source[first].at[:tile], held.at[first], sems.at[at, first])
+            for at, (source, held) in enumerate(pairs)
+        ]
+
+    def sent(first):
+        pairs = [(near_images, image_held), (near_again, more_held)]
+        copies = [
+            pltpu.make_async_copy(source[first].at[:tile], held.at[first], sems.at[at, first])
+            for at, (source, held) in enumerate(pairs)
+        ]
+        if first == carrier:
+            copies.append(pltpu.make_async_copy(near_again[first].at[tile:], code, sems.at[2, first]))
+        return copies
+
+    def each(firsts, act):
+        for first in firsts:
+            @pl.when(leading)
+            def _():
+                for copy in own(first):
+                    act(copy)
+
+            @pl.when(jnp.logical_not(leading))
+            def _():
+                for copy in sent(first):
+                    act(copy)
+
+    order = [first for first in range(local) if first == carrier] + [first for first in range(local) if first != carrier]
+    each(order, lambda copy: copy.start())
+    scale = theta = None
+    out_copies = []
+    for first in order:
+        each([first], lambda copy: copy.wait())
+        if scale is None:
+            norm, correlation = stats[0, :1, :1], stats[1, :1, :1]
+            if carrier < local:
+                norm, correlation = (
+                    jnp.where(leading, mine, theirs) for mine, theirs in zip((norm, correlation), decode(code[...]))
+                )
+            scale = lax.rsqrt(norm / entry_count + 1e-06)
+            theta = correlation / norm
+        image = image_held[first].astype(jnp.float32)
+        value = jnp.where(leading, kept_held[first], 0.0) + more_held[first].astype(jnp.float32)
+        out_held[0, first] = (image * scale).astype(out_held.dtype)
+        out_held[1, first] = ((value - theta * image) * scale).astype(out_held.dtype)
+        for at, out in enumerate(outs):
+            copy = pltpu.make_async_copy(
+                out_held.at[at, first], out.at[:, first * tile:(first + 1) * tile], out_sems.at[at, first]
+            )
+            copy.start()
+            out_copies.append(copy)
+    for copy in out_copies:
+        copy.wait()
+
+
+def finish(entry_count, carrier, stats, parts, near_images, again, near_again):
+    local, tile = len(parts), near_images[0].shape[0]
+    out = jax.ShapeDtypeStruct((tile, local * tile), near_images[0].dtype)
+    block = (local, tile, tile)
+    return pl.pallas_call(
+        functools.partial(finish_kernel, entry_count, local, carrier),
+        in_specs=[VMEM] + [ANY] * (5 * local),
+        out_specs=[ANY, ANY],
+        out_shape=[out, out],
+        scratch_shapes=[
+            pltpu.VMEM(block, out.dtype),
+            pltpu.VMEM(block, jnp.float32),
+            pltpu.VMEM(block, out.dtype),
+            pltpu.VMEM((2, *block), out.dtype),
+            pltpu.VMEM((CODE_ROWS, tile), out.dtype),
+            pltpu.SemaphoreType.DMA((3, local)),
+            pltpu.SemaphoreType.DMA((2, local)),
+        ],
         compiler_params=pltpu.CompilerParams(vmem_limit_bytes=VMEM_LIMIT),
         cost_estimate=BRIEF,
-    )(own, sent)
+    )(stats, *parts, *near_images, *(kept for kept, _ in again), *(arrived[0] for _, arrived in again), *near_again)
 
 
 def after(value, *others):
@@ -492,30 +553,12 @@
                 (near,) = emit(kept, arrived[-1], tokens)
             near_again.append(near)
     near_again = [to_partner(part) for part in near_again]
-    if carrier < local:
-        both_scales = scales(entry_count, stats, near_again[carrier])
-        scale, theta = both_scales[0, 0, 0], both_scales[1, 0, 0]
-    else:
+    if carrier == local:
         stats = settle(held, arrived_held, [token])
         for bit in range(pair_bits):
             stats = stats + lax.ppermute(stats, both, leader_swap(1 << bit))
         stats = jnp.where(leading, stats, to_partner(stats))
-        norm, correlation = stats[0, 0, 0], stats[1, 0, 0]
-        scale = lax.rsqrt(norm / entry_count + 1e-06)
-        theta = correlation / norm
-
-    images = [
-        jnp.where(leading, part[0][:tile], near_image).astype(jnp.float32) for part, near_image in zip(parts, near_images)
-    ]
-    again = [
-        jnp.where(leading, kept[:tile] + arrived[0][:tile].astype(jnp.float32), near[:tile].astype(jnp.float32))
-        for (kept, arrived), near in zip(again, near_again)
-    ]
-    first_product = jnp.concatenate([(image * scale).astype(jnp.bfloat16) for image in images], 1)
-    second_product = jnp.concatenate(
-        [((more - theta * image) * scale).astype(jnp.bfloat16) for more, image in zip(again, images)], 1
-    )
-    return (first_product, second_product)
+    return tuple(finish(entry_count, carrier, stats, [part[0] for part in parts], near_images, again, near_again))
 
 
 def solution(mesh):

time: 124 us -> 116 us (0.935)
  other arithmetic: 7.58 us -> 0 us
  local copies, waits for them, and re-layouts: 10.2 us -> 2.82 us
  waiting for transfers between devices: 26.7 us -> 29.8 us
  starting transfers between devices: 37.2 us -> 40.2 us
  Pallas kernels: 40.1 us -> 41.5 us
    unnamed x75 -> x23, local copies, waits for them, and re-layouts: 9.34 us -> 2.54 us
    convert_element_type x4 -> x0, other arithmetic: 6.47 us -> none  [on_device(): ((more - theta * image) * scale).astype(jnp.bfloat16)]
    ppermute x10, waiting for transfers between devices: 12.1 us -> 17.9 us  [to_partner(): return lax.ppermute(part, 'row', swap('row', 1))]
    ppermute x6, waiting for transfers between devices: 12.7 us -> 9.51 us  [far(): lax.ppermute(piece, 'col', swap('col', 1 << bit))]
    ppermute x10, starting transfers between devices: 27.2 us -> 30 us  [to_partner(): return lax.ppermute(part, 'row', swap('row', 1))]
    pallas_call x1, Pallas kernels: 0.75 us -> 2.73 us  [finish(): pl.pallas_call(functools.partial(finish_kernel, entry_count, local, carri...]
  transfers between devices with their start and end apart: 32 -> 32, of which waited for: 9 -> 12; matrix products, arithmetic and copies ran while one was open for 6% -> 1% of each run, Pallas kernels for 27% -> 28%
where the time goes in v6:
time: 116 us
  Pallas kernels  41.5 us (36%)
  starting transfers between devices  40.2 us (35%)
  waiting for transfers between devices  29.8 us (26%)
  local copies, waits for them, and re-layouts  2.82 us (2%)
    ppermute x10, starting transfers between devices, to_partner(): return lax.ppermute(part, 'row', swap('row', 1))  30 us
    pallas_call x8, Pallas kernels, products(): pl.pallas_call(functools.partial(product_kernel, first, local, out_slots,...  24.4 us
    ppermute x10, waiting for transfers between devices, to_partner(): return lax.ppermute(part, 'row', swap('row', 1))  17.9 us
    ppermute x6, waiting for transfers between devices, far(): lax.ppermute(piece, 'col', swap('col', 1 << bit))  9.51 us
    ppermute x6, starting transfers between devices, far(): lax.ppermute(piece, 'col', swap('col', 1 << bit))  7.35 us
    pallas_call x1, Pallas kernels, mask_right(): pl.pallas_call(mask_right_kernel, grid=(terms // 2,), in_specs=[SMEM, SME...  5.09 us
    pallas_call x4, Pallas kernels, combine(): pl.pallas_call(functools.partial(combine_kernel, first, local), in_specs=...  4.01 us
    pallas_call x1, Pallas kernels, mask_left(): pl.pallas_call(mask_left_kernel, in_specs=[SMEM, SMEM, VMEM], out_specs=[...  2.79 us
  transfers between devices with their start and end apart: 32, of which 12 were waited for; matrix products, arithmetic and copies ran while one was open for 1% of the time, Pallas kernels for 28%

profile of v6, /device:TPU:0, one launch (start us, length us, event | category | flops | bytes accessed | tf_op | source)
XLA Modules:
  0.0 115.5 jit_solution(8026327524068997737)
XLA Ops:
  0.6 3.1 %collective-permute-start = (bf16[256,1024]{1,0:T(8,128)(2,1)}, bf16[256,1024]{1,0:T(8,128)(2,1)}, u32[]{:S(2)}, u32[]{:S(2)}) collective-permute-start(bf16[256,1024]{1,0:T(8,128)(2,1)} %refs_0_.1), channel_id=1, source_target_pairs={{0,4},{4,0},{8,12},{12,8},{1,5},{5,1},{9,13},{13,9},{2,6},{6,2},{1... | collective-permute-start | bytes 1572872 | tf_op jit(solution)/shard_map/ppermute | solution.py:468
  3.7 1.5 %collective-permute-start.3 = (bf16[256,1024]{1,0:T(8,128)(2,1)}, bf16[256,1024]{1,0:T(8,128)(2,1)S(1)}, u32[]{:S(2)}, u32[]{:S(2)}) collective-permute-start(bf16[256,1024]{1,0:T(8,128)(2,1)} %refs_0_.1), channel_id=1, source_target_pairs={{0,2},{1,3},{2,0},{3,1},{4,6},{5,7},{6,4},{7,5},{8,10},{9,11},{10,... | collective-permute-start | bytes 1572872 | tf_op jit(solution)/shard_map/ppermute | solution.py:458
  5.2 1.3 %copy.19.left_dest.target = s32[8,4]{1,0:T(8,128)} copy(s32[8,4]{0,1:T(4,128)} %param.10) | data formatting | bytes 256 | tf_op args[3]
  6.6 2.8 %shard_map.86 = (bf16[8,256,256]{2,1,0:T(8,128)(2,1)}, bf16[4,256,256]{2,1,0:T(8,128)(2,1)}) custom-call(s32[8,4]{1,0:T(8,128)} %copy.19.left_dest.target, s32[4]{0:T(128)} %left_sizes.9, bf16[8,1,256,256]{3,2,1,0:T(8,128)(2,1)} %left.1), custom_call_target="tpu_custom_call" | custom-call | flops 1000000000 | tf_op jit(solution)/shard_map/pallas_call | solution.py:74
  9.3 5.1 %shard_map.87 = (bf16[8,256,256]{2,1,0:T(8,128)(2,1)}, bf16[8,256,256]{2,1,0:T(8,128)(2,1)}, bf16[8,256,256]{2,1,0:T(8,128)(2,1)}, bf16[8,256,256]{2,1,0:T(8,128)(2,1)}) custom-call(s32[8,16]{1,0:T(8,128)} %source.15, s32[16]{0:T(128)} %right_sizes.9, bf16[8,4,256,256]{3,2,1,0:T(8,128)(2,1)} %right.1), custom_call_target="tpu_custom_call" | custom-call | flops 1000000000 | tf_op jit(solution)/shard_map/pallas_call | solution.py:95
  14.4 1.5 %collective-permute-done.refs_0_ = bf16[256,1024]{1,0:T(8,128)(2,1)} collective-permute-done((bf16[256,1024]{1,0:T(8,128)(2,1)}, bf16[256,1024]{1,0:T(8,128)(2,1)}, u32[]{:S(2)}, u32[]{:S(2)}) %collective-permute-start) | collective-permute-done | bytes 524320 | tf_op jit(solution)/shard_map/ppermute | solution.py:468
  16.0 1.7 %collective-permute-start.1 = (bf16[256,1024]{1,0:T(8,128)(2,1)}, bf16[256,1024]{1,0:T(8,128)(2,1)S(1)}, u32[]{:S(2)}, u32[]{:S(2)}) collective-permute-start(bf16[256,1024]{1,0:T(8,128)(2,1)} %shard_map.88.refs_2_), channel_id=1, source_target_pairs={{0,2},{1,3},{2,0},{3,1},{4,6},{5,7},{6,4},{7,5},{8,10},{9,11},{10,... | collective-permute-start | bytes 1572872 | tf_op jit(solution)/shard_map/ppermute | solution.py:458
  17.6 1.6 %collective-permute-start.7 = (bf16[4,256,256]{2,1,0:T(8,128)(2,1)S(1)}, bf16[4,256,256]{2,1,0:T(8,128)(2,1)S(1)}, u32[]{:S(2)}, u32[]{:S(2)}) collective-permute-start(bf16[4,256,256]{2,1,0:T(8,128)(2,1)S(1)} %copy-done.10), channel_id=1, source_target_pairs={{0,4},{4,0},{8,12},{12,8},{1,5},{5,1},{9,13},{13,9},{2,6},{6,2},{1... | collective-permute-start | bytes 1572872 | tf_op jit(solution)/shard_map/ppermute | solution.py:468
  19.2 0.5 collective-permute-start.5
  19.8 9.5 %collective-permute-done.1.refs_0_ = bf16[256,1024]{1,0:T(8,128)(2,1)S(1)} collective-permute-done((bf16[256,1024]{1,0:T(8,128)(2,1)}, bf16[256,1024]{1,0:T(8,128)(2,1)S(1)}, u32[]{:S(2)}, u32[]{:S(2)}) %collective-permute-start.1) | collective-permute-done | bytes 524320 | tf_op jit(solution)/shard_map/ppermute | solution.py:458
  29.3 0.8 collective-permute-done.7.left_near
  30.2 1.5 %shard_map.89.refs_2_ = bf16[16,512,256]{2,1,0:T(8,128)(2,1)S(1)} custom-call(bf16[256,1024]{1,0:T(8,128)(2,1)S(1)} %copy-done.5, bf16[256,1024]{1,0:T(8,128)(2,1)S(1)} %collective-permute-done.3.refs_1_, bf16[256,1024]{1,0:T(8,128)(2,1)} %shard_map.88.refs_2_, bf16[256,1024]{1,0:T(8,128)(2,1)S(1)} %collective-permute-done.4.refs_3_, ...), custom_call_target="tpu_custom_call" | custom-call | flops 1000000000 | tf_op jit(solution)/shard_map/pallas_call | solution.py:131
  32.0 0.8 copy-done
  32.9 0.3 copy-done.4
  33.2 3.0 %shard_map.91 = (f32[512,256]{1,0:T(8,128)S(1)}, bf16[512,256]{1,0:T(8,128)(2,1)S(1)}, f32[2,8,128]{2,1,0:T(8,128)S(1)}) custom-call(s32[8,16]{1,0:T(8,128)S(1)} %copy-done.6, s32[8,4]{1,0:T(8,128)S(1)} %copy-done.7, bf16[16,512,256]{2,1,0:T(8,128)(2,1)S(1)} %shard_map.90.blocks, bf16[8,256,256]{2,1,0:T(8,128)(2,1)S(1)} %copy-done, ...), custom_call_target="tpu_custom_call" | custom-call | flops 1000000000 | tf_op jit(solution)/shard_map/pallas_call | solution.py:245
  36.3 0.6 collective-permute-start.9
  36.8 3.0 %shard_map.92 = (f32[512,256]{1,0:T(8,128)S(1)}, bf16[512,256]{1,0:T(8,128)(2,1)S(1)}, f32[2,8,128]{2,1,0:T(8,128)S(1)}) custom-call(s32[8,16]{1,0:T(8,128)S(1)} %copy-done.6, s32[8,4]{1,0:T(8,128)S(1)} %copy-done.7, bf16[16,512,256]{2,1,0:T(8,128)(2,1)S(1)} %shard_map.90.blocks, bf16[8,256,256]{2,1,0:T(8,128)(2,1)S(1)} %copy-done, ...), custom_call_target="tpu_custom_call" | custom-call | flops 1000000000 | tf_op jit(solution)/shard_map/pallas_call | solution.py:245
  40.0 0.8 shard_map.93
  40.8 1.0 collective-permute-start.13
  41.8 3.0 %shard_map.94 = (f32[512,256]{1,0:T(8,128)S(1)}, bf16[512,256]{1,0:T(8,128)(2,1)S(1)}, f32[2,8,128]{2,1,0:T(8,128)S(1)}) custom-call(s32[8,16]{1,0:T(8,128)S(1)} %copy-done.6, s32[8,4]{1,0:T(8,128)S(1)} %copy-done.7, bf16[16,512,256]{2,1,0:T(8,128)(2,1)S(1)} %shard_map.90.blocks, bf16[8,256,256]{2,1,0:T(8,128)(2,1)S(1)} %copy-done, ...), custom_call_target="tpu_custom_call" | custom-call | flops 1000000000 | tf_op jit(solution)/shard_map/pallas_call | solution.py:245
  45.0 0.8 shard_map.95
  45.8 1.3 %collective-permute-start.15 = (bf16[512,256]{1,0:T(8,128)(2,1)S(1)}, bf16[512,256]{1,0:T(8,128)(2,1)S(1)}, u32[]{:S(2)}, u32[]{:S(2)}) collective-permute-start(bf16[512,256]{1,0:T(8,128)(2,1)S(1)} %get-tuple-element.69.refs_1_), channel_id=1, source_target_pairs={{0,2},{1,3},{2,0},{3,1},{4,6},{5,7},{6,4},{7,5},{8,10},{9,11},{10,... | collective-permute-start | bytes 786440 | tf_op jit(solution)/shard_map/ppermute | solution.py:458
  47.1 3.0 %shard_map.96 = (f32[512,256]{1,0:T(8,128)S(1)}, bf16[512,256]{1,0:T(8,128)(2,1)S(1)}, f32[2,8,128]{2,1,0:T(8,128)S(1)}) custom-call(s32[8,16]{1,0:T(8,128)S(1)} %copy-done.6, s32[8,4]{1,0:T(8,128)S(1)} %copy-done.7, bf16[16,512,256]{2,1,0:T(8,128)(2,1)S(1)} %shard_map.90.blocks, bf16[8,256,256]{2,1,0:T(8,128)(2,1)S(1)} %copy-done, ...), custom_call_target="tpu_custom_call" | custom-call | flops 1000000000 | tf_op jit(solution)/shard_map/pallas_call | solution.py:245
  50.2 1.0 shard_map.97
  51.2 1.0 collective-permute-start.16
  52.3 9.1 %collective-permute-start.17 = (bf16[256,256]{1,0:T(8,128)(2,1)S(1)}, bf16[256,256]{1,0:T(8,128)(2,1)S(1)}, u32[]{:S(2)}, u32[]{:S(2)}) collective-permute-start(bf16[256,256]{1,0:T(8,128)(2,1)S(1)} %get-tuple-element.71), channel_id=1, source_target_pairs={{0,4},{4,0},{8,12},{12,8},{1,5},{5,1},{9,13},{13,9},{2,6},{6,2},{1... | collective-permute-start | bytes 393224 | tf_op jit(solution)/shard_map/ppermute | solution.py:468
  61.4 1.4 %shard_map.98 = (bf16[528,256]{1,0:T(8,128)(2,1)S(1)}, bf16[256,256]{1,0:T(8,128)(2,1)S(1)}, f32[2,8,256]{2,1,0:T(8,128)}) custom-call(s32[4]{0:T(128)S(1)} %copy-done.9, s32[16]{0:T(128)S(1)} %copy-done.8, f32[512,256]{1,0:T(8,128)S(1)} %get-tuple-element.61.kept, bf16[512,256]{1,0:T(8,128)(2,1)S(1)} %collective-permute-done.11.arrived, ...), custom_call_target="tpu_custom_call" | custom-call | flops 1000000000 | tf_op jit(solution)/shard_map/pallas_call | solution.py:310
  62.8 2.1 %collective-permute-done.17.refs_7_.refs_4_ = bf16[256,256]{1,0:T(8,128)(2,1)S(1)} collective-permute-done((bf16[256,256]{1,0:T(8,128)(2,1)S(1)}, bf16[256,256]{1,0:T(8,128)(2,1)S(1)}, u32[]{:S(2)}, u32[]{:S(2)}) %collective-permute-start.17) | collective-permute-done | bytes 131104 | tf_op jit(solution)/shard_map/ppermute | solution.py:468
  64.9 1.4 %collective-permute-done.18.refs_8_.refs_5_ = bf16[256,256]{1,0:T(8,128)(2,1)S(1)} collective-permute-done((bf16[256,256]{1,0:T(8,128)(2,1)S(1)}, bf16[256,256]{1,0:T(8,128)(2,1)S(1)}, u32[]{:S(2)}, u32[]{:S(2)}) %collective-permute-start.18) | collective-permute-done | bytes 131104 | tf_op jit(solution)/shard_map/ppermute | solution.py:468
  66.6 0.9 collective-permute-start.14
  67.4 1.4 %collective-permute-start.20 = (bf16[256,256]{1,0:T(8,128)(2,1)S(1)}, bf16[256,256]{1,0:T(8,128)(2,1)S(1)}, u32[]{:S(2)}, u32[]{:S(2)}) collective-permute-start(bf16[256,256]{1,0:T(8,128)(2,1)S(1)} %get-tuple-element.73), channel_id=1, source_target_pairs={{0,4},{4,0},{8,12},{12,8},{1,5},{5,1},{9,13},{13,9},{2,6},{6,2},{1... | collective-permute-start | bytes 393224 | tf_op jit(solution)/shard_map/ppermute | solution.py:468
  68.8 0.6 collective-permute-start.21
  69.6 0.4 collective-permute-done.19
  70.4 3.4 %collective-permute-done.20.refs_3_.refs_6_ = bf16[256,256]{1,0:T(8,128)(2,1)S(1)} collective-permute-done((bf16[256,256]{1,0:T(8,128)(2,1)S(1)}, bf16[256,256]{1,0:T(8,128)(2,1)S(1)}, u32[]{:S(2)}, u32[]{:S(2)}) %collective-permute-start.20) | collective-permute-done | bytes 131104 | tf_op jit(solution)/shard_map/ppermute | solution.py:468
  73.8 2.0 %collective-permute-done.21.refs_4_.refs_7_ = bf16[256,256]{1,0:T(8,128)(2,1)S(1)} collective-permute-done((bf16[256,256]{1,0:T(8,128)(2,1)S(1)}, bf16[256,256]{1,0:T(8,128)(2,1)S(1)}, u32[]{:S(2)}, u32[]{:S(2)}) %collective-permute-start.21) | collective-permute-done | bytes 131104 | tf_op jit(solution)/shard_map/ppermute | solution.py:468
  76.0 1.9 %collective-permute-done.22.refs_1_ = bf16[2,528,256]{2,1,0:T(8,128)(2,1)S(1)} collective-permute-done((bf16[2,528,256]{2,1,0:T(8,128)(2,1)S(1)}, bf16[2,528,256]{2,1,0:T(8,128)(2,1)S(1)}, u32[]{:S(2)}, u32[]{:S(2)}) %collective-permute-start.22) | collective-permute-done | bytes 540704 | tf_op jit(solution)/shard_map/ppermute | solution.py:462
  78.1 3.0 %shard_map.103 = (f32[512,256]{1,0:T(8,128)S(1)}, bf16[512,256]{1,0:T(8,128)(2,1)S(1)}, f32[2,8,128]{2,1,0:T(8,128)S(1)}) custom-call(s32[8,16]{1,0:T(8,128)S(1)} %copy-done.6, s32[8,4]{1,0:T(8,128)S(1)} %copy-done.7, bf16[16,512,256]{2,1,0:T(8,128)(2,1)S(1)} %shard_map.102.blocks, bf16[8,256,256]{2,1,0:T(8,128)(2,1)S(1)} %copy-done, ...), custom_call_target="tpu_custom_call" | custom-call | flops 1000000000 | tf_op jit(solution)/shard_map/pallas_call | solution.py:245
  81.3 3.0 %shard_map.104 = (f32[512,256]{1,0:T(8,128)S(1)}, bf16[512,256]{1,0:T(8,128)(2,1)S(1)}, f32[2,8,128]{2,1,0:T(8,128)S(1)}) custom-call(s32[8,16]{1,0:T(8,128)S(1)} %copy-done.6, s32[8,4]{1,0:T(8,128)S(1)} %copy-done.7, bf16[16,512,256]{2,1,0:T(8,128)(2,1)S(1)} %shard_map.102.blocks, bf16[8,256,256]{2,1,0:T(8,128)(2,1)S(1)} %copy-done, ...), custom_call_target="tpu_custom_call" | custom-call | flops 1000000000 | tf_op jit(solution)/shard_map/pallas_call | solution.py:245
  84.4 0.4 collective-permute-start.25
  84.8 3.2 %shard_map.106 = (f32[512,256]{1,0:T(8,128)S(1)}, bf16[528,256]{1,0:T(8,128)(2,1)S(1)}, f32[2,8,128]{2,1,0:T(8,128)S(1)}) custom-call(s32[8,16]{1,0:T(8,128)S(1)} %copy-done.6, s32[8,4]{1,0:T(8,128)S(1)} %copy-done.7, bf16[16,512,256]{2,1,0:T(8,128)(2,1)S(1)} %shard_map.102.blocks, bf16[8,256,256]{2,1,0:T(8,128)(2,1)S(1)} %copy-done, ...), custom_call_target="tpu_custom_call" | custom-call | flops 1000000000 | tf_op jit(solution)/shard_map/pallas_call | solution.py:245
  88.3 3.0 %shard_map.108 = (f32[512,256]{1,0:T(8,128)S(1)}, bf16[256,256]{1,0:T(8,128)(2,1)S(1)}, bf16[256,256]{1,0:T(8,128)(2,1)S(1)}, f32[2,8,128]{2,1,0:T(8,128)S(1)}) custom-call(s32[8,16]{1,0:T(8,128)S(1)} %copy-done.6, s32[8,4]{1,0:T(8,128)S(1)} %copy-done.7, bf16[16,512,256]{2,1,0:T(8,128)(2,1)S(1)} %shard_map.102.blocks, bf16[8,256,256]{2,1,0:T(8,128)(2,1)S(1)} %copy-done, ...), custom_call_target="tpu_custom_call" | custom-call | flops 1000000000 | tf_op jit(solution)/shard_map/pallas_call | solution.py:245
  91.3 0.4 collective-permute-start.30
  91.7 9.9 %collective-permute-start.28 = (bf16[256,256]{1,0:T(8,128)(2,1)S(1)}, bf16[256,256]{1,0:T(8,128)(2,1)S(1)}, u32[]{:S(2)}, u32[]{:S(2)}) collective-permute-start(bf16[256,256]{1,0:T(8,128)(2,1)S(1)} %shard_map.107.refs_1_), channel_id=1, source_target_pairs={{0,4},{4,0},{8,12},{12,8},{1,5},{5,1},{9,13},{13,9},{2,6},{6,2},{1... | collective-permute-start | bytes 393224 | tf_op jit(solution)/shard_map/ppermute | solution.py:468
  101.8 2.5 %collective-permute-start.29 = (bf16[272,256]{1,0:T(8,128)(2,1)S(1)}, bf16[272,256]{1,0:T(8,128)(2,1)S(1)}, u32[]{:S(2)}, u32[]{:S(2)}) collective-permute-start(bf16[272,256]{1,0:T(8,128)(2,1)S(1)} %get-tuple-element.88), channel_id=1, source_target_pairs={{0,4},{4,0},{8,12},{12,8},{1,5},{5,1},{9,13},{13,9},{2,6},{6,2},{1... | collective-permute-start | bytes 417800 | tf_op jit(solution)/shard_map/ppermute | solution.py:468
  104.3 1.8 %collective-permute-start.31 = (bf16[256,256]{1,0:T(8,128)(2,1)S(1)}, bf16[256,256]{1,0:T(8,128)(2,1)S(1)}, u32[]{:S(2)}, u32[]{:S(2)}) collective-permute-start(bf16[256,256]{1,0:T(8,128)(2,1)S(1)} %shard_map.110), channel_id=1, source_target_pairs={{0,4},{4,0},{8,12},{12,8},{1,5},{5,1},{9,13},{13,9},{2,6},{6,2},{1... | collective-permute-start | bytes 393224 | tf_op jit(solution)/shard_map/ppermute | solution.py:468
  106.1 2.6 %collective-permute-done.27.refs_16_ = bf16[256,256]{1,0:T(8,128)(2,1)S(1)} collective-permute-done((bf16[256,256]{1,0:T(8,128)(2,1)S(1)}, bf16[256,256]{1,0:T(8,128)(2,1)S(1)}, u32[]{:S(2)}, u32[]{:S(2)}) %collective-permute-start.27) | collective-permute-done | bytes 131104 | tf_op jit(solution)/shard_map/ppermute | solution.py:468
  108.7 4.0 %collective-permute-done.31.refs_19_ = bf16[256,256]{1,0:T(8,128)(2,1)S(1)} collective-permute-done((bf16[256,256]{1,0:T(8,128)(2,1)S(1)}, bf16[256,256]{1,0:T(8,128)(2,1)S(1)}, u32[]{:S(2)}, u32[]{:S(2)}) %collective-permute-start.31) | collective-permute-done | bytes 131104 | tf_op jit(solution)/shard_map/ppermute | solution.py:468
  112.6 2.7 %shard_map.111 = (bf16[256,1024]{1,0:T(8,128)(2,1)}, bf16[256,1024]{1,0:T(8,128)(2,1)}) custom-call(f32[2,8,128]{2,1,0:T(8,128)S(1)} %get-tuple-element.85.stats, bf16[512,256]{1,0:T(8,128)(2,1)S(1)} %get-tuple-element.66.refs_0_, bf16[512,256]{1,0:T(8,128)(2,1)S(1)} %get-tuple-element.69.refs_1_, bf16[512,256]{1,0:T(8,128)(2,1)S(1)} %get-tuple-element.70.refs_2_, ...), custom_call_target="tpu_custom_call" | custom-call | flops 1000000000 | tf_op jit(solution)/shard_map/pallas_call | solution.py:414
  (69 shorter events, 2.5 us)
Async XLA Ops:
  0.6 15.3 %collective-permute-start = (bf16[256,1024]{1,0:T(8,128)(2,1)}, bf16[256,1024]{1,0:T(8,128)(2,1)}, u32[]{:S(2)}, u32[]{:S(2)}) collective-permute-start(bf16[256,1024]{1,0:T(8,128)(2,1)} %refs_0_.1), channel_id=1, source_target_pairs={{0,4},{4,0},{8,12},{12,8},{1,5},{5,1},{9,13},{13,9},{2,6},{6,2},{1... | collective-permute-start | bytes 1572872 | tf_op jit(solution)/shard_map/ppermute | solution.py:468
  3.7 15.5 %collective-permute-start.3 = (bf16[256,1024]{1,0:T(8,128)(2,1)}, bf16[256,1024]{1,0:T(8,128)(2,1)S(1)}, u32[]{:S(2)}, u32[]{:S(2)}) collective-permute-start(bf16[256,1024]{1,0:T(8,128)(2,1)} %refs_0_.1), channel_id=1, source_target_pairs={{0,2},{1,3},{2,0},{3,1},{4,6},{5,7},{6,4},{7,5},{8,10},{9,11},{10,... | collective-permute-start | bytes 1572872 | tf_op jit(solution)/shard_map/ppermute | solution.py:458
  9.3 8.3 %copy-start.10 = (bf16[4,256,256]{2,1,0:T(8,128)(2,1)S(1)}, bf16[4,256,256]{2,1,0:T(8,128)(2,1)}, u32[]{:S(2)}) copy-start(bf16[4,256,256]{2,1,0:T(8,128)(2,1)} %get-tuple-element.48) | copy-start | bytes 1572868
  9.3 9.8 %copy-start.5 = (bf16[256,1024]{1,0:T(8,128)(2,1)S(1)}, bf16[256,1024]{1,0:T(8,128)(2,1)}, u32[]{:S(2)}) copy-start(bf16[256,1024]{1,0:T(8,128)(2,1)} %refs_0_.1) | copy-start | bytes 1572868
  16.0 13.3 %collective-permute-start.1 = (bf16[256,1024]{1,0:T(8,128)(2,1)}, bf16[256,1024]{1,0:T(8,128)(2,1)S(1)}, u32[]{:S(2)}, u32[]{:S(2)}) collective-permute-start(bf16[256,1024]{1,0:T(8,128)(2,1)} %shard_map.88.refs_2_), channel_id=1, source_target_pairs={{0,2},{1,3},{2,0},{3,1},{4,6},{5,7},{6,4},{7,5},{8,10},{9,11},{10,... | collective-permute-start | bytes 1572872 | tf_op jit(solution)/shard_map/ppermute | solution.py:458
  17.6 12.5 %collective-permute-start.7 = (bf16[4,256,256]{2,1,0:T(8,128)(2,1)S(1)}, bf16[4,256,256]{2,1,0:T(8,128)(2,1)S(1)}, u32[]{:S(2)}, u32[]{:S(2)}) collective-permute-start(bf16[4,256,256]{2,1,0:T(8,128)(2,1)S(1)} %copy-done.10), channel_id=1, source_target_pairs={{0,4},{4,0},{8,12},{12,8},{1,5},{5,1},{9,13},{13,9},{2,6},{6,2},{1... | collective-permute-start | bytes 1572872 | tf_op jit(solution)/shard_map/ppermute | solution.py:468
  19.2 10.9 %collective-permute-start.4 = (bf16[256,1024]{1,0:T(8,128)(2,1)S(1)}, bf16[256,1024]{1,0:T(8,128)(2,1)S(1)}, u32[]{:S(2)}, u32[]{:S(2)}) collective-permute-start(bf16[256,1024]{1,0:T(8,128)(2,1)S(1)} %copy-done.5), channel_id=1, source_target_pairs={{0,1},{1,0},{2,3},{3,2},{4,5},{5,4},{6,7},{7,6},{8,9},{9,8},{10,11... | collective-permute-start | bytes 1572872 | tf_op jit(solution)/shard_map/ppermute | solution.py:462
  19.2 10.9 %collective-permute-start.5 = (bf16[256,1024]{1,0:T(8,128)(2,1)S(1)}, bf16[256,1024]{1,0:T(8,128)(2,1)S(1)}, u32[]{:S(2)}, u32[]{:S(2)}) collective-permute-start(bf16[256,1024]{1,0:T(8,128)(2,1)S(1)} %collective-permute-done.3.refs_1_), channel_id=1, source_target_pairs={{0,1},{1,0},{2,3},{3,2},{4,5},{5,4},{6,7},{7,6},{8,9},{9,8},{10,11... | collective-permute-start | bytes 1572872 | tf_op jit(solution)/shard_map/ppermute | solution.py:462
  19.7 10.4 %collective-permute-start.6 = (bf16[256,1024]{1,0:T(8,128)(2,1)}, bf16[256,1024]{1,0:T(8,128)(2,1)S(1)}, u32[]{:S(2)}, u32[]{:S(2)}) collective-permute-start(bf16[256,1024]{1,0:T(8,128)(2,1)} %shard_map.88.refs_2_), channel_id=1, source_target_pairs={{0,1},{1,0},{2,3},{3,2},{4,5},{5,4},{6,7},{7,6},{8,9},{9,8},{10,11... | collective-permute-start | bytes 1572872 | tf_op jit(solution)/shard_map/ppermute | solution.py:462
  29.3 2.4 %collective-permute-start.2 = (bf16[256,1024]{1,0:T(8,128)(2,1)S(1)}, bf16[256,1024]{1,0:T(8,128)(2,1)S(1)}, u32[]{:S(2)}, u32[]{:S(2)}) collective-permute-start(bf16[256,1024]{1,0:T(8,128)(2,1)S(1)} %collective-permute-done.1.refs_0_), channel_id=1, source_target_pairs={{0,1},{1,0},{2,3},{3,2},{4,5},{5,4},{6,7},{7,6},{8,9},{9,8},{10,11... | collective-permute-start | bytes 1572872 | tf_op jit(solution)/shard_map/ppermute | solution.py:462
  30.1 1.9 %collective-permute-start.8 = (bf16[4,256,256]{2,1,0:T(8,128)(2,1)S(1)}, bf16[4,256,256]{2,1,0:T(8,128)(2,1)S(1)}, u32[]{:S(2)}, u32[]{:S(2)}) collective-permute-start(bf16[4,256,256]{2,1,0:T(8,128)(2,1)S(1)} %collective-permute-done.7.left_near), channel_id=1, source_target_pairs={{0,1},{1,0},{2,3},{3,2},{4,5},{5,4},{6,7},{7,6},{8,9},{9,8},{10,11... | collective-permute-start | bytes 1572872 | tf_op jit(solution)/shard_map/ppermute | solution.py:462
  31.6 1.2 %copy-start = (bf16[8,256,256]{2,1,0:T(8,128)(2,1)S(1)}, bf16[8,256,256]{2,1,0:T(8,128)(2,1)}, u32[]{:S(2)}) copy-start(bf16[8,256,256]{2,1,0:T(8,128)(2,1)} %get-tuple-element.46.refs_1_.left_own) | copy-start | bytes 3145732
  31.7 1.5 %copy-start.4 = (bf16[8,256,256]{2,1,0:T(8,128)(2,1)S(1)}, bf16[8,256,256]{2,1,0:T(8,128)(2,1)}, u32[]{:S(2)}) copy-start(bf16[8,256,256]{2,1,0:T(8,128)(2,1)} %get-tuple-element.47.refs_2_.right) | copy-start | bytes 3145732
  31.7 1.5 %copy-start.6 = (s32[8,16]{1,0:T(8,128)S(1)}, s32[8,16]{1,0:T(8,128)}, u32[]{:S(2)}) copy-start(s32[8,16]{1,0:T(8,128)} %source.15) | copy-start | bytes 1540
  31.7 1.5 %copy-start.7 = (s32[8,4]{1,0:T(8,128)S(1)}, s32[8,4]{1,0:T(8,128)}, u32[]{:S(2)}) copy-start(s32[8,4]{1,0:T(8,128)} %copy.19.left_dest.target) | copy-start | bytes 388
  31.9 4.9 %copy-start.2 = (bf16[8,256,256]{2,1,0:T(8,128)(2,1)S(1)}, bf16[8,256,256]{2,1,0:T(8,128)(2,1)}, u32[]{:S(2)}) copy-start(bf16[8,256,256]{2,1,0:T(8,128)(2,1)} %get-tuple-element.51.right) | copy-start | bytes 3145732
  36.2 3.7 %copy-start.8 = (s32[16]{0:T(128)S(1)}, s32[16]{0:T(128)}, u32[]{:S(2)}) copy-start(s32[16]{0:T(128)} %right_sizes.9) | copy-start | bytes 196
  36.2 3.7 %copy-start.9 = (s32[4]{0:T(128)S(1)}, s32[4]{0:T(128)}, u32[]{:S(2)}) copy-start(s32[4]{0:T(128)} %left_sizes.9) | copy-start | bytes 52
  36.3 3.7 %collective-permute-start.9 = (bf16[512,256]{1,0:T(8,128)(2,1)S(1)}, bf16[512,256]{1,0:T(8,128)(2,1)S(1)}, u32[]{:S(2)}, u32[]{:S(2)}) collective-permute-start(bf16[512,256]{1,0:T(8,128)(2,1)S(1)} %get-tuple-element.55), channel_id=1, source_target_pairs={{0,1},{1,0},{2,3},{3,2},{4,8},{5,9},{6,10},{7,11},{8,4},{9,5},{10,... | collective-permute-start | bytes 786440 | tf_op jit(solution)/shard_map/ppermute | solution.py:482
  39.9 2.0 %copy-start.3 = (bf16[8,256,256]{2,1,0:T(8,128)(2,1)S(1)}, bf16[8,256,256]{2,1,0:T(8,128)(2,1)}, u32[]{:S(2)}) copy-start(bf16[8,256,256]{2,1,0:T(8,128)(2,1)} %get-tuple-element.50.right) | copy-start | bytes 3145732
  39.9 5.1 %collective-permute-start.10 = (bf16[512,256]{1,0:T(8,128)(2,1)S(1)}, bf16[512,256]{1,0:T(8,128)(2,1)S(1)}, u32[]{:S(2)}, u32[]{:S(2)}) collective-permute-start(bf16[512,256]{1,0:T(8,128)(2,1)S(1)} %get-tuple-element.59), channel_id=1, source_target_pairs={{0,1},{1,0},{2,3},{3,2},{4,8},{5,9},{6,10},{7,11},{8,4},{9,5},{10,... | collective-permute-start | bytes 786440 | tf_op jit(solution)/shard_map/ppermute | solution.py:482
  40.8 9.4 %collective-permute-start.13 = (bf16[512,256]{1,0:T(8,128)(2,1)S(1)}, bf16[512,256]{1,0:T(8,128)(2,1)S(1)}, u32[]{:S(2)}, u32[]{:S(2)}) collective-permute-start(bf16[512,256]{1,0:T(8,128)(2,1)S(1)} %get-tuple-element.66.refs_0_), channel_id=1, source_target_pairs={{0,2},{1,3},{2,0},{3,1},{4,6},{5,7},{6,4},{7,5},{8,10},{9,11},{10,... | collective-permute-start | bytes 786440 | tf_op jit(solution)/shard_map/ppermute | solution.py:458
  44.9 2.2 %copy-start.1 = (bf16[8,256,256]{2,1,0:T(8,128)(2,1)S(1)}, bf16[8,256,256]{2,1,0:T(8,128)(2,1)}, u32[]{:S(2)}) copy-start(bf16[8,256,256]{2,1,0:T(8,128)(2,1)} %get-tuple-element.49.right) | copy-start | bytes 3145732
  44.9 5.4 %collective-permute-start.12 = (bf16[512,256]{1,0:T(8,128)(2,1)S(1)}, bf16[512,256]{1,0:T(8,128)(2,1)S(1)}, u32[]{:S(2)}, u32[]{:S(2)}) collective-permute-start(bf16[512,256]{1,0:T(8,128)(2,1)S(1)} %get-tuple-element.64), channel_id=1, source_target_pairs={{0,1},{1,0},{2,3},{3,2},{4,8},{5,9},{6,10},{7,11},{8,4},{9,5},{10,... | collective-permute-start | bytes 786440 | tf_op jit(solution)/shard_map/ppermute | solution.py:482
  45.8 20.5 %collective-permute-start.15 = (bf16[512,256]{1,0:T(8,128)(2,1)S(1)}, bf16[512,256]{1,0:T(8,128)(2,1)S(1)}, u32[]{:S(2)}, u32[]{:S(2)}) collective-permute-start(bf16[512,256]{1,0:T(8,128)(2,1)S(1)} %get-tuple-element.69.refs_1_), channel_id=1, source_target_pairs={{0,2},{1,3},{2,0},{3,1},{4,6},{5,7},{6,4},{7,5},{8,10},{9,11},{10,... | collective-permute-start | bytes 786440 | tf_op jit(solution)/shard_map/ppermute | solution.py:458
  50.1 11.3 %collective-permute-start.11 = (bf16[512,256]{1,0:T(8,128)(2,1)S(1)}, bf16[512,256]{1,0:T(8,128)(2,1)S(1)}, u32[]{:S(2)}, u32[]{:S(2)}) collective-permute-start(bf16[512,256]{1,0:T(8,128)(2,1)S(1)} %get-tuple-element.62), channel_id=1, source_target_pairs={{0,1},{1,0},{2,3},{3,2},{4,8},{5,9},{6,10},{7,11},{8,4},{9,5},{10,... | collective-permute-start | bytes 786440 | tf_op jit(solution)/shard_map/ppermute | solution.py:482
  51.2 15.1 %collective-permute-start.16 = (bf16[512,256]{1,0:T(8,128)(2,1)S(1)}, bf16[512,256]{1,0:T(8,128)(2,1)S(1)}, u32[]{:S(2)}, u32[]{:S(2)}) collective-permute-start(bf16[512,256]{1,0:T(8,128)(2,1)S(1)} %get-tuple-element.70.refs_2_), channel_id=1, source_target_pairs={{0,2},{1,3},{2,0},{3,1},{4,6},{5,7},{6,4},{7,5},{8,10},{9,11},{10,... | collective-permute-start | bytes 786440 | tf_op jit(solution)/shard_map/ppermute | solution.py:458
  52.3 12.6 %collective-permute-start.17 = (bf16[256,256]{1,0:T(8,128)(2,1)S(1)}, bf16[256,256]{1,0:T(8,128)(2,1)S(1)}, u32[]{:S(2)}, u32[]{:S(2)}) collective-permute-start(bf16[256,256]{1,0:T(8,128)(2,1)S(1)} %get-tuple-element.71), channel_id=1, source_target_pairs={{0,4},{4,0},{8,12},{12,8},{1,5},{5,1},{9,13},{13,9},{2,6},{6,2},{1... | collective-permute-start | bytes 393224 | tf_op jit(solution)/shard_map/ppermute | solution.py:468
  61.4 5.0 %collective-permute-start.18 = (bf16[256,256]{1,0:T(8,128)(2,1)S(1)}, bf16[256,256]{1,0:T(8,128)(2,1)S(1)}, u32[]{:S(2)}, u32[]{:S(2)}) collective-permute-start(bf16[256,256]{1,0:T(8,128)(2,1)S(1)} %get-tuple-element.72), channel_id=1, source_target_pairs={{0,4},{4,0},{8,12},{12,8},{1,5},{5,1},{9,13},{13,9},{2,6},{6,2},{1... | collective-permute-start | bytes 393224 | tf_op jit(solution)/shard_map/ppermute | solution.py:468
  66.5 3.5 %collective-permute-start.19 = (bf16[6,512,256]{2,1,0:T(8,128)(2,1)S(1)}, bf16[6,512,256]{2,1,0:T(8,128)(2,1)S(1)}, u32[]{:S(2)}, u32[]{:S(2)}) collective-permute-start(bf16[6,512,256]{2,1,0:T(8,128)(2,1)S(1)} %shard_map.99), channel_id=1, source_target_pairs={{0,1},{1,0},{2,3},{3,2},{4,5},{5,4},{6,7},{7,6},{8,9},{9,8},{10,11... | collective-permute-start | bytes 4718600 | tf_op jit(solution)/shard_map/ppermute | solution.py:462
  66.6 9.2 %collective-permute-start.14 = (bf16[528,256]{1,0:T(8,128)(2,1)S(1)}, bf16[528,256]{1,0:T(8,128)(2,1)S(1)}, u32[]{:S(2)}, u32[]{:S(2)}) collective-permute-start(bf16[528,256]{1,0:T(8,128)(2,1)S(1)} %get-tuple-element.68.refs_6_.refs_0_.refs_3_), channel_id=1, source_target_pairs={{0,2},{1,3},{2,0},{3,1},{4,6},{5,7},{6,4},{7,5},{8,10},{9,11},{10,... | collective-permute-start | bytes 811016 | tf_op jit(solution)/shard_map/ppermute | solution.py:458
  67.4 6.3 %collective-permute-start.20 = (bf16[256,256]{1,0:T(8,128)(2,1)S(1)}, bf16[256,256]{1,0:T(8,128)(2,1)S(1)}, u32[]{:S(2)}, u32[]{:S(2)}) collective-permute-start(bf16[256,256]{1,0:T(8,128)(2,1)S(1)} %get-tuple-element.73), channel_id=1, source_target_pairs={{0,4},{4,0},{8,12},{12,8},{1,5},{5,1},{9,13},{13,9},{2,6},{6,2},{1... | collective-permute-start | bytes 393224 | tf_op jit(solution)/shard_map/ppermute | solution.py:468
  68.8 7.0 %collective-permute-start.21 = (bf16[256,256]{1,0:T(8,128)(2,1)S(1)}, bf16[256,256]{1,0:T(8,128)(2,1)S(1)}, u32[]{:S(2)}, u32[]{:S(2)}) collective-permute-start(bf16[256,256]{1,0:T(8,128)(2,1)S(1)} %get-tuple-element.74), channel_id=1, source_target_pairs={{0,4},{4,0},{8,12},{12,8},{1,5},{5,1},{9,13},{13,9},{2,6},{6,2},{1... | collective-permute-start | bytes 393224 | tf_op jit(solution)/shard_map/ppermute | solution.py:468
  75.9 2.0 %collective-permute-start.22 = (bf16[2,528,256]{2,1,0:T(8,128)(2,1)S(1)}, bf16[2,528,256]{2,1,0:T(8,128)(2,1)S(1)}, u32[]{:S(2)}, u32[]{:S(2)}) collective-permute-start(bf16[2,528,256]{2,1,0:T(8,128)(2,1)S(1)} %shard_map.101.refs_0_), channel_id=1, source_target_pairs={{0,1},{1,0},{2,3},{3,2},{4,5},{5,4},{6,7},{7,6},{8,9},{9,8},{10,11... | collective-permute-start | bytes 1622024 | tf_op jit(solution)/shard_map/ppermute | solution.py:462
  81.1 3.7 %collective-permute-start.23 = (bf16[512,256]{1,0:T(8,128)(2,1)S(1)}, bf16[512,256]{1,0:T(8,128)(2,1)S(1)}, u32[]{:S(2)}, u32[]{:S(2)}) collective-permute-start(bf16[512,256]{1,0:T(8,128)(2,1)S(1)} %get-tuple-element.78), channel_id=1, source_target_pairs={{0,1},{1,0},{2,3},{3,2},{4,8},{5,9},{6,10},{7,11},{8,4},{9,5},{10,... | collective-permute-start | bytes 786440 | tf_op jit(solution)/shard_map/ppermute | solution.py:482
  84.4 3.9 %collective-permute-start.25 = (bf16[512,256]{1,0:T(8,128)(2,1)S(1)}, bf16[512,256]{1,0:T(8,128)(2,1)S(1)}, u32[]{:S(2)}, u32[]{:S(2)}) collective-permute-start(bf16[512,256]{1,0:T(8,128)(2,1)S(1)} %get-tuple-element.83), channel_id=1, source_target_pairs={{0,1},{1,0},{2,3},{3,2},{4,8},{5,9},{6,10},{7,11},{8,4},{9,5},{10,... | collective-permute-start | bytes 786440 | tf_op jit(solution)/shard_map/ppermute | solution.py:482
  88.0 13.7 %collective-permute-start.24 = (bf16[528,256]{1,0:T(8,128)(2,1)S(1)}, bf16[528,256]{1,0:T(8,128)(2,1)S(1)}, u32[]{:S(2)}, u32[]{:S(2)}) collective-permute-start(bf16[528,256]{1,0:T(8,128)(2,1)S(1)} %get-tuple-element.80), channel_id=1, source_target_pairs={{0,1},{1,0},{2,3},{3,2},{4,8},{5,9},{6,10},{7,11},{8,4},{9,5},{10,... | collective-permute-start | bytes 811016 | tf_op jit(solution)/shard_map/ppermute | solution.py:482
  91.3 13.0 %collective-permute-start.30 = (bf16[256,256]{1,0:T(8,128)(2,1)S(1)}, bf16[256,256]{1,0:T(8,128)(2,1)S(1)}, u32[]{:S(2)}, u32[]{:S(2)}) collective-permute-start(bf16[256,256]{1,0:T(8,128)(2,1)S(1)} %get-tuple-element.89), channel_id=1, source_target_pairs={{0,1},{1,0},{2,3},{3,2},{4,8},{5,9},{6,10},{7,11},{8,4},{9,5},{10,... | collective-permute-start | bytes 393224 | tf_op jit(solution)/shard_map/ppermute | solution.py:482
  91.7 14.4 %collective-permute-start.28 = (bf16[256,256]{1,0:T(8,128)(2,1)S(1)}, bf16[256,256]{1,0:T(8,128)(2,1)S(1)}, u32[]{:S(2)}, u32[]{:S(2)}) collective-permute-start(bf16[256,256]{1,0:T(8,128)(2,1)S(1)} %shard_map.107.refs_1_), channel_id=1, source_target_pairs={{0,4},{4,0},{8,12},{12,8},{1,5},{5,1},{9,13},{13,9},{2,6},{6,2},{1... | collective-permute-start | bytes 393224 | tf_op jit(solution)/shard_map/ppermute | solution.py:468
  101.6 7.0 %collective-permute-start.27 = (bf16[256,256]{1,0:T(8,128)(2,1)S(1)}, bf16[256,256]{1,0:T(8,128)(2,1)S(1)}, u32[]{:S(2)}, u32[]{:S(2)}) collective-permute-start(bf16[256,256]{1,0:T(8,128)(2,1)S(1)} %shard_map.105.refs_3_), channel_id=1, source_target_pairs={{0,4},{4,0},{8,12},{12,8},{1,5},{5,1},{9,13},{13,9},{2,6},{6,2},{1... | collective-permute-start | bytes 393224 | tf_op jit(solution)/shard_map/ppermute | solution.py:468
  101.7 4.4 %collective-permute-start.26 = (bf16[256,256]{1,0:T(8,128)(2,1)S(1)}, bf16[256,256]{1,0:T(8,128)(2,1)S(1)}, u32[]{:S(2)}, u32[]{:S(2)}) collective-permute-start(bf16[256,256]{1,0:T(8,128)(2,1)S(1)} %get-tuple-element.87), channel_id=1, source_target_pairs={{0,1},{1,0},{2,3},{3,2},{4,8},{5,9},{6,10},{7,11},{8,4},{9,5},{10,... | collective-permute-start | bytes 393224 | tf_op jit(solution)/shard_map/ppermute | solution.py:482
  101.8 10.9 %collective-permute-start.29 = (bf16[272,256]{1,0:T(8,128)(2,1)S(1)}, bf16[272,256]{1,0:T(8,128)(2,1)S(1)}, u32[]{:S(2)}, u32[]{:S(2)}) collective-permute-start(bf16[272,256]{1,0:T(8,128)(2,1)S(1)} %get-tuple-element.88), channel_id=1, source_target_pairs={{0,4},{4,0},{8,12},{12,8},{1,5},{5,1},{9,13},{13,9},{2,6},{6,2},{1... | collective-permute-start | bytes 417800 | tf_op jit(solution)/shard_map/ppermute | solution.py:468
  104.3 8.3 %collective-permute-start.31 = (bf16[256,256]{1,0:T(8,128)(2,1)S(1)}, bf16[256,256]{1,0:T(8,128)(2,1)S(1)}, u32[]{:S(2)}, u32[]{:S(2)}) collective-permute-start(bf16[256,256]{1,0:T(8,128)(2,1)S(1)} %shard_map.110), channel_id=1, source_target_pairs={{0,4},{4,0},{8,12},{12,8},{1,5},{5,1},{9,13},{13,9},{2,6},{6,2},{1... | collective-permute-start | bytes 393224 | tf_op jit(solution)/shard_map/ppermute | solution.py:468

commit v7 on v6

--- a/solution.py
+++ b/solution.py
@@ -60,7 +60,8 @@
     return jnp.where(inside, block.astype(jnp.float32), 0.0).astype(block.dtype)
 
 
-def mask_left_kernel(left_dest, left_sizes, left, out, near):
+def mask_left_kernel(left_dest, left_sizes, left, out, near, token):
+    token[...] = jnp.zeros_like(token)
     row, col = lax.axis_index("row"), lax.axis_index("col")
     terms, half = out.shape[0], near.shape[0]
     for term in range(terms):
@@ -74,14 +75,16 @@
     return pl.pallas_call(
         mask_left_kernel,
         in_specs=[SMEM, SMEM, VMEM],
-        out_specs=[VMEM, VMEM],
-        out_shape=[jax.ShapeDtypeStruct((count, tile, tile), left.dtype) for count in (terms, terms // 2)],
+        out_specs=[VMEM] * 3,
+        out_shape=[jax.ShapeDtypeStruct((count, tile, tile), left.dtype) for count in (terms, terms // 2)] + [TOKEN],
         compiler_params=pltpu.CompilerParams(vmem_limit_bytes=MASK_LIMIT),
         cost_estimate=BRIEF,
     )(left_dest, left_sizes, left)
 
 
 def mask_right_kernel(right_src, right_sizes, right, *outs):
+    *outs, token = outs
+    token[...] = jnp.zeros_like(token)
     col = lax.axis_index("col")
     for step in range(right.shape[0]):
         term = pl.program_id(0) * right.shape[0] + step
@@ -96,8 +99,9 @@
         mask_right_kernel,
         grid=(terms // 2,),
         in_specs=[SMEM, SMEM, pl.BlockSpec((2, local, tile, tile), lambda step: (step, 0, 0, 0))],
-        out_specs=[pl.BlockSpec((2, tile, tile), lambda step: (step, 0, 0))] * local,
-        out_shape=[jax.ShapeDtypeStruct((terms, tile, tile), right.dtype)] * local,
+        out_specs=[pl.BlockSpec((2, tile, tile), lambda step: (step, 0, 0))] * local
+        + [pl.BlockSpec(TOKEN.shape, lambda step: (0, 0, 0))],
+        out_shape=[jax.ShapeDtypeStruct((terms, tile, tile), right.dtype)] * local + [TOKEN],
         compiler_params=pltpu.CompilerParams(vmem_limit_bytes=MASK_LIMIT),
         cost_estimate=BRIEF,
     )(right_src, right_sizes, right)
@@ -346,7 +350,7 @@
 
 def finish_kernel(entry_count, local, carrier, stats, *refs):
     parts, near_images, kept, arrived, near_again = (refs[at * local:(at + 1) * local] for at in range(5))
-    outs, (image_held, kept_held, more_held, out_held, code, sems, out_sems) = refs[5 * local:5 * local + 2], refs[-7:]
+    outs, (image_held, kept_held, more_held, out_held, code, sems, out_sems) = refs[-9:-7], refs[-7:]
     tile = image_held.shape[1]
     leading = leads(lax.axis_index("row")) == 1
 
@@ -407,13 +411,13 @@
         copy.wait()
 
 
-def finish(entry_count, carrier, stats, parts, near_images, again, near_again):
+def finish(entry_count, carrier, stats, parts, near_images, again, near_again, tokens):
     local, tile = len(parts), near_images[0].shape[0]
     out = jax.ShapeDtypeStruct((tile, local * tile), near_images[0].dtype)
     block = (local, tile, tile)
     return pl.pallas_call(
         functools.partial(finish_kernel, entry_count, local, carrier),
-        in_specs=[VMEM] + [ANY] * (5 * local),
+        in_specs=[VMEM] + [ANY] * (5 * local + len(tokens)),
         out_specs=[ANY, ANY],
         out_shape=[out, out],
         scratch_shapes=[
@@ -427,18 +431,37 @@
         ],
         compiler_params=pltpu.CompilerParams(vmem_limit_bytes=VMEM_LIMIT),
         cost_estimate=BRIEF,
-    )(stats, *parts, *near_images, *(kept for kept, _ in again), *(arrived[0] for _, arrived in again), *near_again)
+    )(stats, *parts, *near_images, *(kept for kept, _ in again), *(arrived[0] for _, arrived in again), *near_again, *tokens)
+
+
+def after_kernel(value, *refs):
+    refs[-1][...] = value[...]
 
 
 def after(value, *others):
     return pl.pallas_call(
-        lambda *refs: None,
-        in_specs=[ANY] * (1 + len(others)),
-        out_specs=ANY,
+        after_kernel,
+        in_specs=[VMEM] + [ANY] * len(others),
+        out_specs=VMEM,
         out_shape=jax.ShapeDtypeStruct(value.shape, value.dtype),
-        input_output_aliases={0: 0},
+        compiler_params=pltpu.CompilerParams(vmem_limit_bytes=VMEM_LIMIT),
         cost_estimate=BRIEF,
     )(value, *others)
+
+
+def arrive_kernel(*refs):
+    refs[-1][...] = jnp.zeros_like(refs[-1])
+
+
+def arrive(cost, *values):
+    return pl.pallas_call(
+        arrive_kernel,
+        in_specs=[ANY] * len(values),
+        out_specs=VMEM,
+        out_shape=TOKEN,
+        compiler_params=pltpu.CompilerParams(vmem_limit_bytes=VMEM_LIMIT),
+        cost_estimate=pl.CostEstimate(flops=cost, bytes_accessed=0, transcendentals=0),
+    )(*values)
 
 
 def on_device(wavefunction, left_ops, right_ops, left_dest, right_src, left_sizes, right_sizes):
@@ -468,11 +491,11 @@
         return lax.ppermute(part, "row", swap("row", 1))
 
     near = to_partner(wavefunction)
-    left_own, left_near = mask_left(left_dest, left_sizes, left_ops)
+    left_own, left_near, left_token = mask_left(left_dest, left_sizes, left_ops)
     left_near = to_partner(left_near)
     left = [left_own, left_near, other_core(left_near)]
-    right = mask_right(right_src, right_sizes, right_ops)
-    near = after(near, left_own, right[0])
+    *right, right_token = mask_right(right_src, right_sizes, right_ops)
+    near = after(near, left_token, right_token)
 
     def exchange(sums):
         kept, sums = sums[0], sums[1:]
@@ -495,6 +518,8 @@
     def multiply(blocks, slots, first, tokens, coded=()):
         return products(blocks, left, right, right_src, left_dest, slots, first, tokens, coded)
 
+    left_there = arrive(2 * 10**9, left[2])
+
     pieces = [((block_of(at, 0), 0), piece) for at, piece in enumerate(far(wavefunction))]
     near_pieces = [((block_of(at, 0), 1), piece) for at, piece in enumerate(far(near))]
     blocks = None
@@ -506,7 +531,7 @@
     once, parts, near_images, stats, token = [], [], [], None, None
     for first in range(local + 1):
         if first < local:
-            *sums, token = multiply(blocks, joined, first, ([token] if first else []) + ([stats] if parts else []))
+            *sums, token = multiply(blocks, joined, first, ([token] if first else [left_there]) + ([stats] if parts else []))
             once.append(exchange(sums))
         for done in range(len(parts), first if first < local else local):
             kept, (arrived,) = once[done]
@@ -526,7 +551,7 @@
                 [parts[-1][0], *near_images[:-2]],
             )
         else:
-            held = join(parts[-1], [blocks, *near_images[-2:]])
+            held = join(parts[-1], [blocks, near_images[-2]])
         arrived_held = other_core(held)
         blocks = place(blocks, blocks_shape, [
             ((block_of(at, odd) + group[0], 0), half[at * len(group):(at + 1) * len(group)])
@@ -535,7 +560,7 @@
         ])
 
     carrier = local - 2 if pair_bits == 1 else local
-    again, near_again, token, stats = [], [], None, None
+    again, near_again, sent, token, stats = [], [], [], None, None
     for first in range(local + 1):
         if first < local:
             slots = apart if first == local - 1 else joined
@@ -546,19 +571,19 @@
             again.append(exchange(sums))
         for done in range(len(near_again), first if first < local else local):
             kept, arrived = again[done]
-            tokens = [token]
+            tokens = [token] + (sent[done - 2:done - 1] if done > 1 else []) + (near_images[-1:] if done == 1 else [])
             if done == carrier:
                 near, stats = emit(kept, arrived[-1], tokens, stats)
             else:
                 (near,) = emit(kept, arrived[-1], tokens)
             near_again.append(near)
-    near_again = [to_partner(part) for part in near_again]
+            sent.append(to_partner(near))
     if carrier == local:
         stats = settle(held, arrived_held, [token])
         for bit in range(pair_bits):
             stats = stats + lax.ppermute(stats, both, leader_swap(1 << bit))
         stats = jnp.where(leading, stats, to_partner(stats))
-    return tuple(finish(entry_count, carrier, stats, [part[0] for part in parts], near_images, again, near_again))
+    return tuple(finish(entry_count, carrier, stats, [part[0] for part in parts], near_images, again, sent, [arrive(2 * 10**9, *sent[:-1])]))
 
 
 def solution(mesh):

time: 116 us -> 113 us (0.974)
  waiting for transfers between devices: 29.8 us -> 26.6 us
  starting transfers between devices: 40.2 us -> 41.6 us
    ppermute x6, waiting for transfers between devices: 9.51 us -> 4.71 us  [far(): lax.ppermute(piece, 'col', swap('col', 1 << bit))]
    unnamed x23 -> x25, local copies, waits for them, and re-layouts: 2.54 us -> 2.22 us
  transfers between devices with their start and end apart: 32 -> 32, of which waited for: 12 -> 11; matrix products, arithmetic and copies ran while one was open for 1% -> 1% of each run, Pallas kernels for 28% -> 28%
where the time goes in v7:
time: 113 us; the launch traced here: 112 us
  starting transfers between devices  41.6 us (37%)
  Pallas kernels  40.6 us (36%)
  waiting for transfers between devices  26.6 us (24%)
  local copies, waits for them, and re-layouts  2.5 us (2%)
  between operations  1.18 us (1%)
    ppermute x10, starting transfers between devices, to_partner(): return lax.ppermute(part, 'row', swap('row', 1))  30.6 us
    pallas_call x8, Pallas kernels, products(): pl.pallas_call(functools.partial(product_kernel, first, local, out_slots,...  24.3 us
    ppermute x10, waiting for transfers between devices, to_partner(): return lax.ppermute(part, 'row', swap('row', 1))  18.6 us
    ppermute x6, starting transfers between devices, far(): lax.ppermute(piece, 'col', swap('col', 1 << bit))  8.39 us
    pallas_call x1, Pallas kernels, mask_right(): pl.pallas_call(mask_right_kernel, grid=(terms // 2,), in_specs=[SMEM, SME...  4.95 us
    ppermute x6, waiting for transfers between devices, far(): lax.ppermute(piece, 'col', swap('col', 1 << bit))  4.71 us
    pallas_call x4, Pallas kernels, combine(): pl.pallas_call(functools.partial(combine_kernel, first, local), in_specs=...  4.01 us
    ppermute x7, waiting for transfers between devices, other_core(): return lax.ppermute(part, 'col', swap('col', 1))  3.33 us
  transfers between devices with their start and end apart: 32, of which 11 were waited for; matrix products, arithmetic and copies ran while one was open for 1% of the time, Pallas kernels for 28%

profile of v7, /device:TPU:0, one launch (start us, length us, event | category | flops | bytes accessed | tf_op | source)
XLA Modules:
  0.0 112.5 jit_solution(13793107426344867012)
XLA Ops:
  0.6 3.1 %collective-permute-start = (bf16[256,1024]{1,0:T(8,128)(2,1)}, bf16[256,1024]{1,0:T(8,128)(2,1)S(1)}, u32[]{:S(2)}, u32[]{:S(2)}) collective-permute-start(bf16[256,1024]{1,0:T(8,128)(2,1)} %refs_0_.1), channel_id=1, source_target_pairs={{0,4},{4,0},{8,12},{12,8},{1,5},{5,1},{9,13},{13,9},{2,6},{6,2},{1... | collective-permute-start | bytes 1572872 | tf_op jit(solution)/shard_map/ppermute | solution.py:491
  3.7 1.5 %collective-permute-start.3 = (bf16[256,1024]{1,0:T(8,128)(2,1)}, bf16[256,1024]{1,0:T(8,128)(2,1)S(1)}, u32[]{:S(2)}, u32[]{:S(2)}) collective-permute-start(bf16[256,1024]{1,0:T(8,128)(2,1)} %refs_0_.1), channel_id=1, source_target_pairs={{0,2},{1,3},{2,0},{3,1},{4,6},{5,7},{6,4},{7,5},{8,10},{9,11},{10,... | collective-permute-start | bytes 1572872 | tf_op jit(solution)/shard_map/ppermute | solution.py:481
  5.2 1.3 %copy.18.left_dest.target = s32[8,4]{1,0:T(8,128)} copy(s32[8,4]{0,1:T(4,128)} %param.10) | data formatting | bytes 256 | tf_op args[3]
  6.6 2.8 %shard_map.86 = (bf16[8,256,256]{2,1,0:T(8,128)(2,1)}, bf16[4,256,256]{2,1,0:T(8,128)(2,1)}, f32[2,8,128]{2,1,0:T(8,128)}) custom-call(s32[8,4]{1,0:T(8,128)} %copy.18.left_dest.target, s32[4]{0:T(128)} %left_sizes.9, bf16[8,1,256,256]{3,2,1,0:T(8,128)(2,1)} %left.1), custom_call_target="tpu_custom_call" | custom-call | flops 1000000000 | tf_op jit(solution)/shard_map/pallas_call | solution.py:75
  9.4 0.4 collective-permute-start.7
  9.8 4.9 %shard_map.87 = (bf16[8,256,256]{2,1,0:T(8,128)(2,1)}, bf16[8,256,256]{2,1,0:T(8,128)(2,1)}, bf16[8,256,256]{2,1,0:T(8,128)(2,1)}, bf16[8,256,256]{2,1,0:T(8,128)(2,1)}, f32[2,8,128]{2,1,0:T(8,128)}) custom-call(s32[8,16]{1,0:T(8,128)} %source.15, s32[16]{0:T(128)} %right_sizes.9, bf16[8,4,256,256]{3,2,1,0:T(8,128)(2,1)} %right.1), custom_call_target="tpu_custom_call" | custom-call | flops 1000000000 | tf_op jit(solution)/shard_map/pallas_call | solution.py:98
  14.7 1.9 %collective-permute-done.value = bf16[256,1024]{1,0:T(8,128)(2,1)S(1)} collective-permute-done((bf16[256,1024]{1,0:T(8,128)(2,1)}, bf16[256,1024]{1,0:T(8,128)(2,1)S(1)}, u32[]{:S(2)}, u32[]{:S(2)}) %collective-permute-start) | collective-permute-done | bytes 524320 | tf_op jit(solution)/shard_map/ppermute | solution.py:491
  16.7 0.7 copy-done.10
  17.4 2.0 %collective-permute-start.1 = (bf16[256,1024]{1,0:T(8,128)(2,1)S(1)}, bf16[256,1024]{1,0:T(8,128)(2,1)S(1)}, u32[]{:S(2)}, u32[]{:S(2)}) collective-permute-start(bf16[256,1024]{1,0:T(8,128)(2,1)S(1)} %shard_map.88.refs_2_), channel_id=1, source_target_pairs={{0,2},{1,3},{2,0},{3,1},{4,6},{5,7},{6,4},{7,5},{8,10},{9,11},{10,... | collective-permute-start | bytes 1572872 | tf_op jit(solution)/shard_map/ppermute | solution.py:481
  19.5 0.5 collective-permute-start.5
  20.0 7.0 %collective-permute-done.7.left_near = bf16[4,256,256]{2,1,0:T(8,128)(2,1)S(1)} collective-permute-done((bf16[4,256,256]{2,1,0:T(8,128)(2,1)}, bf16[4,256,256]{2,1,0:T(8,128)(2,1)S(1)}, u32[]{:S(2)}, u32[]{:S(2)}) %collective-permute-start.7) | collective-permute-done | bytes 524320 | tf_op jit(solution)/shard_map/ppermute | solution.py:491
  27.1 2.7 %collective-permute-done.1.refs_0_ = bf16[256,1024]{1,0:T(8,128)(2,1)S(1)} collective-permute-done((bf16[256,1024]{1,0:T(8,128)(2,1)S(1)}, bf16[256,1024]{1,0:T(8,128)(2,1)S(1)}, u32[]{:S(2)}, u32[]{:S(2)}) %collective-permute-start.1) | collective-permute-done | bytes 524320 | tf_op jit(solution)/shard_map/ppermute | solution.py:481
  29.8 0.7 shard_map.89.refs_2_
  30.6 1.1 collective-permute-done.2.refs_1_
  32.1 3.0 %shard_map.92 = (f32[512,256]{1,0:T(8,128)S(1)}, bf16[512,256]{1,0:T(8,128)(2,1)S(1)}, f32[2,8,128]{2,1,0:T(8,128)S(1)}) custom-call(s32[8,16]{1,0:T(8,128)S(1)} %copy-done.6, s32[8,4]{1,0:T(8,128)S(1)} %copy-done.7, bf16[16,512,256]{2,1,0:T(8,128)(2,1)S(1)} %shard_map.90.blocks, bf16[8,256,256]{2,1,0:T(8,128)(2,1)S(1)} %copy-done, ...), custom_call_target="tpu_custom_call" | custom-call | flops 1000000000 | tf_op jit(solution)/shard_map/pallas_call | solution.py:249
  35.1 0.6 collective-permute-start.9
  35.7 3.0 %shard_map.93 = (f32[512,256]{1,0:T(8,128)S(1)}, bf16[512,256]{1,0:T(8,128)(2,1)S(1)}, f32[2,8,128]{2,1,0:T(8,128)S(1)}) custom-call(s32[8,16]{1,0:T(8,128)S(1)} %copy-done.6, s32[8,4]{1,0:T(8,128)S(1)} %copy-done.7, bf16[16,512,256]{2,1,0:T(8,128)(2,1)S(1)} %shard_map.90.blocks, bf16[8,256,256]{2,1,0:T(8,128)(2,1)S(1)} %copy-done, ...), custom_call_target="tpu_custom_call" | custom-call | flops 1000000000 | tf_op jit(solution)/shard_map/pallas_call | solution.py:249
  38.8 0.8 shard_map.94
  39.7 1.4 %collective-permute-start.13 = (bf16[512,256]{1,0:T(8,128)(2,1)S(1)}, bf16[512,256]{1,0:T(8,128)(2,1)S(1)}, u32[]{:S(2)}, u32[]{:S(2)}) collective-permute-start(bf16[512,256]{1,0:T(8,128)(2,1)S(1)} %get-tuple-element.70.refs_0_), channel_id=1, source_target_pairs={{0,2},{1,3},{2,0},{3,1},{4,6},{5,7},{6,4},{7,5},{8,10},{9,11},{10,... | collective-permute-start | bytes 786440 | tf_op jit(solution)/shard_map/ppermute | solution.py:481
  41.1 3.0 %shard_map.95 = (f32[512,256]{1,0:T(8,128)S(1)}, bf16[512,256]{1,0:T(8,128)(2,1)S(1)}, f32[2,8,128]{2,1,0:T(8,128)S(1)}) custom-call(s32[8,16]{1,0:T(8,128)S(1)} %copy-done.6, s32[8,4]{1,0:T(8,128)S(1)} %copy-done.7, bf16[16,512,256]{2,1,0:T(8,128)(2,1)S(1)} %shard_map.90.blocks, bf16[8,256,256]{2,1,0:T(8,128)(2,1)S(1)} %copy-done, ...), custom_call_target="tpu_custom_call" | custom-call | flops 1000000000 | tf_op jit(solution)/shard_map/pallas_call | solution.py:249
  44.1 0.3 collective-permute-start.12
  44.4 0.8 shard_map.96
  45.2 0.8 collective-permute-start.15
  45.9 3.0 %shard_map.97 = (f32[512,256]{1,0:T(8,128)S(1)}, bf16[512,256]{1,0:T(8,128)(2,1)S(1)}, f32[2,8,128]{2,1,0:T(8,128)S(1)}) custom-call(s32[8,16]{1,0:T(8,128)S(1)} %copy-done.6, s32[8,4]{1,0:T(8,128)S(1)} %copy-done.7, bf16[16,512,256]{2,1,0:T(8,128)(2,1)S(1)} %shard_map.90.blocks, bf16[8,256,256]{2,1,0:T(8,128)(2,1)S(1)} %copy-done, ...), custom_call_target="tpu_custom_call" | custom-call | flops 1000000000 | tf_op jit(solution)/shard_map/pallas_call | solution.py:249
  49.1 1.0 shard_map.98
  50.1 1.4 %collective-permute-start.16 = (bf16[512,256]{1,0:T(8,128)(2,1)S(1)}, bf16[512,256]{1,0:T(8,128)(2,1)S(1)}, u32[]{:S(2)}, u32[]{:S(2)}) collective-permute-start(bf16[512,256]{1,0:T(8,128)(2,1)S(1)} %get-tuple-element.74.refs_2_), channel_id=1, source_target_pairs={{0,2},{1,3},{2,0},{3,1},{4,6},{5,7},{6,4},{7,5},{8,10},{9,11},{10,... | collective-permute-start | bytes 786440 | tf_op jit(solution)/shard_map/ppermute | solution.py:481
  51.5 8.8 %collective-permute-start.17 = (bf16[256,256]{1,0:T(8,128)(2,1)S(1)}, bf16[256,256]{1,0:T(8,128)(2,1)S(1)}, u32[]{:S(2)}, u32[]{:S(2)}) collective-permute-start(bf16[256,256]{1,0:T(8,128)(2,1)S(1)} %get-tuple-element.75), channel_id=1, source_target_pairs={{0,4},{4,0},{8,12},{12,8},{1,5},{5,1},{9,13},{13,9},{2,6},{6,2},{1... | collective-permute-start | bytes 393224 | tf_op jit(solution)/shard_map/ppermute | solution.py:491
  60.3 1.4 %shard_map.99 = (bf16[528,256]{1,0:T(8,128)(2,1)S(1)}, bf16[256,256]{1,0:T(8,128)(2,1)S(1)}, f32[2,8,256]{2,1,0:T(8,128)}) custom-call(s32[4]{0:T(128)S(1)} %copy-done.9, s32[16]{0:T(128)S(1)} %copy-done.8, f32[512,256]{1,0:T(8,128)S(1)} %get-tuple-element.65.kept, bf16[512,256]{1,0:T(8,128)(2,1)S(1)} %collective-permute-done.11.arrived, ...), custom_call_target="tpu_custom_call" | custom-call | flops 1000000000 | tf_op jit(solution)/shard_map/pallas_call | solution.py:314
  61.7 1.9 %collective-permute-done.17.refs_7_.refs_4_ = bf16[256,256]{1,0:T(8,128)(2,1)S(1)} collective-permute-done((bf16[256,256]{1,0:T(8,128)(2,1)S(1)}, bf16[256,256]{1,0:T(8,128)(2,1)S(1)}, u32[]{:S(2)}, u32[]{:S(2)}) %collective-permute-start.17) | collective-permute-done | bytes 131104 | tf_op jit(solution)/shard_map/ppermute | solution.py:491
  63.6 1.7 %collective-permute-done.18.refs_8_.refs_5_ = bf16[256,256]{1,0:T(8,128)(2,1)S(1)} collective-permute-done((bf16[256,256]{1,0:T(8,128)(2,1)S(1)}, bf16[256,256]{1,0:T(8,128)(2,1)S(1)}, u32[]{:S(2)}, u32[]{:S(2)}) %collective-permute-start.18) | collective-permute-done | bytes 131104 | tf_op jit(solution)/shard_map/ppermute | solution.py:491
  65.5 1.3 %collective-permute-start.14 = (bf16[528,256]{1,0:T(8,128)(2,1)S(1)}, bf16[528,256]{1,0:T(8,128)(2,1)S(1)}, u32[]{:S(2)}, u32[]{:S(2)}) collective-permute-start(bf16[528,256]{1,0:T(8,128)(2,1)S(1)} %get-tuple-element.72.refs_6_.refs_0_.refs_3_), channel_id=1, source_target_pairs={{0,2},{1,3},{2,0},{3,1},{4,6},{5,7},{6,4},{7,5},{8,10},{9,11},{10,... | collective-permute-start | bytes 811016 | tf_op jit(solution)/shard_map/ppermute | solution.py:481
  66.9 1.7 %collective-permute-start.20 = (bf16[256,256]{1,0:T(8,128)(2,1)S(1)}, bf16[256,256]{1,0:T(8,128)(2,1)S(1)}, u32[]{:S(2)}, u32[]{:S(2)}) collective-permute-start(bf16[256,256]{1,0:T(8,128)(2,1)S(1)} %get-tuple-element.77), channel_id=1, source_target_pairs={{0,4},{4,0},{8,12},{12,8},{1,5},{5,1},{9,13},{13,9},{2,6},{6,2},{1... | collective-permute-start | bytes 393224 | tf_op jit(solution)/shard_map/ppermute | solution.py:491
  68.6 0.3 collective-permute-done.19
  69.3 3.1 %collective-permute-done.20.refs_3_.refs_6_ = bf16[256,256]{1,0:T(8,128)(2,1)S(1)} collective-permute-done((bf16[256,256]{1,0:T(8,128)(2,1)S(1)}, bf16[256,256]{1,0:T(8,128)(2,1)S(1)}, u32[]{:S(2)}, u32[]{:S(2)}) %collective-permute-start.20) | collective-permute-done | bytes 131104 | tf_op jit(solution)/shard_map/ppermute | solution.py:491
  72.4 2.0 %collective-permute-done.14.refs_1_ = bf16[528,256]{1,0:T(8,128)(2,1)S(1)} collective-permute-done((bf16[528,256]{1,0:T(8,128)(2,1)S(1)}, bf16[528,256]{1,0:T(8,128)(2,1)S(1)}, u32[]{:S(2)}, u32[]{:S(2)}) %collective-permute-start.14) | collective-permute-done | bytes 270368 | tf_op jit(solution)/shard_map/ppermute | solution.py:481
  74.7 1.9 %collective-permute-done.21.refs_1_ = bf16[2,528,256]{2,1,0:T(8,128)(2,1)S(1)} collective-permute-done((bf16[2,528,256]{2,1,0:T(8,128)(2,1)S(1)}, bf16[2,528,256]{2,1,0:T(8,128)(2,1)S(1)}, u32[]{:S(2)}, u32[]{:S(2)}) %collective-permute-start.21) | collective-permute-done | bytes 540704 | tf_op jit(solution)/shard_map/ppermute | solution.py:485
  76.7 3.0 %shard_map.104 = (f32[512,256]{1,0:T(8,128)S(1)}, bf16[512,256]{1,0:T(8,128)(2,1)S(1)}, f32[2,8,128]{2,1,0:T(8,128)S(1)}) custom-call(s32[8,16]{1,0:T(8,128)S(1)} %copy-done.6, s32[8,4]{1,0:T(8,128)S(1)} %copy-done.7, bf16[16,512,256]{2,1,0:T(8,128)(2,1)S(1)} %shard_map.103.blocks, bf16[8,256,256]{2,1,0:T(8,128)(2,1)S(1)} %copy-done, ...), custom_call_target="tpu_custom_call" | custom-call | flops 1000000000 | tf_op jit(solution)/shard_map/pallas_call | solution.py:249
  79.9 2.8 %collective-permute-start.25 = (bf16[256,256]{1,0:T(8,128)(2,1)S(1)}, bf16[256,256]{1,0:T(8,128)(2,1)S(1)}, u32[]{:S(2)}, u32[]{:S(2)}) collective-permute-start(bf16[256,256]{1,0:T(8,128)(2,1)S(1)} %get-tuple-element.87), channel_id=1, source_target_pairs={{0,4},{4,0},{8,12},{12,8},{1,5},{5,1},{9,13},{13,9},{2,6},{6,2},{1... | collective-permute-start | bytes 393224 | tf_op jit(solution)/shard_map/ppermute | solution.py:491
  82.8 3.0 %shard_map.105 = (f32[512,256]{1,0:T(8,128)S(1)}, bf16[512,256]{1,0:T(8,128)(2,1)S(1)}, f32[2,8,128]{2,1,0:T(8,128)S(1)}) custom-call(s32[8,16]{1,0:T(8,128)S(1)} %copy-done.6, s32[8,4]{1,0:T(8,128)S(1)} %copy-done.7, bf16[16,512,256]{2,1,0:T(8,128)(2,1)S(1)} %shard_map.103.blocks, bf16[8,256,256]{2,1,0:T(8,128)(2,1)S(1)} %copy-done, ...), custom_call_target="tpu_custom_call" | custom-call | flops 1000000000 | tf_op jit(solution)/shard_map/pallas_call | solution.py:249
  85.9 3.2 %shard_map.107 = (f32[512,256]{1,0:T(8,128)S(1)}, bf16[528,256]{1,0:T(8,128)(2,1)S(1)}, f32[2,8,128]{2,1,0:T(8,128)S(1)}) custom-call(s32[8,16]{1,0:T(8,128)S(1)} %copy-done.6, s32[8,4]{1,0:T(8,128)S(1)} %copy-done.7, bf16[16,512,256]{2,1,0:T(8,128)(2,1)S(1)} %shard_map.103.blocks, bf16[8,256,256]{2,1,0:T(8,128)(2,1)S(1)} %copy-done, ...), custom_call_target="tpu_custom_call" | custom-call | flops 1000000000 | tf_op jit(solution)/shard_map/pallas_call | solution.py:249
  89.1 0.6 collective-permute-start.23
  89.7 5.5 %collective-permute-start.26 = (bf16[256,256]{1,0:T(8,128)(2,1)S(1)}, bf16[256,256]{1,0:T(8,128)(2,1)S(1)}, u32[]{:S(2)}, u32[]{:S(2)}) collective-permute-start(bf16[256,256]{1,0:T(8,128)(2,1)S(1)} %shard_map.106.refs_3_), channel_id=1, source_target_pairs={{0,4},{4,0},{8,12},{12,8},{1,5},{5,1},{9,13},{13,9},{2,6},{6,2},{1... | collective-permute-start | bytes 393224 | tf_op jit(solution)/shard_map/ppermute | solution.py:491
  95.3 0.4 collective-permute-start.28
  95.6 3.0 %shard_map.109 = (f32[512,256]{1,0:T(8,128)S(1)}, bf16[256,256]{1,0:T(8,128)(2,1)S(1)}, bf16[256,256]{1,0:T(8,128)(2,1)S(1)}, f32[2,8,128]{2,1,0:T(8,128)S(1)}) custom-call(s32[8,16]{1,0:T(8,128)S(1)} %copy-done.6, s32[8,4]{1,0:T(8,128)S(1)} %copy-done.7, bf16[16,512,256]{2,1,0:T(8,128)(2,1)S(1)} %shard_map.103.blocks, bf16[8,256,256]{2,1,0:T(8,128)(2,1)S(1)} %copy-done, ...), custom_call_target="tpu_custom_call" | custom-call | flops 1000000000 | tf_op jit(solution)/shard_map/pallas_call | solution.py:249
  98.8 2.4 %collective-permute-start.29 = (bf16[272,256]{1,0:T(8,128)(2,1)S(1)}, bf16[272,256]{1,0:T(8,128)(2,1)S(1)}, u32[]{:S(2)}, u32[]{:S(2)}) collective-permute-start(bf16[272,256]{1,0:T(8,128)(2,1)S(1)} %get-tuple-element.92), channel_id=1, source_target_pairs={{0,4},{4,0},{8,12},{12,8},{1,5},{5,1},{9,13},{13,9},{2,6},{6,2},{1... | collective-permute-start | bytes 417800 | tf_op jit(solution)/shard_map/ppermute | solution.py:491
  101.3 5.3 %collective-permute-start.31 = (bf16[256,256]{1,0:T(8,128)(2,1)S(1)}, bf16[256,256]{1,0:T(8,128)(2,1)S(1)}, u32[]{:S(2)}, u32[]{:S(2)}) collective-permute-start(bf16[256,256]{1,0:T(8,128)(2,1)S(1)} %shard_map.111), channel_id=1, source_target_pairs={{0,4},{4,0},{8,12},{12,8},{1,5},{5,1},{9,13},{13,9},{2,6},{6,2},{1... | collective-permute-start | bytes 393224 | tf_op jit(solution)/shard_map/ppermute | solution.py:491
  106.6 2.9 %collective-permute-done.31.refs_19_ = bf16[256,256]{1,0:T(8,128)(2,1)S(1)} collective-permute-done((bf16[256,256]{1,0:T(8,128)(2,1)S(1)}, bf16[256,256]{1,0:T(8,128)(2,1)S(1)}, u32[]{:S(2)}, u32[]{:S(2)}) %collective-permute-start.31) | collective-permute-done | bytes 131104 | tf_op jit(solution)/shard_map/ppermute | solution.py:491
  109.6 2.7 %shard_map.113 = (bf16[256,1024]{1,0:T(8,128)(2,1)}, bf16[256,1024]{1,0:T(8,128)(2,1)}) custom-call(f32[2,8,128]{2,1,0:T(8,128)S(1)} %get-tuple-element.89.stats, bf16[512,256]{1,0:T(8,128)(2,1)S(1)} %get-tuple-element.70.refs_0_, bf16[512,256]{1,0:T(8,128)(2,1)S(1)} %get-tuple-element.73.refs_1_, bf16[512,256]{1,0:T(8,128)(2,1)S(1)} %get-tuple-element.74.refs_2_, ...), custom_call_target="tpu_custom_call" | custom-call | flops 1000000000 | tf_op jit(solution)/shard_map/pallas_call | solution.py:418
  (73 shorter events, 2.4 us)
Async XLA Ops:
  0.6 16.1 %collective-permute-start = (bf16[256,1024]{1,0:T(8,128)(2,1)}, bf16[256,1024]{1,0:T(8,128)(2,1)S(1)}, u32[]{:S(2)}, u32[]{:S(2)}) collective-permute-start(bf16[256,1024]{1,0:T(8,128)(2,1)} %refs_0_.1), channel_id=1, source_target_pairs={{0,4},{4,0},{8,12},{12,8},{1,5},{5,1},{9,13},{13,9},{2,6},{6,2},{1... | collective-permute-start | bytes 1572872 | tf_op jit(solution)/shard_map/ppermute | solution.py:491
  3.7 15.7 %collective-permute-start.3 = (bf16[256,1024]{1,0:T(8,128)(2,1)}, bf16[256,1024]{1,0:T(8,128)(2,1)S(1)}, u32[]{:S(2)}, u32[]{:S(2)}) collective-permute-start(bf16[256,1024]{1,0:T(8,128)(2,1)} %refs_0_.1), channel_id=1, source_target_pairs={{0,2},{1,3},{2,0},{3,1},{4,6},{5,7},{6,4},{7,5},{8,10},{9,11},{10,... | collective-permute-start | bytes 1572872 | tf_op jit(solution)/shard_map/ppermute | solution.py:481
  9.3 7.3 %copy-start.11 = (f32[2,8,128]{2,1,0:T(8,128)S(1)}, f32[2,8,128]{2,1,0:T(8,128)}, u32[]{:S(2)}) copy-start(f32[2,8,128]{2,1,0:T(8,128)} %get-tuple-element.48.refs_0_) | copy-start | bytes 24580
  9.3 10.1 %copy-start.5 = (bf16[256,1024]{1,0:T(8,128)(2,1)S(1)}, bf16[256,1024]{1,0:T(8,128)(2,1)}, u32[]{:S(2)}) copy-start(bf16[256,1024]{1,0:T(8,128)(2,1)} %refs_0_.1) | copy-start | bytes 1572868
  9.4 17.7 %collective-permute-start.7 = (bf16[4,256,256]{2,1,0:T(8,128)(2,1)}, bf16[4,256,256]{2,1,0:T(8,128)(2,1)S(1)}, u32[]{:S(2)}, u32[]{:S(2)}) collective-permute-start(bf16[4,256,256]{2,1,0:T(8,128)(2,1)} %get-tuple-element.51), channel_id=1, source_target_pairs={{0,4},{4,0},{8,12},{12,8},{1,5},{5,1},{9,13},{13,9},{2,6},{6,2},{1... | collective-permute-start | bytes 1572872 | tf_op jit(solution)/shard_map/ppermute | solution.py:491
  16.7 0.7 copy-start.10
  17.4 12.3 %collective-permute-start.1 = (bf16[256,1024]{1,0:T(8,128)(2,1)S(1)}, bf16[256,1024]{1,0:T(8,128)(2,1)S(1)}, u32[]{:S(2)}, u32[]{:S(2)}) collective-permute-start(bf16[256,1024]{1,0:T(8,128)(2,1)S(1)} %shard_map.88.refs_2_), channel_id=1, source_target_pairs={{0,2},{1,3},{2,0},{3,1},{4,6},{5,7},{6,4},{7,5},{8,10},{9,11},{10,... | collective-permute-start | bytes 1572872 | tf_op jit(solution)/shard_map/ppermute | solution.py:481
  19.5 10.3 %collective-permute-start.4 = (bf16[256,1024]{1,0:T(8,128)(2,1)S(1)}, bf16[256,1024]{1,0:T(8,128)(2,1)S(1)}, u32[]{:S(2)}, u32[]{:S(2)}) collective-permute-start(bf16[256,1024]{1,0:T(8,128)(2,1)S(1)} %copy-done.5), channel_id=1, source_target_pairs={{0,1},{1,0},{2,3},{3,2},{4,5},{5,4},{6,7},{7,6},{8,9},{9,8},{10,11... | collective-permute-start | bytes 1572872 | tf_op jit(solution)/shard_map/ppermute | solution.py:485
  19.5 10.3 %collective-permute-start.5 = (bf16[256,1024]{1,0:T(8,128)(2,1)S(1)}, bf16[256,1024]{1,0:T(8,128)(2,1)S(1)}, u32[]{:S(2)}, u32[]{:S(2)}) collective-permute-start(bf16[256,1024]{1,0:T(8,128)(2,1)S(1)} %collective-permute-done.3.refs_1_), channel_id=1, source_target_pairs={{0,1},{1,0},{2,3},{3,2},{4,5},{5,4},{6,7},{7,6},{8,9},{9,8},{10,11... | collective-permute-start | bytes 1572872 | tf_op jit(solution)/shard_map/ppermute | solution.py:485
  20.0 9.8 %collective-permute-start.6 = (bf16[256,1024]{1,0:T(8,128)(2,1)S(1)}, bf16[256,1024]{1,0:T(8,128)(2,1)S(1)}, u32[]{:S(2)}, u32[]{:S(2)}) collective-permute-start(bf16[256,1024]{1,0:T(8,128)(2,1)S(1)} %shard_map.88.refs_2_), channel_id=1, source_target_pairs={{0,1},{1,0},{2,3},{3,2},{4,5},{5,4},{6,7},{7,6},{8,9},{9,8},{10,11... | collective-permute-start | bytes 1572872 | tf_op jit(solution)/shard_map/ppermute | solution.py:485
  27.1 3.4 %collective-permute-start.8 = (bf16[4,256,256]{2,1,0:T(8,128)(2,1)S(1)}, bf16[4,256,256]{2,1,0:T(8,128)(2,1)S(1)}, u32[]{:S(2)}, u32[]{:S(2)}) collective-permute-start(bf16[4,256,256]{2,1,0:T(8,128)(2,1)S(1)} %collective-permute-done.7.left_near), channel_id=1, source_target_pairs={{0,1},{1,0},{2,3},{3,2},{4,5},{5,4},{6,7},{7,6},{8,9},{9,8},{10,11... | collective-permute-start | bytes 1572872 | tf_op jit(solution)/shard_map/ppermute | solution.py:485
  29.8 1.9 %collective-permute-start.2 = (bf16[256,1024]{1,0:T(8,128)(2,1)S(1)}, bf16[256,1024]{1,0:T(8,128)(2,1)S(1)}, u32[]{:S(2)}, u32[]{:S(2)}) collective-permute-start(bf16[256,1024]{1,0:T(8,128)(2,1)S(1)} %collective-permute-done.1.refs_0_), channel_id=1, source_target_pairs={{0,1},{1,0},{2,3},{3,2},{4,5},{5,4},{6,7},{7,6},{8,9},{9,8},{10,11... | collective-permute-start | bytes 1572872 | tf_op jit(solution)/shard_map/ppermute | solution.py:485
  30.5 1.4 %copy-start = (bf16[8,256,256]{2,1,0:T(8,128)(2,1)S(1)}, bf16[8,256,256]{2,1,0:T(8,128)(2,1)}, u32[]{:S(2)}) copy-start(bf16[8,256,256]{2,1,0:T(8,128)(2,1)} %get-tuple-element.50.left_own) | copy-start | bytes 3145732
  30.5 1.5 %copy-start.3 = (bf16[8,256,256]{2,1,0:T(8,128)(2,1)S(1)}, bf16[8,256,256]{2,1,0:T(8,128)(2,1)}, u32[]{:S(2)}) copy-start(bf16[8,256,256]{2,1,0:T(8,128)(2,1)} %get-tuple-element.55.right) | copy-start | bytes 3145732
  30.5 1.5 %copy-start.6 = (s32[8,16]{1,0:T(8,128)S(1)}, s32[8,16]{1,0:T(8,128)}, u32[]{:S(2)}) copy-start(s32[8,16]{1,0:T(8,128)} %source.15) | copy-start | bytes 1540
  30.6 1.5 %copy-start.7 = (s32[8,4]{1,0:T(8,128)S(1)}, s32[8,4]{1,0:T(8,128)}, u32[]{:S(2)}) copy-start(s32[8,4]{1,0:T(8,128)} %copy.18.left_dest.target) | copy-start | bytes 388
  31.9 3.8 %copy-start.2 = (bf16[8,256,256]{2,1,0:T(8,128)(2,1)S(1)}, bf16[8,256,256]{2,1,0:T(8,128)(2,1)}, u32[]{:S(2)}) copy-start(bf16[8,256,256]{2,1,0:T(8,128)(2,1)} %get-tuple-element.54.right) | copy-start | bytes 3145732
  35.1 3.7 %copy-start.8 = (s32[16]{0:T(128)S(1)}, s32[16]{0:T(128)}, u32[]{:S(2)}) copy-start(s32[16]{0:T(128)} %right_sizes.9) | copy-start | bytes 196
  35.1 3.7 %copy-start.9 = (s32[4]{0:T(128)S(1)}, s32[4]{0:T(128)}, u32[]{:S(2)}) copy-start(s32[4]{0:T(128)} %left_sizes.9) | copy-start | bytes 52
  35.1 3.7 %collective-permute-start.9 = (bf16[512,256]{1,0:T(8,128)(2,1)S(1)}, bf16[512,256]{1,0:T(8,128)(2,1)S(1)}, u32[]{:S(2)}, u32[]{:S(2)}) collective-permute-start(bf16[512,256]{1,0:T(8,128)(2,1)S(1)} %get-tuple-element.59), channel_id=1, source_target_pairs={{0,1},{1,0},{2,3},{3,2},{4,8},{5,9},{6,10},{7,11},{8,4},{9,5},{10,... | collective-permute-start | bytes 786440 | tf_op jit(solution)/shard_map/ppermute | solution.py:505
  38.7 2.3 %copy-start.4 = (bf16[8,256,256]{2,1,0:T(8,128)(2,1)S(1)}, bf16[8,256,256]{2,1,0:T(8,128)(2,1)}, u32[]{:S(2)}) copy-start(bf16[8,256,256]{2,1,0:T(8,128)(2,1)} %get-tuple-element.53.right) | copy-start | bytes 3145732
  38.7 5.6 %collective-permute-start.10 = (bf16[512,256]{1,0:T(8,128)(2,1)S(1)}, bf16[512,256]{1,0:T(8,128)(2,1)S(1)}, u32[]{:S(2)}, u32[]{:S(2)}) collective-permute-start(bf16[512,256]{1,0:T(8,128)(2,1)S(1)} %get-tuple-element.63), channel_id=1, source_target_pairs={{0,1},{1,0},{2,3},{3,2},{4,8},{5,9},{6,10},{7,11},{8,4},{9,5},{10,... | collective-permute-start | bytes 786440 | tf_op jit(solution)/shard_map/ppermute | solution.py:505
  39.7 9.4 %collective-permute-start.13 = (bf16[512,256]{1,0:T(8,128)(2,1)S(1)}, bf16[512,256]{1,0:T(8,128)(2,1)S(1)}, u32[]{:S(2)}, u32[]{:S(2)}) collective-permute-start(bf16[512,256]{1,0:T(8,128)(2,1)S(1)} %get-tuple-element.70.refs_0_), channel_id=1, source_target_pairs={{0,2},{1,3},{2,0},{3,1},{4,6},{5,7},{6,4},{7,5},{8,10},{9,11},{10,... | collective-permute-start | bytes 786440 | tf_op jit(solution)/shard_map/ppermute | solution.py:481
  44.1 1.9 %copy-start.1 = (bf16[8,256,256]{2,1,0:T(8,128)(2,1)S(1)}, bf16[8,256,256]{2,1,0:T(8,128)(2,1)}, u32[]{:S(2)}) copy-start(bf16[8,256,256]{2,1,0:T(8,128)(2,1)} %get-tuple-element.52.right) | copy-start | bytes 3145732
  44.1 5.0 %collective-permute-start.12 = (bf16[512,256]{1,0:T(8,128)(2,1)S(1)}, bf16[512,256]{1,0:T(8,128)(2,1)S(1)}, u32[]{:S(2)}, u32[]{:S(2)}) collective-permute-start(bf16[512,256]{1,0:T(8,128)(2,1)S(1)} %get-tuple-element.68), channel_id=1, source_target_pairs={{0,1},{1,0},{2,3},{3,2},{4,8},{5,9},{6,10},{7,11},{8,4},{9,5},{10,... | collective-permute-start | bytes 786440 | tf_op jit(solution)/shard_map/ppermute | solution.py:505
  45.2 20.1 %collective-permute-start.15 = (bf16[512,256]{1,0:T(8,128)(2,1)S(1)}, bf16[512,256]{1,0:T(8,128)(2,1)S(1)}, u32[]{:S(2)}, u32[]{:S(2)}) collective-permute-start(bf16[512,256]{1,0:T(8,128)(2,1)S(1)} %get-tuple-element.73.refs_1_), channel_id=1, source_target_pairs={{0,2},{1,3},{2,0},{3,1},{4,6},{5,7},{6,4},{7,5},{8,10},{9,11},{10,... | collective-permute-start | bytes 786440 | tf_op jit(solution)/shard_map/ppermute | solution.py:481
  49.0 11.4 %collective-permute-start.11 = (bf16[512,256]{1,0:T(8,128)(2,1)S(1)}, bf16[512,256]{1,0:T(8,128)(2,1)S(1)}, u32[]{:S(2)}, u32[]{:S(2)}) collective-permute-start(bf16[512,256]{1,0:T(8,128)(2,1)S(1)} %get-tuple-element.66), channel_id=1, source_target_pairs={{0,1},{1,0},{2,3},{3,2},{4,8},{5,9},{6,10},{7,11},{8,4},{9,5},{10,... | collective-permute-start | bytes 786440 | tf_op jit(solution)/shard_map/ppermute | solution.py:505
  50.1 15.2 %collective-permute-start.16 = (bf16[512,256]{1,0:T(8,128)(2,1)S(1)}, bf16[512,256]{1,0:T(8,128)(2,1)S(1)}, u32[]{:S(2)}, u32[]{:S(2)}) collective-permute-start(bf16[512,256]{1,0:T(8,128)(2,1)S(1)} %get-tuple-element.74.refs_2_), channel_id=1, source_target_pairs={{0,2},{1,3},{2,0},{3,1},{4,6},{5,7},{6,4},{7,5},{8,10},{9,11},{10,... | collective-permute-start | bytes 786440 | tf_op jit(solution)/shard_map/ppermute | solution.py:481
  51.5 12.1 %collective-permute-start.17 = (bf16[256,256]{1,0:T(8,128)(2,1)S(1)}, bf16[256,256]{1,0:T(8,128)(2,1)S(1)}, u32[]{:S(2)}, u32[]{:S(2)}) collective-permute-start(bf16[256,256]{1,0:T(8,128)(2,1)S(1)} %get-tuple-element.75), channel_id=1, source_target_pairs={{0,4},{4,0},{8,12},{12,8},{1,5},{5,1},{9,13},{13,9},{2,6},{6,2},{1... | collective-permute-start | bytes 393224 | tf_op jit(solution)/shard_map/ppermute | solution.py:491
  60.3 5.0 %collective-permute-start.18 = (bf16[256,256]{1,0:T(8,128)(2,1)S(1)}, bf16[256,256]{1,0:T(8,128)(2,1)S(1)}, u32[]{:S(2)}, u32[]{:S(2)}) collective-permute-start(bf16[256,256]{1,0:T(8,128)(2,1)S(1)} %get-tuple-element.76), channel_id=1, source_target_pairs={{0,4},{4,0},{8,12},{12,8},{1,5},{5,1},{9,13},{13,9},{2,6},{6,2},{1... | collective-permute-start | bytes 393224 | tf_op jit(solution)/shard_map/ppermute | solution.py:491
  65.5 3.5 %collective-permute-start.19 = (bf16[6,512,256]{2,1,0:T(8,128)(2,1)S(1)}, bf16[6,512,256]{2,1,0:T(8,128)(2,1)S(1)}, u32[]{:S(2)}, u32[]{:S(2)}) collective-permute-start(bf16[6,512,256]{2,1,0:T(8,128)(2,1)S(1)} %shard_map.100), channel_id=1, source_target_pairs={{0,1},{1,0},{2,3},{3,2},{4,5},{5,4},{6,7},{7,6},{8,9},{9,8},{10,11... | collective-permute-start | bytes 4718600 | tf_op jit(solution)/shard_map/ppermute | solution.py:485
  65.5 8.9 %collective-permute-start.14 = (bf16[528,256]{1,0:T(8,128)(2,1)S(1)}, bf16[528,256]{1,0:T(8,128)(2,1)S(1)}, u32[]{:S(2)}, u32[]{:S(2)}) collective-permute-start(bf16[528,256]{1,0:T(8,128)(2,1)S(1)} %get-tuple-element.72.refs_6_.refs_0_.refs_3_), channel_id=1, source_target_pairs={{0,2},{1,3},{2,0},{3,1},{4,6},{5,7},{6,4},{7,5},{8,10},{9,11},{10,... | collective-permute-start | bytes 811016 | tf_op jit(solution)/shard_map/ppermute | solution.py:481
  66.9 5.6 %collective-permute-start.20 = (bf16[256,256]{1,0:T(8,128)(2,1)S(1)}, bf16[256,256]{1,0:T(8,128)(2,1)S(1)}, u32[]{:S(2)}, u32[]{:S(2)}) collective-permute-start(bf16[256,256]{1,0:T(8,128)(2,1)S(1)} %get-tuple-element.77), channel_id=1, source_target_pairs={{0,4},{4,0},{8,12},{12,8},{1,5},{5,1},{9,13},{13,9},{2,6},{6,2},{1... | collective-permute-start | bytes 393224 | tf_op jit(solution)/shard_map/ppermute | solution.py:491
  74.5 2.0 %collective-permute-start.21 = (bf16[2,528,256]{2,1,0:T(8,128)(2,1)S(1)}, bf16[2,528,256]{2,1,0:T(8,128)(2,1)S(1)}, u32[]{:S(2)}, u32[]{:S(2)}) collective-permute-start(bf16[2,528,256]{2,1,0:T(8,128)(2,1)S(1)} %shard_map.102.refs_0_), channel_id=1, source_target_pairs={{0,1},{1,0},{2,3},{3,2},{4,5},{5,4},{6,7},{7,6},{8,9},{9,8},{10,11... | collective-permute-start | bytes 1622024 | tf_op jit(solution)/shard_map/ppermute | solution.py:485
  79.7 6.2 %collective-permute-start.22 = (bf16[512,256]{1,0:T(8,128)(2,1)S(1)}, bf16[512,256]{1,0:T(8,128)(2,1)S(1)}, u32[]{:S(2)}, u32[]{:S(2)}) collective-permute-start(bf16[512,256]{1,0:T(8,128)(2,1)S(1)} %get-tuple-element.81), channel_id=1, source_target_pairs={{0,1},{1,0},{2,3},{3,2},{4,8},{5,9},{6,10},{7,11},{8,4},{9,5},{10,... | collective-permute-start | bytes 786440 | tf_op jit(solution)/shard_map/ppermute | solution.py:505
  79.9 15.3 %collective-permute-start.25 = (bf16[256,256]{1,0:T(8,128)(2,1)S(1)}, bf16[256,256]{1,0:T(8,128)(2,1)S(1)}, u32[]{:S(2)}, u32[]{:S(2)}) collective-permute-start(bf16[256,256]{1,0:T(8,128)(2,1)S(1)} %get-tuple-element.87), channel_id=1, source_target_pairs={{0,4},{4,0},{8,12},{12,8},{1,5},{5,1},{9,13},{13,9},{2,6},{6,2},{1... | collective-permute-start | bytes 393224 | tf_op jit(solution)/shard_map/ppermute | solution.py:491
  85.8 9.4 %collective-permute-start.24 = (bf16[512,256]{1,0:T(8,128)(2,1)S(1)}, bf16[512,256]{1,0:T(8,128)(2,1)S(1)}, u32[]{:S(2)}, u32[]{:S(2)}) collective-permute-start(bf16[512,256]{1,0:T(8,128)(2,1)S(1)} %get-tuple-element.86), channel_id=1, source_target_pairs={{0,1},{1,0},{2,3},{3,2},{4,8},{5,9},{6,10},{7,11},{8,4},{9,5},{10,... | collective-permute-start | bytes 786440 | tf_op jit(solution)/shard_map/ppermute | solution.py:505
  89.1 9.6 %collective-permute-start.23 = (bf16[528,256]{1,0:T(8,128)(2,1)S(1)}, bf16[528,256]{1,0:T(8,128)(2,1)S(1)}, u32[]{:S(2)}, u32[]{:S(2)}) collective-permute-start(bf16[528,256]{1,0:T(8,128)(2,1)S(1)} %get-tuple-element.83), channel_id=1, source_target_pairs={{0,1},{1,0},{2,3},{3,2},{4,8},{5,9},{6,10},{7,11},{8,4},{9,5},{10,... | collective-permute-start | bytes 811016 | tf_op jit(solution)/shard_map/ppermute | solution.py:505
  89.7 9.1 %collective-permute-start.26 = (bf16[256,256]{1,0:T(8,128)(2,1)S(1)}, bf16[256,256]{1,0:T(8,128)(2,1)S(1)}, u32[]{:S(2)}, u32[]{:S(2)}) collective-permute-start(bf16[256,256]{1,0:T(8,128)(2,1)S(1)} %shard_map.106.refs_3_), channel_id=1, source_target_pairs={{0,4},{4,0},{8,12},{12,8},{1,5},{5,1},{9,13},{13,9},{2,6},{6,2},{1... | collective-permute-start | bytes 393224 | tf_op jit(solution)/shard_map/ppermute | solution.py:491
  95.3 6.0 %collective-permute-start.28 = (bf16[256,256]{1,0:T(8,128)(2,1)S(1)}, bf16[256,256]{1,0:T(8,128)(2,1)S(1)}, u32[]{:S(2)}, u32[]{:S(2)}) collective-permute-start(bf16[256,256]{1,0:T(8,128)(2,1)S(1)} %shard_map.108.refs_1_), channel_id=1, source_target_pairs={{0,4},{4,0},{8,12},{12,8},{1,5},{5,1},{9,13},{13,9},{2,6},{6,2},{1... | collective-permute-start | bytes 393224 | tf_op jit(solution)/shard_map/ppermute | solution.py:491
  98.7 2.6 %collective-permute-start.30 = (bf16[256,256]{1,0:T(8,128)(2,1)S(1)}, bf16[256,256]{1,0:T(8,128)(2,1)S(1)}, u32[]{:S(2)}, u32[]{:S(2)}) collective-permute-start(bf16[256,256]{1,0:T(8,128)(2,1)S(1)} %get-tuple-element.93), channel_id=1, source_target_pairs={{0,1},{1,0},{2,3},{3,2},{4,8},{5,9},{6,10},{7,11},{8,4},{9,5},{10,... | collective-permute-start | bytes 393224 | tf_op jit(solution)/shard_map/ppermute | solution.py:505
  98.8 7.8 %collective-permute-start.29 = (bf16[272,256]{1,0:T(8,128)(2,1)S(1)}, bf16[272,256]{1,0:T(8,128)(2,1)S(1)}, u32[]{:S(2)}, u32[]{:S(2)}) collective-permute-start(bf16[272,256]{1,0:T(8,128)(2,1)S(1)} %get-tuple-element.92), channel_id=1, source_target_pairs={{0,4},{4,0},{8,12},{12,8},{1,5},{5,1},{9,13},{13,9},{2,6},{6,2},{1... | collective-permute-start | bytes 417800 | tf_op jit(solution)/shard_map/ppermute | solution.py:491
  101.3 5.4 %collective-permute-start.27 = (bf16[256,256]{1,0:T(8,128)(2,1)S(1)}, bf16[256,256]{1,0:T(8,128)(2,1)S(1)}, u32[]{:S(2)}, u32[]{:S(2)}) collective-permute-start(bf16[256,256]{1,0:T(8,128)(2,1)S(1)} %get-tuple-element.91), channel_id=1, source_target_pairs={{0,1},{1,0},{2,3},{3,2},{4,8},{5,9},{6,10},{7,11},{8,4},{9,5},{10,... | collective-permute-start | bytes 393224 | tf_op jit(solution)/shard_map/ppermute | solution.py:505
  101.3 8.3 %collective-permute-start.31 = (bf16[256,256]{1,0:T(8,128)(2,1)S(1)}, bf16[256,256]{1,0:T(8,128)(2,1)S(1)}, u32[]{:S(2)}, u32[]{:S(2)}) collective-permute-start(bf16[256,256]{1,0:T(8,128)(2,1)S(1)} %shard_map.111), channel_id=1, source_target_pairs={{0,4},{4,0},{8,12},{12,8},{1,5},{5,1},{9,13},{13,9},{2,6},{6,2},{1... | collective-permute-start | bytes 393224 | tf_op jit(solution)/shard_map/ppermute | solution.py:491

commit v8 on v7

--- a/solution.py
+++ b/solution.py
@@ -348,9 +348,10 @@
     )(kept, arrived, *([stats] if coded else []), *tokens)
 
 
-def finish_kernel(entry_count, local, carrier, stats, *refs):
+def finish_kernel(entry_count, local, carrier, firsts, stats, *refs):
     parts, near_images, kept, arrived, near_again = (refs[at * local:(at + 1) * local] for at in range(5))
-    outs, (image_held, kept_held, more_held, out_held, code, sems, out_sems) = refs[-9:-7], refs[-7:]
+    *outs, scales = refs[-10:-7]
+    image_held, kept_held, more_held, out_held, code, sems, out_sems = refs[-7:]
     tile = image_held.shape[1]
     leading = leads(lax.axis_index("row")) == 1
 
@@ -383,20 +384,24 @@
                 for copy in sent(first):
                     act(copy)
 
-    order = [first for first in range(local) if first == carrier] + [first for first in range(local) if first != carrier]
+    order = sorted(firsts, key=lambda first: first != carrier)
     each(order, lambda copy: copy.start())
     scale = theta = None
     out_copies = []
     for first in order:
         each([first], lambda copy: copy.wait())
         if scale is None:
-            norm, correlation = stats[0, :1, :1], stats[1, :1, :1]
-            if carrier < local:
-                norm, correlation = (
-                    jnp.where(leading, mine, theirs) for mine, theirs in zip((norm, correlation), decode(code[...]))
-                )
-            scale = lax.rsqrt(norm / entry_count + 1e-06)
-            theta = correlation / norm
+            scale, theta = stats[0, :1, :1], stats[1, :1, :1]
+            if 0 in firsts:
+                norm, correlation = scale, theta
+                if carrier < local:
+                    norm, correlation = (
+                        jnp.where(leading, mine, theirs) for mine, theirs in zip((norm, correlation), decode(code[...]))
+                    )
+                scale = lax.rsqrt(norm / entry_count + 1e-06)
+                theta = correlation / norm
+            for at, value in enumerate((scale, theta)):
+                scales[at] = jnp.broadcast_to(value, scales.shape[1:])
         image = image_held[first].astype(jnp.float32)
         value = jnp.where(leading, kept_held[first], 0.0) + more_held[first].astype(jnp.float32)
         out_held[0, first] = (image * scale).astype(out_held.dtype)
@@ -411,15 +416,16 @@
         copy.wait()
 
 
-def finish(entry_count, carrier, stats, parts, near_images, again, near_again, tokens):
+def finish(entry_count, carrier, firsts, stats, parts, near_images, again, near_again, tokens, outs=()):
     local, tile = len(parts), near_images[0].shape[0]
     out = jax.ShapeDtypeStruct((tile, local * tile), near_images[0].dtype)
     block = (local, tile, tile)
     return pl.pallas_call(
-        functools.partial(finish_kernel, entry_count, local, carrier),
-        in_specs=[VMEM] + [ANY] * (5 * local + len(tokens)),
-        out_specs=[ANY, ANY],
-        out_shape=[out, out],
+        functools.partial(finish_kernel, entry_count, local, carrier, firsts),
+        in_specs=[VMEM] + [ANY] * (5 * local + len(outs) + len(tokens)),
+        out_specs=[ANY, ANY, VMEM],
+        out_shape=[out, out, TOKEN],
+        input_output_aliases={5 * local + 1 + at: at for at in range(len(outs))},
         scratch_shapes=[
             pltpu.VMEM(block, out.dtype),
             pltpu.VMEM(block, jnp.float32),
@@ -431,7 +437,7 @@
         ],
         compiler_params=pltpu.CompilerParams(vmem_limit_bytes=VMEM_LIMIT),
         cost_estimate=BRIEF,
-    )(stats, *parts, *near_images, *(kept for kept, _ in again), *(arrived[0] for _, arrived in again), *near_again, *tokens)
+    )(stats, *parts, *near_images, *(kept for kept, _ in again), *(arrived[0] for _, arrived in again), *near_again, *outs, *tokens)
 
 
 def after_kernel(value, *refs):
@@ -583,7 +589,15 @@
         for bit in range(pair_bits):
             stats = stats + lax.ppermute(stats, both, leader_swap(1 << bit))
         stats = jnp.where(leading, stats, to_partner(stats))
-    return tuple(finish(entry_count, carrier, stats, [part[0] for part in parts], near_images, again, sent, [arrive(2 * 10**9, *sent[:-1])]))
+    images = [part[0] for part in parts]
+    last = local - 1
+    early = [*sent[:last], sent[0]]
+    *outs, scales = finish(
+        entry_count, carrier, list(range(last)), stats, images, near_images, again[:last] + again[:1], early,
+        [arrive(2 * 10**9, *sent[:last])],
+    )
+    *outs, _ = finish(entry_count, carrier, [last], scales, images, near_images, again, sent, [], outs)
+    return tuple(outs)
 
 
 def solution(mesh):

time: 113 us -> 112 us (level)
  waiting for transfers between devices: 26.6 us -> 24.3 us
  Pallas kernels: 40.6 us -> 42.1 us
    ppermute x10, waiting for transfers between devices: 18.6 us -> 16.3 us  [to_partner(): return lax.ppermute(part, 'row', swap('row', 1))]
    pallas_call x1 -> x2, Pallas kernels: 2.74 us -> 4.23 us  [finish(): pl.pallas_call(functools.partial(finish_kernel, entry_count, local, carri...]
  transfers between devices with their start and end apart: 32 -> 32, of which waited for: 11 -> 11; matrix products, arithmetic and copies ran while one was open for 1% -> 1% of each run, Pallas kernels for 28% -> 30%
where the time goes in v8:
time: 112 us
  Pallas kernels  42.1 us (38%)
  starting transfers between devices  41.6 us (37%)
  waiting for transfers between devices  24.3 us (22%)
  local copies, waits for them, and re-layouts  2.5 us (2%)
  between operations  1.2 us (1%)
    ppermute x10, starting transfers between devices, to_partner(): return lax.ppermute(part, 'row', swap('row', 1))  30.6 us
    pallas_call x8, Pallas kernels, products(): pl.pallas_call(functools.partial(product_kernel, first, local, out_slots,...  24.3 us
    ppermute x10, waiting for transfers between devices, to_partner(): return lax.ppermute(part, 'row', swap('row', 1))  16.3 us
    ppermute x6, starting transfers between devices, far(): lax.ppermute(piece, 'col', swap('col', 1 << bit))  8.39 us
    pallas_call x1, Pallas kernels, mask_right(): pl.pallas_call(mask_right_kernel, grid=(terms // 2,), in_specs=[SMEM, SME...  4.93 us
    ppermute x6, waiting for transfers between devices, far(): lax.ppermute(piece, 'col', swap('col', 1 << bit))  4.7 us
    pallas_call x2, Pallas kernels, finish(): pl.pallas_call(functools.partial(finish_kernel, entry_count, local, carri...  4.23 us
    pallas_call x4, Pallas kernels, combine(): pl.pallas_call(functools.partial(combine_kernel, first, local), in_specs=...  4 us
  transfers between devices with their start and end apart: 32, of which 11 were waited for; matrix products, arithmetic and copies ran while one was open for 1% of the time, Pallas kernels for 30%

profile of v8, /device:TPU:0, one launch (start us, length us, event | category | flops | bytes accessed | tf_op | source)
XLA Modules:
  0.0 111.7 jit_solution(3771672881019901836)
XLA Ops:
  0.6 3.1 %collective-permute-start = (bf16[256,1024]{1,0:T(8,128)(2,1)}, bf16[256,1024]{1,0:T(8,128)(2,1)S(1)}, u32[]{:S(2)}, u32[]{:S(2)}) collective-permute-start(bf16[256,1024]{1,0:T(8,128)(2,1)} %refs_0_.1), channel_id=1, source_target_pairs={{0,4},{4,0},{8,12},{12,8},{1,5},{5,1},{9,13},{13,9},{2,6},{6,2},{1... | collective-permute-start | bytes 1572872 | tf_op jit(solution)/shard_map/ppermute | solution.py:497
  3.7 1.5 %collective-permute-start.3 = (bf16[256,1024]{1,0:T(8,128)(2,1)}, bf16[256,1024]{1,0:T(8,128)(2,1)S(1)}, u32[]{:S(2)}, u32[]{:S(2)}) collective-permute-start(bf16[256,1024]{1,0:T(8,128)(2,1)} %refs_0_.1), channel_id=1, source_target_pairs={{0,2},{1,3},{2,0},{3,1},{4,6},{5,7},{6,4},{7,5},{8,10},{9,11},{10,... | collective-permute-start | bytes 1572872 | tf_op jit(solution)/shard_map/ppermute | solution.py:487
  5.2 1.3 %copy.20.left_dest.target = s32[8,4]{1,0:T(8,128)} copy(s32[8,4]{0,1:T(4,128)} %param.10) | data formatting | bytes 256 | tf_op args[3]
  6.6 2.8 %shard_map.86 = (bf16[8,256,256]{2,1,0:T(8,128)(2,1)}, bf16[4,256,256]{2,1,0:T(8,128)(2,1)}, f32[2,8,128]{2,1,0:T(8,128)}) custom-call(s32[8,4]{1,0:T(8,128)} %copy.20.left_dest.target, s32[4]{0:T(128)} %left_sizes.9, bf16[8,1,256,256]{3,2,1,0:T(8,128)(2,1)} %left.1), custom_call_target="tpu_custom_call" | custom-call | flops 1000000000 | tf_op jit(solution)/shard_map/pallas_call | solution.py:75
  9.3 0.4 collective-permute-start.7
  9.8 4.9 %shard_map.87 = (bf16[8,256,256]{2,1,0:T(8,128)(2,1)}, bf16[8,256,256]{2,1,0:T(8,128)(2,1)}, bf16[8,256,256]{2,1,0:T(8,128)(2,1)}, bf16[8,256,256]{2,1,0:T(8,128)(2,1)}, f32[2,8,128]{2,1,0:T(8,128)}) custom-call(s32[8,16]{1,0:T(8,128)} %source.15, s32[16]{0:T(128)} %right_sizes.9, bf16[8,4,256,256]{3,2,1,0:T(8,128)(2,1)} %right.1), custom_call_target="tpu_custom_call" | custom-call | flops 1000000000 | tf_op jit(solution)/shard_map/pallas_call | solution.py:98
  14.7 1.9 %collective-permute-done.value = bf16[256,1024]{1,0:T(8,128)(2,1)S(1)} collective-permute-done((bf16[256,1024]{1,0:T(8,128)(2,1)}, bf16[256,1024]{1,0:T(8,128)(2,1)S(1)}, u32[]{:S(2)}, u32[]{:S(2)}) %collective-permute-start) | collective-permute-done | bytes 524320 | tf_op jit(solution)/shard_map/ppermute | solution.py:497
  16.7 0.7 copy-done.10
  17.4 2.0 %collective-permute-start.1 = (bf16[256,1024]{1,0:T(8,128)(2,1)S(1)}, bf16[256,1024]{1,0:T(8,128)(2,1)S(1)}, u32[]{:S(2)}, u32[]{:S(2)}) collective-permute-start(bf16[256,1024]{1,0:T(8,128)(2,1)S(1)} %shard_map.88.refs_2_), channel_id=1, source_target_pairs={{0,2},{1,3},{2,0},{3,1},{4,6},{5,7},{6,4},{7,5},{8,10},{9,11},{10,... | collective-permute-start | bytes 1572872 | tf_op jit(solution)/shard_map/ppermute | solution.py:487
  19.5 0.5 collective-permute-start.5
  20.0 7.0 %collective-permute-done.7.left_near = bf16[4,256,256]{2,1,0:T(8,128)(2,1)S(1)} collective-permute-done((bf16[4,256,256]{2,1,0:T(8,128)(2,1)}, bf16[4,256,256]{2,1,0:T(8,128)(2,1)S(1)}, u32[]{:S(2)}, u32[]{:S(2)}) %collective-permute-start.7) | collective-permute-done | bytes 524320 | tf_op jit(solution)/shard_map/ppermute | solution.py:497
  27.1 2.7 %collective-permute-done.1.refs_0_ = bf16[256,1024]{1,0:T(8,128)(2,1)S(1)} collective-permute-done((bf16[256,1024]{1,0:T(8,128)(2,1)S(1)}, bf16[256,1024]{1,0:T(8,128)(2,1)S(1)}, u32[]{:S(2)}, u32[]{:S(2)}) %collective-permute-start.1) | collective-permute-done | bytes 524320 | tf_op jit(solution)/shard_map/ppermute | solution.py:487
  29.8 0.7 shard_map.89.refs_2_
  30.6 1.1 %collective-permute-done.2.refs_1_ = bf16[256,1024]{1,0:T(8,128)(2,1)S(1)} collective-permute-done((bf16[256,1024]{1,0:T(8,128)(2,1)S(1)}, bf16[256,1024]{1,0:T(8,128)(2,1)S(1)}, u32[]{:S(2)}, u32[]{:S(2)}) %collective-permute-start.2) | collective-permute-done | bytes 524320 | tf_op jit(solution)/shard_map/ppermute | solution.py:491
  32.1 3.0 %shard_map.92 = (f32[512,256]{1,0:T(8,128)S(1)}, bf16[512,256]{1,0:T(8,128)(2,1)S(1)}, f32[2,8,128]{2,1,0:T(8,128)S(1)}) custom-call(s32[8,16]{1,0:T(8,128)S(1)} %copy-done.6, s32[8,4]{1,0:T(8,128)S(1)} %copy-done.7, bf16[16,512,256]{2,1,0:T(8,128)(2,1)S(1)} %shard_map.90.blocks, bf16[8,256,256]{2,1,0:T(8,128)(2,1)S(1)} %copy-done, ...), custom_call_target="tpu_custom_call" | custom-call | flops 1000000000 | tf_op jit(solution)/shard_map/pallas_call | solution.py:249
  35.1 0.6 collective-permute-start.9
  35.7 3.0 %shard_map.93 = (f32[512,256]{1,0:T(8,128)S(1)}, bf16[512,256]{1,0:T(8,128)(2,1)S(1)}, f32[2,8,128]{2,1,0:T(8,128)S(1)}) custom-call(s32[8,16]{1,0:T(8,128)S(1)} %copy-done.6, s32[8,4]{1,0:T(8,128)S(1)} %copy-done.7, bf16[16,512,256]{2,1,0:T(8,128)(2,1)S(1)} %shard_map.90.blocks, bf16[8,256,256]{2,1,0:T(8,128)(2,1)S(1)} %copy-done, ...), custom_call_target="tpu_custom_call" | custom-call | flops 1000000000 | tf_op jit(solution)/shard_map/pallas_call | solution.py:249
  38.8 0.8 shard_map.94
  39.7 1.4 %collective-permute-start.13 = (bf16[512,256]{1,0:T(8,128)(2,1)S(1)}, bf16[512,256]{1,0:T(8,128)(2,1)S(1)}, u32[]{:S(2)}, u32[]{:S(2)}) collective-permute-start(bf16[512,256]{1,0:T(8,128)(2,1)S(1)} %get-tuple-element.75.refs_0_), channel_id=1, source_target_pairs={{0,2},{1,3},{2,0},{3,1},{4,6},{5,7},{6,4},{7,5},{8,10},{9,11},{10,... | collective-permute-start | bytes 786440 | tf_op jit(solution)/shard_map/ppermute | solution.py:487
  41.1 3.0 %shard_map.95 = (f32[512,256]{1,0:T(8,128)S(1)}, bf16[512,256]{1,0:T(8,128)(2,1)S(1)}, f32[2,8,128]{2,1,0:T(8,128)S(1)}) custom-call(s32[8,16]{1,0:T(8,128)S(1)} %copy-done.6, s32[8,4]{1,0:T(8,128)S(1)} %copy-done.7, bf16[16,512,256]{2,1,0:T(8,128)(2,1)S(1)} %shard_map.90.blocks, bf16[8,256,256]{2,1,0:T(8,128)(2,1)S(1)} %copy-done, ...), custom_call_target="tpu_custom_call" | custom-call | flops 1000000000 | tf_op jit(solution)/shard_map/pallas_call | solution.py:249
  44.4 0.8 shard_map.96
  45.2 0.8 collective-permute-start.15
  45.9 3.0 %shard_map.97 = (f32[512,256]{1,0:T(8,128)S(1)}, bf16[512,256]{1,0:T(8,128)(2,1)S(1)}, f32[2,8,128]{2,1,0:T(8,128)S(1)}) custom-call(s32[8,16]{1,0:T(8,128)S(1)} %copy-done.6, s32[8,4]{1,0:T(8,128)S(1)} %copy-done.7, bf16[16,512,256]{2,1,0:T(8,128)(2,1)S(1)} %shard_map.90.blocks, bf16[8,256,256]{2,1,0:T(8,128)(2,1)S(1)} %copy-done, ...), custom_call_target="tpu_custom_call" | custom-call | flops 1000000000 | tf_op jit(solution)/shard_map/pallas_call | solution.py:249
  49.1 1.0 shard_map.98
  50.1 1.4 %collective-permute-start.16 = (bf16[512,256]{1,0:T(8,128)(2,1)S(1)}, bf16[512,256]{1,0:T(8,128)(2,1)S(1)}, u32[]{:S(2)}, u32[]{:S(2)}) collective-permute-start(bf16[512,256]{1,0:T(8,128)(2,1)S(1)} %get-tuple-element.79.refs_2_), channel_id=1, source_target_pairs={{0,2},{1,3},{2,0},{3,1},{4,6},{5,7},{6,4},{7,5},{8,10},{9,11},{10,... | collective-permute-start | bytes 786440 | tf_op jit(solution)/shard_map/ppermute | solution.py:487
  51.5 8.8 %collective-permute-start.17 = (bf16[256,256]{1,0:T(8,128)(2,1)S(1)}, bf16[256,256]{1,0:T(8,128)(2,1)S(1)}, u32[]{:S(2)}, u32[]{:S(2)}) collective-permute-start(bf16[256,256]{1,0:T(8,128)(2,1)S(1)} %get-tuple-element.80), channel_id=1, source_target_pairs={{0,4},{4,0},{8,12},{12,8},{1,5},{5,1},{9,13},{13,9},{2,6},{6,2},{1... | collective-permute-start | bytes 393224 | tf_op jit(solution)/shard_map/ppermute | solution.py:497
  60.3 1.4 %shard_map.99 = (bf16[528,256]{1,0:T(8,128)(2,1)S(1)}, bf16[256,256]{1,0:T(8,128)(2,1)S(1)}, f32[2,8,256]{2,1,0:T(8,128)}) custom-call(s32[4]{0:T(128)S(1)} %copy-done.9, s32[16]{0:T(128)S(1)} %copy-done.8, f32[512,256]{1,0:T(8,128)S(1)} %get-tuple-element.70.kept, bf16[512,256]{1,0:T(8,128)(2,1)S(1)} %collective-permute-done.11.arrived, ...), custom_call_target="tpu_custom_call" | custom-call | flops 1000000000 | tf_op jit(solution)/shard_map/pallas_call | solution.py:314
  61.7 1.9 %collective-permute-done.17.refs_7_.refs_4_ = bf16[256,256]{1,0:T(8,128)(2,1)S(1)} collective-permute-done((bf16[256,256]{1,0:T(8,128)(2,1)S(1)}, bf16[256,256]{1,0:T(8,128)(2,1)S(1)}, u32[]{:S(2)}, u32[]{:S(2)}) %collective-permute-start.17) | collective-permute-done | bytes 131104 | tf_op jit(solution)/shard_map/ppermute | solution.py:497
  63.6 1.7 %collective-permute-done.18.refs_8_.refs_5_ = bf16[256,256]{1,0:T(8,128)(2,1)S(1)} collective-permute-done((bf16[256,256]{1,0:T(8,128)(2,1)S(1)}, bf16[256,256]{1,0:T(8,128)(2,1)S(1)}, u32[]{:S(2)}, u32[]{:S(2)}) %collective-permute-start.18) | collective-permute-done | bytes 131104 | tf_op jit(solution)/shard_map/ppermute | solution.py:497
  65.5 1.3 %collective-permute-start.14 = (bf16[528,256]{1,0:T(8,128)(2,1)S(1)}, bf16[528,256]{1,0:T(8,128)(2,1)S(1)}, u32[]{:S(2)}, u32[]{:S(2)}) collective-permute-start(bf16[528,256]{1,0:T(8,128)(2,1)S(1)} %get-tuple-element.77.refs_6_.refs_0_.refs_3_), channel_id=1, source_target_pairs={{0,2},{1,3},{2,0},{3,1},{4,6},{5,7},{6,4},{7,5},{8,10},{9,11},{10,... | collective-permute-start | bytes 811016 | tf_op jit(solution)/shard_map/ppermute | solution.py:487
  66.8 1.7 %collective-permute-start.20 = (bf16[256,256]{1,0:T(8,128)(2,1)S(1)}, bf16[256,256]{1,0:T(8,128)(2,1)S(1)}, u32[]{:S(2)}, u32[]{:S(2)}) collective-permute-start(bf16[256,256]{1,0:T(8,128)(2,1)S(1)} %get-tuple-element.82), channel_id=1, source_target_pairs={{0,4},{4,0},{8,12},{12,8},{1,5},{5,1},{9,13},{13,9},{2,6},{6,2},{1... | collective-permute-start | bytes 393224 | tf_op jit(solution)/shard_map/ppermute | solution.py:497
  68.6 0.3 collective-permute-done.19
  69.3 3.1 %collective-permute-done.20.refs_3_.refs_6_ = bf16[256,256]{1,0:T(8,128)(2,1)S(1)} collective-permute-done((bf16[256,256]{1,0:T(8,128)(2,1)S(1)}, bf16[256,256]{1,0:T(8,128)(2,1)S(1)}, u32[]{:S(2)}, u32[]{:S(2)}) %collective-permute-start.20) | collective-permute-done | bytes 131104 | tf_op jit(solution)/shard_map/ppermute | solution.py:497
  72.4 2.0 %collective-permute-done.14.refs_1_ = bf16[528,256]{1,0:T(8,128)(2,1)S(1)} collective-permute-done((bf16[528,256]{1,0:T(8,128)(2,1)S(1)}, bf16[528,256]{1,0:T(8,128)(2,1)S(1)}, u32[]{:S(2)}, u32[]{:S(2)}) %collective-permute-start.14) | collective-permute-done | bytes 270368 | tf_op jit(solution)/shard_map/ppermute | solution.py:487
  74.6 1.9 %collective-permute-done.21.refs_1_ = bf16[2,528,256]{2,1,0:T(8,128)(2,1)S(1)} collective-permute-done((bf16[2,528,256]{2,1,0:T(8,128)(2,1)S(1)}, bf16[2,528,256]{2,1,0:T(8,128)(2,1)S(1)}, u32[]{:S(2)}, u32[]{:S(2)}) %collective-permute-start.21) | collective-permute-done | bytes 540704 | tf_op jit(solution)/shard_map/ppermute | solution.py:491
  76.7 3.0 %shard_map.104 = (f32[512,256]{1,0:T(8,128)S(1)}, bf16[512,256]{1,0:T(8,128)(2,1)S(1)}, f32[2,8,128]{2,1,0:T(8,128)S(1)}) custom-call(s32[8,16]{1,0:T(8,128)S(1)} %copy-done.6, s32[8,4]{1,0:T(8,128)S(1)} %copy-done.7, bf16[16,512,256]{2,1,0:T(8,128)(2,1)S(1)} %shard_map.103.blocks, bf16[8,256,256]{2,1,0:T(8,128)(2,1)S(1)} %copy-done, ...), custom_call_target="tpu_custom_call" | custom-call | flops 1000000000 | tf_op jit(solution)/shard_map/pallas_call | solution.py:249
  79.9 2.8 %collective-permute-start.25 = (bf16[256,256]{1,0:T(8,128)(2,1)S(1)}, bf16[256,256]{1,0:T(8,128)(2,1)S(1)}, u32[]{:S(2)}, u32[]{:S(2)}) collective-permute-start(bf16[256,256]{1,0:T(8,128)(2,1)S(1)} %get-tuple-element.92), channel_id=1, source_target_pairs={{0,4},{4,0},{8,12},{12,8},{1,5},{5,1},{9,13},{13,9},{2,6},{6,2},{1... | collective-permute-start | bytes 393224 | tf_op jit(solution)/shard_map/ppermute | solution.py:497
  82.8 3.0 %shard_map.105 = (f32[512,256]{1,0:T(8,128)S(1)}, bf16[512,256]{1,0:T(8,128)(2,1)S(1)}, f32[2,8,128]{2,1,0:T(8,128)S(1)}) custom-call(s32[8,16]{1,0:T(8,128)S(1)} %copy-done.6, s32[8,4]{1,0:T(8,128)S(1)} %copy-done.7, bf16[16,512,256]{2,1,0:T(8,128)(2,1)S(1)} %shard_map.103.blocks, bf16[8,256,256]{2,1,0:T(8,128)(2,1)S(1)} %copy-done, ...), custom_call_target="tpu_custom_call" | custom-call | flops 1000000000 | tf_op jit(solution)/shard_map/pallas_call | solution.py:249
  85.9 3.2 %shard_map.107 = (f32[512,256]{1,0:T(8,128)S(1)}, bf16[528,256]{1,0:T(8,128)(2,1)S(1)}, f32[2,8,128]{2,1,0:T(8,128)S(1)}) custom-call(s32[8,16]{1,0:T(8,128)S(1)} %copy-done.6, s32[8,4]{1,0:T(8,128)S(1)} %copy-done.7, bf16[16,512,256]{2,1,0:T(8,128)(2,1)S(1)} %shard_map.103.blocks, bf16[8,256,256]{2,1,0:T(8,128)(2,1)S(1)} %copy-done, ...), custom_call_target="tpu_custom_call" | custom-call | flops 1000000000 | tf_op jit(solution)/shard_map/pallas_call | solution.py:249
  89.1 0.5 collective-permute-start.23
  89.7 5.5 %collective-permute-start.26 = (bf16[256,256]{1,0:T(8,128)(2,1)S(1)}, bf16[256,256]{1,0:T(8,128)(2,1)S(1)}, u32[]{:S(2)}, u32[]{:S(2)}) collective-permute-start(bf16[256,256]{1,0:T(8,128)(2,1)S(1)} %shard_map.106.refs_3_), channel_id=1, source_target_pairs={{0,4},{4,0},{8,12},{12,8},{1,5},{5,1},{9,13},{13,9},{2,6},{6,2},{1... | collective-permute-start | bytes 393224 | tf_op jit(solution)/shard_map/ppermute | solution.py:497
  95.2 0.4 collective-permute-start.27
  95.6 3.0 %shard_map.109 = (f32[512,256]{1,0:T(8,128)S(1)}, bf16[256,256]{1,0:T(8,128)(2,1)S(1)}, bf16[256,256]{1,0:T(8,128)(2,1)S(1)}, f32[2,8,128]{2,1,0:T(8,128)S(1)}) custom-call(s32[8,16]{1,0:T(8,128)S(1)} %copy-done.6, s32[8,4]{1,0:T(8,128)S(1)} %copy-done.7, bf16[16,512,256]{2,1,0:T(8,128)(2,1)S(1)} %shard_map.103.blocks, bf16[8,256,256]{2,1,0:T(8,128)(2,1)S(1)} %copy-done, ...), custom_call_target="tpu_custom_call" | custom-call | flops 1000000000 | tf_op jit(solution)/shard_map/pallas_call | solution.py:249
  98.9 2.4 %collective-permute-start.28 = (bf16[272,256]{1,0:T(8,128)(2,1)S(1)}, bf16[272,256]{1,0:T(8,128)(2,1)S(1)}, u32[]{:S(2)}, u32[]{:S(2)}) collective-permute-start(bf16[272,256]{1,0:T(8,128)(2,1)S(1)} %get-tuple-element.95), channel_id=1, source_target_pairs={{0,4},{4,0},{8,12},{12,8},{1,5},{5,1},{9,13},{13,9},{2,6},{6,2},{1... | collective-permute-start | bytes 417800 | tf_op jit(solution)/shard_map/ppermute | solution.py:497
  101.3 5.3 %collective-permute-start.31 = (bf16[256,256]{1,0:T(8,128)(2,1)S(1)}, bf16[256,256]{1,0:T(8,128)(2,1)S(1)}, u32[]{:S(2)}, u32[]{:S(2)}) collective-permute-start(bf16[256,256]{1,0:T(8,128)(2,1)S(1)} %shard_map.113), channel_id=1, source_target_pairs={{0,4},{4,0},{8,12},{12,8},{1,5},{5,1},{9,13},{13,9},{2,6},{6,2},{1... | collective-permute-start | bytes 393224 | tf_op jit(solution)/shard_map/ppermute | solution.py:497
  106.7 2.3 %shard_map.112 = (bf16[256,1024]{1,0:T(8,128)(2,1)}, bf16[256,1024]{1,0:T(8,128)(2,1)}, f32[2,8,128]{2,1,0:T(8,128)S(1)}) custom-call(f32[2,8,128]{2,1,0:T(8,128)S(1)} %get-tuple-element.94.stats, bf16[512,256]{1,0:T(8,128)(2,1)S(1)} %get-tuple-element.75.refs_0_, bf16[512,256]{1,0:T(8,128)(2,1)S(1)} %get-tuple-element.78.refs_1_, ...), custom_call_target="tpu_custom_call" | custom-call | flops 1000000000 | tf_op jit(solution)/shard_map/pallas_call | solution.py:423
  109.0 0.6 collective-permute-done.31.refs_19_
  109.6 1.9 %shard_map.114 = (bf16[256,1024]{1,0:T(8,128)(2,1)}, bf16[256,1024]{1,0:T(8,128)(2,1)}, f32[2,8,128]{2,1,0:T(8,128)}) custom-call(f32[2,8,128]{2,1,0:T(8,128)S(1)} %get-tuple-element.96.stats, bf16[512,256]{1,0:T(8,128)(2,1)S(1)} %get-tuple-element.75.refs_0_, ...), custom_call_target="tpu_custom_call", output_to_operand_aliasing={{0}: (21, {}), {1}: (22, {})} | custom-call | flops 1000000000 | tf_op jit(solution)/shard_map/pallas_call | solution.py:423
  (74 shorter events, 2.6 us)
Async XLA Ops:
  0.6 16.1 %collective-permute-start = (bf16[256,1024]{1,0:T(8,128)(2,1)}, bf16[256,1024]{1,0:T(8,128)(2,1)S(1)}, u32[]{:S(2)}, u32[]{:S(2)}) collective-permute-start(bf16[256,1024]{1,0:T(8,128)(2,1)} %refs_0_.1), channel_id=1, source_target_pairs={{0,4},{4,0},{8,12},{12,8},{1,5},{5,1},{9,13},{13,9},{2,6},{6,2},{1... | collective-permute-start | bytes 1572872 | tf_op jit(solution)/shard_map/ppermute | solution.py:497
  3.7 15.7 %collective-permute-start.3 = (bf16[256,1024]{1,0:T(8,128)(2,1)}, bf16[256,1024]{1,0:T(8,128)(2,1)S(1)}, u32[]{:S(2)}, u32[]{:S(2)}) collective-permute-start(bf16[256,1024]{1,0:T(8,128)(2,1)} %refs_0_.1), channel_id=1, source_target_pairs={{0,2},{1,3},{2,0},{3,1},{4,6},{5,7},{6,4},{7,5},{8,10},{9,11},{10,... | collective-permute-start | bytes 1572872 | tf_op jit(solution)/shard_map/ppermute | solution.py:487
  9.3 7.3 %copy-start.11 = (f32[2,8,128]{2,1,0:T(8,128)S(1)}, f32[2,8,128]{2,1,0:T(8,128)}, u32[]{:S(2)}) copy-start(f32[2,8,128]{2,1,0:T(8,128)} %get-tuple-element.53.refs_0_) | copy-start | bytes 24580
  9.3 10.1 %copy-start.5 = (bf16[256,1024]{1,0:T(8,128)(2,1)S(1)}, bf16[256,1024]{1,0:T(8,128)(2,1)}, u32[]{:S(2)}) copy-start(bf16[256,1024]{1,0:T(8,128)(2,1)} %refs_0_.1) | copy-start | bytes 1572868
  9.3 17.7 %collective-permute-start.7 = (bf16[4,256,256]{2,1,0:T(8,128)(2,1)}, bf16[4,256,256]{2,1,0:T(8,128)(2,1)S(1)}, u32[]{:S(2)}, u32[]{:S(2)}) collective-permute-start(bf16[4,256,256]{2,1,0:T(8,128)(2,1)} %get-tuple-element.56), channel_id=1, source_target_pairs={{0,4},{4,0},{8,12},{12,8},{1,5},{5,1},{9,13},{13,9},{2,6},{6,2},{1... | collective-permute-start | bytes 1572872 | tf_op jit(solution)/shard_map/ppermute | solution.py:497
  16.7 0.7 copy-start.10
  17.4 12.3 %collective-permute-start.1 = (bf16[256,1024]{1,0:T(8,128)(2,1)S(1)}, bf16[256,1024]{1,0:T(8,128)(2,1)S(1)}, u32[]{:S(2)}, u32[]{:S(2)}) collective-permute-start(bf16[256,1024]{1,0:T(8,128)(2,1)S(1)} %shard_map.88.refs_2_), channel_id=1, source_target_pairs={{0,2},{1,3},{2,0},{3,1},{4,6},{5,7},{6,4},{7,5},{8,10},{9,11},{10,... | collective-permute-start | bytes 1572872 | tf_op jit(solution)/shard_map/ppermute | solution.py:487
  19.5 10.3 %collective-permute-start.4 = (bf16[256,1024]{1,0:T(8,128)(2,1)S(1)}, bf16[256,1024]{1,0:T(8,128)(2,1)S(1)}, u32[]{:S(2)}, u32[]{:S(2)}) collective-permute-start(bf16[256,1024]{1,0:T(8,128)(2,1)S(1)} %copy-done.5), channel_id=1, source_target_pairs={{0,1},{1,0},{2,3},{3,2},{4,5},{5,4},{6,7},{7,6},{8,9},{9,8},{10,11... | collective-permute-start | bytes 1572872 | tf_op jit(solution)/shard_map/ppermute | solution.py:491
  19.5 10.3 %collective-permute-start.5 = (bf16[256,1024]{1,0:T(8,128)(2,1)S(1)}, bf16[256,1024]{1,0:T(8,128)(2,1)S(1)}, u32[]{:S(2)}, u32[]{:S(2)}) collective-permute-start(bf16[256,1024]{1,0:T(8,128)(2,1)S(1)} %collective-permute-done.3.refs_1_), channel_id=1, source_target_pairs={{0,1},{1,0},{2,3},{3,2},{4,5},{5,4},{6,7},{7,6},{8,9},{9,8},{10,11... | collective-permute-start | bytes 1572872 | tf_op jit(solution)/shard_map/ppermute | solution.py:491
  20.0 9.8 %collective-permute-start.6 = (bf16[256,1024]{1,0:T(8,128)(2,1)S(1)}, bf16[256,1024]{1,0:T(8,128)(2,1)S(1)}, u32[]{:S(2)}, u32[]{:S(2)}) collective-permute-start(bf16[256,1024]{1,0:T(8,128)(2,1)S(1)} %shard_map.88.refs_2_), channel_id=1, source_target_pairs={{0,1},{1,0},{2,3},{3,2},{4,5},{5,4},{6,7},{7,6},{8,9},{9,8},{10,11... | collective-permute-start | bytes 1572872 | tf_op jit(solution)/shard_map/ppermute | solution.py:491
  27.1 3.4 %collective-permute-start.8 = (bf16[4,256,256]{2,1,0:T(8,128)(2,1)S(1)}, bf16[4,256,256]{2,1,0:T(8,128)(2,1)S(1)}, u32[]{:S(2)}, u32[]{:S(2)}) collective-permute-start(bf16[4,256,256]{2,1,0:T(8,128)(2,1)S(1)} %collective-permute-done.7.left_near), channel_id=1, source_target_pairs={{0,1},{1,0},{2,3},{3,2},{4,5},{5,4},{6,7},{7,6},{8,9},{9,8},{10,11... | collective-permute-start | bytes 1572872 | tf_op jit(solution)/shard_map/ppermute | solution.py:491
  29.8 1.9 %collective-permute-start.2 = (bf16[256,1024]{1,0:T(8,128)(2,1)S(1)}, bf16[256,1024]{1,0:T(8,128)(2,1)S(1)}, u32[]{:S(2)}, u32[]{:S(2)}) collective-permute-start(bf16[256,1024]{1,0:T(8,128)(2,1)S(1)} %collective-permute-done.1.refs_0_), channel_id=1, source_target_pairs={{0,1},{1,0},{2,3},{3,2},{4,5},{5,4},{6,7},{7,6},{8,9},{9,8},{10,11... | collective-permute-start | bytes 1572872 | tf_op jit(solution)/shard_map/ppermute | solution.py:491
  30.5 1.4 %copy-start = (bf16[8,256,256]{2,1,0:T(8,128)(2,1)S(1)}, bf16[8,256,256]{2,1,0:T(8,128)(2,1)}, u32[]{:S(2)}) copy-start(bf16[8,256,256]{2,1,0:T(8,128)(2,1)} %get-tuple-element.55.left_own) | copy-start | bytes 3145732
  30.5 1.5 %copy-start.3 = (bf16[8,256,256]{2,1,0:T(8,128)(2,1)S(1)}, bf16[8,256,256]{2,1,0:T(8,128)(2,1)}, u32[]{:S(2)}) copy-start(bf16[8,256,256]{2,1,0:T(8,128)(2,1)} %get-tuple-element.60.right) | copy-start | bytes 3145732
  30.5 1.5 %copy-start.6 = (s32[8,16]{1,0:T(8,128)S(1)}, s32[8,16]{1,0:T(8,128)}, u32[]{:S(2)}) copy-start(s32[8,16]{1,0:T(8,128)} %source.15) | copy-start | bytes 1540
  30.6 1.5 %copy-start.7 = (s32[8,4]{1,0:T(8,128)S(1)}, s32[8,4]{1,0:T(8,128)}, u32[]{:S(2)}) copy-start(s32[8,4]{1,0:T(8,128)} %copy.20.left_dest.target) | copy-start | bytes 388
  31.9 3.8 %copy-start.2 = (bf16[8,256,256]{2,1,0:T(8,128)(2,1)S(1)}, bf16[8,256,256]{2,1,0:T(8,128)(2,1)}, u32[]{:S(2)}) copy-start(bf16[8,256,256]{2,1,0:T(8,128)(2,1)} %get-tuple-element.59.right) | copy-start | bytes 3145732
  35.1 3.7 %copy-start.8 = (s32[16]{0:T(128)S(1)}, s32[16]{0:T(128)}, u32[]{:S(2)}) copy-start(s32[16]{0:T(128)} %right_sizes.9) | copy-start | bytes 196
  35.1 3.7 %copy-start.9 = (s32[4]{0:T(128)S(1)}, s32[4]{0:T(128)}, u32[]{:S(2)}) copy-start(s32[4]{0:T(128)} %left_sizes.9) | copy-start | bytes 52
  35.1 3.7 %collective-permute-start.9 = (bf16[512,256]{1,0:T(8,128)(2,1)S(1)}, bf16[512,256]{1,0:T(8,128)(2,1)S(1)}, u32[]{:S(2)}, u32[]{:S(2)}) collective-permute-start(bf16[512,256]{1,0:T(8,128)(2,1)S(1)} %get-tuple-element.64), channel_id=1, source_target_pairs={{0,1},{1,0},{2,3},{3,2},{4,8},{5,9},{6,10},{7,11},{8,4},{9,5},{10,... | collective-permute-start | bytes 786440 | tf_op jit(solution)/shard_map/ppermute | solution.py:511
  38.7 2.3 %copy-start.4 = (bf16[8,256,256]{2,1,0:T(8,128)(2,1)S(1)}, bf16[8,256,256]{2,1,0:T(8,128)(2,1)}, u32[]{:S(2)}) copy-start(bf16[8,256,256]{2,1,0:T(8,128)(2,1)} %get-tuple-element.58.right) | copy-start | bytes 3145732
  38.7 5.6 %collective-permute-start.10 = (bf16[512,256]{1,0:T(8,128)(2,1)S(1)}, bf16[512,256]{1,0:T(8,128)(2,1)S(1)}, u32[]{:S(2)}, u32[]{:S(2)}) collective-permute-start(bf16[512,256]{1,0:T(8,128)(2,1)S(1)} %get-tuple-element.68), channel_id=1, source_target_pairs={{0,1},{1,0},{2,3},{3,2},{4,8},{5,9},{6,10},{7,11},{8,4},{9,5},{10,... | collective-permute-start | bytes 786440 | tf_op jit(solution)/shard_map/ppermute | solution.py:511
  39.7 9.4 %collective-permute-start.13 = (bf16[512,256]{1,0:T(8,128)(2,1)S(1)}, bf16[512,256]{1,0:T(8,128)(2,1)S(1)}, u32[]{:S(2)}, u32[]{:S(2)}) collective-permute-start(bf16[512,256]{1,0:T(8,128)(2,1)S(1)} %get-tuple-element.75.refs_0_), channel_id=1, source_target_pairs={{0,2},{1,3},{2,0},{3,1},{4,6},{5,7},{6,4},{7,5},{8,10},{9,11},{10,... | collective-permute-start | bytes 786440 | tf_op jit(solution)/shard_map/ppermute | solution.py:487
  44.1 1.9 %copy-start.1 = (bf16[8,256,256]{2,1,0:T(8,128)(2,1)S(1)}, bf16[8,256,256]{2,1,0:T(8,128)(2,1)}, u32[]{:S(2)}) copy-start(bf16[8,256,256]{2,1,0:T(8,128)(2,1)} %get-tuple-element.57.right) | copy-start | bytes 3145732
  44.1 5.0 %collective-permute-start.12 = (bf16[512,256]{1,0:T(8,128)(2,1)S(1)}, bf16[512,256]{1,0:T(8,128)(2,1)S(1)}, u32[]{:S(2)}, u32[]{:S(2)}) collective-permute-start(bf16[512,256]{1,0:T(8,128)(2,1)S(1)} %get-tuple-element.73), channel_id=1, source_target_pairs={{0,1},{1,0},{2,3},{3,2},{4,8},{5,9},{6,10},{7,11},{8,4},{9,5},{10,... | collective-permute-start | bytes 786440 | tf_op jit(solution)/shard_map/ppermute | solution.py:511
  45.2 20.1 %collective-permute-start.15 = (bf16[512,256]{1,0:T(8,128)(2,1)S(1)}, bf16[512,256]{1,0:T(8,128)(2,1)S(1)}, u32[]{:S(2)}, u32[]{:S(2)}) collective-permute-start(bf16[512,256]{1,0:T(8,128)(2,1)S(1)} %get-tuple-element.78.refs_1_), channel_id=1, source_target_pairs={{0,2},{1,3},{2,0},{3,1},{4,6},{5,7},{6,4},{7,5},{8,10},{9,11},{10,... | collective-permute-start | bytes 786440 | tf_op jit(solution)/shard_map/ppermute | solution.py:487
  49.0 11.4 %collective-permute-start.11 = (bf16[512,256]{1,0:T(8,128)(2,1)S(1)}, bf16[512,256]{1,0:T(8,128)(2,1)S(1)}, u32[]{:S(2)}, u32[]{:S(2)}) collective-permute-start(bf16[512,256]{1,0:T(8,128)(2,1)S(1)} %get-tuple-element.71), channel_id=1, source_target_pairs={{0,1},{1,0},{2,3},{3,2},{4,8},{5,9},{6,10},{7,11},{8,4},{9,5},{10,... | collective-permute-start | bytes 786440 | tf_op jit(solution)/shard_map/ppermute | solution.py:511
  50.1 15.2 %collective-permute-start.16 = (bf16[512,256]{1,0:T(8,128)(2,1)S(1)}, bf16[512,256]{1,0:T(8,128)(2,1)S(1)}, u32[]{:S(2)}, u32[]{:S(2)}) collective-permute-start(bf16[512,256]{1,0:T(8,128)(2,1)S(1)} %get-tuple-element.79.refs_2_), channel_id=1, source_target_pairs={{0,2},{1,3},{2,0},{3,1},{4,6},{5,7},{6,4},{7,5},{8,10},{9,11},{10,... | collective-permute-start | bytes 786440 | tf_op jit(solution)/shard_map/ppermute | solution.py:487
  51.5 12.1 %collective-permute-start.17 = (bf16[256,256]{1,0:T(8,128)(2,1)S(1)}, bf16[256,256]{1,0:T(8,128)(2,1)S(1)}, u32[]{:S(2)}, u32[]{:S(2)}) collective-permute-start(bf16[256,256]{1,0:T(8,128)(2,1)S(1)} %get-tuple-element.80), channel_id=1, source_target_pairs={{0,4},{4,0},{8,12},{12,8},{1,5},{5,1},{9,13},{13,9},{2,6},{6,2},{1... | collective-permute-start | bytes 393224 | tf_op jit(solution)/shard_map/ppermute | solution.py:497
  60.3 5.0 %collective-permute-start.18 = (bf16[256,256]{1,0:T(8,128)(2,1)S(1)}, bf16[256,256]{1,0:T(8,128)(2,1)S(1)}, u32[]{:S(2)}, u32[]{:S(2)}) collective-permute-start(bf16[256,256]{1,0:T(8,128)(2,1)S(1)} %get-tuple-element.81), channel_id=1, source_target_pairs={{0,4},{4,0},{8,12},{12,8},{1,5},{5,1},{9,13},{13,9},{2,6},{6,2},{1... | collective-permute-start | bytes 393224 | tf_op jit(solution)/shard_map/ppermute | solution.py:497
  65.5 3.5 %collective-permute-start.19 = (bf16[6,512,256]{2,1,0:T(8,128)(2,1)S(1)}, bf16[6,512,256]{2,1,0:T(8,128)(2,1)S(1)}, u32[]{:S(2)}, u32[]{:S(2)}) collective-permute-start(bf16[6,512,256]{2,1,0:T(8,128)(2,1)S(1)} %shard_map.100), channel_id=1, source_target_pairs={{0,1},{1,0},{2,3},{3,2},{4,5},{5,4},{6,7},{7,6},{8,9},{9,8},{10,11... | collective-permute-start | bytes 4718600 | tf_op jit(solution)/shard_map/ppermute | solution.py:491
  65.5 8.9 %collective-permute-start.14 = (bf16[528,256]{1,0:T(8,128)(2,1)S(1)}, bf16[528,256]{1,0:T(8,128)(2,1)S(1)}, u32[]{:S(2)}, u32[]{:S(2)}) collective-permute-start(bf16[528,256]{1,0:T(8,128)(2,1)S(1)} %get-tuple-element.77.refs_6_.refs_0_.refs_3_), channel_id=1, source_target_pairs={{0,2},{1,3},{2,0},{3,1},{4,6},{5,7},{6,4},{7,5},{8,10},{9,11},{10,... | collective-permute-start | bytes 811016 | tf_op jit(solution)/shard_map/ppermute | solution.py:487
  66.8 5.6 %collective-permute-start.20 = (bf16[256,256]{1,0:T(8,128)(2,1)S(1)}, bf16[256,256]{1,0:T(8,128)(2,1)S(1)}, u32[]{:S(2)}, u32[]{:S(2)}) collective-permute-start(bf16[256,256]{1,0:T(8,128)(2,1)S(1)} %get-tuple-element.82), channel_id=1, source_target_pairs={{0,4},{4,0},{8,12},{12,8},{1,5},{5,1},{9,13},{13,9},{2,6},{6,2},{1... | collective-permute-start | bytes 393224 | tf_op jit(solution)/shard_map/ppermute | solution.py:497
  74.5 2.0 %collective-permute-start.21 = (bf16[2,528,256]{2,1,0:T(8,128)(2,1)S(1)}, bf16[2,528,256]{2,1,0:T(8,128)(2,1)S(1)}, u32[]{:S(2)}, u32[]{:S(2)}) collective-permute-start(bf16[2,528,256]{2,1,0:T(8,128)(2,1)S(1)} %shard_map.102.refs_0_), channel_id=1, source_target_pairs={{0,1},{1,0},{2,3},{3,2},{4,5},{5,4},{6,7},{7,6},{8,9},{9,8},{10,11... | collective-permute-start | bytes 1622024 | tf_op jit(solution)/shard_map/ppermute | solution.py:491
  79.7 6.2 %collective-permute-start.22 = (bf16[512,256]{1,0:T(8,128)(2,1)S(1)}, bf16[512,256]{1,0:T(8,128)(2,1)S(1)}, u32[]{:S(2)}, u32[]{:S(2)}) collective-permute-start(bf16[512,256]{1,0:T(8,128)(2,1)S(1)} %get-tuple-element.86), channel_id=1, source_target_pairs={{0,1},{1,0},{2,3},{3,2},{4,8},{5,9},{6,10},{7,11},{8,4},{9,5},{10,... | collective-permute-start | bytes 786440 | tf_op jit(solution)/shard_map/ppermute | solution.py:511
  79.9 15.3 %collective-permute-start.25 = (bf16[256,256]{1,0:T(8,128)(2,1)S(1)}, bf16[256,256]{1,0:T(8,128)(2,1)S(1)}, u32[]{:S(2)}, u32[]{:S(2)}) collective-permute-start(bf16[256,256]{1,0:T(8,128)(2,1)S(1)} %get-tuple-element.92), channel_id=1, source_target_pairs={{0,4},{4,0},{8,12},{12,8},{1,5},{5,1},{9,13},{13,9},{2,6},{6,2},{1... | collective-permute-start | bytes 393224 | tf_op jit(solution)/shard_map/ppermute | solution.py:497
  85.8 9.4 %collective-permute-start.24 = (bf16[512,256]{1,0:T(8,128)(2,1)S(1)}, bf16[512,256]{1,0:T(8,128)(2,1)S(1)}, u32[]{:S(2)}, u32[]{:S(2)}) collective-permute-start(bf16[512,256]{1,0:T(8,128)(2,1)S(1)} %get-tuple-element.91), channel_id=1, source_target_pairs={{0,1},{1,0},{2,3},{3,2},{4,8},{5,9},{6,10},{7,11},{8,4},{9,5},{10,... | collective-permute-start | bytes 786440 | tf_op jit(solution)/shard_map/ppermute | solution.py:511
  89.1 9.7 %collective-permute-start.23 = (bf16[528,256]{1,0:T(8,128)(2,1)S(1)}, bf16[528,256]{1,0:T(8,128)(2,1)S(1)}, u32[]{:S(2)}, u32[]{:S(2)}) collective-permute-start(bf16[528,256]{1,0:T(8,128)(2,1)S(1)} %get-tuple-element.88), channel_id=1, source_target_pairs={{0,1},{1,0},{2,3},{3,2},{4,8},{5,9},{6,10},{7,11},{8,4},{9,5},{10,... | collective-permute-start | bytes 811016 | tf_op jit(solution)/shard_map/ppermute | solution.py:511
  89.7 9.1 %collective-permute-start.26 = (bf16[256,256]{1,0:T(8,128)(2,1)S(1)}, bf16[256,256]{1,0:T(8,128)(2,1)S(1)}, u32[]{:S(2)}, u32[]{:S(2)}) collective-permute-start(bf16[256,256]{1,0:T(8,128)(2,1)S(1)} %shard_map.106.refs_3_), channel_id=1, source_target_pairs={{0,4},{4,0},{8,12},{12,8},{1,5},{5,1},{9,13},{13,9},{2,6},{6,2},{1... | collective-permute-start | bytes 393224 | tf_op jit(solution)/shard_map/ppermute | solution.py:497
  95.2 6.1 %collective-permute-start.27 = (bf16[256,256]{1,0:T(8,128)(2,1)S(1)}, bf16[256,256]{1,0:T(8,128)(2,1)S(1)}, u32[]{:S(2)}, u32[]{:S(2)}) collective-permute-start(bf16[256,256]{1,0:T(8,128)(2,1)S(1)} %shard_map.108.refs_1_), channel_id=1, source_target_pairs={{0,4},{4,0},{8,12},{12,8},{1,5},{5,1},{9,13},{13,9},{2,6},{6,2},{1... | collective-permute-start | bytes 393224 | tf_op jit(solution)/shard_map/ppermute | solution.py:497
  98.7 2.6 %collective-permute-start.30 = (bf16[256,256]{1,0:T(8,128)(2,1)S(1)}, bf16[256,256]{1,0:T(8,128)(2,1)S(1)}, u32[]{:S(2)}, u32[]{:S(2)}) collective-permute-start(bf16[256,256]{1,0:T(8,128)(2,1)S(1)} %get-tuple-element.99), channel_id=1, source_target_pairs={{0,1},{1,0},{2,3},{3,2},{4,8},{5,9},{6,10},{7,11},{8,4},{9,5},{10,... | collective-permute-start | bytes 393224 | tf_op jit(solution)/shard_map/ppermute | solution.py:511
  98.9 7.8 %collective-permute-start.28 = (bf16[272,256]{1,0:T(8,128)(2,1)S(1)}, bf16[272,256]{1,0:T(8,128)(2,1)S(1)}, u32[]{:S(2)}, u32[]{:S(2)}) collective-permute-start(bf16[272,256]{1,0:T(8,128)(2,1)S(1)} %get-tuple-element.95), channel_id=1, source_target_pairs={{0,4},{4,0},{8,12},{12,8},{1,5},{5,1},{9,13},{13,9},{2,6},{6,2},{1... | collective-permute-start | bytes 417800 | tf_op jit(solution)/shard_map/ppermute | solution.py:497
  101.3 7.7 %collective-permute-start.29 = (bf16[256,256]{1,0:T(8,128)(2,1)S(1)}, bf16[256,256]{1,0:T(8,128)(2,1)S(1)}, u32[]{:S(2)}, u32[]{:S(2)}) collective-permute-start(bf16[256,256]{1,0:T(8,128)(2,1)S(1)} %get-tuple-element.98), channel_id=1, source_target_pairs={{0,1},{1,0},{2,3},{3,2},{4,8},{5,9},{6,10},{7,11},{8,4},{9,5},{10,... | collective-permute-start | bytes 393224 | tf_op jit(solution)/shard_map/ppermute | solution.py:511
  101.3 8.3 %collective-permute-start.31 = (bf16[256,256]{1,0:T(8,128)(2,1)S(1)}, bf16[256,256]{1,0:T(8,128)(2,1)S(1)}, u32[]{:S(2)}, u32[]{:S(2)}) collective-permute-start(bf16[256,256]{1,0:T(8,128)(2,1)S(1)} %shard_map.113), channel_id=1, source_target_pairs={{0,4},{4,0},{8,12},{12,8},{1,5},{5,1},{9,13},{13,9},{2,6},{6,2},{1... | collective-permute-start | bytes 393224 | tf_op jit(solution)/shard_map/ppermute | solution.py:497
